TPU v7x, 32 devices: a whole 2x2x4 slice. The times are simulated.
32 devices in a mesh: dp: 4 (over x, core), expert: 8 (over z, y).
Axes of the slice: x: 2, y: 2, z: 4, core: 2. Of those that a mesh axis runs over, the one named last changes fastest.
Arguments:
- tokens: bfloat16 [1536, 4096], P('expert', 'dp'), may hold values from -6 to 6
- routes: int32 [1536, 2], P('expert'), may hold values from 0 to 7, all different within a row; in each aligned block of 192 rows (0 to 191, 192 to 383, ...) at most 60 rows name the same one
- route_weight: float32 [1536, 2], P('expert'), may hold values from 0.2 to 1
- cotangent: bfloat16 [1536, 4096], P('expert', 'dp'), may hold values from -4 to 4
- w_in: bfloat16 [8, 4096, 2048], P('expert', 'dp'), may hold values from -0.09375 to 0.09375
- w_out: bfloat16 [8, 1024, 4096], P('expert', None, 'dp'), may hold values from -0.1875 to 0.1875
Outputs:
- mixed: bfloat16 [1536, 4096], P('expert', 'dp')
- grad_tokens: bfloat16 [1536, 4096], P('expert', 'dp')
- grad_in: bfloat16 [8, 4096, 2048], P('expert', 'dp')
- grad_out: bfloat16 [8, 1024, 4096], P('expert', None, 'dp')
Inputs may be any that keep to these rules, and one draw needn't show every extreme that they name: `routes`: each row names 2 different experts. Among the 192 rows of one index of the expert axis no expert is named more than 60 times, and in every draw some expert is named exactly 60 times by such a block.
All inputs are finite; a program needn't handle non-finite values.
Results may differ from a plain program's by a relative error of at most 0.0065.
Values may be sent and summed in bfloat16 or wider, within the bound.
No kernel may reach another device: no remote copies, remote signals or barrier semaphores. Data moves between devices by JAX's collectives and lax.ppermute only.
A program may use at most 64 MiB of HBM per device.

v0:
```python
import jax
import jax.numpy as jnp
from jax import lax
from jax.sharding import PartitionSpec as P


def activate(pre_act, grad_hidden):
    units = pre_act.shape[1] // 2
    gate_part = pre_act[:, :units]
    up_part = pre_act[:, units:]
    sigmoid_gate = jax.nn.sigmoid(gate_part)
    silu_gate = gate_part * sigmoid_gate
    hidden = (silu_gate * up_part).astype(jnp.bfloat16)
    grad_gate = grad_hidden * up_part * sigmoid_gate * (1.0 + gate_part * (1.0 - sigmoid_gate))
    grad_up = grad_hidden * silu_gate
    return (hidden, jnp.concatenate([grad_gate, grad_up], axis=1).astype(jnp.bfloat16))


def per_device(tokens, routes, route_weight, cotangent, w_in, w_out):
    tok_rows, features = tokens.shape
    top_count = routes.shape[1]
    n_expert = lax.axis_size("expert")
    local_experts = w_in.shape[0]
    hidden_units = w_out.shape[1]
    experts = n_expert * local_experts
    capacity = tok_rows * top_count * 5 // (4 * experts)
    slot_count = experts * capacity
    flat_routes = routes.reshape(-1)
    onehot = (flat_routes[:, None] == jnp.arange(experts, dtype=jnp.int32)[None, :]).astype(
        jnp.int32
    )
    slot_rank = jnp.sum((jnp.cumsum(onehot, axis=0) - onehot) * onehot, axis=1)
    target = flat_routes * capacity + slot_rank
    placing = (target[None, :] == jnp.arange(slot_count, dtype=jnp.int32)[:, None]).astype(
        jnp.bfloat16
    )
    choose_token = jnp.sum(placing.reshape(slot_count, tok_rows, top_count), axis=2)
    scaled_grads = (route_weight[:, :, None] * cotangent[:, None, :].astype(jnp.float32)).astype(
        jnp.bfloat16
    )
    scaled_grads = scaled_grads.reshape(tok_rows * top_count, features)
    send_rows = jnp.dot(choose_token, tokens, preferred_element_type=jnp.float32).astype(
        jnp.bfloat16
    )
    send_grads = jnp.dot(placing, scaled_grads, preferred_element_type=jnp.float32).astype(
        jnp.bfloat16
    )
    send_rows = send_rows.reshape(n_expert, local_experts * capacity, features)
    send_grads = send_grads.reshape(n_expert, local_experts * capacity, features)
    routed_rows, routed_grads = (
        lax.all_to_all(send_rows, "expert", split_axis=0, concat_axis=0, tiled=True),
        lax.all_to_all(send_grads, "expert", split_axis=0, concat_axis=0, tiled=True),
    )
    rows_four = routed_rows.reshape(n_expert, local_experts, capacity, features)
    grads_four = routed_grads.reshape(n_expert, local_experts, capacity, features)
    total_rows = n_expert * local_experts * capacity
    pre_part = jnp.einsum("secd,edf->secf", rows_four, w_in, preferred_element_type=jnp.float32)
    back_part = jnp.einsum("secd,efd->secf", grads_four, w_out, preferred_element_type=jnp.float32)
    pre_flat = pre_part.reshape(total_rows, 2 * hidden_units)
    back_flat = back_part.reshape(total_rows, hidden_units)
    pre_share, back_share = (
        lax.psum_scatter(pre_flat, "dp", scatter_dimension=0, tiled=True),
        lax.psum_scatter(back_flat, "dp", scatter_dimension=0, tiled=True),
    )
    hidden_share, both_share = activate(pre_share, back_share)
    hidden, grad_both = (
        lax.all_gather(hidden_share, "dp", axis=0, tiled=True),
        lax.all_gather(both_share, "dp", axis=0, tiled=True),
    )
    hidden_four = hidden.reshape(n_expert, local_experts, capacity, hidden_units)
    both_four = grad_both.reshape(n_expert, local_experts, capacity, 2 * hidden_units)
    out_rows = jnp.einsum(
        "secf,efd->secd", hidden_four, w_out, preferred_element_type=jnp.float32
    ).astype(jnp.bfloat16)
    grad_rows = jnp.einsum(
        "secf,edf->secd", both_four, w_in, preferred_element_type=jnp.float32
    ).astype(jnp.bfloat16)
    grad_out = jnp.einsum(
        "secf,secd->efd", hidden_four, grads_four, preferred_element_type=jnp.float32
    ).astype(jnp.bfloat16)
    grad_in = jnp.einsum(
        "secd,secf->edf", rows_four, both_four, preferred_element_type=jnp.float32
    ).astype(jnp.bfloat16)
    home_out, home_grad = (
        lax.all_to_all(
            out_rows.reshape(n_expert, local_experts * capacity, features),
            "expert",
            split_axis=0,
            concat_axis=0,
            tiled=True,
        ),
        lax.all_to_all(
            grad_rows.reshape(n_expert, local_experts * capacity, features),
            "expert",
            split_axis=0,
            concat_axis=0,
            tiled=True,
        ),
    )
    route_out = jnp.dot(
        placing.T, home_out.reshape(slot_count, features), preferred_element_type=jnp.float32
    )
    route_out = route_out.reshape(tok_rows, top_count, features)
    mixed = jnp.sum(route_weight[:, :, None] * route_out, axis=1).astype(jnp.bfloat16)
    grad_tokens = jnp.dot(
        choose_token.T, home_grad.reshape(slot_count, features), preferred_element_type=jnp.float32
    )
    return (mixed, grad_tokens.astype(jnp.bfloat16), grad_in, grad_out)


def solution(mesh):
    placed = (
        P("expert", "dp"),
        P("expert", None),
        P("expert", None),
        P("expert", "dp"),
        P("expert", "dp", None),
        P("expert", None, "dp"),
    )
    return jax.shard_map(
        per_device,
        mesh=mesh,
        in_specs=placed,
        out_specs=(
            P("expert", "dp"),
            P("expert", "dp"),
            P("expert", "dp", None),
            P("expert", None, "dp"),
        ),
        check_vma=False,
    )
```

profile of v0, /device:TPU:0, one launch (start us, length us, event | category | flops | bytes accessed | tf_op | source)
XLA Modules:
  0.0 233.3 jit_solution(6956831545183078740)
XLA Ops:
  7.2 0.9 copy.24
  8.2 0.1 eq.65
  8.3 0.1 reshape.133
  8.5 0.9 reduce-window.6
  9.3 0.2 slice_reduce_fusion
  9.6 0.1 fusion.31
  9.7 2.6 %mul.77 = f32[192,2,1024]{2,1,0:T(2,128)} broadcast(bf16[192,1024]{1,0:T(8,128)(2,1)} %param.9), dimensions={0,2} | broadcast | bytes 1966080 | tf_op jit(solution)/shard_map/mul | solution.py:38
  12.3 3.1 %mul.78 = f32[384,1024]{1,0:T(8,128)} reshape(f32[192,2,1024]{2,1,0:T(2,128)} %mul.77) | data formatting | bytes 3145728 | tf_op jit(solution)/shard_map/mul | solution.py:38
  15.4 0.1 copy.27
  15.5 0.1 mul.75
  15.7 3.1 %convolution_convert_fusion.1 = bf16[480,1024]{1,0:T(8,128)(2,1)} fusion(f32[384,1024]{1,0:T(8,128)} %mul.78, f32[384]{0:T(512)S(1)} %mul.75, s32[384]{0:T(512)S(1)} %multiply_add_fusion), kind=kOutput, calls=%fused_computation.19 | convolution fusion | flops 378949632 | bytes 2558976 | tf_op jit(solution)/shard_map/dot_general | solution.py:45
  18.8 1.3 reshape.141
  20.2 32.9 %all_to_all.20 = bf16[8,60,1024]{2,1,0:T(8,128)(2,1)S(1)} all-to-all(bf16[8,60,1024]{2,1,0:T(8,128)(2,1)S(1)} %reshape.141), channel_id=1, replica_groups=mesh['dp'=4,'expert'=8] {'expert'}, dimensions={0} | all-to-all | bytes 1966080 | tf_op jit(solution)/shard_map/all_to_all | solution.py:52
  53.0 1.0 copy-done.2
  54.0 2.6 %fusion.12 = f32[8,1,60,1024]{3,2,0,1:T(8,128)} fusion(bf16[8,60,1024]{2,1,0:T(8,128)(2,1)S(1)} %all_to_all.20, bf16[1,1024,1024]{2,1,0:T(8,128)(2,1)S(1)} %copy-done), kind=kOutput, calls=%fused_computation.12 | convolution fusion | flops 1006632960 | bytes 5046272 | tf_op jit(solution)/shard_map/secd,efd->secf/dot_general | solution.py:58
  56.6 2.9 %reshape.142 = f32[480,1024]{1,0:T(8,128)} reshape(f32[8,1,60,1024]{3,2,0,1:T(8,128)} %fusion.12) | data formatting | bytes 3932160 | tf_op jit(solution)/shard_map/reshape | solution.py:60
  59.5 0.0 reduce-scatter.3.cloned.1.call-start
  59.5 0.1 reduce_sum.33
  59.7 0.1 copy.26
  59.7 0.4 copy-done.5
  60.1 0.1 fusion.27
  60.3 0.2 copy-done.4
  60.4 1.4 convolution_convert_fusion
  61.8 1.3 reshape.135
  63.2 28.9 %all_to_all.21 = bf16[8,60,1024]{2,1,0:T(8,128)(2,1)S(1)} all-to-all(bf16[8,60,1024]{2,1,0:T(8,128)(2,1)S(1)} %reshape.135), channel_id=1, replica_groups=mesh['dp'=4,'expert'=8] {'expert'}, dimensions={0} | all-to-all | bytes 1966080 | tf_op jit(solution)/shard_map/all_to_all | solution.py:51
  92.0 1.0 copy-done.3
  93.1 6.5 %fusion.5 = f32[8,1,60,2048]{3,2,0,1:T(8,128)} fusion(bf16[8,60,1024]{2,1,0:T(8,128)(2,1)S(1)} %all_to_all.21, bf16[1,1024,2048]{2,1,0:T(8,128)(2,1)} %param.10), kind=kOutput, calls=%fused_computation.7 | convolution fusion | flops 2013265920 | bytes 9109504 | tf_op jit(solution)/shard_map/secd,edf->secf/dot_general | solution.py:57
  99.6 3.7 %reshape.137 = f32[480,2048]{1,0:T(8,128)} reshape(f32[8,1,60,2048]{3,2,0,1:T(8,128)} %fusion.5) | data formatting | bytes 7864320 | tf_op jit(solution)/shard_map/reshape | solution.py:59
  103.3 0.0 all-gather.2.cloned.1.call-start
  103.4 41.9 %reduce-scatter.3.cloned.1.call-done = f32[120,2048]{1,0:T(8,128)} async-done(((f32[480,2048]{1,0:T(8,128)}), f32[120,2048]{1,0:T(8,128)}) %reduce-scatter.3.cloned.1.call-update) | async-done | bytes 983056 | tf_op jit(solution)/shard_map/reduce_scatter | solution.py:62
  145.3 2.3 multiply_convert_fusion.3
  147.6 0.8 pad_maximum_fusion
  148.5 9.5 %all_gather.6 = bf16[480,1024]{1,0:T(8,128)(2,1)S(1)} all-gather(bf16[120,1024]{1,0:T(8,128)(2,1)} %get-tuple-element.6), channel_id=1, replica_groups=mesh['dp'=4,'expert'=8] {'dp'}, dimensions={0}, use_global_device_ids=true | all-gather | bytes 1228800 | tf_op jit(solution)/shard_map/all_gather | solution.py:67
  158.0 1.2 reshape.138
  159.1 3.4 %fusion.16 = bf16[8,60,1024]{2,1,0:T(8,128)(2,1)} fusion(bf16[8,60,1024]{2,1,0:T(8,128)(2,1)} %reshape.138, bf16[1,1024,1024]{2,1,0:T(8,128)(2,1)S(1)} %copy-done), kind=kOutput, calls=%fused_computation.16 | convolution fusion | flops 1007124480 | bytes 4063232 | tf_op jit(solution)/shard_map/secf,efd->secd/dot_general | solution.py:72
  162.6 5.5 %all-to-all-start.1 = ((bf16[8,60,1024]{2,1,0:T(8,128)(2,1)}), bf16[8,60,1024]{2,1,0:T(8,128)(2,1)S(1)}, u32[]{:S(2)}, u32[]{:S(2)}) async-start(bf16[8,60,1024]{2,1,0:T(8,128)(2,1)} %fusion.16), calls=%async_computation.2 | async-start | bytes 2097152 | tf_op jit(solution)/shard_map/all_to_all | solution.py:85
  168.1 2.4 %all-gather.2.cloned.1.call-done = bf16[480,2048]{1,0:T(8,128)(2,1)} async-done(((bf16[120,2048]{1,0:T(8,128)(2,1)}), bf16[480,2048]{1,0:T(8,128)(2,1)}) %all-gather.2.cloned.1.call-update) | async-done | bytes 1966096 | tf_op jit(solution)/shard_map/all_gather | solution.py:68
  170.5 2.7 %reshape.143 = bf16[8,60,2048]{2,1,0:T(8,128)(2,1)} reshape(bf16[480,2048]{1,0:T(8,128)(2,1)} %all-gather.2.cloned.1.call-done) | data formatting | bytes 3932160 | tf_op jit(solution)/shard_map/reshape.13
  173.2 6.2 %fusion.19 = bf16[8,60,1024]{2,1,0:T(8,128)(2,1)} fusion(bf16[8,60,2048]{2,1,0:T(8,128)(2,1)} %reshape.143, bf16[1,1024,2048]{2,1,0:T(8,128)(2,1)} %param.10), kind=kOutput, calls=%fused_computation.17 | convolution fusion | flops 2013757440 | bytes 7143424 | tf_op jit(solution)/shard_map/secf,edf->secd/dot_general | solution.py:75
  179.4 15.0 %all-to-all-done.1 = bf16[8,60,1024]{2,1,0:T(8,128)(2,1)S(1)} async-done(((bf16[8,60,1024]{2,1,0:T(8,128)(2,1)}), bf16[8,60,1024]{2,1,0:T(8,128)(2,1)S(1)}, u32[]{:S(2)}, u32[]{:S(2)}) %all-to-all-start.1) | async-done | bytes 983072 | tf_op jit(solution)/shard_map/all_to_all | solution.py:85
  194.4 4.2 %all-to-all-start.3 = ((bf16[8,60,1024]{2,1,0:T(8,128)(2,1)}), bf16[8,60,1024]{2,1,0:T(8,128)(2,1)}, u32[]{:S(2)}, u32[]{:S(2)}) async-start(bf16[8,60,1024]{2,1,0:T(8,128)(2,1)} %fusion.19), calls=%async_computation.5 | async-start | bytes 2097152 | tf_op jit(solution)/shard_map/all_to_all | solution.py:92
  198.6 4.2 %fusion.15 = bf16[1,1024,1024]{2,1,0:T(8,128)(2,1)} fusion(bf16[8,60,1024]{2,1,0:T(8,128)(2,1)} %reshape.138, bf16[8,60,1024]{2,1,0:T(8,128)(2,1)} %copy-done.2), kind=kOutput, calls=%fused_computation.13 | convolution fusion | flops 1007681536 | bytes 4063232 | tf_op jit(solution)/shard_map/secf,secd->efd/dot_general | solution.py:78
  202.8 1.1 reshape.147
  203.9 2.8 %multiply_reduce_fusion = bf16[192,1024]{1,0:T(8,128)(2,1)} fusion(bf16[480,1024,1]{1,0,2:T(8,128)(2,1)} %reshape.147, f32[192,2]{0,1:T(2,128)S(1)} %copy-done.6, s32[192,2]{0,1:T(2,128)S(1)} %multiply_add_fusion.1), kind=kOutput, calls=%fused_computation.15 | convolution fusion | flops 378261504 | bytes 1379328 | tf_op jit(solution)/shard_map/dot_general | solution.py:100
  206.7 5.6 %fusion.4 = bf16[1,1024,2048]{2,1,0:T(8,128)(2,1)} fusion(bf16[8,60,1024]{2,1,0:T(8,128)(2,1)} %copy-done.3, bf16[8,60,2048]{2,1,0:T(8,128)(2,1)S(1)} %copy-done.1), kind=kOutput, calls=%fused_computation.6 | convolution fusion | flops 2015363072 | bytes 7143424 | tf_op jit(solution)/shard_map/secd,secf->edf/dot_general | solution.py:81
  212.4 11.9 %all-to-all-done.3 = bf16[8,60,1024]{2,1,0:T(8,128)(2,1)} async-done(((bf16[8,60,1024]{2,1,0:T(8,128)(2,1)}), bf16[8,60,1024]{2,1,0:T(8,128)(2,1)}, u32[]{:S(2)}, u32[]{:S(2)}) %all-to-all-start.3) | async-done | bytes 983072 | tf_op jit(solution)/shard_map/all_to_all | solution.py:92
  224.2 1.4 reshape.144
  225.6 1.1 convolution_convert_fusion.2
  (19 shorter events, 0.2 us)
Async XLA Ops:
  7.2 46.8 %copy-start = (bf16[1,1024,1024]{2,1,0:T(8,128)(2,1)S(1)}, bf16[1,1024,1024]{2,1,0:T(8,128)(2,1)}, u32[]{:S(2)}) copy-start(bf16[1,1024,1024]{2,1,0:T(8,128)(2,1)} %param.11) | copy-start | bytes 6291460
  7.2 96.2 %reduce-scatter.5.cloned.1.call-start = ((), (), s32[]{:S(2)}) async-start(), calls=%async_computation.7 | async-start | bytes 2457600 | tf_op jit(solution)/shard_map/reduce_scatter | solution.py:63
  9.7 5.7 %copy-start.6 = (f32[192,2]{0,1:T(2,128)S(1)}, f32[192,2]{0,1:T(2,128)}, u32[]{:S(2)}) copy-start(f32[192,2]{0,1:T(2,128)} %param.8) | copy-start | bytes 4612
  53.0 1.0 copy-start.2
  59.4 0.7 copy-start.5
  59.4 1.0 copy-start.4
  59.5 85.9 %reduce-scatter.3.cloned.1.call-start = ((), (), s32[]{:S(2)}) async-start(), calls=%async_computation.6 | async-start | bytes 4915200 | tf_op jit(solution)/shard_map/reduce_scatter | solution.py:62
  92.0 1.0 copy-start.3
  103.3 67.2 %all-gather.2.cloned.1.call-start = ((), (), s32[]{:S(2)}) async-start(), calls=%async_computation.8 | async-start | bytes 2457600 | tf_op jit(solution)/shard_map/all_gather | solution.py:68
  162.6 31.8 %all-to-all-start.1 = ((bf16[8,60,1024]{2,1,0:T(8,128)(2,1)}), bf16[8,60,1024]{2,1,0:T(8,128)(2,1)S(1)}, u32[]{:S(2)}, u32[]{:S(2)}) async-start(bf16[8,60,1024]{2,1,0:T(8,128)(2,1)} %fusion.16), calls=%async_computation.2 | async-start | bytes 2097152 | tf_op jit(solution)/shard_map/all_to_all | solution.py:85
  194.4 29.9 %all-to-all-start.3 = ((bf16[8,60,1024]{2,1,0:T(8,128)(2,1)}), bf16[8,60,1024]{2,1,0:T(8,128)(2,1)}, u32[]{:S(2)}, u32[]{:S(2)}) async-start(bf16[8,60,1024]{2,1,0:T(8,128)(2,1)} %fusion.19), calls=%async_computation.5 | async-start | bytes 2097152 | tf_op jit(solution)/shard_map/all_to_all | solution.py:92
  203.9 2.8 %copy-start.1 = (bf16[8,60,2048]{2,1,0:T(8,128)(2,1)S(1)}, bf16[8,60,2048]{2,1,0:T(8,128)(2,1)}, u32[]{:S(2)}) copy-start(bf16[8,60,2048]{2,1,0:T(8,128)(2,1)} %reshape.143) | copy-start | bytes 5898244
Sparse Core Ops, SparseCore 0:
  59.6 29.6 reduce-scatter.4
  103.4 41.8 reduce-scatter.2
  148.6 21.8 all-gather.1
where the time goes:
time: 234 us; the launch traced here: 233 us
  blocking collectives  71.2 us (30%)
  waiting for transfers between devices  71.2 us (30%)
  matrix products  37 us (16%)
  local copies, waits for them, and re-layouts  25.8 us (11%)
  between operations  13.9 us (6%)
  starting transfers between devices  9.88 us (4%)
  other arithmetic  4.29 us (2%)
    reduce_scatter x1, waiting for transfers between devices, per_device(): lax.psum_scatter(pre_flat, 'dp', scatter_dimension=0, tiled=True)  41.9 us
    all_to_all x1, blocking collectives, per_device(): lax.all_to_all(send_grads, 'expert', split_axis=0, concat_axis=0, tiled=T...  32.9 us
    all_to_all x1, blocking collectives, per_device(): lax.all_to_all(send_rows, 'expert', split_axis=0, concat_axis=0, tiled=True)  28.9 us
    all_to_all x1, waiting for transfers between devices, per_device(): lax.all_to_all(out_rows.reshape(n_expert, local_experts * capacity, featu...  15 us
    all_to_all x1, waiting for transfers between devices, per_device(): lax.all_to_all(grad_rows.reshape(n_expert, local_experts * capacity, feat...  11.9 us
    all_gather x1, blocking collectives, per_device(): lax.all_gather(hidden_share, 'dp', axis=0, tiled=True)  9.48 us
    dot_general x1, matrix products, per_device(): jnp.einsum('secd,edf->secf', rows_four, w_in, preferred_element_type=jnp....  6.54 us
    dot_general x1, matrix products, per_device(): jnp.einsum('secf,edf->secd', both_four, w_in, preferred_element_type=jnp....  6.22 us
  transfers between devices with their start and end apart: 5, of which 4 were waited for; matrix products, arithmetic and copies ran while one was open for 17% of the time, Pallas kernels for 0%

commit v1 on v0

--- a/solution.py
+++ b/solution.py
@@ -1,7 +1,423 @@
 import jax
 import jax.numpy as jnp
 from jax import lax
+from jax.experimental import pallas as pl
+from jax.experimental.pallas import tpu as pltpu
 from jax.sharding import PartitionSpec as P
+
+BF = jnp.bfloat16
+F32 = jnp.float32
+VMEM_LIMIT = 48 * 1024 * 1024
+
+
+def dot(a, b):
+    return lax.dot_general(a, b, (((1,), (0,)), ((), ())), preferred_element_type=F32)
+
+
+def dot_t(a, b):
+    return lax.dot_general(a, b, (((1,), (1,)), ((), ())), preferred_element_type=F32)
+
+
+def t_dot(a, b):
+    return lax.dot_general(a, b, (((0,), (0,)), ((), ())), preferred_element_type=F32)
+
+
+def iota(shape, dim):
+    return lax.broadcasted_iota(jnp.int32, shape, dim)
+
+
+def padded(capacity):
+    return -(-capacity // 16) * 16
+
+
+def prep_kernel(capacity, ids, tokens, routes, weight, cotangent, *outs):
+    count = len(outs)
+    rows = tokens.shape[0]
+    me = ids[0]
+    eye = iota((rows, rows), 0) == iota((rows, rows), 1)
+
+    def lane(column, zero):
+        return jnp.sum(jnp.where(eye, column, zero), axis=0, keepdims=True)
+
+    first, second = lane(routes[:, 0:1], 0), lane(routes[:, 1:2], 0)
+    w_first, w_second = lane(weight[:, 0:1], 0.0), lane(weight[:, 1:2], 0.0)
+    expert = iota((count, rows), 0) ^ me
+    hit_first, hit_second = first == expert, second == expert
+    named = hit_first | hit_second
+    w_named = jnp.where(hit_first, w_first, 0.0) + jnp.where(hit_second, w_second, 0.0)
+    before = (iota((rows, rows), 0) < iota((rows, rows), 1)).astype(BF)
+    rank = dot(named.astype(F32).astype(BF), before).astype(jnp.int32)
+    key = jnp.where(named, rank, -2 * capacity)
+    slot = iota((2 * capacity, rows), 0)
+    for s, out in enumerate(outs):
+        row_key = key[s : s + 1, :]
+        pick_token = (row_key == slot).astype(F32)
+        pick_grad = (row_key + capacity == slot).astype(F32)
+        scale = jnp.sum(pick_grad * w_named[s : s + 1, :], axis=1, keepdims=True)
+        scale = scale + (slot[:, 0:1] < capacity).astype(F32)
+        picked = dot(pick_token.astype(BF), tokens[...]) + dot(pick_grad.astype(BF), cotangent[...])
+        out[...] = (scale * picked).astype(BF)
+
+
+def prep(ids, tokens, routes, weight, cotangent, count, capacity):
+    rows, features = tokens.shape
+    whole = pl.BlockSpec(memory_space=pltpu.VMEM)
+    return pl.pallas_call(
+        lambda *refs: prep_kernel(capacity, *refs),
+        out_shape=[jax.ShapeDtypeStruct((2 * capacity, features), BF)] * count,
+        in_specs=[pl.BlockSpec(memory_space=pltpu.SMEM)] + [whole] * 4,
+        out_specs=[whole] * count,
+        compiler_params=pltpu.CompilerParams(vmem_limit_bytes=VMEM_LIMIT),
+        cost_estimate=pl.CostEstimate(
+            flops=8 * count * capacity * rows * features,
+            bytes_accessed=4 * (rows + count * capacity) * features,
+            transcendentals=0,
+        ),
+        name="prep",
+    )(ids, tokens, routes, weight, cotangent)
+
+
+def up_kernel(count, capacity, ids, *refs):
+    blocks, (w_gate, w_up, w_out, row_out, grad_out, send, keep) = refs[:count], refs[count:]
+    step = pl.program_id(0)
+    pad = padded(capacity)
+
+    @pl.when(step == 0)
+    def _():
+        spot = iota((2 * pad, 2 * capacity), 0)
+        col = iota((2 * pad, 2 * capacity), 1)
+        target = jnp.where(col < capacity, col, col + pad - capacity)
+        spread = (spot == target).astype(F32).astype(BF)
+        for i, block in enumerate(blocks):
+            laid = dot(spread, block[...]).astype(BF)
+            row_out[pl.ds(i * pad, pad), :] = laid[:pad]
+            grad_out[pl.ds(i * pad, pad), :] = laid[pad:]
+
+    gate = dot(row_out[...], w_gate[...])
+    up = dot(row_out[...], w_up[...])
+    back = dot_t(grad_out[...], w_out[...])
+    width = gate.shape[1]
+
+    @pl.when(step < 2)
+    def _():
+        send[:, 0:width] = gate.astype(BF)
+        send[:, width : 2 * width] = up.astype(BF)
+        send[:, 2 * width :] = back.astype(BF)
+
+    @pl.when(step >= 2)
+    def _():
+        keep[:, 0:width] = gate
+        keep[:, width : 2 * width] = up
+        keep[:, 2 * width :] = back
+
+
+def up_step(ids, blocks, w_in, w_out, capacity):
+    features, both_units = w_in.shape
+    units = both_units // 2
+    width = units // 4
+    count = len(blocks)
+    pad = padded(capacity)
+    rows = count * pad
+
+    def tile(step, ids):
+        half = jnp.where(step < 2, 1 - ids[1], ids[1])
+        return half * 2 + step % 2
+
+    return pl.pallas_call(
+        lambda *refs: up_kernel(count, capacity, *refs),
+        grid_spec=pltpu.PrefetchScalarGridSpec(
+            num_scalar_prefetch=1,
+            grid=(4,),
+            in_specs=[pl.BlockSpec((2 * capacity, features), lambda j, ids: (0, 0))] * count
+            + [
+                pl.BlockSpec((features, width), lambda j, ids: (0, tile(j, ids))),
+                pl.BlockSpec((features, width), lambda j, ids: (0, 4 + tile(j, ids))),
+                pl.BlockSpec((width, features), lambda j, ids: (tile(j, ids), 0)),
+            ],
+            out_specs=[
+                pl.BlockSpec((rows, features), lambda j, ids: (0, 0)),
+                pl.BlockSpec((rows, features), lambda j, ids: (0, 0)),
+                pl.BlockSpec((rows, 3 * width), lambda j, ids: (0, jnp.minimum(j, 1))),
+                pl.BlockSpec((rows, 3 * width), lambda j, ids: (0, jnp.maximum(j - 2, 0))),
+            ],
+        ),
+        out_shape=[
+            jax.ShapeDtypeStruct((rows, features), BF),
+            jax.ShapeDtypeStruct((rows, features), BF),
+            jax.ShapeDtypeStruct((rows, 6 * width), BF),
+            jax.ShapeDtypeStruct((rows, 6 * width), F32),
+        ],
+        compiler_params=pltpu.CompilerParams(vmem_limit_bytes=VMEM_LIMIT),
+        cost_estimate=pl.CostEstimate(
+            flops=6 * rows * features * units,
+            bytes_accessed=6 * features * units + 12 * rows * features,
+            transcendentals=0,
+        ),
+        name="up",
+    )(ids, *blocks, w_in, w_in, w_out)
+
+
+def act_kernel(total, other, out):
+    width = total.shape[1] // 6
+    for j in range(2):
+        base = 3 * width * j
+        gate, up, back = (
+            total[:, base + i * width : base + (i + 1) * width]
+            + other[:, base + i * width : base + (i + 1) * width].astype(F32)
+            for i in range(3)
+        )
+        sigmoid = jax.nn.sigmoid(gate)
+        silu = gate * sigmoid
+        out[:, base : base + width] = (silu * up).astype(BF)
+        out[:, base + width : base + 2 * width] = (
+            back * up * sigmoid * (1.0 + gate * (1.0 - sigmoid))
+        ).astype(BF)
+        out[:, base + 2 * width : base + 3 * width] = (back * silu).astype(BF)
+
+
+def act_step(total, other):
+    whole = pl.BlockSpec(memory_space=pltpu.VMEM)
+    return pl.pallas_call(
+        act_kernel,
+        out_shape=jax.ShapeDtypeStruct(total.shape, BF),
+        in_specs=[whole] * 2,
+        out_specs=whole,
+        compiler_params=pltpu.CompilerParams(vmem_limit_bytes=VMEM_LIMIT),
+        cost_estimate=pl.CostEstimate(
+            flops=4 * total.size, bytes_accessed=8 * total.size, transcendentals=total.size
+        ),
+        name="act",
+    )(total, other)
+
+
+def down_kernel(count, capacity, ids, own, core, w_in, w_out, *outs):
+    pad = padded(capacity)
+    units = w_out.shape[0]
+    width = units // 4
+    out_rows = grad_rows = None
+    for held, half in ((own, ids[1]), (core, 1 - ids[1])):
+        for j in range(2):
+            base = 3 * width * j
+            at = pl.multiple_of((half * 2 + j) * width, width)
+            at_up = pl.multiple_of(units + (half * 2 + j) * width, width)
+            a = dot(held[:, base : base + width], w_out[pl.ds(at, width), :])
+            b = dot_t(held[:, base + width : base + 2 * width], w_in[:, pl.ds(at, width)])
+            c = dot_t(held[:, base + 2 * width : base + 3 * width], w_in[:, pl.ds(at_up, width)])
+            out_rows = a if out_rows is None else out_rows + a
+            grad_rows = b + c if grad_rows is None else grad_rows + (b + c)
+    spot = iota((2 * capacity, pad), 0)
+    col = iota((2 * capacity, pad), 1)
+    pack_out = (spot == jnp.where(col < capacity, col, -1)).astype(F32).astype(BF)
+    pack_grad = (spot - capacity == jnp.where(col < capacity, col, -capacity - 1)).astype(F32).astype(BF)
+    out_rows, grad_rows = out_rows.astype(BF), grad_rows.astype(BF)
+    for i, out in enumerate(outs):
+        out[...] = (
+            dot(pack_out, out_rows[i * pad : (i + 1) * pad])
+            + dot(pack_grad, grad_rows[i * pad : (i + 1) * pad])
+        ).astype(BF)
+
+
+def down_step(ids, own, core, w_in, w_out, count, capacity):
+    features, both_units = w_in.shape
+    units = both_units // 2
+    rows = own.shape[0]
+    width = features // 4
+    return pl.pallas_call(
+        lambda *refs: down_kernel(count, capacity, *refs),
+        grid_spec=pltpu.PrefetchScalarGridSpec(
+            num_scalar_prefetch=1,
+            grid=(4,),
+            in_specs=[
+                pl.BlockSpec(own.shape, lambda j, ids: (0, 0)),
+                pl.BlockSpec(core.shape, lambda j, ids: (0, 0)),
+                pl.BlockSpec((width, both_units), lambda j, ids: (j, 0)),
+                pl.BlockSpec((units, width), lambda j, ids: (0, j)),
+            ],
+            out_specs=[pl.BlockSpec((2 * capacity, width), lambda j, ids: (0, j))] * count,
+        ),
+        out_shape=[jax.ShapeDtypeStruct((2 * capacity, features), BF)] * count,
+        compiler_params=pltpu.CompilerParams(vmem_limit_bytes=VMEM_LIMIT),
+        cost_estimate=pl.CostEstimate(
+            flops=6 * rows * features * units,
+            bytes_accessed=6 * features * units + 12 * rows * features,
+            transcendentals=0,
+        ),
+        name="down",
+    )(ids, own, core, w_in, w_out)
+
+
+def grads_kernel(chunks, ids, *refs):
+    groups = [refs[5 * i : 5 * i + 5] for i in range(chunks)]
+    grad_in, grad_out = refs[5 * chunks :]
+    step = pl.program_id(0)
+    width = groups[0][2].shape[1] // 6
+    units = grad_in.shape[1] // 2
+    for which, half in ((2, ids[1]), (3, 1 - ids[1])):
+        for j in range(2):
+            base = 3 * width * j
+            for part in range(2):
+                total = None
+                for group in groups:
+                    term = t_dot(
+                        group[0][...],
+                        group[which][:, base + (part + 1) * width : base + (part + 2) * width],
+                    )
+                    total = term if total is None else total + term
+                at = pl.multiple_of(part * units + (half * 2 + j) * width, width)
+                grad_in[:, pl.ds(at, width)] = total.astype(BF)
+    for at_step in range(4):
+
+        @pl.when(step == at_step)
+        def _():
+            which, j = 2 + at_step // 2, at_step % 2
+            base = 3 * width * j
+            total = None
+            for group in groups:
+                term = t_dot(group[which][:, base : base + width], group[4][...])
+                total = term if total is None else total + term
+            grad_out[...] = total.astype(BF)
+
+
+def grads_step(ids, groups, units):
+    features = groups[0][0].shape[1]
+    f_tile, u_tile = features // 4, units // 4
+    operands, specs = [], []
+    rows_all = 0
+    for rows, grads, own, core in groups:
+        operands += [rows, own, core, grads]
+        n = rows.shape[0]
+        rows_all += n
+        specs += [
+            pl.BlockSpec((n, f_tile), lambda j, ids: (0, j)),
+            pl.BlockSpec(own.shape, lambda j, ids: (0, 0)),
+            pl.BlockSpec(core.shape, lambda j, ids: (0, 0)),
+            pl.BlockSpec(grads.shape, lambda j, ids: (0, 0)),
+        ]
+
+    def unit_tile(j, ids):
+        return jnp.where(j < 2, ids[1] * 2 + j, (1 - ids[1]) * 2 + j - 2)
+
+    def kernel(ids, *refs):
+        laid = []
+        for i in range(len(groups)):
+            rows, own, core, grads = refs[4 * i : 4 * i + 4]
+            laid += [rows, rows, own, core, grads]
+        grads_kernel(len(groups), ids, *laid, *refs[4 * len(groups) :])
+
+    return pl.pallas_call(
+        kernel,
+        grid_spec=pltpu.PrefetchScalarGridSpec(
+            num_scalar_prefetch=1,
+            grid=(4,),
+            in_specs=specs,
+            out_specs=[
+                pl.BlockSpec((f_tile, 2 * units), lambda j, ids: (j, 0)),
+                pl.BlockSpec((u_tile, features), lambda j, ids: (unit_tile(j, ids), 0)),
+            ],
+        ),
+        out_shape=[
+            jax.ShapeDtypeStruct((features, 2 * units), BF),
+            jax.ShapeDtypeStruct((units, features), BF),
+        ],
+        compiler_params=pltpu.CompilerParams(vmem_limit_bytes=VMEM_LIMIT),
+        cost_estimate=pl.CostEstimate(
+            flops=6 * rows_all * features * units,
+            bytes_accessed=6 * features * units + 12 * rows_all * features,
+            transcendentals=0,
+        ),
+        name="grads",
+    )(ids, *operands)
+
+
+def final_kernel(capacity, ids, routes, weight, *refs):
+    homes, (mixed, grad_tokens) = refs[:-2], refs[-2:]
+    rows = routes.shape[0]
+    me = ids[0]
+    count = len(homes)
+    first, second = routes[:, 0:1], routes[:, 1:2]
+    expert = iota((rows, count), 1) ^ me
+    hit_first, hit_second = first == expert, second == expert
+    named = hit_first | hit_second
+    w_named = jnp.where(hit_first, weight[:, 0:1], 0.0) + jnp.where(hit_second, weight[:, 1:2], 0.0)
+    before = (iota((rows, rows), 1) < iota((rows, rows), 0)).astype(BF)
+    rank = dot(before, named.astype(F32).astype(BF)).astype(jnp.int32)
+    key = jnp.where(named, rank, -2 * capacity)
+    slot = iota((rows, 2 * capacity), 1)
+    total_out = total_grad = None
+    for s, home in enumerate(homes):
+        column = key[:, s : s + 1]
+        pick_out = (column == slot).astype(F32).astype(BF)
+        pick_grad = (column + capacity == slot).astype(F32).astype(BF)
+        out = w_named[:, s : s + 1] * dot(pick_out, home[...])
+        grad = dot(pick_grad, home[...])
+        total_out = out if total_out is None else total_out + out
+        total_grad = grad if total_grad is None else total_grad + grad
+    mixed[...] = total_out.astype(BF)
+    grad_tokens[...] = total_grad.astype(BF)
+
+
+def final(ids, routes, weight, homes, capacity):
+    rows = routes.shape[0]
+    features = homes[0].shape[1]
+    width = features // 4
+    count = len(homes)
+    return pl.pallas_call(
+        lambda *refs: final_kernel(capacity, *refs),
+        grid_spec=pltpu.PrefetchScalarGridSpec(
+            num_scalar_prefetch=1,
+            grid=(4,),
+            in_specs=[
+                pl.BlockSpec(routes.shape, lambda j, ids: (0, 0)),
+                pl.BlockSpec(weight.shape, lambda j, ids: (0, 0)),
+            ]
+            + [pl.BlockSpec((2 * capacity, width), lambda j, ids: (0, j))] * count,
+            out_specs=[pl.BlockSpec((rows, width), lambda j, ids: (0, j))] * 2,
+        ),
+        out_shape=[jax.ShapeDtypeStruct((rows, features), BF)] * 2,
+        compiler_params=pltpu.CompilerParams(vmem_limit_bytes=VMEM_LIMIT),
+        cost_estimate=pl.CostEstimate(
+            flops=8 * count * capacity * rows * features,
+            bytes_accessed=4 * (rows + count * capacity) * features,
+            transcendentals=0,
+        ),
+        name="final",
+    )(ids, routes, weight, *homes)
+
+
+def per_device_chunked(tokens, routes, route_weight, cotangent, w_in, w_out):
+    tok_rows = tokens.shape[0]
+    top_count = routes.shape[1]
+    n_expert = lax.axis_size("expert")
+    n_dp = lax.axis_size("dp")
+    capacity = tok_rows * top_count * 5 // (4 * n_expert)
+    w_in, w_out = w_in[0], w_out[0]
+    units = w_out.shape[0]
+    ids = jnp.stack([lax.axis_index("expert"), lax.axis_index("dp") % 2]).astype(jnp.int32)
+
+    def across(x, s):
+        return lax.ppermute(x, "expert", [(i, i ^ s) for i in range(n_expert)]) if s else x
+
+    def beside(x, s):
+        return lax.ppermute(x, "dp", [(i, i ^ s) for i in range(n_dp)])
+
+    half, quarter = n_expert // 2, n_expert // 4
+    plan = [list(range(half)), list(range(half, half + quarter)), list(range(half + quarter, n_expert))]
+    sent = prep(ids, tokens, routes, route_weight, cotangent, n_expert, capacity)
+    homes = [None] * n_expert
+    groups = []
+    for sources in plan:
+        blocks = [across(sent[s], s) for s in sources]
+        rows, grads, send, keep = up_step(ids, blocks, w_in, w_out, capacity)
+        total = keep + beside(send, 1).astype(F32)
+        own = act_step(total, beside(total.astype(BF), 2))
+        core = beside(own, 1)
+        groups.append((rows, grads, own, core))
+        back = down_step(ids, own, core, w_in, w_out, len(sources), capacity)
+        for s, block in zip(sources, back):
+            homes[s] = across(block, s)
+    grad_in, grad_out = grads_step(ids, groups, units)
+    mixed, grad_tokens = final(ids, routes, route_weight, homes, capacity)
+    return mixed, grad_tokens, grad_in[None], grad_out[None]
 
 
 def activate(pre_act, grad_hidden):
@@ -117,8 +533,10 @@
         P("expert", "dp", None),
         P("expert", None, "dp"),
     )
+    sizes = dict(mesh.shape)
+    chunked = sizes["dp"] == 4 and sizes["expert"] in (4, 8)
     return jax.shard_map(
-        per_device,
+        per_device_chunked if chunked else per_device,
         mesh=mesh,
         in_specs=placed,
         out_specs=(

time: 234 us -> 181 us (0.77)
  blocking collectives: 71.2 us -> 0 us
  Pallas kernels: 0 us -> 51.5 us
  matrix products: 37 us -> 0 us
  starting transfers between devices: 9.88 us -> 40.1 us
  local copies, waits for them, and re-layouts: 25.8 us -> 3.58 us
  between operations: 13.9 us -> 0.85 us
  waiting for transfers between devices: 71.2 us -> 83.8 us
  other arithmetic: 4.29 us -> 0.54 us
    ppermute x0 -> x23, waiting for transfers between devices: none -> 83.8 us  [the longest x14 51.6 us: across(): lax.ppermute(x, 'expert', [(i, i ^ s) for i in range(n_expert)])]
    all_to_all x2 -> x0, blocking collectives: 61.7 us -> none  [the longest x1 32.9 us: per_device(): lax.all_to_all(send_grads, 'expert', split_axis=0, concat_axis=0, tiled=T...]
    pallas_call x0 -> x12, Pallas kernels: none -> 51.5 us  [the longest x3 17.8 us: down_step(): pl.pallas_call(lambda *refs: down_kernel(count, capacity, *refs), grid_sp...]
    reduce_scatter x2 -> x0, waiting for transfers between devices: 41.9 us -> none  [the longest x1 41.9 us: per_device(): lax.psum_scatter(pre_flat, 'dp', scatter_dimension=0, tiled=True)]
    ppermute x0 -> x23, starting transfers between devices: none -> 40.1 us  [the longest x14 35.9 us: across(): lax.ppermute(x, 'expert', [(i, i ^ s) for i in range(n_expert)])]
    dot_general x10 -> x0, matrix products: 37 us -> none  [the longest x1 6.54 us: per_device(): jnp.einsum('secd,edf->secf', rows_four, w_in, preferred_element_type=jnp....]
    all_to_all x2 -> x0, waiting for transfers between devices: 26.9 us -> none  [the longest x1 15 us: per_device(): lax.all_to_all(out_rows.reshape(n_expert, local_experts * capacity, featu...]
    reshape x7 -> x0, local copies, waits for them, and re-layouts: 11.9 us -> none  [the longest x1 3.7 us: per_device(): pre_flat = pre_part.reshape(total_rows, 2 * hidden_units)]
  transfers between devices with their start and end apart: 5 -> 23, of which waited for: 4 -> 13; matrix products, arithmetic and copies ran while one was open for 17% -> 0% of each run, Pallas kernels for 0% -> 21%
where the time goes in v1:
time: 181 us; the launch traced here: 180 us
  waiting for transfers between devices  83.8 us (46%)
  Pallas kernels  51.5 us (28%)
  starting transfers between devices  40.1 us (22%)
  local copies, waits for them, and re-layouts  3.58 us (2%)
    ppermute x14, waiting for transfers between devices, across(): lax.ppermute(x, 'expert', [(i, i ^ s) for i in range(n_expert)])  51.6 us
    ppermute x14, starting transfers between devices, across(): lax.ppermute(x, 'expert', [(i, i ^ s) for i in range(n_expert)])  35.9 us
    ppermute x9, waiting for transfers between devices, beside(): return lax.ppermute(x, 'dp', [(i, i ^ s) for i in range(n_dp)])  32.2 us
    pallas_call x3, Pallas kernels, down_step(): pl.pallas_call(lambda *refs: down_kernel(count, capacity, *refs), grid_sp...  17.8 us
    pallas_call x3, Pallas kernels, up_step(): pl.pallas_call(lambda *refs: up_kernel(count, capacity, *refs), grid_spec...  16.2 us
    pallas_call x1, Pallas kernels, grads_step(): pl.pallas_call(kernel, grid_spec=pltpu.PrefetchScalarGridSpec(num_scalar_...  8.76 us
    pallas_call x1, Pallas kernels, final(): pl.pallas_call(lambda *refs: final_kernel(capacity, *refs), grid_spec=plt...  5.79 us
    ppermute x9, starting transfers between devices, beside(): return lax.ppermute(x, 'dp', [(i, i ^ s) for i in range(n_dp)])  4.13 us
  transfers between devices with their start and end apart: 23, of which 13 were waited for; matrix products, arithmetic and copies ran while one was open for 0% of the time, Pallas kernels for 21%

profile of v1, /device:TPU:0, one launch (start us, length us, event | category | flops | bytes accessed | tf_op | source)
XLA Modules:
  0.0 180.3 jit_solution(4952802767703985024)
XLA Ops:
  0.6 0.8 copy.12.refs_2_.refs_1_
  1.4 0.8 copy.13.refs_3_.refs_2_
  2.2 0.1 pad_add_fusion.refs_0_.ids
  2.3 1.0 copy-done.1
  3.3 1.0 copy-done.2
  4.3 2.1 %prep.1 = (bf16[120,1024]{1,0:T(8,128)(2,1)S(1)}, bf16[120,1024]{1,0:T(8,128)(2,1)S(1)}, bf16[120,1024]{1,0:T(8,128)(2,1)S(1)}, bf16[120,1024]{1,0:T(8,128)(2,1)...) custom-call(s32[2]{0:T(128)S(1)} %pad_add_fusion.refs_0_.ids, ...), custom_call_target="tpu_custom_call" | custom-call | flops 754974720 | bytes 2752512 | tf_op jit(solution)/shard_map/prep/pallas_call | solution.py:65
  6.4 3.0 %collective-permute-start = (bf16[120,1024]{1,0:T(8,128)(2,1)S(1)}, bf16[120,1024]{1,0:T(8,128)(2,1)S(1)}, u32[]{:S(2)}, u32[]{:S(2)}) collective-permute-start(bf16[120,1024]{1,0:T(8,128)(2,1)S(1)} %get-tuple-element.37), channel_id=1, source_target_pairs={{0,1},{1,0},{2,3},{3,2},{4,5},{5,4},{6,7},{7,6},{8,9},{9,8},{10,11... | collective-permute-start | bytes 737288 | tf_op jit(solution)/shard_map/ppermute | solution.py:398
  9.5 1.6 collective-permute-start.1
  11.1 4.4 %collective-permute-done.refs_2_ = bf16[120,1024]{1,0:T(8,128)(2,1)S(1)} collective-permute-done((bf16[120,1024]{1,0:T(8,128)(2,1)S(1)}, bf16[120,1024]{1,0:T(8,128)(2,1)S(1)}, u32[]{:S(2)}, u32[]{:S(2)}) %collective-permute-start) | collective-permute-done | bytes 245792 | tf_op jit(solution)/shard_map/ppermute | solution.py:398
  15.4 2.9 %collective-permute-done.1.refs_3_ = bf16[120,1024]{1,0:T(8,128)(2,1)S(1)} collective-permute-done((bf16[120,1024]{1,0:T(8,128)(2,1)S(1)}, bf16[120,1024]{1,0:T(8,128)(2,1)S(1)}, u32[]{:S(2)}, u32[]{:S(2)}) %collective-permute-start.1) | collective-permute-done | bytes 245792 | tf_op jit(solution)/shard_map/ppermute | solution.py:398
  18.4 3.6 %collective-permute-done.2.refs_4_ = bf16[120,1024]{1,0:T(8,128)(2,1)S(1)} collective-permute-done((bf16[120,1024]{1,0:T(8,128)(2,1)S(1)}, bf16[120,1024]{1,0:T(8,128)(2,1)S(1)}, u32[]{:S(2)}, u32[]{:S(2)}) %collective-permute-start.2) | collective-permute-done | bytes 245792 | tf_op jit(solution)/shard_map/ppermute | solution.py:398
  22.0 6.1 %up.3 = (bf16[256,1024]{1,0:T(8,128)(2,1)S(1)}, bf16[256,1024]{1,0:T(8,128)(2,1)S(1)}, bf16[256,1536]{1,0:T(8,128)(2,1)S(1)}, f32[256,1536]{1,0:T(8,128)S(1)}) custom-call(s32[2]{0:T(128)S(1)} %pad_add_fusion.refs_0_.ids, bf16[120,1024]{1,0:T(8,128)(2,1)S(1)} %get-tuple-element.36.refs_1_, bf16[120,1024]{1,0:T(8,128)(2,1)S(1)} %collective-permute-done.refs_2_, ...), custom_call_target="tpu_custom_call" | custom-call | flops 1610612736 | bytes 9437184 | tf_op jit(solution)/shard_map/up/pallas_call | solution.py:126
  28.2 3.8 %collective-permute-start.16 = (bf16[120,1024]{1,0:T(8,128)(2,1)S(1)}, bf16[120,1024]{1,0:T(8,128)(2,1)S(1)}, u32[]{:S(2)}, u32[]{:S(2)}) collective-permute-start(bf16[120,1024]{1,0:T(8,128)(2,1)S(1)} %get-tuple-element.52), channel_id=1, source_target_pairs={{0,6},{1,7},{2,4},{3,5},{4,2},{5,3},{6,0},{7,1},{8,14},{9,15},{10,... | collective-permute-start | bytes 737288 | tf_op jit(solution)/shard_map/ppermute | solution.py:398
  32.0 1.2 collective-permute-start.17
  33.1 0.7 collective-permute-start.10
  33.9 2.0 %collective-permute-start.9 = (bf16[120,1024]{1,0:T(8,128)(2,1)S(1)}, bf16[120,1024]{1,0:T(8,128)(2,1)S(1)}, u32[]{:S(2)}, u32[]{:S(2)}) collective-permute-start(bf16[120,1024]{1,0:T(8,128)(2,1)S(1)} %get-tuple-element.46), channel_id=1, source_target_pairs={{0,4},{1,5},{2,6},{3,7},{4,0},{5,1},{6,2},{7,3},{8,12},{9,13},{10,... | collective-permute-start | bytes 737288 | tf_op jit(solution)/shard_map/ppermute | solution.py:398
  35.9 3.1 %collective-permute-done.16.refs_1_ = bf16[120,1024]{1,0:T(8,128)(2,1)S(1)} collective-permute-done((bf16[120,1024]{1,0:T(8,128)(2,1)S(1)}, bf16[120,1024]{1,0:T(8,128)(2,1)S(1)}, u32[]{:S(2)}, u32[]{:S(2)}) %collective-permute-start.16) | collective-permute-done | bytes 245792 | tf_op jit(solution)/shard_map/ppermute | solution.py:398
  38.9 6.3 %collective-permute-done.17.refs_2_ = bf16[120,1024]{1,0:T(8,128)(2,1)S(1)} collective-permute-done((bf16[120,1024]{1,0:T(8,128)(2,1)S(1)}, bf16[120,1024]{1,0:T(8,128)(2,1)S(1)}, u32[]{:S(2)}, u32[]{:S(2)}) %collective-permute-start.17) | collective-permute-done | bytes 245792 | tf_op jit(solution)/shard_map/ppermute | solution.py:398
  45.2 5.1 %up.5 = (bf16[128,1024]{1,0:T(8,128)(2,1)S(1)}, bf16[128,1024]{1,0:T(8,128)(2,1)S(1)}, bf16[128,1536]{1,0:T(8,128)(2,1)S(1)}, f32[128,1536]{1,0:T(8,128)S(1)}) custom-call(s32[2]{0:T(128)S(1)} %pad_add_fusion.refs_0_.ids, bf16[120,1024]{1,0:T(8,128)(2,1)S(1)} %collective-permute-done.16.refs_1_, bf16[120,1024]{1,0:T(8,128)(2,1)S(1)} %collective-permute-done.17.refs_2_, ...), custom_call_target="tpu_custom_call" | custom-call | flops 805306368 | bytes 7864320 | tf_op jit(solution)/shard_map/up/pallas_call | solution.py:126
  50.4 20.3 %collective-permute-done.10.refs_2_ = bf16[120,1024]{1,0:T(8,128)(2,1)S(1)} collective-permute-done((bf16[120,1024]{1,0:T(8,128)(2,1)S(1)}, bf16[120,1024]{1,0:T(8,128)(2,1)S(1)}, u32[]{:S(2)}, u32[]{:S(2)}) %collective-permute-start.10) | collective-permute-done | bytes 245792 | tf_op jit(solution)/shard_map/ppermute | solution.py:398
  70.7 3.9 %collective-permute-done.9.refs_1_ = bf16[120,1024]{1,0:T(8,128)(2,1)S(1)} collective-permute-done((bf16[120,1024]{1,0:T(8,128)(2,1)S(1)}, bf16[120,1024]{1,0:T(8,128)(2,1)S(1)}, u32[]{:S(2)}, u32[]{:S(2)}) %collective-permute-start.9) | collective-permute-done | bytes 245792 | tf_op jit(solution)/shard_map/ppermute | solution.py:398
  74.6 5.1 %up.4 = (bf16[128,1024]{1,0:T(8,128)(2,1)S(1)}, bf16[128,1024]{1,0:T(8,128)(2,1)S(1)}, bf16[128,1536]{1,0:T(8,128)(2,1)S(1)}, f32[128,1536]{1,0:T(8,128)S(1)}) custom-call(s32[2]{0:T(128)S(1)} %pad_add_fusion.refs_0_.ids, bf16[120,1024]{1,0:T(8,128)(2,1)S(1)} %collective-permute-done.9.refs_1_, bf16[120,1024]{1,0:T(8,128)(2,1)S(1)} %collective-permute-done.10.refs_2_, ...), custom_call_target="tpu_custom_call" | custom-call | flops 805306368 | bytes 7864320 | tf_op jit(solution)/shard_map/up/pallas_call | solution.py:126
  79.7 0.3 fusion.2
  80.0 1.5 collective-permute-start.4
  81.5 0.1 fusion
  81.6 0.6 collective-permute-start.19
  82.3 0.1 fusion.1
  82.4 1.5 collective-permute-start.12
  83.9 16.5 %collective-permute-done.4.other = bf16[256,1536]{1,0:T(8,128)(2,1)S(1)} collective-permute-done((bf16[256,1536]{1,0:T(8,128)(2,1)S(1)}, bf16[256,1536]{1,0:T(8,128)(2,1)S(1)}, u32[]{:S(2)}, u32[]{:S(2)}) %collective-permute-start.4) | collective-permute-done | bytes 786464 | tf_op jit(solution)/shard_map/ppermute | solution.py:401
  100.4 0.4 act.3.refs_1_
  100.8 8.0 %collective-permute-done.19.other = bf16[128,1536]{1,0:T(8,128)(2,1)S(1)} collective-permute-done((bf16[128,1536]{1,0:T(8,128)(2,1)S(1)}, bf16[128,1536]{1,0:T(8,128)(2,1)S(1)}, u32[]{:S(2)}, u32[]{:S(2)}) %collective-permute-start.19) | collective-permute-done | bytes 393248 | tf_op jit(solution)/shard_map/ppermute | solution.py:401
  108.8 0.2 act.5.refs_1_.refs_9_
  109.1 7.8 %collective-permute-done.12.other = bf16[128,1536]{1,0:T(8,128)(2,1)S(1)} collective-permute-done((bf16[128,1536]{1,0:T(8,128)(2,1)S(1)}, bf16[128,1536]{1,0:T(8,128)(2,1)S(1)}, u32[]{:S(2)}, u32[]{:S(2)}) %collective-permute-start.12) | collective-permute-done | bytes 393248 | tf_op jit(solution)/shard_map/ppermute | solution.py:401
  116.8 0.2 act.4.refs_1_.refs_5_
  117.1 5.7 %down.5 = (bf16[120,1024]{1,0:T(8,128)(2,1)S(1)}, bf16[120,1024]{1,0:T(8,128)(2,1)S(1)}) custom-call(s32[2]{0:T(128)S(1)} %pad_add_fusion.refs_0_.ids, bf16[128,1536]{1,0:T(8,128)(2,1)S(1)} %act.5.refs_1_.refs_9_, bf16[128,1536]{1,0:T(8,128)(2,1)S(1)} %collective-permute-done.20.refs_2_.refs_10_, bf16[1024,2048]{1,0:T(8,128)(2,1)} %bitcast.18, ...), custom_call_target="tpu_custom_call" | custom-call | flops 805306368 | bytes 7864320 | tf_op jit(solution)/shard_map/down/pallas_call | solution.py:225
  122.8 2.5 %collective-permute-start.21 = (bf16[120,1024]{1,0:T(8,128)(2,1)S(1)}, bf16[120,1024]{1,0:T(8,128)(2,1)S(1)}, u32[]{:S(2)}, u32[]{:S(2)}) collective-permute-start(bf16[120,1024]{1,0:T(8,128)(2,1)S(1)} %get-tuple-element.56), channel_id=1, source_target_pairs={{0,6},{1,7},{2,4},{3,5},{4,2},{5,3},{6,0},{7,1},{8,14},{9,15},{10,... | collective-permute-start | bytes 737288 | tf_op jit(solution)/shard_map/ppermute | solution.py:398
  125.4 2.3 %collective-permute-start.22 = (bf16[120,1024]{1,0:T(8,128)(2,1)S(1)}, bf16[120,1024]{1,0:T(8,128)(2,1)S(1)}, u32[]{:S(2)}, u32[]{:S(2)}) collective-permute-start(bf16[120,1024]{1,0:T(8,128)(2,1)S(1)} %get-tuple-element.57), channel_id=1, source_target_pairs={{0,7},{1,6},{2,5},{3,4},{4,3},{5,2},{6,1},{7,0},{8,15},{9,14},{10,... | collective-permute-start | bytes 737288 | tf_op jit(solution)/shard_map/ppermute | solution.py:398
  127.7 5.7 %down.4 = (bf16[120,1024]{1,0:T(8,128)(2,1)S(1)}, bf16[120,1024]{1,0:T(8,128)(2,1)S(1)}) custom-call(s32[2]{0:T(128)S(1)} %pad_add_fusion.refs_0_.ids, bf16[128,1536]{1,0:T(8,128)(2,1)S(1)} %act.4.refs_1_.refs_5_, bf16[128,1536]{1,0:T(8,128)(2,1)S(1)} %collective-permute-done.13.refs_2_.refs_6_, bf16[1024,2048]{1,0:T(8,128)(2,1)} %bitcast.19, ...), custom_call_target="tpu_custom_call" | custom-call | flops 805306368 | bytes 7864320 | tf_op jit(solution)/shard_map/down/pallas_call | solution.py:225
  133.5 2.9 %collective-permute-start.15 = (bf16[120,1024]{1,0:T(8,128)(2,1)S(1)}, bf16[120,1024]{1,0:T(8,128)(2,1)S(1)}, u32[]{:S(2)}, u32[]{:S(2)}) collective-permute-start(bf16[120,1024]{1,0:T(8,128)(2,1)S(1)} %get-tuple-element.51), channel_id=1, source_target_pairs={{0,5},{1,4},{2,7},{3,6},{4,1},{5,0},{6,3},{7,2},{8,13},{9,12},{10,... | collective-permute-start | bytes 737288 | tf_op jit(solution)/shard_map/ppermute | solution.py:398
  136.3 6.4 %down.3 = (bf16[120,1024]{1,0:T(8,128)(2,1)S(1)}, bf16[120,1024]{1,0:T(8,128)(2,1)S(1)}, bf16[120,1024]{1,0:T(8,128)(2,1)S(1)}, bf16[120,1024]{1,0:T(8,128)(2,1)S(1)}) custom-call(s32[2]{0:T(128)S(1)} %pad_add_fusion.refs_0_.ids, bf16[256,1536]{1,0:T(8,128)(2,1)S(1)} %act.3.refs_1_, bf16[256,1536]{1,0:T(8,128)(2,1)S(1)} %collective-permute-done.5.refs_2_, ...), custom_call_target="tpu_custom_call" | custom-call | flops 1610612736 | bytes 9437184 | tf_op jit(solution)/shard_map/down/pallas_call | solution.py:225
  142.8 1.6 collective-permute-start.6
  144.3 8.0 %collective-permute-start.7 = (bf16[120,1024]{1,0:T(8,128)(2,1)S(1)}, bf16[120,1024]{1,0:T(8,128)(2,1)S(1)}, u32[]{:S(2)}, u32[]{:S(2)}) collective-permute-start(bf16[120,1024]{1,0:T(8,128)(2,1)S(1)} %get-tuple-element.44), channel_id=1, source_target_pairs={{0,2},{1,3},{2,0},{3,1},{4,6},{5,7},{6,4},{7,5},{8,10},{9,11},{10,... | collective-permute-start | bytes 737288 | tf_op jit(solution)/shard_map/ppermute | solution.py:398
  152.4 6.2 %collective-permute-start.8 = (bf16[120,1024]{1,0:T(8,128)(2,1)S(1)}, bf16[120,1024]{1,0:T(8,128)(2,1)S(1)}, u32[]{:S(2)}, u32[]{:S(2)}) collective-permute-start(bf16[120,1024]{1,0:T(8,128)(2,1)S(1)} %get-tuple-element.45), channel_id=1, source_target_pairs={{0,3},{1,2},{2,1},{3,0},{4,7},{5,6},{6,5},{7,4},{8,11},{9,10},{10,... | collective-permute-start | bytes 737288 | tf_op jit(solution)/shard_map/ppermute | solution.py:398
  158.6 8.8 %grads.1 = (bf16[1024,2048]{1,0:T(8,128)(2,1)}, bf16[1024,1024]{1,0:T(8,128)(2,1)}) custom-call(s32[2]{0:T(128)S(1)} %pad_add_fusion.refs_0_.ids, bf16[256,1024]{1,0:T(8,128)(2,1)S(1)} %get-tuple-element.60.refs_0_, bf16[256,1536]{1,0:T(8,128)(2,1)S(1)} %act.3.refs_1_, bf16[256,1536]{1,0:T(8,128)(2,1)S(1)} %collective-permute-done.5.refs_2_, ...), custom_call_target="tpu_custom_call" | custom-call | flops 3221225472 | bytes 12582912 | tf_op jit(solution)/shard_map/grads/pallas_call | solution.py:307
  167.4 0.9 collective-permute-done.15.refs_8_
  168.3 0.9 collective-permute-done.7.refs_5_
  169.2 5.3 %collective-permute-done.8.refs_6_ = bf16[120,1024]{1,0:T(8,128)(2,1)S(1)} collective-permute-done((bf16[120,1024]{1,0:T(8,128)(2,1)S(1)}, bf16[120,1024]{1,0:T(8,128)(2,1)S(1)}, u32[]{:S(2)}, u32[]{:S(2)}) %collective-permute-start.8) | collective-permute-done | bytes 245792 | tf_op jit(solution)/shard_map/ppermute | solution.py:398
  174.5 5.8 %final.1 = (bf16[192,1024]{1,0:T(8,128)(2,1)}, bf16[192,1024]{1,0:T(8,128)(2,1)}) custom-call(s32[2]{0:T(128)S(1)} %pad_add_fusion.refs_0_.ids, s32[192,2]{1,0:T(8,128)S(1)} %copy.12.refs_2_.refs_1_, f32[192,2]{1,0:T(8,128)S(1)} %copy.13.refs_3_.refs_2_, bf16[120,1024]{1,0:T(8,128)(2,1)S(1)} %get-tuple-element.42.refs_3_, ...), custom_call_target="tpu_custom_call" | custom-call | flops 754974720 | bytes 2752512 | tf_op jit(solution)/shard_map/final/pallas_call | solution.py:364
  (22 shorter events, 0.5 us)
Async XLA Ops:
  2.3 1.0 copy-start.1
  3.3 1.0 copy-start.2
  6.4 9.0 %collective-permute-start = (bf16[120,1024]{1,0:T(8,128)(2,1)S(1)}, bf16[120,1024]{1,0:T(8,128)(2,1)S(1)}, u32[]{:S(2)}, u32[]{:S(2)}) collective-permute-start(bf16[120,1024]{1,0:T(8,128)(2,1)S(1)} %get-tuple-element.37), channel_id=1, source_target_pairs={{0,1},{1,0},{2,3},{3,2},{4,5},{5,4},{6,7},{7,6},{8,9},{9,8},{10,11... | collective-permute-start | bytes 737288 | tf_op jit(solution)/shard_map/ppermute | solution.py:398
  9.5 8.9 %collective-permute-start.1 = (bf16[120,1024]{1,0:T(8,128)(2,1)S(1)}, bf16[120,1024]{1,0:T(8,128)(2,1)S(1)}, u32[]{:S(2)}, u32[]{:S(2)}) collective-permute-start(bf16[120,1024]{1,0:T(8,128)(2,1)S(1)} %get-tuple-element.38), channel_id=1, source_target_pairs={{0,2},{1,3},{2,0},{3,1},{4,6},{5,7},{6,4},{7,5},{8,10},{9,11},{10,... | collective-permute-start | bytes 737288 | tf_op jit(solution)/shard_map/ppermute | solution.py:398
  11.1 10.9 %collective-permute-start.2 = (bf16[120,1024]{1,0:T(8,128)(2,1)S(1)}, bf16[120,1024]{1,0:T(8,128)(2,1)S(1)}, u32[]{:S(2)}, u32[]{:S(2)}) collective-permute-start(bf16[120,1024]{1,0:T(8,128)(2,1)S(1)} %get-tuple-element.39), channel_id=1, source_target_pairs={{0,3},{1,2},{2,1},{3,0},{4,7},{5,6},{6,5},{7,4},{8,11},{9,10},{10,... | collective-permute-start | bytes 737288 | tf_op jit(solution)/shard_map/ppermute | solution.py:398
  22.0 23.3 %copy-start = (bf16[1,1024,1024]{2,1,0:T(8,128)(2,1)S(1)}, bf16[1,1024,1024]{2,1,0:T(8,128)(2,1)}, u32[]{:S(2)}) copy-start(bf16[1,1024,1024]{2,1,0:T(8,128)(2,1)} %param.11) | copy-start | bytes 6291460
  28.1 51.6 %collective-permute-start.3 = (bf16[256,1536]{1,0:T(8,128)(2,1)S(1)}, bf16[256,1536]{1,0:T(8,128)(2,1)S(1)}, u32[]{:S(2)}, u32[]{:S(2)}) collective-permute-start(bf16[256,1536]{1,0:T(8,128)(2,1)S(1)} %get-tuple-element.41), channel_id=1, source_target_pairs={{0,8},{8,0},{16,24},{24,16},{1,9},{9,1},{17,25},{25,17},{2,10},{10... | collective-permute-start | bytes 2359304 | tf_op jit(solution)/shard_map/ppermute | solution.py:401
  28.2 10.8 %collective-permute-start.16 = (bf16[120,1024]{1,0:T(8,128)(2,1)S(1)}, bf16[120,1024]{1,0:T(8,128)(2,1)S(1)}, u32[]{:S(2)}, u32[]{:S(2)}) collective-permute-start(bf16[120,1024]{1,0:T(8,128)(2,1)S(1)} %get-tuple-element.52), channel_id=1, source_target_pairs={{0,6},{1,7},{2,4},{3,5},{4,2},{5,3},{6,0},{7,1},{8,14},{9,15},{10,... | collective-permute-start | bytes 737288 | tf_op jit(solution)/shard_map/ppermute | solution.py:398
  32.0 13.3 %collective-permute-start.17 = (bf16[120,1024]{1,0:T(8,128)(2,1)S(1)}, bf16[120,1024]{1,0:T(8,128)(2,1)S(1)}, u32[]{:S(2)}, u32[]{:S(2)}) collective-permute-start(bf16[120,1024]{1,0:T(8,128)(2,1)S(1)} %get-tuple-element.53), channel_id=1, source_target_pairs={{0,7},{1,6},{2,5},{3,4},{4,3},{5,2},{6,1},{7,0},{8,15},{9,14},{10,... | collective-permute-start | bytes 737288 | tf_op jit(solution)/shard_map/ppermute | solution.py:398
  33.1 37.5 %collective-permute-start.10 = (bf16[120,1024]{1,0:T(8,128)(2,1)S(1)}, bf16[120,1024]{1,0:T(8,128)(2,1)S(1)}, u32[]{:S(2)}, u32[]{:S(2)}) collective-permute-start(bf16[120,1024]{1,0:T(8,128)(2,1)S(1)} %get-tuple-element.47), channel_id=1, source_target_pairs={{0,5},{1,4},{2,7},{3,6},{4,1},{5,0},{6,3},{7,2},{8,13},{9,12},{10,... | collective-permute-start | bytes 737288 | tf_op jit(solution)/shard_map/ppermute | solution.py:398
  33.9 40.7 %collective-permute-start.9 = (bf16[120,1024]{1,0:T(8,128)(2,1)S(1)}, bf16[120,1024]{1,0:T(8,128)(2,1)S(1)}, u32[]{:S(2)}, u32[]{:S(2)}) collective-permute-start(bf16[120,1024]{1,0:T(8,128)(2,1)S(1)} %get-tuple-element.46), channel_id=1, source_target_pairs={{0,4},{1,5},{2,6},{3,7},{4,0},{5,1},{6,2},{7,3},{8,12},{9,13},{10,... | collective-permute-start | bytes 737288 | tf_op jit(solution)/shard_map/ppermute | solution.py:398
  50.3 31.2 %collective-permute-start.18 = (bf16[128,1536]{1,0:T(8,128)(2,1)S(1)}, bf16[128,1536]{1,0:T(8,128)(2,1)S(1)}, u32[]{:S(2)}, u32[]{:S(2)}) collective-permute-start(bf16[128,1536]{1,0:T(8,128)(2,1)S(1)} %get-tuple-element.55), channel_id=1, source_target_pairs={{0,8},{8,0},{16,24},{24,16},{1,9},{9,1},{17,25},{25,17},{2,10},{10... | collective-permute-start | bytes 1179656 | tf_op jit(solution)/shard_map/ppermute | solution.py:401
  79.6 2.6 %collective-permute-start.11 = (bf16[128,1536]{1,0:T(8,128)(2,1)S(1)}, bf16[128,1536]{1,0:T(8,128)(2,1)S(1)}, u32[]{:S(2)}, u32[]{:S(2)}) collective-permute-start(bf16[128,1536]{1,0:T(8,128)(2,1)S(1)} %get-tuple-element.49), channel_id=1, source_target_pairs={{0,8},{8,0},{16,24},{24,16},{1,9},{9,1},{17,25},{25,17},{2,10},{10... | collective-permute-start | bytes 1179656 | tf_op jit(solution)/shard_map/ppermute | solution.py:401
  80.0 20.4 %collective-permute-start.4 = (bf16[256,1536]{1,0:T(8,128)(2,1)S(1)}, bf16[256,1536]{1,0:T(8,128)(2,1)S(1)}, u32[]{:S(2)}, u32[]{:S(2)}) collective-permute-start(bf16[256,1536]{1,0:T(8,128)(2,1)S(1)} %get-tuple-element.72), channel_id=1, source_target_pairs={{0,16},{8,24},{16,0},{24,8},{1,17},{9,25},{17,1},{25,9},{2,18},{10... | collective-permute-start | bytes 2359304 | tf_op jit(solution)/shard_map/ppermute | solution.py:401
  81.6 27.2 %collective-permute-start.19 = (bf16[128,1536]{1,0:T(8,128)(2,1)S(1)}, bf16[128,1536]{1,0:T(8,128)(2,1)S(1)}, u32[]{:S(2)}, u32[]{:S(2)}) collective-permute-start(bf16[128,1536]{1,0:T(8,128)(2,1)S(1)} %get-tuple-element.68), channel_id=1, source_target_pairs={{0,16},{8,24},{16,0},{24,8},{1,17},{9,25},{17,1},{25,9},{2,18},{10... | collective-permute-start | bytes 1179656 | tf_op jit(solution)/shard_map/ppermute | solution.py:401
  82.4 34.5 %collective-permute-start.12 = (bf16[128,1536]{1,0:T(8,128)(2,1)S(1)}, bf16[128,1536]{1,0:T(8,128)(2,1)S(1)}, u32[]{:S(2)}, u32[]{:S(2)}) collective-permute-start(bf16[128,1536]{1,0:T(8,128)(2,1)S(1)} %get-tuple-element.70), channel_id=1, source_target_pairs={{0,16},{8,24},{16,0},{24,8},{1,17},{9,25},{17,1},{25,9},{2,18},{10... | collective-permute-start | bytes 1179656 | tf_op jit(solution)/shard_map/ppermute | solution.py:401
  100.7 35.6 %collective-permute-start.5 = (bf16[256,1536]{1,0:T(8,128)(2,1)S(1)}, bf16[256,1536]{1,0:T(8,128)(2,1)S(1)}, u32[]{:S(2)}, u32[]{:S(2)}) collective-permute-start(bf16[256,1536]{1,0:T(8,128)(2,1)S(1)} %act.3.refs_1_), channel_id=1, source_target_pairs={{0,8},{8,0},{16,24},{24,16},{1,9},{9,1},{17,25},{25,17},{2,10},{10... | collective-permute-start | bytes 2359304 | tf_op jit(solution)/shard_map/ppermute | solution.py:401
  109.0 8.1 %collective-permute-start.20 = (bf16[128,1536]{1,0:T(8,128)(2,1)S(1)}, bf16[128,1536]{1,0:T(8,128)(2,1)S(1)}, u32[]{:S(2)}, u32[]{:S(2)}) collective-permute-start(bf16[128,1536]{1,0:T(8,128)(2,1)S(1)} %act.5.refs_1_.refs_9_), channel_id=1, source_target_pairs={{0,8},{8,0},{16,24},{24,16},{1,9},{9,1},{17,25},{25,17},{2,10},{10... | collective-permute-start | bytes 1179656 | tf_op jit(solution)/shard_map/ppermute | solution.py:401
  117.0 10.6 %collective-permute-start.13 = (bf16[128,1536]{1,0:T(8,128)(2,1)S(1)}, bf16[128,1536]{1,0:T(8,128)(2,1)S(1)}, u32[]{:S(2)}, u32[]{:S(2)}) collective-permute-start(bf16[128,1536]{1,0:T(8,128)(2,1)S(1)} %act.4.refs_1_.refs_5_), channel_id=1, source_target_pairs={{0,8},{8,0},{16,24},{24,16},{1,9},{9,1},{17,25},{25,17},{2,10},{10... | collective-permute-start | bytes 1179656 | tf_op jit(solution)/shard_map/ppermute | solution.py:401
  122.8 21.5 %collective-permute-start.21 = (bf16[120,1024]{1,0:T(8,128)(2,1)S(1)}, bf16[120,1024]{1,0:T(8,128)(2,1)S(1)}, u32[]{:S(2)}, u32[]{:S(2)}) collective-permute-start(bf16[120,1024]{1,0:T(8,128)(2,1)S(1)} %get-tuple-element.56), channel_id=1, source_target_pairs={{0,6},{1,7},{2,4},{3,5},{4,2},{5,3},{6,0},{7,1},{8,14},{9,15},{10,... | collective-permute-start | bytes 737288 | tf_op jit(solution)/shard_map/ppermute | solution.py:398
  125.4 27.0 %collective-permute-start.22 = (bf16[120,1024]{1,0:T(8,128)(2,1)S(1)}, bf16[120,1024]{1,0:T(8,128)(2,1)S(1)}, u32[]{:S(2)}, u32[]{:S(2)}) collective-permute-start(bf16[120,1024]{1,0:T(8,128)(2,1)S(1)} %get-tuple-element.57), channel_id=1, source_target_pairs={{0,7},{1,6},{2,5},{3,4},{4,3},{5,2},{6,1},{7,0},{8,15},{9,14},{10,... | collective-permute-start | bytes 737288 | tf_op jit(solution)/shard_map/ppermute | solution.py:398
  133.4 34.0 %collective-permute-start.14 = (bf16[120,1024]{1,0:T(8,128)(2,1)S(1)}, bf16[120,1024]{1,0:T(8,128)(2,1)S(1)}, u32[]{:S(2)}, u32[]{:S(2)}) collective-permute-start(bf16[120,1024]{1,0:T(8,128)(2,1)S(1)} %get-tuple-element.50), channel_id=1, source_target_pairs={{0,4},{1,5},{2,6},{3,7},{4,0},{5,1},{6,2},{7,3},{8,12},{9,13},{10,... | collective-permute-start | bytes 737288 | tf_op jit(solution)/shard_map/ppermute | solution.py:398
  133.5 34.8 %collective-permute-start.15 = (bf16[120,1024]{1,0:T(8,128)(2,1)S(1)}, bf16[120,1024]{1,0:T(8,128)(2,1)S(1)}, u32[]{:S(2)}, u32[]{:S(2)}) collective-permute-start(bf16[120,1024]{1,0:T(8,128)(2,1)S(1)} %get-tuple-element.51), channel_id=1, source_target_pairs={{0,5},{1,4},{2,7},{3,6},{4,1},{5,0},{6,3},{7,2},{8,13},{9,12},{10,... | collective-permute-start | bytes 737288 | tf_op jit(solution)/shard_map/ppermute | solution.py:398
  142.8 25.5 %collective-permute-start.6 = (bf16[120,1024]{1,0:T(8,128)(2,1)S(1)}, bf16[120,1024]{1,0:T(8,128)(2,1)S(1)}, u32[]{:S(2)}, u32[]{:S(2)}) collective-permute-start(bf16[120,1024]{1,0:T(8,128)(2,1)S(1)} %get-tuple-element.43), channel_id=1, source_target_pairs={{0,1},{1,0},{2,3},{3,2},{4,5},{5,4},{6,7},{7,6},{8,9},{9,8},{10,11... | collective-permute-start | bytes 737288 | tf_op jit(solution)/shard_map/ppermute | solution.py:398
  144.3 24.9 %collective-permute-start.7 = (bf16[120,1024]{1,0:T(8,128)(2,1)S(1)}, bf16[120,1024]{1,0:T(8,128)(2,1)S(1)}, u32[]{:S(2)}, u32[]{:S(2)}) collective-permute-start(bf16[120,1024]{1,0:T(8,128)(2,1)S(1)} %get-tuple-element.44), channel_id=1, source_target_pairs={{0,2},{1,3},{2,0},{3,1},{4,6},{5,7},{6,4},{7,5},{8,10},{9,11},{10,... | collective-permute-start | bytes 737288 | tf_op jit(solution)/shard_map/ppermute | solution.py:398
  152.4 22.1 %collective-permute-start.8 = (bf16[120,1024]{1,0:T(8,128)(2,1)S(1)}, bf16[120,1024]{1,0:T(8,128)(2,1)S(1)}, u32[]{:S(2)}, u32[]{:S(2)}) collective-permute-start(bf16[120,1024]{1,0:T(8,128)(2,1)S(1)} %get-tuple-element.45), channel_id=1, source_target_pairs={{0,3},{1,2},{2,1},{3,0},{4,7},{5,6},{6,5},{7,4},{8,11},{9,10},{10,... | collective-permute-start | bytes 737288 | tf_op jit(solution)/shard_map/ppermute | solution.py:398

commit v2 on v0

--- a/solution.py
+++ b/solution.py
@@ -1,7 +1,494 @@
 import jax
 import jax.numpy as jnp
 from jax import lax
+from jax.experimental import pallas as pl
+from jax.experimental.pallas import tpu as pltpu
 from jax.sharding import PartitionSpec as P
+
+BF = jnp.bfloat16
+F32 = jnp.float32
+VMEM_LIMIT = 18 * 1024 * 1024
+GRADS_LIMIT = 32 * 1024 * 1024
+FIRST_LIMIT = 54 * 1024 * 1024
+PREP_LIMIT = 60 * 1024 * 1024
+COST = pl.CostEstimate(flops=1, bytes_accessed=1, transcendentals=0)
+
+
+def dot(a, b):
+    return lax.dot_general(a, b, (((1,), (0,)), ((), ())), preferred_element_type=F32)
+
+
+def dot_t(a, b):
+    return lax.dot_general(a, b, (((1,), (1,)), ((), ())), preferred_element_type=F32)
+
+
+def t_dot(a, b):
+    return lax.dot_general(a, b, (((0,), (0,)), ((), ())), preferred_element_type=F32)
+
+
+def iota(shape, dim):
+    return lax.broadcasted_iota(jnp.int32, shape, dim)
+
+
+def padded(capacity):
+    return -(-capacity // 16) * 16
+
+
+def prep_kernel(capacity, ids, tokens, routes, weight, cotangent, *refs):
+    outs, (token_rows, grad_rows, route_lines, weight_lines, sems) = refs[:-5], refs[-5:]
+    pairs = ((routes, route_lines), (weight, weight_lines), (tokens, token_rows), (cotangent, grad_rows))
+    copies = [pltpu.make_async_copy(x, held, sems.at[i]) for i, (x, held) in enumerate(pairs)]
+    for copy in copies:
+        copy.start()
+    for copy in copies[:2]:
+        copy.wait()
+    routes, weight = route_lines, weight_lines
+    count = len(outs)
+    rows = routes.shape[1]
+    expert = iota((count, rows), 0) ^ ids[0]
+    named, w_named = None, None
+    for k in range(routes.shape[0]):
+        hit = routes[k : k + 1, :] == expert
+        w_hit = jnp.where(hit, weight[k : k + 1, :], 0.0)
+        named = hit if named is None else named | hit
+        w_named = w_hit if w_named is None else w_named + w_hit
+    before = (iota((rows, rows), 0) < iota((rows, rows), 1)).astype(F32).astype(BF)
+    rank = dot(named.astype(F32).astype(BF), before).astype(jnp.int32)
+    key = jnp.where(named, rank, -2 * capacity)
+    slot = iota((2 * capacity, rows), 0)
+    picks = []
+    for s in range(count):
+        row_key = key[s : s + 1, :]
+        pick_token = (row_key == slot).astype(F32)
+        pick_grad = (row_key + capacity == slot).astype(F32)
+        scale = jnp.sum(pick_grad * w_named[s : s + 1, :], axis=1, keepdims=True)
+        scale = scale + (slot[:, 0:1] < capacity).astype(F32)
+        picks.append((pick_token.astype(BF), pick_grad.astype(BF), scale))
+    for copy in copies[2:]:
+        copy.wait()
+    for out, (pick_token, pick_grad, scale) in zip(outs, picks):
+        out[...] = (scale * (dot(pick_token, token_rows[...]) + dot(pick_grad, grad_rows[...]))).astype(BF)
+
+
+def prep(ids, tokens, routes, weight, cotangent, count, capacity):
+    rows, features = tokens.shape
+    whole = pl.BlockSpec(memory_space=pltpu.VMEM)
+    away = pl.BlockSpec(memory_space=pltpu.HBM)
+    return pl.pallas_call(
+        lambda *refs: prep_kernel(capacity, *refs),
+        out_shape=[jax.ShapeDtypeStruct((2 * capacity, features), BF)] * count,
+        in_specs=[pl.BlockSpec(memory_space=pltpu.SMEM)] + [away] * 4,
+        out_specs=[whole] * count,
+        scratch_shapes=[pltpu.VMEM((rows, features), BF)] * 2
+        + [pltpu.VMEM(routes.T.shape, routes.dtype), pltpu.VMEM(weight.T.shape, weight.dtype)]
+        + [pltpu.SemaphoreType.DMA((4,))],
+        compiler_params=pltpu.CompilerParams(vmem_limit_bytes=PREP_LIMIT),
+        cost_estimate=COST,
+        name="prep",
+    )(ids, tokens, routes.T, weight.T, cotangent)
+
+
+def call(kernel, name, out_shapes, scalars, *arrays):
+    whole = pl.BlockSpec(memory_space=pltpu.VMEM)
+    return pl.pallas_call(
+        kernel,
+        out_shape=out_shapes,
+        in_specs=[pl.BlockSpec(memory_space=pltpu.SMEM)] * len(scalars) + [whole] * len(arrays),
+        out_specs=jax.tree.map(lambda _: whole, out_shapes),
+        compiler_params=pltpu.CompilerParams(vmem_limit_bytes=VMEM_LIMIT),
+        cost_estimate=COST,
+        name=name,
+    )(*scalars, *arrays)
+
+
+def up_kernel(capacity, held, ids, *refs):
+    if held:
+        blocks, (*parts, w_out, row_out, grad_out, send, keep, sent) = refs[:-8], refs[-8:]
+    else:
+        blocks, (far_in, far_out, row_out, grad_out, send, keep, *parts, w_out, sent, sems) = refs[:-11], refs[-11:]
+    depth, both_units = parts[0].shape
+    units = both_units // 2
+    width = units // 4
+    copies = []
+    if not held:
+        for k, part in enumerate(parts):
+            copies.append(pltpu.make_async_copy(far_in.at[k * depth : (k + 1) * depth, :], part, sems.at[k]))
+        copies.append(pltpu.make_async_copy(far_out, w_out, sems.at[len(parts)]))
+        for copy in copies:
+            copy.start()
+    pad = padded(capacity)
+    spot = iota((2 * pad, 2 * capacity), 0)
+    col = iota((2 * pad, 2 * capacity), 1)
+    target = jnp.where(col < capacity, col, col + pad - capacity)
+    spread = (spot == target).astype(F32).astype(BF)
+    for i, block in enumerate(blocks):
+        laid = dot(spread, block[...]).astype(BF)
+        row_out[i * pad : (i + 1) * pad, :] = laid[:pad]
+        grad_out[i * pad : (i + 1) * pad, :] = laid[pad:]
+    tiles = [(out, half, j) for out, half in ((sent, 1 - ids[1]), (keep, ids[1])) for j in range(2)]
+    for k, w_in in enumerate(parts):
+        if not held:
+            copies[k].wait()
+        at = slice(k * depth, (k + 1) * depth)
+        for out, half, j in tiles:
+            for part in range(2):
+                base = (3 * j + part) * width
+                column = pl.multiple_of(part * units + (half * 2 + j) * width, width)
+                term = dot(row_out[:, at], w_in[:, pl.ds(column, width)])
+                if k:
+                    out[:, base : base + width] += term
+                else:
+                    out[:, base : base + width] = term
+    if not held:
+        copies[-1].wait()
+    for out, half, j in tiles:
+        row = pl.multiple_of((half * 2 + j) * width, width)
+        out[:, (3 * j + 2) * width : (3 * j + 3) * width] = dot_t(grad_out[...], w_out[pl.ds(row, width), :])
+    send[...] = sent[...].astype(BF)
+
+
+def up_step(ids, blocks, weights, capacity, held):
+    *_, w_out = weights
+    units, features = w_out.shape
+    rows = len(blocks) * padded(capacity)
+    shape = jax.ShapeDtypeStruct
+    whole = pl.BlockSpec(memory_space=pltpu.VMEM)
+    away = pl.BlockSpec(memory_space=pl.ANY)
+    out_shape = [
+        shape((rows, features), BF),
+        shape((rows, features), BF),
+        shape((rows, 3 * units // 2), BF),
+        shape((rows, 3 * units // 2), F32),
+    ]
+    scratch = [pltpu.VMEM((rows, 3 * units // 2), F32)]
+    if not held:
+        out_shape += [shape((features // 2, 2 * units), BF)] * 2 + [shape(w_out.shape, BF)]
+        scratch += [pltpu.SemaphoreType.DMA((3,))]
+    return pl.pallas_call(
+        lambda *refs: up_kernel(capacity, held, *refs),
+        out_shape=out_shape,
+        in_specs=[pl.BlockSpec(memory_space=pltpu.SMEM)]
+        + [whole] * len(blocks)
+        + [whole if held else away] * len(weights),
+        out_specs=[whole] * len(out_shape),
+        scratch_shapes=scratch,
+        compiler_params=pltpu.CompilerParams(vmem_limit_bytes=VMEM_LIMIT if held else FIRST_LIMIT),
+        cost_estimate=COST,
+        name="up",
+    )(ids, *blocks, *weights)
+
+
+def sum_kernel(keep, core, out):
+    out[...] = (keep[...] + core[...].astype(F32)).astype(BF)
+
+
+def sum_step(keep, core):
+    return call(sum_kernel, "total", jax.ShapeDtypeStruct(keep.shape, BF), [], keep, core)
+
+
+def act_kernel(keep, core, other, out):
+    width = keep.shape[1] // 6
+    for j in range(2):
+        base = 3 * width * j
+        gate, up, back = (
+            keep[:, at : at + width] + core[:, at : at + width].astype(F32) + other[:, at : at + width].astype(F32)
+            for at in (base, base + width, base + 2 * width)
+        )
+        sigmoid = jax.nn.sigmoid(gate)
+        silu = gate * sigmoid
+        out[:, base : base + width] = (silu * up).astype(BF)
+        out[:, base + width : base + 2 * width] = (
+            back * up * sigmoid * (1.0 + gate * (1.0 - sigmoid))
+        ).astype(BF)
+        out[:, base + 2 * width : base + 3 * width] = (back * silu).astype(BF)
+
+
+def act_step(keep, core, other):
+    return call(act_kernel, "act", jax.ShapeDtypeStruct(keep.shape, BF), [], keep, core, other)
+
+
+def down_kernel(capacity, cuts, ids, own, core, *refs):
+    *parts, w_out = refs[:3]
+    outs = refs[3:]
+    pad = padded(capacity)
+    units = w_out.shape[0]
+    width = units // 4
+    out_rows, grad_parts = None, [None] * len(parts)
+    for held, half in ((own, ids[1]), (core, 1 - ids[1])):
+        for j in range(2):
+            base = 3 * width * j
+            at = pl.multiple_of((half * 2 + j) * width, width)
+            at_up = pl.multiple_of(units + (half * 2 + j) * width, width)
+            a = dot(held[:, base : base + width], w_out[pl.ds(at, width), :])
+            out_rows = a if out_rows is None else out_rows + a
+            for k, w_in in enumerate(parts):
+                b = dot_t(held[:, base + width : base + 2 * width], w_in[:, pl.ds(at, width)])
+                b = b + dot_t(held[:, base + 2 * width : base + 3 * width], w_in[:, pl.ds(at_up, width)])
+                grad_parts[k] = b if grad_parts[k] is None else grad_parts[k] + b
+    grad_rows = jnp.concatenate(grad_parts, axis=1)
+    spot = iota((2 * capacity, pad), 0)
+    col = iota((2 * capacity, pad), 1)
+    pack_out = (spot == jnp.where(col < capacity, col, -1)).astype(F32).astype(BF)
+    pack_grad = (spot - capacity == jnp.where(col < capacity, col, -capacity - 1)).astype(F32).astype(BF)
+    out_rows, grad_rows = out_rows.astype(BF), grad_rows.astype(BF)
+    for i in range(out_rows.shape[0] // pad):
+        packed = (
+            dot(pack_out, out_rows[i * pad : (i + 1) * pad])
+            + dot(pack_grad, grad_rows[i * pad : (i + 1) * pad])
+        ).astype(BF)
+        cut = packed.shape[1] // cuts
+        for j in range(cuts):
+            outs[i * cuts + j][...] = packed[:, j * cut : (j + 1) * cut]
+
+
+def down_step(ids, own, core, weights, count, capacity, cuts):
+    features = weights[-1].shape[1]
+    outs = call(
+        lambda *refs: down_kernel(capacity, cuts, *refs),
+        "down",
+        [jax.ShapeDtypeStruct((2 * capacity, features // cuts), BF)] * (count * cuts),
+        [ids],
+        own,
+        core,
+        *weights,
+    )
+    return [outs[i * cuts : (i + 1) * cuts] for i in range(count)]
+
+
+def grads_kernel(count, ids, *refs):
+    groups = [refs[4 * i : 4 * i + 4] for i in range(count)]
+    grad_in, grad_out, rows, grads, own, core, tiles_in, tiles_out, sems = refs[4 * count :]
+    at = 0
+    for group in groups:
+        n = group[0].shape[0]
+        for held, part in zip((rows, grads, own, core), group):
+            held[at : at + n, :] = part[...]
+        at += n
+    features, units = rows.shape[1], grad_out.shape[0]
+    f_tile, width = features // 4, units // 4
+    copies = []
+    for j in range(4):
+        turned = rows[:, j * f_tile : (j + 1) * f_tile].T
+        for held, half in ((own, ids[1]), (core, 1 - ids[1])):
+            for i in range(2):
+                both = dot(turned, held[:, (3 * i + 1) * width : (3 * i + 3) * width]).astype(BF)
+                for part in range(2):
+                    to = pl.multiple_of(part * units + (half * 2 + i) * width, width)
+                    tiles_in[j, :, pl.ds(to, width)] = both[:, part * width : (part + 1) * width]
+        copies.append(pltpu.make_async_copy(tiles_in.at[j], grad_in.at[j * f_tile : (j + 1) * f_tile, :], sems.at[j]))
+        copies[-1].start()
+    for j, (held, half) in enumerate(((own, ids[1]), (core, 1 - ids[1]))):
+        for i in range(2):
+            turned = held[:, 3 * i * width : (3 * i + 1) * width].T
+            tiles_out[2 * j + i] = dot(turned, grads[...]).astype(BF)
+            to = pl.multiple_of((half * 2 + i) * width, width)
+            copies.append(pltpu.make_async_copy(tiles_out.at[2 * j + i], grad_out.at[pl.ds(to, width), :], sems.at[4 + 2 * j + i]))
+            copies[-1].start()
+    for copy in copies:
+        copy.wait()
+
+
+def grads_step(ids, groups, units):
+    features = groups[0][0].shape[1]
+    rows = sum(group[0].shape[0] for group in groups)
+    whole = pl.BlockSpec(memory_space=pltpu.VMEM)
+    arrays = [x for group in groups for x in group]
+    return pl.pallas_call(
+        lambda *refs: grads_kernel(len(groups), *refs),
+        out_shape=[
+            jax.ShapeDtypeStruct((features, 2 * units), BF),
+            jax.ShapeDtypeStruct((units, features), BF),
+        ],
+        in_specs=[pl.BlockSpec(memory_space=pltpu.SMEM)] + [whole] * len(arrays),
+        out_specs=[pl.BlockSpec(memory_space=pltpu.HBM)] * 2,
+        scratch_shapes=[
+            pltpu.VMEM((rows, features), BF),
+            pltpu.VMEM((rows, features), BF),
+            pltpu.VMEM((rows, units * 3 // 2), BF),
+            pltpu.VMEM((rows, units * 3 // 2), BF),
+            pltpu.VMEM((4, features // 4, 2 * units), BF),
+            pltpu.VMEM((4, units // 4, features), BF),
+            pltpu.SemaphoreType.DMA((8,)),
+        ],
+        compiler_params=pltpu.CompilerParams(vmem_limit_bytes=GRADS_LIMIT),
+        cost_estimate=COST,
+        name="grads",
+    )(ids, *arrays)
+
+
+def final_kernel(capacity, sources, cuts, ids, routes, weight, *refs):
+    taken = cuts * len(sources)
+    homes, partial, (mixed, grad_tokens) = refs[:taken], refs[taken:-2], refs[-2:]
+    rows = routes.shape[1]
+    me = ids[0]
+    count = len(sources)
+    eye = iota((rows, rows), 0) == iota((rows, rows), 1)
+
+    def column(line, zero):
+        return jnp.sum(jnp.where(eye, line, zero), axis=1, keepdims=True)
+
+    lane = iota((rows, count), 1)
+    expert = lane * 0
+    for i, s in enumerate(sources):
+        expert = jnp.where(lane == i, s, expert)
+    expert = expert ^ me
+    named, w_named = None, None
+    for k in range(routes.shape[0]):
+        hit = column(routes[k : k + 1, :], 0) == expert
+        w_hit = jnp.where(hit, column(weight[k : k + 1, :], 0.0), 0.0)
+        named = hit if named is None else named | hit
+        w_named = w_hit if w_named is None else w_named + w_hit
+    before = (iota((rows, rows), 1) < iota((rows, rows), 0)).astype(BF)
+    rank = dot(before, named.astype(F32).astype(BF)).astype(jnp.int32)
+    key = jnp.where(named, rank, -2 * capacity)
+    slot = iota((rows, 2 * capacity), 1)
+    width = mixed.shape[1] // cuts
+    for j in range(cuts):
+        at = slice(j * width, (j + 1) * width)
+        total_out, total_grad = (p[:, at] for p in partial) if partial else (None, None)
+        for i in range(count):
+            home = homes[i * cuts + j]
+            row_key = key[:, i : i + 1]
+            pick_out = (row_key == slot).astype(F32).astype(BF)
+            pick_grad = (row_key + capacity == slot).astype(F32).astype(BF)
+            out = w_named[:, i : i + 1] * dot(pick_out, home[...])
+            grad = dot(pick_grad, home[...])
+            total_out = out if total_out is None else total_out + out
+            total_grad = grad if total_grad is None else total_grad + grad
+        mixed[:, at] = total_out.astype(mixed.dtype)
+        grad_tokens[:, at] = total_grad.astype(mixed.dtype)
+
+
+def final(ids, routes, weight, homes, sources, capacity, partial, dtype):
+    cuts = len(homes[0])
+    shape = (routes.shape[0], homes[0][0].shape[1] * cuts)
+    return call(
+        lambda *refs: final_kernel(capacity, sources, cuts, *refs),
+        "final",
+        [jax.ShapeDtypeStruct(shape, dtype)] * 2,
+        [ids],
+        routes.T,
+        weight.T,
+        *[x for home in homes for x in home],
+        *partial,
+    )
+
+
+def per_device_chunked(tokens, routes, route_weight, cotangent, w_in, w_out):
+    tok_rows = tokens.shape[0]
+    top_count = routes.shape[1]
+    n_expert = lax.axis_size("expert")
+    n_dp = lax.axis_size("dp")
+    capacity = tok_rows * top_count * 5 // (4 * n_expert)
+    w_in, w_out = w_in[0], w_out[0]
+    units = w_out.shape[0]
+    ids = jnp.stack([lax.axis_index("expert"), lax.axis_index("dp") % 2]).astype(jnp.int32)
+
+    def across(x, s):
+        return lax.ppermute(x, "expert", [(i, i ^ s) for i in range(n_expert)]) if s else x
+
+    def beside(x, s):
+        return lax.ppermute(x, "dp", [(i, i ^ s) for i in range(n_dp)])
+
+    def after(x, *earlier):
+        return lax.optimization_barrier((x, *earlier))[0]
+
+    def after(x, *earlier):
+        return lax.optimization_barrier((x, *earlier))[0]
+
+    inside = lax.axis_index("expert") >= 0
+
+    def stage(body, *args):
+        shapes = jax.eval_shape(body, *args)
+        return lax.cond(inside, body, lambda *_: jax.tree.map(lambda x: jnp.zeros(x.shape, x.dtype), shapes), *args)
+
+    def up_part(blocks, *earlier):
+        first, *others = blocks
+        rows, grads, send, keep = up_step(ids, [after(first, *earlier), *others], weights, capacity, True)
+        return rows, grads, keep, beside(send, 1)
+
+    def x_part(state, *earlier):
+        rows, grads, keep, core = state
+        total = sum_step(after(keep, *earlier), core)
+        return (rows, grads, keep, core, beside(total, 2)), total
+
+    def act_part(state, *earlier):
+        rows, grads, keep, core, other = state
+        own = act_step(after(keep, *earlier), core, other)
+        return rows, grads, own, beside(own, 1)
+
+    def down_part(group, count):
+        return down_step(ids, *group[2:], weights, count, capacity, 1)
+
+    def with_next(state, count, next_blocks):
+        state, total = x_part(state)
+        next_state = up_part(next_blocks, total)
+        group = act_part(state)
+        next_state, _ = x_part(next_state, group[2])
+        return group, down_part(group, count), next_state
+
+    def own_stage(begun, next_blocks):
+        rows, grads, send, keep = begun
+        return with_next((rows, grads, keep, beside(send, 1)), size, next_blocks)
+
+    def far_stage(blocks, before):
+        state, total = x_part(up_part(blocks))
+        before = act_part(before, total)
+        back = down_part(before, size)
+        group = act_part(state, *[x for parts in back for x in parts])
+        return group, down_part(group, len(blocks)), before, back
+
+    def last_stage(blocks, next_blocks):
+        return with_next(up_part(blocks), len(blocks), next_blocks)
+
+    def rest_stage(state):
+        group = act_part(state)
+        return group, down_part(group, half - 2 * size)
+
+    half, quarter = n_expert // 2, n_expert // 4
+    size = half // 4
+    near, rest = [list(range(size)), list(range(size, 2 * size))], list(range(2 * size, half))
+    far, last = list(range(half, half + quarter)), list(range(half + quarter, n_expert))
+    sent = prep(ids, tokens, routes, route_weight, cotangent, n_expert, capacity)
+    came, home = {0: sent[0]}, {}
+
+    def blocks(sources, *earlier):
+        first, *others = [came[s] for s in sources]
+        return [after(first, *earlier), *others]
+
+    def start(sources, *earlier):
+        came.update({s: across(after(sent[s], *earlier) if earlier else sent[s], s) for s in sources if s})
+
+    def start_back(sources, back, *earlier):
+        for s, parts in zip(sources, back):
+            home[s] = [across(after(x, *earlier) if earlier else x, s) for x in parts]
+
+    def arrived(sources):
+        return [x for s in sources for x in home[s]]
+
+    rest_first, rest_second = rest[:size], rest[size:]
+    start(far + near[0] + near[1] + rest_first)
+    begun = up_step(ids, blocks(near[0]), [w_in, w_out], capacity, False)
+    begun, weights = begun[:4], begun[4:]
+    group_0, back_0, state_1 = stage(own_stage, begun, blocks(near[1]))
+    start_back(near[0], back_0)
+    start(last + rest_second, *blocks(far + rest_first), group_0[3])
+    group_far, back_far, group_1, back_1 = stage(far_stage, blocks(far, group_0[3]), state_1)
+    start_back(far + near[1], back_far + back_1, *blocks(last))
+    group_last, back_last, state_rest = stage(last_stage, blocks(last, group_far[3]), blocks(rest))
+    start_back(last, back_last, *arrived(far + near[1]))
+    group_rest, back_rest = stage(rest_stage, state_rest)
+    start_back(rest, back_rest)
+
+    def add(sources, partial, dtype):
+        return final(ids, routes, route_weight, [home[s] for s in sources], sources, capacity, partial, dtype)
+
+    groups = [group_0, group_far, group_1, group_last, group_rest]
+    grad_in, grad_out = grads_step(ids, groups, units)
+    partial = add(near[0] + near[1] + far, [], F32)
+    partial = add(last, partial, F32)
+    mixed, grad_tokens = add(rest, partial, BF)
+    return mixed, grad_tokens, grad_in[None], grad_out[None]
 
 
 def activate(pre_act, grad_hidden):
@@ -117,8 +604,10 @@
         P("expert", "dp", None),
         P("expert", None, "dp"),
     )
+    sizes = dict(mesh.shape)
+    chunked = sizes["dp"] == 4 and sizes["expert"] in (8, 16)
     return jax.shard_map(
-        per_device,
+        per_device_chunked if chunked else per_device,
         mesh=mesh,
         in_specs=placed,
         out_specs=(

time: 234 us -> 134 us (0.57)
  blocking collectives: 71.2 us -> 0 us
  Pallas kernels: 0 us -> 69.4 us
  waiting for transfers between devices: 71.2 us -> 30.9 us
  matrix products: 37 us -> 0 us
  local copies, waits for them, and re-layouts: 25.8 us -> 0.8 us
  starting transfers between devices: 9.88 us -> 31.5 us
  between operations: 13.9 us -> 0.8 us
  other arithmetic: 4.29 us -> 0.08 us
    pallas_call x0 -> x25, Pallas kernels: none -> 69.4 us  [the longest x18 34.4 us: call(): pl.pallas_call(kernel, out_shape=out_shapes, in_specs=[pl.BlockSpec(memor...]
    all_to_all x2 -> x0, blocking collectives: 61.7 us -> none  [the longest x1 32.9 us: per_device(): lax.all_to_all(send_grads, 'expert', split_axis=0, concat_axis=0, tiled=T...]
    reduce_scatter x2 -> x0, waiting for transfers between devices: 41.9 us -> none  [the longest x1 41.9 us: per_device(): lax.psum_scatter(pre_flat, 'dp', scatter_dimension=0, tiled=True)]
    dot_general x10 -> x0, matrix products: 37 us -> none  [the longest x1 6.54 us: per_device(): jnp.einsum('secd,edf->secf', rows_four, w_in, preferred_element_type=jnp....]
    ppermute x0 -> x29, starting transfers between devices: none -> 31.5 us  [the longest x14 23.7 us: across(): lax.ppermute(x, 'expert', [(i, i ^ s) for i in range(n_expert)])]
    ppermute x0 -> x29, waiting for transfers between devices: none -> 30.9 us  [the longest x15 30.2 us: beside(): return lax.ppermute(x, 'dp', [(i, i ^ s) for i in range(n_dp)])]
    all_to_all x2 -> x0, waiting for transfers between devices: 26.9 us -> none  [the longest x1 15 us: per_device(): lax.all_to_all(out_rows.reshape(n_expert, local_experts * capacity, featu...]
    reshape x7 -> x0, local copies, waits for them, and re-layouts: 11.9 us -> none  [the longest x1 3.7 us: per_device(): pre_flat = pre_part.reshape(total_rows, 2 * hidden_units)]
  transfers between devices with their start and end apart: 5 -> 29, of which waited for: 4 -> 13; matrix products, arithmetic and copies ran while one was open for 17% -> 0% of each run, Pallas kernels for 0% -> 47%
where the time goes in v2:
time: 134 us
  Pallas kernels  69.4 us (52%)
  starting transfers between devices  31.5 us (24%)
  waiting for transfers between devices  30.9 us (23%)
    pallas_call x18, Pallas kernels, call(): pl.pallas_call(kernel, out_shape=out_shapes, in_specs=[pl.BlockSpec(memor...  34.4 us
    ppermute x15, waiting for transfers between devices, beside(): return lax.ppermute(x, 'dp', [(i, i ^ s) for i in range(n_dp)])  30.2 us
    pallas_call x5, Pallas kernels, up_step(): pl.pallas_call(lambda *refs: up_kernel(capacity, held, *refs), out_shape=...  24.1 us
    ppermute x14, starting transfers between devices, across(): lax.ppermute(x, 'expert', [(i, i ^ s) for i in range(n_expert)])  23.7 us
    ppermute x15, starting transfers between devices, beside(): return lax.ppermute(x, 'dp', [(i, i ^ s) for i in range(n_dp)])  7.81 us
    pallas_call x1, Pallas kernels, grads_step(): pl.pallas_call(lambda *refs: grads_kernel(len(groups), *refs), out_shape=...  7.17 us
    pallas_call x1, Pallas kernels, prep(): pl.pallas_call(lambda *refs: prep_kernel(capacity, *refs), out_shape=[jax...  3.76 us
  transfers between devices with their start and end apart: 29, of which 13 were waited for; matrix products, arithmetic and copies ran while one was open for 0% of the time, Pallas kernels for 47%

profile of v2, /device:TPU:0, one launch (start us, length us, event | category | flops | bytes accessed | tf_op | source)
XLA Modules:
  0.0 133.6 jit_solution(9222559283558108634)
XLA Ops:
  0.7 3.8 %prep.1 = (bf16[120,1024]{1,0:T(8,128)(2,1)}, bf16[120,1024]{1,0:T(8,128)(2,1)}, bf16[120,1024]{1,0:T(8,128)(2,1)}, bf16[120,1024]{1,0:T(8,128)(2,1)}, bf16[120,...) custom-call(s32[2]{0:T(128)S(1)} %pad_add_fusion.refs_0_, ...), custom_call_target="tpu_custom_call" | custom-call | flops 1 | bytes 1 | tf_op jit(solution)/shard_map/prep/pallas_call | solution.py:77
  4.5 3.0 %collective-permute-start.18 = (bf16[120,1024]{1,0:T(8,128)(2,1)}, bf16[120,1024]{1,0:T(8,128)(2,1)S(1)}, u32[]{:S(2)}, u32[]{:S(2)}) collective-permute-start(bf16[120,1024]{1,0:T(8,128)(2,1)} %get-tuple-element.224), channel_id=1, source_target_pairs={{0,1},{1,0},{2,3},{3,2},{4,5},{5,4},{6,7},{7,6},{8,9},{9,8},{10,11... | collective-permute-start | bytes 737288 | tf_op jit(solution)/shard_map/ppermute | solution.py:388
  7.5 2.6 %collective-permute-start.15 = (bf16[120,1024]{1,0:T(8,128)(2,1)}, bf16[120,1024]{1,0:T(8,128)(2,1)S(1)}, u32[]{:S(2)}, u32[]{:S(2)}) collective-permute-start(bf16[120,1024]{1,0:T(8,128)(2,1)} %get-tuple-element.215), channel_id=1, source_target_pairs={{0,4},{1,5},{2,6},{3,7},{4,0},{5,1},{6,2},{7,3},{8,12},{9,13},{10,... | collective-permute-start | bytes 737288 | tf_op jit(solution)/shard_map/ppermute | solution.py:388
  10.1 1.9 %collective-permute-start.17 = (bf16[120,1024]{1,0:T(8,128)(2,1)}, bf16[120,1024]{1,0:T(8,128)(2,1)S(1)}, u32[]{:S(2)}, u32[]{:S(2)}) collective-permute-start(bf16[120,1024]{1,0:T(8,128)(2,1)} %get-tuple-element.217), channel_id=1, source_target_pairs={{0,2},{1,3},{2,0},{3,1},{4,6},{5,7},{6,4},{7,5},{8,10},{9,11},{10,... | collective-permute-start | bytes 737288 | tf_op jit(solution)/shard_map/ppermute | solution.py:388
  12.0 6.0 %up.9 = (bf16[64,1024]{1,0:T(8,128)(2,1)}, bf16[64,1024]{1,0:T(8,128)(2,1)}, bf16[64,1536]{1,0:T(8,128)(2,1)}, f32[64,1536]{1,0:T(8,128)S(1)}, bf16[512,2048]{1,...) custom-call(s32[2]{0:T(128)S(1)} %pad_add_fusion.refs_0_, ...), custom_call_target="tpu_custom_call" | custom-call | flops 1 | bytes 1 | tf_op jit(solution)/shard_map/up/pallas_call | solution.py:167
  18.0 18.2 %conditional.4 = (bf16[64,1024]{1,0:T(8,128)(2,1)}, bf16[64,1024]{1,0:T(8,128)(2,1)}, bf16[64,1536]{1,0:T(8,128)(2,1)}, bf16[64,1536]{1,0:T(8,128)(2,1)}, bf16[1...) conditional(s32[]{:T(128)} %convert_element_type.2, () %tuple.58, ...), branch_computations={%region_0.1_spmd, %region_1.2_spmd} | conditional | flops 5 | bytes 21692784 | solution.py:403
  18.1 1.6 %collective-permute-done.core = bf16[64,1536]{1,0:T(8,128)(2,1)S(1)} collective-permute-done((bf16[64,1536]{1,0:T(8,128)(2,1)}, bf16[64,1536]{1,0:T(8,128)(2,1)S(1)}, u32[]{:S(2)}, u32[]{:S(2)}) %collective-permute-start) | collective-permute-done | bytes 196640 | tf_op jit(solution)/shard_map/cond/branch_1_fun/ppermute | solution.py:391
  19.8 1.6 %collective-permute-start.1 = (bf16[64,1536]{1,0:T(8,128)(2,1)S(1)}, bf16[64,1536]{1,0:T(8,128)(2,1)S(1)}, u32[]{:S(2)}, u32[]{:S(2)}) collective-permute-start(bf16[64,1536]{1,0:T(8,128)(2,1)S(1)} %total.5), channel_id=1, source_target_pairs={{0,16},{8,24},{16,0},{24,8},{1,17},{9,25},{17,1},{25,9},{2,18},{10... | collective-permute-start | bytes 589832 | tf_op jit(solution)/shard_map/cond/branch_1_fun/ppermute | solution.py:391
  21.3 4.8 %up.5 = (bf16[64,1024]{1,0:T(8,128)(2,1)S(1)}, bf16[64,1024]{1,0:T(8,128)(2,1)S(1)}, bf16[64,1536]{1,0:T(8,128)(2,1)S(1)}, f32[64,1536]{1,0:T(8,128)}) custom-call(s32[2]{0:T(128)S(1)} %get-tuple-element.78.refs_0_, bf16[120,1024]{1,0:T(8,128)(2,1)} %copy-done.18, bf16[512,2048]{1,0:T(8,128)(2,1)S(1)} %get-tuple-element.79.refs_3_.refs_2_, ...), custom_call_target="tpu_custom_call" | custom-call | flops 1 | bytes 1 | tf_op jit(solution)/shard_map/cond/branch_1_fun/up/pallas_call | solution.py:167
  27.7 1.1 total.6
  28.8 1.4 %collective-permute-start.4 = (bf16[64,1536]{1,0:T(8,128)(2,1)S(1)}, bf16[64,1536]{1,0:T(8,128)(2,1)}, u32[]{:S(2)}, u32[]{:S(2)}) collective-permute-start(bf16[64,1536]{1,0:T(8,128)(2,1)S(1)} %total.6), channel_id=1, source_target_pairs={{0,16},{8,24},{16,0},{24,8},{1,17},{9,25},{17,1},{25,9},{2,18},{10... | collective-permute-start | bytes 589832 | tf_op jit(solution)/shard_map/cond/branch_1_fun/ppermute | solution.py:391
  30.3 3.0 %down.5 = bf16[120,1024]{1,0:T(8,128)(2,1)S(1)} custom-call(s32[2]{0:T(128)S(1)} %get-tuple-element.78.refs_0_, bf16[64,1536]{1,0:T(8,128)(2,1)} %act.5.refs_1_, bf16[64,1536]{1,0:T(8,128)(2,1)} %collective-permute-done.2.refs_2_, bf16[512,2048]{1,0:T(8,128)(2,1)S(1)} %get-tuple-element.79.refs_3_.refs_2_, bf16[512,2048]{1,0:T(8,128)(2,1)S(1)} %copy-done.2, ...), custom_call_target="tpu_custom_call" | custom-call | flops 1 | bytes 1 | tf_op jit(solution)/shard_map/cond/branch_1_fun/down/pallas_call | solution.py:93
  33.3 2.9 %collective-permute-done.4 = bf16[64,1536]{1,0:T(8,128)(2,1)} collective-permute-done((bf16[64,1536]{1,0:T(8,128)(2,1)S(1)}, bf16[64,1536]{1,0:T(8,128)(2,1)}, u32[]{:S(2)}, u32[]{:S(2)}) %collective-permute-start.4) | collective-permute-done | bytes 196640 | tf_op jit(solution)/shard_map/cond/branch_1_fun/ppermute | solution.py:391
  36.2 2.5 %collective-permute-start.19 = (bf16[120,1024]{1,0:T(8,128)(2,1)}, bf16[120,1024]{1,0:T(8,128)(2,1)S(1)}, u32[]{:S(2)}, u32[]{:S(2)}) collective-permute-start(bf16[120,1024]{1,0:T(8,128)(2,1)} %get-tuple-element.228), channel_id=1, source_target_pairs={{0,6},{1,7},{2,4},{3,5},{4,2},{5,3},{6,0},{7,1},{8,14},{9,15},{10,... | collective-permute-start | bytes 737288 | tf_op jit(solution)/shard_map/ppermute | solution.py:388
  38.8 2.3 %collective-permute-start.20 = (bf16[120,1024]{1,0:T(8,128)(2,1)}, bf16[120,1024]{1,0:T(8,128)(2,1)}, u32[]{:S(2)}, u32[]{:S(2)}) collective-permute-start(bf16[120,1024]{1,0:T(8,128)(2,1)} %get-tuple-element.238), channel_id=1, source_target_pairs={{0,7},{1,6},{2,5},{3,4},{4,3},{5,2},{6,1},{7,0},{8,15},{9,14},{10,... | collective-permute-start | bytes 737288 | tf_op jit(solution)/shard_map/ppermute | solution.py:388
  41.1 24.8 %conditional.5 = (bf16[128,1024]{1,0:T(8,128)(2,1)}, bf16[128,1024]{1,0:T(8,128)(2,1)}, bf16[128,1536]{1,0:T(8,128)(2,1)}, bf16[128,1536]{1,0:T(8,128)(2,1)}, bf...) conditional(s32[]{:T(128)} %convert_element_type.2, () %tuple.61, ...), branch_computations={%region_2.3_spmd, %region_3.4_spmd} | conditional | flops 6 | bytes 24641928 | solution.py:403
  41.1 4.7 %up.6 = (bf16[128,1024]{1,0:T(8,128)(2,1)}, bf16[128,1024]{1,0:T(8,128)(2,1)}, bf16[128,1536]{1,0:T(8,128)(2,1)S(1)}, f32[128,1536]{1,0:T(8,128)S(1)}) custom-call(s32[2]{0:T(128)S(1)} %get-tuple-element.89.refs_0_, bf16[120,1024]{1,0:T(8,128)(2,1)S(1)} %get-tuple-element.90.refs_1_, bf16[120,1024]{1,0:T(8,128)(2,1)} %get-tuple-element.91.refs_2_, ...), custom_call_target="tpu_custom_call" | custom-call | flops 1 | bytes 1 | tf_op jit(solution)/shard_map/cond/branch_1_fun/up/pallas_call | solution.py:167
  45.8 1.7 %collective-permute-done.5.core = bf16[128,1536]{1,0:T(8,128)(2,1)S(1)} collective-permute-done((bf16[128,1536]{1,0:T(8,128)(2,1)S(1)}, bf16[128,1536]{1,0:T(8,128)(2,1)S(1)}, u32[]{:S(2)}, u32[]{:S(2)}) %collective-permute-start.5) | collective-permute-done | bytes 393248 | tf_op jit(solution)/shard_map/cond/branch_1_fun/ppermute | solution.py:391
  47.6 1.6 %collective-permute-start.7 = (bf16[128,1536]{1,0:T(8,128)(2,1)S(1)}, bf16[128,1536]{1,0:T(8,128)(2,1)S(1)}, u32[]{:S(2)}, u32[]{:S(2)}) collective-permute-start(bf16[128,1536]{1,0:T(8,128)(2,1)S(1)} %total.7), channel_id=1, source_target_pairs={{0,16},{8,24},{16,0},{24,8},{1,17},{9,25},{17,1},{25,9},{2,18},{10... | collective-permute-start | bytes 1179656 | tf_op jit(solution)/shard_map/cond/branch_1_fun/ppermute | solution.py:391
  49.1 1.3 act.6.refs_1_
  50.5 1.4 %collective-permute-done.6.refs_2_ = bf16[64,1536]{1,0:T(8,128)(2,1)S(1)} collective-permute-done((bf16[64,1536]{1,0:T(8,128)(2,1)S(1)}, bf16[64,1536]{1,0:T(8,128)(2,1)S(1)}, u32[]{:S(2)}, u32[]{:S(2)}) %collective-permute-start.6) | collective-permute-done | bytes 196640 | tf_op jit(solution)/shard_map/cond/branch_1_fun/ppermute | solution.py:391
  51.9 3.2 %down.6 = bf16[120,1024]{1,0:T(8,128)(2,1)} custom-call(s32[2]{0:T(128)S(1)} %get-tuple-element.89.refs_0_, bf16[64,1536]{1,0:T(8,128)(2,1)S(1)} %act.6.refs_1_, bf16[64,1536]{1,0:T(8,128)(2,1)S(1)} %collective-permute-done.6.refs_2_, bf16[512,2048]{1,0:T(8,128)(2,1)S(1)} %get-tuple-element.92.refs_3_, bf16[512,2048]{1,0:T(8,128)(2,1)S(1)} %copy-done.3, ...), custom_call_target="tpu_custom_call" | custom-call | flops 1 | bytes 1 | tf_op jit(solution)/shard_map/cond/branch_1_fun/down/pallas_call | solution.py:93
  55.1 3.6 %collective-permute-done.7.other = bf16[128,1536]{1,0:T(8,128)(2,1)S(1)} collective-permute-done((bf16[128,1536]{1,0:T(8,128)(2,1)S(1)}, bf16[128,1536]{1,0:T(8,128)(2,1)S(1)}, u32[]{:S(2)}, u32[]{:S(2)}) %collective-permute-start.7) | collective-permute-done | bytes 393248 | tf_op jit(solution)/shard_map/cond/branch_1_fun/ppermute | solution.py:391
  58.8 1.0 act.7.refs_1_
  59.8 2.1 %collective-permute-done.8.refs_2_ = bf16[128,1536]{1,0:T(8,128)(2,1)} collective-permute-done((bf16[128,1536]{1,0:T(8,128)(2,1)}, bf16[128,1536]{1,0:T(8,128)(2,1)}, u32[]{:S(2)}, u32[]{:S(2)}) %collective-permute-start.8) | collective-permute-done | bytes 393248 | tf_op jit(solution)/shard_map/cond/branch_1_fun/ppermute | solution.py:391
  61.9 4.0 %down.7 = (bf16[120,1024]{1,0:T(8,128)(2,1)}, bf16[120,1024]{1,0:T(8,128)(2,1)}) custom-call(s32[2]{0:T(128)S(1)} %get-tuple-element.89.refs_0_, bf16[128,1536]{1,0:T(8,128)(2,1)} %act.7.refs_1_, bf16[128,1536]{1,0:T(8,128)(2,1)} %collective-permute-done.8.refs_2_, bf16[512,2048]{1,0:T(8,128)(2,1)S(1)} %get-tuple-element.92.refs_3_, ...), custom_call_target="tpu_custom_call" | custom-call | flops 1 | bytes 1 | tf_op jit(solution)/shard_map/cond/branch_1_fun/down/pallas_call | solution.py:93
  67.5 3.6 %collective-permute-start.25 = (bf16[120,1024]{1,0:T(8,128)(2,1)}, bf16[120,1024]{1,0:T(8,128)(2,1)S(1)}, u32[]{:S(2)}, u32[]{:S(2)}) collective-permute-start(bf16[120,1024]{1,0:T(8,128)(2,1)} %get-tuple-element.252), channel_id=1, source_target_pairs={{0,5},{1,4},{2,7},{3,6},{4,1},{5,0},{6,3},{7,2},{8,13},{9,12},{10,... | collective-permute-start | bytes 737288 | tf_op jit(solution)/shard_map/ppermute | solution.py:388
  71.2 32.1 %conditional.6 = (bf16[128,1024]{1,0:T(8,128)(2,1)}, bf16[128,1024]{1,0:T(8,128)(2,1)}, bf16[128,1536]{1,0:T(8,128)(2,1)}, bf16[128,1536]{1,0:T(8,128)(2,1)}, bf...) conditional(s32[]{:T(128)} %convert_element_type.2, () %tuple.57, ...), branch_computations={%region_4.5_spmd, %region_5.6_spmd} | conditional | flops 6 | bytes 24641884 | solution.py:403
  71.2 5.1 %up.7 = (bf16[128,1024]{1,0:T(8,128)(2,1)}, bf16[128,1024]{1,0:T(8,128)(2,1)}, bf16[128,1536]{1,0:T(8,128)(2,1)S(1)}, f32[128,1536]{1,0:T(8,128)S(1)}) custom-call(s32[2]{0:T(128)S(1)} %get-tuple-element.108.refs_0_, bf16[120,1024]{1,0:T(8,128)(2,1)} %get-tuple-element.109.refs_1_, bf16[120,1024]{1,0:T(8,128)(2,1)} %get-tuple-element.110.refs_2_, ...), custom_call_target="tpu_custom_call" | custom-call | flops 1 | bytes 1 | tf_op jit(solution)/shard_map/cond/branch_1_fun/up/pallas_call | solution.py:167
  76.3 1.7 %collective-permute-done.9.core = bf16[128,1536]{1,0:T(8,128)(2,1)S(1)} collective-permute-done((bf16[128,1536]{1,0:T(8,128)(2,1)S(1)}, bf16[128,1536]{1,0:T(8,128)(2,1)S(1)}, u32[]{:S(2)}, u32[]{:S(2)}) %collective-permute-start.9) | collective-permute-done | bytes 393248 | tf_op jit(solution)/shard_map/cond/branch_1_fun/ppermute | solution.py:391
  78.1 1.6 %collective-permute-start.10 = (bf16[128,1536]{1,0:T(8,128)(2,1)S(1)}, bf16[128,1536]{1,0:T(8,128)(2,1)S(1)}, u32[]{:S(2)}, u32[]{:S(2)}) collective-permute-start(bf16[128,1536]{1,0:T(8,128)(2,1)S(1)} %total.8), channel_id=1, source_target_pairs={{0,16},{8,24},{16,0},{24,8},{1,17},{9,25},{17,1},{25,9},{2,18},{10... | collective-permute-start | bytes 1179656 | tf_op jit(solution)/shard_map/cond/branch_1_fun/ppermute | solution.py:391
  79.6 3.5 %up.8 = (bf16[128,1024]{1,0:T(8,128)(2,1)S(1)}, bf16[128,1024]{1,0:T(8,128)(2,1)S(1)}, bf16[128,1536]{1,0:T(8,128)(2,1)S(1)}, f32[128,1536]{1,0:T(8,128)}) custom-call(s32[2]{0:T(128)S(1)} %get-tuple-element.108.refs_0_, bf16[120,1024]{1,0:T(8,128)(2,1)S(1)} %get-tuple-element.121.refs_1_, bf16[120,1024]{1,0:T(8,128)(2,1)} %get-tuple-element.122.refs_2_, ...), custom_call_target="tpu_custom_call" | custom-call | flops 1 | bytes 1 | tf_op jit(solution)/shard_map/cond/branch_1_fun/up/pallas_call | solution.py:167
  83.1 6.2 %collective-permute-done.10.other = bf16[128,1536]{1,0:T(8,128)(2,1)S(1)} collective-permute-done((bf16[128,1536]{1,0:T(8,128)(2,1)S(1)}, bf16[128,1536]{1,0:T(8,128)(2,1)S(1)}, u32[]{:S(2)}, u32[]{:S(2)}) %collective-permute-start.10) | collective-permute-done | bytes 393248 | tf_op jit(solution)/shard_map/cond/branch_1_fun/ppermute | solution.py:391
  90.3 1.3 total.9
  91.6 1.6 %collective-permute-start.13 = (bf16[128,1536]{1,0:T(8,128)(2,1)S(1)}, bf16[128,1536]{1,0:T(8,128)(2,1)}, u32[]{:S(2)}, u32[]{:S(2)}) collective-permute-start(bf16[128,1536]{1,0:T(8,128)(2,1)S(1)} %total.9), channel_id=1, source_target_pairs={{0,16},{8,24},{16,0},{24,8},{1,17},{9,25},{17,1},{25,9},{2,18},{10... | collective-permute-start | bytes 1179656 | tf_op jit(solution)/shard_map/cond/branch_1_fun/ppermute | solution.py:391
  93.1 4.0 %down.8 = (bf16[120,1024]{1,0:T(8,128)(2,1)}, bf16[120,1024]{1,0:T(8,128)(2,1)}) custom-call(s32[2]{0:T(128)S(1)} %get-tuple-element.108.refs_0_, bf16[128,1536]{1,0:T(8,128)(2,1)} %act.8.refs_1_, bf16[128,1536]{1,0:T(8,128)(2,1)} %collective-permute-done.11.refs_2_, bf16[512,2048]{1,0:T(8,128)(2,1)S(1)} %get-tuple-element.111.refs_3_, ...), custom_call_target="tpu_custom_call" | custom-call | flops 1 | bytes 1 | tf_op jit(solution)/shard_map/cond/branch_1_fun/down/pallas_call | solution.py:93
  97.1 6.1 %collective-permute-done.13 = bf16[128,1536]{1,0:T(8,128)(2,1)} collective-permute-done((bf16[128,1536]{1,0:T(8,128)(2,1)S(1)}, bf16[128,1536]{1,0:T(8,128)(2,1)}, u32[]{:S(2)}, u32[]{:S(2)}) %collective-permute-start.13) | collective-permute-done | bytes 393248 | tf_op jit(solution)/shard_map/cond/branch_1_fun/ppermute | solution.py:391
  103.3 3.0 %collective-permute-start.28 = (bf16[120,1024]{1,0:T(8,128)(2,1)}, bf16[120,1024]{1,0:T(8,128)(2,1)S(1)}, u32[]{:S(2)}, u32[]{:S(2)}) collective-permute-start(bf16[120,1024]{1,0:T(8,128)(2,1)} %get-tuple-element.257), channel_id=1, source_target_pairs={{0,7},{1,6},{2,5},{3,4},{4,3},{5,2},{6,1},{7,0},{8,15},{9,14},{10,... | collective-permute-start | bytes 737288 | tf_op jit(solution)/shard_map/ppermute | solution.py:388
  106.3 1.7 %collective-permute-start.27 = (bf16[120,1024]{1,0:T(8,128)(2,1)}, bf16[120,1024]{1,0:T(8,128)(2,1)S(1)}, u32[]{:S(2)}, u32[]{:S(2)}) collective-permute-start(bf16[120,1024]{1,0:T(8,128)(2,1)} %get-tuple-element.255), channel_id=1, source_target_pairs={{0,6},{1,7},{2,4},{3,5},{4,2},{5,3},{6,0},{7,1},{8,14},{9,15},{10,... | collective-permute-start | bytes 737288 | tf_op jit(solution)/shard_map/ppermute | solution.py:388
  108.0 9.7 %conditional.7 = (bf16[128,1024]{1,0:T(8,128)(2,1)S(1)}, bf16[128,1024]{1,0:T(8,128)(2,1)S(1)}, bf16[128,1536]{1,0:T(8,128)(2,1)}, bf16[128,1536]{1,0:T(8,128)(2...) conditional(s32[]{:T(128)} %convert_element_type.2, () %tuple.56, (f32[128,1536]{1,0:T(8,128)}, ...), branch_computations={%region_6.7_spmd, %region_7.8_spmd} | conditional | flops 2 | bytes 1802300 | solution.py:403
  108.0 2.3 %act.9.refs_1_ = bf16[128,1536]{1,0:T(8,128)(2,1)} custom-call(f32[128,1536]{1,0:T(8,128)} %get-tuple-element.130.keep, bf16[128,1536]{1,0:T(8,128)(2,1)} %get-tuple-element.131.core, bf16[128,1536]{1,0:T(8,128)(2,1)} %get-tuple-element.132.other), custom_call_target="tpu_custom_call" | custom-call | flops 1 | bytes 1 | tf_op jit(solution)/shard_map/cond/branch_1_fun/act/pallas_call | solution.py:93
  110.3 2.1 %collective-permute-done.14.refs_2_ = bf16[128,1536]{1,0:T(8,128)(2,1)} collective-permute-done((bf16[128,1536]{1,0:T(8,128)(2,1)}, bf16[128,1536]{1,0:T(8,128)(2,1)}, u32[]{:S(2)}, u32[]{:S(2)}) %collective-permute-start.14) | collective-permute-done | bytes 393248 | tf_op jit(solution)/shard_map/cond/branch_1_fun/ppermute | solution.py:391
  112.4 5.4 %down.9 = (bf16[120,1024]{1,0:T(8,128)(2,1)}, bf16[120,1024]{1,0:T(8,128)(2,1)}) custom-call(s32[2]{0:T(128)S(1)} %get-tuple-element.133.refs_0_, bf16[128,1536]{1,0:T(8,128)(2,1)} %act.9.refs_1_, bf16[128,1536]{1,0:T(8,128)(2,1)} %collective-permute-done.14.refs_2_, bf16[512,2048]{1,0:T(8,128)(2,1)S(1)} %get-tuple-element.134.refs_3_, ...), custom_call_target="tpu_custom_call" | custom-call | flops 1 | bytes 1 | tf_op jit(solution)/shard_map/cond/branch_1_fun/down/pallas_call | solution.py:93
  117.9 2.0 %collective-permute-start.23 = (bf16[120,1024]{1,0:T(8,128)(2,1)}, bf16[120,1024]{1,0:T(8,128)(2,1)S(1)}, u32[]{:S(2)}, u32[]{:S(2)}) collective-permute-start(bf16[120,1024]{1,0:T(8,128)(2,1)} %get-tuple-element.247), channel_id=1, source_target_pairs={{0,3},{1,2},{2,1},{3,0},{4,7},{5,6},{6,5},{7,4},{8,11},{9,10},{10,... | collective-permute-start | bytes 737288 | tf_op jit(solution)/shard_map/ppermute | solution.py:388
  119.9 7.2 %grads.1 = (bf16[1024,2048]{1,0:T(8,128)(2,1)}, bf16[1024,1024]{1,0:T(8,128)(2,1)}) custom-call(s32[2]{0:T(128)S(1)} %pad_add_fusion.refs_0_, bf16[64,1024]{1,0:T(8,128)(2,1)} %get-tuple-element.265.refs_1_, bf16[64,1024]{1,0:T(8,128)(2,1)} %get-tuple-element.266.refs_2_, bf16[64,1536]{1,0:T(8,128)(2,1)} %get-tuple-element.267.refs_3_, ...), custom_call_target="tpu_custom_call" | custom-call | flops 1 | bytes 1 | tf_op jit(solution)/shard_map/grads/pallas_call | solution.py:296
  127.1 2.0 %final.3 = (f32[192,1024]{1,0:T(8,128)S(1)}, f32[192,1024]{1,0:T(8,128)S(1)}) custom-call(s32[2]{0:T(128)S(1)} %pad_add_fusion.refs_0_, s32[2,192]{1,0:T(2,128)S(1)} %bitcast.9, f32[2,192]{1,0:T(2,128)S(1)} %bitcast.13, bf16[120,1024]{1,0:T(8,128)(2,1)S(1)} %copy-done.14, bf16[120,1024]{1,0:T(8,128)(2,1)S(1)} %collective-permute-done.26.refs_4_, ...), custom_call_target="tpu_custom_call" | custom-call | flops 1 | bytes 1 | tf_op jit(solution)/shard_map/final/pallas_call | solution.py:93
  129.1 1.5 %final.4 = (f32[192,1024]{1,0:T(8,128)S(1)}, f32[192,1024]{1,0:T(8,128)S(1)}) custom-call(s32[2]{0:T(128)S(1)} %pad_add_fusion.refs_0_, s32[2,192]{1,0:T(2,128)S(1)} %bitcast.10, f32[2,192]{1,0:T(2,128)S(1)} %bitcast.14, bf16[120,1024]{1,0:T(8,128)(2,1)S(1)} %collective-permute-done.27.refs_3_, bf16[120,1024]{1,0:T(8,128)(2,1)S(1)} %collective-permute-done.28.refs_4_, ...), custom_call_target="tpu_custom_call" | custom-call | flops 1 | bytes 1 | tf_op jit(solution)/shard_map/final/pallas_call | solution.py:93
  131.3 2.3 %final.5 = (bf16[192,1024]{1,0:T(8,128)(2,1)}, bf16[192,1024]{1,0:T(8,128)(2,1)}) custom-call(s32[2]{0:T(128)S(1)} %pad_add_fusion.refs_0_, s32[2,192]{1,0:T(2,128)S(1)} %bitcast.11, f32[2,192]{1,0:T(2,128)S(1)} %bitcast.15, bf16[120,1024]{1,0:T(8,128)(2,1)S(1)} %collective-permute-done.22.refs_3_, bf16[120,1024]{1,0:T(8,128)(2,1)S(1)} %collective-permute-done.23.refs_4_, ...), custom_call_target="tpu_custom_call" | custom-call | flops 1 | bytes 1 | tf_op jit(solution)/shard_map/final/pallas_call | solution.py:93
  (78 shorter events, 5.6 us)
Async XLA Ops:
  4.5 13.5 %collective-permute-start.18 = (bf16[120,1024]{1,0:T(8,128)(2,1)}, bf16[120,1024]{1,0:T(8,128)(2,1)S(1)}, u32[]{:S(2)}, u32[]{:S(2)}) collective-permute-start(bf16[120,1024]{1,0:T(8,128)(2,1)} %get-tuple-element.224), channel_id=1, source_target_pairs={{0,1},{1,0},{2,3},{3,2},{4,5},{5,4},{6,7},{7,6},{8,9},{9,8},{10,11... | collective-permute-start | bytes 737288 | tf_op jit(solution)/shard_map/ppermute | solution.py:388
  7.5 28.7 %collective-permute-start.15 = (bf16[120,1024]{1,0:T(8,128)(2,1)}, bf16[120,1024]{1,0:T(8,128)(2,1)S(1)}, u32[]{:S(2)}, u32[]{:S(2)}) collective-permute-start(bf16[120,1024]{1,0:T(8,128)(2,1)} %get-tuple-element.215), channel_id=1, source_target_pairs={{0,4},{1,5},{2,6},{3,7},{4,0},{5,1},{6,2},{7,3},{8,12},{9,13},{10,... | collective-permute-start | bytes 737288 | tf_op jit(solution)/shard_map/ppermute | solution.py:388
  10.1 26.1 %collective-permute-start.16 = (bf16[120,1024]{1,0:T(8,128)(2,1)}, bf16[120,1024]{1,0:T(8,128)(2,1)}, u32[]{:S(2)}, u32[]{:S(2)}) collective-permute-start(bf16[120,1024]{1,0:T(8,128)(2,1)} %get-tuple-element.216), channel_id=1, source_target_pairs={{0,5},{1,4},{2,7},{3,6},{4,1},{5,0},{6,3},{7,2},{8,13},{9,12},{10,... | collective-permute-start | bytes 737288 | tf_op jit(solution)/shard_map/ppermute | solution.py:388
  10.1 26.1 %collective-permute-start.17 = (bf16[120,1024]{1,0:T(8,128)(2,1)}, bf16[120,1024]{1,0:T(8,128)(2,1)S(1)}, u32[]{:S(2)}, u32[]{:S(2)}) collective-permute-start(bf16[120,1024]{1,0:T(8,128)(2,1)} %get-tuple-element.217), channel_id=1, source_target_pairs={{0,2},{1,3},{2,0},{3,1},{4,6},{5,7},{6,4},{7,5},{8,10},{9,11},{10,... | collective-permute-start | bytes 737288 | tf_op jit(solution)/shard_map/ppermute | solution.py:388
  18.0 3.3 %copy-start.18 = (bf16[120,1024]{1,0:T(8,128)(2,1)}, bf16[120,1024]{1,0:T(8,128)(2,1)S(1)}, u32[]{:S(2)}) copy-start(bf16[120,1024]{1,0:T(8,128)(2,1)S(1)} %get-tuple-element.83.refs_1_) | copy-start | bytes 737284 | tf_op jit(solution)/shard_map/cond
  18.0 1.7 %collective-permute-start = (bf16[64,1536]{1,0:T(8,128)(2,1)}, bf16[64,1536]{1,0:T(8,128)(2,1)S(1)}, u32[]{:S(2)}, u32[]{:S(2)}) collective-permute-start(bf16[64,1536]{1,0:T(8,128)(2,1)} %get-tuple-element.77), channel_id=1, source_target_pairs={{0,8},{8,0},{16,24},{24,16},{1,9},{9,1},{17,25},{25,17},{2,10},{10... | collective-permute-start | bytes 589832 | tf_op jit(solution)/shard_map/cond/branch_1_fun/ppermute | solution.py:391
  19.8 7.0 %collective-permute-start.1 = (bf16[64,1536]{1,0:T(8,128)(2,1)S(1)}, bf16[64,1536]{1,0:T(8,128)(2,1)S(1)}, u32[]{:S(2)}, u32[]{:S(2)}) collective-permute-start(bf16[64,1536]{1,0:T(8,128)(2,1)S(1)} %total.5), channel_id=1, source_target_pairs={{0,16},{8,24},{16,0},{24,8},{1,17},{9,25},{17,1},{25,9},{2,18},{10... | collective-permute-start | bytes 589832 | tf_op jit(solution)/shard_map/cond/branch_1_fun/ppermute | solution.py:391
  21.3 8.9 %copy-start.2 = (bf16[512,2048]{1,0:T(8,128)(2,1)S(1)}, bf16[512,2048]{1,0:T(8,128)(2,1)}, u32[]{:S(2)}) copy-start(bf16[512,2048]{1,0:T(8,128)(2,1)} %get-tuple-element.80.refs_4_.refs_3_) | copy-start | bytes 6291460 | tf_op jit(solution)/shard_map/cond
  21.3 8.9 %copy-start.5 = (bf16[1024,1024]{1,0:T(8,128)(2,1)S(1)}, bf16[1024,1024]{1,0:T(8,128)(2,1)}, u32[]{:S(2)}) copy-start(bf16[1024,1024]{1,0:T(8,128)(2,1)} %get-tuple-element.81.refs_5_.refs_4_) | copy-start | bytes 6291460 | tf_op jit(solution)/shard_map/cond
  26.2 1.6 %collective-permute-start.3 = (bf16[64,1536]{1,0:T(8,128)(2,1)S(1)}, bf16[64,1536]{1,0:T(8,128)(2,1)}, u32[]{:S(2)}, u32[]{:S(2)}) collective-permute-start(bf16[64,1536]{1,0:T(8,128)(2,1)S(1)} %get-tuple-element.87), channel_id=1, source_target_pairs={{0,8},{8,0},{16,24},{24,16},{1,9},{9,1},{17,25},{25,17},{2,10},{10... | collective-permute-start | bytes 589832 | tf_op jit(solution)/shard_map/cond/branch_1_fun/ppermute | solution.py:391
  27.6 2.6 %collective-permute-start.2 = (bf16[64,1536]{1,0:T(8,128)(2,1)}, bf16[64,1536]{1,0:T(8,128)(2,1)}, u32[]{:S(2)}, u32[]{:S(2)}) collective-permute-start(bf16[64,1536]{1,0:T(8,128)(2,1)} %act.5.refs_1_), channel_id=1, source_target_pairs={{0,8},{8,0},{16,24},{24,16},{1,9},{9,1},{17,25},{25,17},{2,10},{10... | collective-permute-start | bytes 589832 | tf_op jit(solution)/shard_map/cond/branch_1_fun/ppermute | solution.py:391
  28.8 7.4 %collective-permute-start.4 = (bf16[64,1536]{1,0:T(8,128)(2,1)S(1)}, bf16[64,1536]{1,0:T(8,128)(2,1)}, u32[]{:S(2)}, u32[]{:S(2)}) collective-permute-start(bf16[64,1536]{1,0:T(8,128)(2,1)S(1)} %total.6), channel_id=1, source_target_pairs={{0,16},{8,24},{16,0},{24,8},{1,17},{9,25},{17,1},{25,9},{2,18},{10... | collective-permute-start | bytes 589832 | tf_op jit(solution)/shard_map/cond/branch_1_fun/ppermute | solution.py:391
  36.2 4.9 %copy-start.13 = (bf16[120,1024]{1,0:T(8,128)(2,1)}, bf16[120,1024]{1,0:T(8,128)(2,1)S(1)}, u32[]{:S(2)}) copy-start(bf16[120,1024]{1,0:T(8,128)(2,1)S(1)} %get-tuple-element.258.refs_3_) | copy-start | bytes 737284
  36.2 29.7 %collective-permute-start.19 = (bf16[120,1024]{1,0:T(8,128)(2,1)}, bf16[120,1024]{1,0:T(8,128)(2,1)S(1)}, u32[]{:S(2)}, u32[]{:S(2)}) collective-permute-start(bf16[120,1024]{1,0:T(8,128)(2,1)} %get-tuple-element.228), channel_id=1, source_target_pairs={{0,6},{1,7},{2,4},{3,5},{4,2},{5,3},{6,0},{7,1},{8,14},{9,15},{10,... | collective-permute-start | bytes 737288 | tf_op jit(solution)/shard_map/ppermute | solution.py:388
  38.8 27.2 %collective-permute-start.20 = (bf16[120,1024]{1,0:T(8,128)(2,1)}, bf16[120,1024]{1,0:T(8,128)(2,1)}, u32[]{:S(2)}, u32[]{:S(2)}) collective-permute-start(bf16[120,1024]{1,0:T(8,128)(2,1)} %get-tuple-element.238), channel_id=1, source_target_pairs={{0,7},{1,6},{2,5},{3,4},{4,3},{5,2},{6,1},{7,0},{8,15},{9,14},{10,... | collective-permute-start | bytes 737288 | tf_op jit(solution)/shard_map/ppermute | solution.py:388
  41.1 30.1 %collective-permute-start.21 = (bf16[120,1024]{1,0:T(8,128)(2,1)}, bf16[120,1024]{1,0:T(8,128)(2,1)}, u32[]{:S(2)}, u32[]{:S(2)}) collective-permute-start(bf16[120,1024]{1,0:T(8,128)(2,1)} %get-tuple-element.240), channel_id=1, source_target_pairs={{0,3},{1,2},{2,1},{3,0},{4,7},{5,6},{6,5},{7,4},{8,11},{9,10},{10,... | collective-permute-start | bytes 737288 | tf_op jit(solution)/shard_map/ppermute | solution.py:388
  41.1 10.8 %copy-start.6 = (bf16[1024,1024]{1,0:T(8,128)(2,1)S(1)}, bf16[1024,1024]{1,0:T(8,128)(2,1)}, u32[]{:S(2)}) copy-start(bf16[1024,1024]{1,0:T(8,128)(2,1)} %get-tuple-element.94.refs_5_) | copy-start | bytes 6291460 | tf_op jit(solution)/shard_map/cond
  45.8 6.1 %copy-start.3 = (bf16[512,2048]{1,0:T(8,128)(2,1)S(1)}, bf16[512,2048]{1,0:T(8,128)(2,1)}, u32[]{:S(2)}) copy-start(bf16[512,2048]{1,0:T(8,128)(2,1)} %get-tuple-element.93.refs_4_) | copy-start | bytes 6291460 | tf_op jit(solution)/shard_map/cond
  45.8 1.7 %collective-permute-start.5 = (bf16[128,1536]{1,0:T(8,128)(2,1)S(1)}, bf16[128,1536]{1,0:T(8,128)(2,1)S(1)}, u32[]{:S(2)}, u32[]{:S(2)}) collective-permute-start(bf16[128,1536]{1,0:T(8,128)(2,1)S(1)} %get-tuple-element.99), channel_id=1, source_target_pairs={{0,8},{8,0},{16,24},{24,16},{1,9},{9,1},{17,25},{25,17},{2,10},{10... | collective-permute-start | bytes 1179656 | tf_op jit(solution)/shard_map/cond/branch_1_fun/ppermute | solution.py:391
  47.6 11.2 %collective-permute-start.7 = (bf16[128,1536]{1,0:T(8,128)(2,1)S(1)}, bf16[128,1536]{1,0:T(8,128)(2,1)S(1)}, u32[]{:S(2)}, u32[]{:S(2)}) collective-permute-start(bf16[128,1536]{1,0:T(8,128)(2,1)S(1)} %total.7), channel_id=1, source_target_pairs={{0,16},{8,24},{16,0},{24,8},{1,17},{9,25},{17,1},{25,9},{2,18},{10... | collective-permute-start | bytes 1179656 | tf_op jit(solution)/shard_map/cond/branch_1_fun/ppermute | solution.py:391
  50.4 4.8 %copy-start.8 = (bf16[64,1536]{1,0:T(8,128)(2,1)}, bf16[64,1536]{1,0:T(8,128)(2,1)S(1)}, u32[]{:S(2)}) copy-start(bf16[64,1536]{1,0:T(8,128)(2,1)S(1)} %act.6.refs_1_) | copy-start | bytes 589828 | tf_op jit(solution)/shard_map/cond
  50.4 1.5 %collective-permute-start.6 = (bf16[64,1536]{1,0:T(8,128)(2,1)S(1)}, bf16[64,1536]{1,0:T(8,128)(2,1)S(1)}, u32[]{:S(2)}, u32[]{:S(2)}) collective-permute-start(bf16[64,1536]{1,0:T(8,128)(2,1)S(1)} %act.6.refs_1_), channel_id=1, source_target_pairs={{0,8},{8,0},{16,24},{24,16},{1,9},{9,1},{17,25},{25,17},{2,10},{10... | collective-permute-start | bytes 589832 | tf_op jit(solution)/shard_map/cond/branch_1_fun/ppermute | solution.py:391
  51.9 3.2 %copy-start.10 = (bf16[64,1536]{1,0:T(8,128)(2,1)}, bf16[64,1536]{1,0:T(8,128)(2,1)S(1)}, u32[]{:S(2)}) copy-start(bf16[64,1536]{1,0:T(8,128)(2,1)S(1)} %collective-permute-done.6.refs_2_) | copy-start | bytes 589828 | tf_op jit(solution)/shard_map/cond
  59.8 6.1 %copy-start.9 = (bf16[64,1536]{1,0:T(8,128)(2,1)S(1)}, bf16[64,1536]{1,0:T(8,128)(2,1)}, u32[]{:S(2)}) copy-start(bf16[64,1536]{1,0:T(8,128)(2,1)} %copy-done.8) | copy-start | bytes 589828 | tf_op jit(solution)/shard_map/cond
  59.8 2.1 %collective-permute-start.8 = (bf16[128,1536]{1,0:T(8,128)(2,1)}, bf16[128,1536]{1,0:T(8,128)(2,1)}, u32[]{:S(2)}, u32[]{:S(2)}) collective-permute-start(bf16[128,1536]{1,0:T(8,128)(2,1)} %act.7.refs_1_), channel_id=1, source_target_pairs={{0,8},{8,0},{16,24},{24,16},{1,9},{9,1},{17,25},{25,17},{2,10},{10... | collective-permute-start | bytes 1179656 | tf_op jit(solution)/shard_map/cond/branch_1_fun/ppermute | solution.py:391
  65.9 1.6 %copy-start.15 = (bf16[64,1024]{1,0:T(8,128)(2,1)}, bf16[64,1024]{1,0:T(8,128)(2,1)S(1)}, u32[]{:S(2)}) copy-start(bf16[64,1024]{1,0:T(8,128)(2,1)S(1)} %get-tuple-element.271.refs_9_) | copy-start | bytes 393220
  65.9 5.2 %copy-start.16 = (bf16[64,1024]{1,0:T(8,128)(2,1)}, bf16[64,1024]{1,0:T(8,128)(2,1)S(1)}, u32[]{:S(2)}) copy-start(bf16[64,1024]{1,0:T(8,128)(2,1)S(1)} %get-tuple-element.272.refs_10_) | copy-start | bytes 393220
  65.9 0.7 copy-start.17
  66.6 36.6 %collective-permute-start.26 = (bf16[120,1024]{1,0:T(8,128)(2,1)}, bf16[120,1024]{1,0:T(8,128)(2,1)S(1)}, u32[]{:S(2)}, u32[]{:S(2)}) collective-permute-start(bf16[120,1024]{1,0:T(8,128)(2,1)} %get-tuple-element.254), channel_id=1, source_target_pairs={{0,1},{1,0},{2,3},{3,2},{4,5},{5,4},{6,7},{7,6},{8,9},{9,8},{10,11... | collective-permute-start | bytes 737288 | tf_op jit(solution)/shard_map/ppermute | solution.py:388
  67.5 35.8 %collective-permute-start.25 = (bf16[120,1024]{1,0:T(8,128)(2,1)}, bf16[120,1024]{1,0:T(8,128)(2,1)S(1)}, u32[]{:S(2)}, u32[]{:S(2)}) collective-permute-start(bf16[120,1024]{1,0:T(8,128)(2,1)} %get-tuple-element.252), channel_id=1, source_target_pairs={{0,5},{1,4},{2,7},{3,6},{4,1},{5,0},{6,3},{7,2},{8,13},{9,12},{10,... | collective-permute-start | bytes 737288 | tf_op jit(solution)/shard_map/ppermute | solution.py:388
  71.1 32.2 %collective-permute-start.24 = (bf16[120,1024]{1,0:T(8,128)(2,1)}, bf16[120,1024]{1,0:T(8,128)(2,1)S(1)}, u32[]{:S(2)}, u32[]{:S(2)}) collective-permute-start(bf16[120,1024]{1,0:T(8,128)(2,1)} %get-tuple-element.250), channel_id=1, source_target_pairs={{0,4},{1,5},{2,6},{3,7},{4,0},{5,1},{6,2},{7,3},{8,12},{9,13},{10,... | collective-permute-start | bytes 737288 | tf_op jit(solution)/shard_map/ppermute | solution.py:388
  71.2 8.4 %copy-start.4 = (bf16[512,2048]{1,0:T(8,128)(2,1)S(1)}, bf16[512,2048]{1,0:T(8,128)(2,1)}, u32[]{:S(2)}) copy-start(bf16[512,2048]{1,0:T(8,128)(2,1)} %get-tuple-element.112.refs_4_) | copy-start | bytes 6291460 | tf_op jit(solution)/shard_map/cond
  71.2 8.4 %copy-start.7 = (bf16[1024,1024]{1,0:T(8,128)(2,1)S(1)}, bf16[1024,1024]{1,0:T(8,128)(2,1)}, u32[]{:S(2)}) copy-start(bf16[1024,1024]{1,0:T(8,128)(2,1)} %get-tuple-element.113.refs_5_) | copy-start | bytes 6291460 | tf_op jit(solution)/shard_map/cond
  76.3 1.7 %collective-permute-start.9 = (bf16[128,1536]{1,0:T(8,128)(2,1)S(1)}, bf16[128,1536]{1,0:T(8,128)(2,1)S(1)}, u32[]{:S(2)}, u32[]{:S(2)}) collective-permute-start(bf16[128,1536]{1,0:T(8,128)(2,1)S(1)} %get-tuple-element.117), channel_id=1, source_target_pairs={{0,8},{8,0},{16,24},{24,16},{1,9},{9,1},{17,25},{25,17},{2,10},{10... | collective-permute-start | bytes 1179656 | tf_op jit(solution)/shard_map/cond/branch_1_fun/ppermute | solution.py:391
  78.1 11.2 %collective-permute-start.10 = (bf16[128,1536]{1,0:T(8,128)(2,1)S(1)}, bf16[128,1536]{1,0:T(8,128)(2,1)S(1)}, u32[]{:S(2)}, u32[]{:S(2)}) collective-permute-start(bf16[128,1536]{1,0:T(8,128)(2,1)S(1)} %total.8), channel_id=1, source_target_pairs={{0,16},{8,24},{16,0},{24,8},{1,17},{9,25},{17,1},{25,9},{2,18},{10... | collective-permute-start | bytes 1179656 | tf_op jit(solution)/shard_map/cond/branch_1_fun/ppermute | solution.py:391
  83.1 7.2 %collective-permute-start.12 = (bf16[128,1536]{1,0:T(8,128)(2,1)S(1)}, bf16[128,1536]{1,0:T(8,128)(2,1)}, u32[]{:S(2)}, u32[]{:S(2)}) collective-permute-start(bf16[128,1536]{1,0:T(8,128)(2,1)S(1)} %get-tuple-element.126), channel_id=1, source_target_pairs={{0,8},{8,0},{16,24},{24,16},{1,9},{9,1},{17,25},{25,17},{2,10},{10... | collective-permute-start | bytes 1179656 | tf_op jit(solution)/shard_map/cond/branch_1_fun/ppermute | solution.py:391
  90.2 2.9 %collective-permute-start.11 = (bf16[128,1536]{1,0:T(8,128)(2,1)}, bf16[128,1536]{1,0:T(8,128)(2,1)}, u32[]{:S(2)}, u32[]{:S(2)}) collective-permute-start(bf16[128,1536]{1,0:T(8,128)(2,1)} %act.8.refs_1_), channel_id=1, source_target_pairs={{0,8},{8,0},{16,24},{24,16},{1,9},{9,1},{17,25},{25,17},{2,10},{10... | collective-permute-start | bytes 1179656 | tf_op jit(solution)/shard_map/cond/branch_1_fun/ppermute | solution.py:391
  91.6 11.7 %collective-permute-start.13 = (bf16[128,1536]{1,0:T(8,128)(2,1)S(1)}, bf16[128,1536]{1,0:T(8,128)(2,1)}, u32[]{:S(2)}, u32[]{:S(2)}) collective-permute-start(bf16[128,1536]{1,0:T(8,128)(2,1)S(1)} %total.9), channel_id=1, source_target_pairs={{0,16},{8,24},{16,0},{24,8},{1,17},{9,25},{17,1},{25,9},{2,18},{10... | collective-permute-start | bytes 1179656 | tf_op jit(solution)/shard_map/cond/branch_1_fun/ppermute | solution.py:391
  103.3 25.8 %collective-permute-start.28 = (bf16[120,1024]{1,0:T(8,128)(2,1)}, bf16[120,1024]{1,0:T(8,128)(2,1)S(1)}, u32[]{:S(2)}, u32[]{:S(2)}) collective-permute-start(bf16[120,1024]{1,0:T(8,128)(2,1)} %get-tuple-element.257), channel_id=1, source_target_pairs={{0,7},{1,6},{2,5},{3,4},{4,3},{5,2},{6,1},{7,0},{8,15},{9,14},{10,... | collective-permute-start | bytes 737288 | tf_op jit(solution)/shard_map/ppermute | solution.py:388
  106.3 22.8 %collective-permute-start.27 = (bf16[120,1024]{1,0:T(8,128)(2,1)}, bf16[120,1024]{1,0:T(8,128)(2,1)S(1)}, u32[]{:S(2)}, u32[]{:S(2)}) collective-permute-start(bf16[120,1024]{1,0:T(8,128)(2,1)} %get-tuple-element.255), channel_id=1, source_target_pairs={{0,6},{1,7},{2,4},{3,5},{4,2},{5,3},{6,0},{7,1},{8,14},{9,15},{10,... | collective-permute-start | bytes 737288 | tf_op jit(solution)/shard_map/ppermute | solution.py:388
  110.3 2.1 %collective-permute-start.14 = (bf16[128,1536]{1,0:T(8,128)(2,1)}, bf16[128,1536]{1,0:T(8,128)(2,1)}, u32[]{:S(2)}, u32[]{:S(2)}) collective-permute-start(bf16[128,1536]{1,0:T(8,128)(2,1)} %act.9.refs_1_), channel_id=1, source_target_pairs={{0,8},{8,0},{16,24},{24,16},{1,9},{9,1},{17,25},{25,17},{2,10},{10... | collective-permute-start | bytes 1179656 | tf_op jit(solution)/shard_map/cond/branch_1_fun/ppermute | solution.py:391
  117.8 2.1 %copy-start.11 = (bf16[128,1024]{1,0:T(8,128)(2,1)}, bf16[128,1024]{1,0:T(8,128)(2,1)S(1)}, u32[]{:S(2)}) copy-start(bf16[128,1024]{1,0:T(8,128)(2,1)S(1)} %get-tuple-element.279.refs_17_) | copy-start | bytes 786436
  117.8 2.1 %copy-start.12 = (bf16[128,1024]{1,0:T(8,128)(2,1)}, bf16[128,1024]{1,0:T(8,128)(2,1)S(1)}, u32[]{:S(2)}) copy-start(bf16[128,1024]{1,0:T(8,128)(2,1)S(1)} %get-tuple-element.280.refs_18_) | copy-start | bytes 786436
  117.8 12.9 %collective-permute-start.22 = (bf16[120,1024]{1,0:T(8,128)(2,1)}, bf16[120,1024]{1,0:T(8,128)(2,1)S(1)}, u32[]{:S(2)}, u32[]{:S(2)}) collective-permute-start(bf16[120,1024]{1,0:T(8,128)(2,1)} %get-tuple-element.246), channel_id=1, source_target_pairs={{0,2},{1,3},{2,0},{3,1},{4,6},{5,7},{6,4},{7,5},{8,10},{9,11},{10,... | collective-permute-start | bytes 737288 | tf_op jit(solution)/shard_map/ppermute | solution.py:388
  117.9 13.4 %collective-permute-start.23 = (bf16[120,1024]{1,0:T(8,128)(2,1)}, bf16[120,1024]{1,0:T(8,128)(2,1)S(1)}, u32[]{:S(2)}, u32[]{:S(2)}) collective-permute-start(bf16[120,1024]{1,0:T(8,128)(2,1)} %get-tuple-element.247), channel_id=1, source_target_pairs={{0,3},{1,2},{2,1},{3,0},{4,7},{5,6},{6,5},{7,4},{8,11},{9,10},{10,... | collective-permute-start | bytes 737288 | tf_op jit(solution)/shard_map/ppermute | solution.py:388
  119.9 7.2 %copy-start = (s32[192,2]{0,1:T(2,128)S(1)}, s32[192,2]{0,1:T(2,128)}, u32[]{:S(2)}) copy-start(s32[192,2]{0,1:T(2,128)} %param.15) | copy-start | bytes 4612
  119.9 7.2 %copy-start.1 = (f32[192,2]{0,1:T(2,128)S(1)}, f32[192,2]{0,1:T(2,128)}, u32[]{:S(2)}) copy-start(f32[192,2]{0,1:T(2,128)} %param.16) | copy-start | bytes 4612
  119.9 7.2 %copy-start.14 = (bf16[120,1024]{1,0:T(8,128)(2,1)S(1)}, bf16[120,1024]{1,0:T(8,128)(2,1)}, u32[]{:S(2)}) copy-start(bf16[120,1024]{1,0:T(8,128)(2,1)} %copy-done.13) | copy-start | bytes 737284

commit v3 on v2

--- a/solution.py
+++ b/solution.py
@@ -9,7 +9,6 @@
 F32 = jnp.float32
 VMEM_LIMIT = 18 * 1024 * 1024
 GRADS_LIMIT = 32 * 1024 * 1024
-FIRST_LIMIT = 54 * 1024 * 1024
 PREP_LIMIT = 60 * 1024 * 1024
 COST = pl.CostEstimate(flops=1, bytes_accessed=1, transcendentals=0)
 
@@ -101,21 +100,7 @@
     )(*scalars, *arrays)
 
 
-def up_kernel(capacity, held, ids, *refs):
-    if held:
-        blocks, (*parts, w_out, row_out, grad_out, send, keep, sent) = refs[:-8], refs[-8:]
-    else:
-        blocks, (far_in, far_out, row_out, grad_out, send, keep, *parts, w_out, sent, sems) = refs[:-11], refs[-11:]
-    depth, both_units = parts[0].shape
-    units = both_units // 2
-    width = units // 4
-    copies = []
-    if not held:
-        for k, part in enumerate(parts):
-            copies.append(pltpu.make_async_copy(far_in.at[k * depth : (k + 1) * depth, :], part, sems.at[k]))
-        copies.append(pltpu.make_async_copy(far_out, w_out, sems.at[len(parts)]))
-        for copy in copies:
-            copy.start()
+def lay_out(capacity, blocks, row_out, grad_out):
     pad = padded(capacity)
     spot = iota((2 * pad, 2 * capacity), 0)
     col = iota((2 * pad, 2 * capacity), 1)
@@ -125,73 +110,136 @@
         laid = dot(spread, block[...]).astype(BF)
         row_out[i * pad : (i + 1) * pad, :] = laid[:pad]
         grad_out[i * pad : (i + 1) * pad, :] = laid[pad:]
-    tiles = [(out, half, j) for out, half in ((sent, 1 - ids[1]), (keep, ids[1])) for j in range(2)]
-    for k, w_in in enumerate(parts):
-        if not held:
-            copies[k].wait()
-        at = slice(k * depth, (k + 1) * depth)
-        for out, half, j in tiles:
-            for part in range(2):
-                base = (3 * j + part) * width
-                column = pl.multiple_of(part * units + (half * 2 + j) * width, width)
-                term = dot(row_out[:, at], w_in[:, pl.ds(column, width)])
-                if k:
-                    out[:, base : base + width] += term
-                else:
-                    out[:, base : base + width] = term
-    if not held:
-        copies[-1].wait()
-    for out, half, j in tiles:
-        row = pl.multiple_of((half * 2 + j) * width, width)
-        out[:, (3 * j + 2) * width : (3 * j + 3) * width] = dot_t(grad_out[...], w_out[pl.ds(row, width), :])
-    send[...] = sent[...].astype(BF)
-
-
-def up_step(ids, blocks, weights, capacity, held):
-    *_, w_out = weights
+
+
+def half_products(half, rows, grads, w_in, w_out, out):
+    units = w_out.shape[0]
+    width = units // 4
+    for j in range(2):
+        at = pl.multiple_of((half * 2 + j) * width, width)
+        at_up = pl.multiple_of(units + (half * 2 + j) * width, width)
+        gate = dot(rows[...], w_in[:, pl.ds(at, width)])
+        up = dot(rows[...], w_in[:, pl.ds(at_up, width)])
+        back = dot_t(grads[...], w_out[pl.ds(at, width), :])
+        for part, term in enumerate((gate, up, back)):
+            out[:, (3 * j + part) * width : (3 * j + part + 1) * width] = term.astype(out.dtype)
+
+
+PIECES = 4
+
+
+def weight_copies(ids, far_in, far_out, w_in, w_out, sems):
+    units = far_out.shape[0]
+    span, depth = units // 2, far_in.shape[0] // PIECES
+    copies = []
+    for half in (1 - ids[1], ids[1]):
+        at = pl.ds(pl.multiple_of(half * span, span), span)
+        at_up = pl.ds(pl.multiple_of(units + half * span, span), span)
+        for k in range(PIECES):
+            rows = slice(k * depth, (k + 1) * depth)
+            step = span // PIECES
+            row = pl.ds(pl.multiple_of(half * span + k * step, step), step)
+            for x, y in (
+                (far_in.at[rows, at], w_in.at[rows, at]),
+                (far_in.at[rows, at_up], w_in.at[rows, at_up]),
+                (far_out.at[row, :], w_out.at[row, :]),
+            ):
+                copies.append(pltpu.make_async_copy(x, y, sems.at[len(copies)]))
+    for copy in copies:
+        copy.start()
+    return copies
+
+
+def other_half(ids, blocks, w_in, w_out, capacity):
     units, features = w_out.shape
     rows = len(blocks) * padded(capacity)
     shape = jax.ShapeDtypeStruct
     whole = pl.BlockSpec(memory_space=pltpu.VMEM)
     away = pl.BlockSpec(memory_space=pl.ANY)
-    out_shape = [
-        shape((rows, features), BF),
-        shape((rows, features), BF),
-        shape((rows, 3 * units // 2), BF),
-        shape((rows, 3 * units // 2), F32),
-    ]
-    scratch = [pltpu.VMEM((rows, 3 * units // 2), F32)]
-    if not held:
-        out_shape += [shape((features // 2, 2 * units), BF)] * 2 + [shape(w_out.shape, BF)]
-        scratch += [pltpu.SemaphoreType.DMA((3,))]
+
+    def kernel(ids, *refs):
+        held, (far_in, far_out, row_out, grad_out, send, near_in, near_out, sems) = refs[:-8], refs[-8:]
+        copies = weight_copies(ids, far_in, far_out, near_in, near_out, sems)
+        lay_out(capacity, held, row_out, grad_out)
+        for copy in copies[: 3 * PIECES]:
+            copy.wait()
+        half_products(1 - ids[1], row_out, grad_out, near_in, near_out, send)
+        for copy in copies[3 * PIECES :]:
+            copy.wait()
+
     return pl.pallas_call(
-        lambda *refs: up_kernel(capacity, held, *refs),
-        out_shape=out_shape,
-        in_specs=[pl.BlockSpec(memory_space=pltpu.SMEM)]
-        + [whole] * len(blocks)
-        + [whole if held else away] * len(weights),
-        out_specs=[whole] * len(out_shape),
-        scratch_shapes=scratch,
-        compiler_params=pltpu.CompilerParams(vmem_limit_bytes=VMEM_LIMIT if held else FIRST_LIMIT),
+        kernel,
+        out_shape=[
+            shape((rows, features), BF),
+            shape((rows, features), BF),
+            shape((rows, 3 * units // 2), BF),
+            shape(w_in.shape, BF),
+            shape(w_out.shape, BF),
+        ],
+        in_specs=[pl.BlockSpec(memory_space=pltpu.SMEM)] + [whole] * len(blocks) + [away] * 2,
+        out_specs=[whole] * 5,
+        scratch_shapes=[pltpu.SemaphoreType.DMA((6 * PIECES,))],
+        compiler_params=pltpu.CompilerParams(vmem_limit_bytes=VMEM_LIMIT),
         cost_estimate=COST,
         name="up",
-    )(ids, *blocks, *weights)
-
-
-def sum_kernel(keep, core, out):
-    out[...] = (keep[...] + core[...].astype(F32)).astype(BF)
-
-
-def sum_step(keep, core):
-    return call(sum_kernel, "total", jax.ShapeDtypeStruct(keep.shape, BF), [], keep, core)
-
-
-def act_kernel(keep, core, other, out):
+    )(ids, *blocks, w_in, w_out)
+
+
+def own_half(ids, rows, grads, weights):
+    def kernel(ids, rows, grads, w_in, w_out, keep):
+        half_products(ids[1], rows, grads, w_in, w_out, keep)
+
+    shape = jax.ShapeDtypeStruct((rows.shape[0], 3 * weights[1].shape[0] // 2), F32)
+    return call(kernel, "up", shape, [ids], rows, grads, *weights)
+
+
+def up_step(ids, blocks, weights, capacity):
+    units, features = weights[1].shape
+    rows = len(blocks) * padded(capacity)
+    shape = jax.ShapeDtypeStruct
+
+    def kernel(ids, *refs):
+        held, (w_in, w_out, row_out, grad_out, send, keep) = refs[:-6], refs[-6:]
+        lay_out(capacity, held, row_out, grad_out)
+        half_products(1 - ids[1], row_out, grad_out, w_in, w_out, send)
+        half_products(ids[1], row_out, grad_out, w_in, w_out, keep)
+
+    return call(
+        kernel,
+        "up",
+        [
+            shape((rows, features), BF),
+            shape((rows, features), BF),
+            shape((rows, 3 * units // 2), BF),
+            shape((rows, 3 * units // 2), F32),
+        ],
+        [ids],
+        *blocks,
+        *weights,
+    )
+
+
+def sum_kernel(keep, core, *outs):
+    cut = keep.shape[1] // len(outs)
+    for j, out in enumerate(outs):
+        at = slice(j * cut, (j + 1) * cut)
+        out[...] = (keep[:, at] + core[:, at].astype(F32)).astype(BF)
+
+
+def sum_step(keep, core, cuts=1):
+    shape = jax.ShapeDtypeStruct((keep.shape[0], keep.shape[1] // cuts), BF)
+    return call(sum_kernel, "total", [shape] * cuts, [], keep, core)
+
+
+def activated(keep, core, others, out):
     width = keep.shape[1] // 6
     for j in range(2):
         base = 3 * width * j
+        other, skip = others[j % len(others)], base * (len(others) - 1)
         gate, up, back = (
-            keep[:, at : at + width] + core[:, at : at + width].astype(F32) + other[:, at : at + width].astype(F32)
+            keep[:, at : at + width]
+            + core[:, at : at + width].astype(F32)
+            + other[:, at - skip : at - skip + width].astype(F32)
             for at in (base, base + width, base + 2 * width)
         )
         sigmoid = jax.nn.sigmoid(gate)
@@ -203,56 +251,104 @@
         out[:, base + 2 * width : base + 3 * width] = (back * silu).astype(BF)
 
 
-def act_step(keep, core, other):
-    return call(act_kernel, "act", jax.ShapeDtypeStruct(keep.shape, BF), [], keep, core, other)
-
-
-def down_kernel(capacity, cuts, ids, own, core, *refs):
-    *parts, w_out = refs[:3]
-    outs = refs[3:]
-    pad = padded(capacity)
+def act_step(keep, core, others):
+    def kernel(keep, core, *refs):
+        activated(keep, core, refs[:-1], refs[-1])
+
+    return call(kernel, "act", jax.ShapeDtypeStruct(keep.shape, BF), [], keep, core, *others)
+
+
+def act_and_sum(keep, core, other, next_keep, next_core):
+    def kernel(keep, core, other, next_keep, next_core, out, total):
+        activated(keep, core, [other], out)
+        sum_kernel(next_keep, next_core, total)
+
+    shapes = [jax.ShapeDtypeStruct(x.shape, BF) for x in (keep, next_keep)]
+    return call(kernel, "act", shapes, [], keep, core, other, next_keep, next_core)
+
+
+def act_and_load(ids, keep, core, other, w_in, w_out):
+    shape = jax.ShapeDtypeStruct
+    whole = pl.BlockSpec(memory_space=pltpu.VMEM)
+    away = pl.BlockSpec(memory_space=pl.ANY)
+
+    def kernel(ids, keep, core, other, far_in, far_out, out, near_in, near_out, sems):
+        copies = weight_copies(ids, far_in, far_out, near_in, near_out, sems)
+        activated(keep, core, [other], out)
+        for copy in copies:
+            copy.wait()
+
+    return pl.pallas_call(
+        kernel,
+        out_shape=[shape(keep.shape, BF), shape(w_in.shape, BF), shape(w_out.shape, BF)],
+        in_specs=[pl.BlockSpec(memory_space=pltpu.SMEM)] + [whole] * 3 + [away] * 2,
+        out_specs=[whole] * 3,
+        scratch_shapes=[pltpu.SemaphoreType.DMA((6 * PIECES,))],
+        compiler_params=pltpu.CompilerParams(vmem_limit_bytes=VMEM_LIMIT),
+        cost_estimate=COST,
+        name="act",
+    )(ids, keep, core, other, w_in, w_out)
+
+
+def half_rows(half, held, w_in, w_out):
     units = w_out.shape[0]
     width = units // 4
-    out_rows, grad_parts = None, [None] * len(parts)
-    for held, half in ((own, ids[1]), (core, 1 - ids[1])):
-        for j in range(2):
-            base = 3 * width * j
-            at = pl.multiple_of((half * 2 + j) * width, width)
-            at_up = pl.multiple_of(units + (half * 2 + j) * width, width)
-            a = dot(held[:, base : base + width], w_out[pl.ds(at, width), :])
-            out_rows = a if out_rows is None else out_rows + a
-            for k, w_in in enumerate(parts):
-                b = dot_t(held[:, base + width : base + 2 * width], w_in[:, pl.ds(at, width)])
-                b = b + dot_t(held[:, base + 2 * width : base + 3 * width], w_in[:, pl.ds(at_up, width)])
-                grad_parts[k] = b if grad_parts[k] is None else grad_parts[k] + b
-    grad_rows = jnp.concatenate(grad_parts, axis=1)
+    out_rows = grad_rows = None
+    for j in range(2):
+        base = 3 * width * j
+        at = pl.multiple_of((half * 2 + j) * width, width)
+        at_up = pl.multiple_of(units + (half * 2 + j) * width, width)
+        a = dot(held[:, base : base + width], w_out[pl.ds(at, width), :])
+        b = dot_t(held[:, base + width : base + 2 * width], w_in[:, pl.ds(at, width)])
+        c = dot_t(held[:, base + 2 * width : base + 3 * width], w_in[:, pl.ds(at_up, width)])
+        out_rows = a if out_rows is None else out_rows + a
+        grad_rows = b + c if grad_rows is None else grad_rows + (b + c)
+    return out_rows, grad_rows
+
+
+def pack(capacity, out_rows, grad_rows, outs):
+    pad = padded(capacity)
     spot = iota((2 * capacity, pad), 0)
     col = iota((2 * capacity, pad), 1)
     pack_out = (spot == jnp.where(col < capacity, col, -1)).astype(F32).astype(BF)
     pack_grad = (spot - capacity == jnp.where(col < capacity, col, -capacity - 1)).astype(F32).astype(BF)
     out_rows, grad_rows = out_rows.astype(BF), grad_rows.astype(BF)
-    for i in range(out_rows.shape[0] // pad):
-        packed = (
-            dot(pack_out, out_rows[i * pad : (i + 1) * pad])
-            + dot(pack_grad, grad_rows[i * pad : (i + 1) * pad])
-        ).astype(BF)
+    sources = out_rows.shape[0] // pad
+    cuts = len(outs) // sources
+    for i in range(sources):
+        at = slice(i * pad, (i + 1) * pad)
+        packed = (dot(pack_out, out_rows[at]) + dot(pack_grad, grad_rows[at])).astype(BF)
         cut = packed.shape[1] // cuts
         for j in range(cuts):
             outs[i * cuts + j][...] = packed[:, j * cut : (j + 1) * cut]
 
 
 def down_step(ids, own, core, weights, count, capacity, cuts):
-    features = weights[-1].shape[1]
-    outs = call(
-        lambda *refs: down_kernel(capacity, cuts, *refs),
-        "down",
-        [jax.ShapeDtypeStruct((2 * capacity, features // cuts), BF)] * (count * cuts),
-        [ids],
-        own,
-        core,
-        *weights,
-    )
+    def kernel(ids, own, core, w_in, w_out, *outs):
+        out_rows, grad_rows = half_rows(ids[1], own, w_in, w_out)
+        more_out, more_grad = half_rows(1 - ids[1], core, w_in, w_out)
+        pack(capacity, out_rows + more_out, grad_rows + more_grad, outs)
+
+    shape = jax.ShapeDtypeStruct((2 * capacity, weights[1].shape[1] // cuts), BF)
+    outs = call(kernel, "down", [shape] * (count * cuts), [ids], own, core, *weights)
     return [outs[i * cuts : (i + 1) * cuts] for i in range(count)]
+
+
+def down_own(ids, own, weights):
+    def kernel(ids, own, w_in, w_out, out_rows, grad_rows):
+        out_rows[...], grad_rows[...] = half_rows(ids[1], own, w_in, w_out)
+
+    shape = jax.ShapeDtypeStruct((own.shape[0], weights[1].shape[1]), F32)
+    return call(kernel, "down", [shape] * 2, [ids], own, *weights)
+
+
+def down_other(ids, out_rows, grad_rows, core, weights, count, capacity):
+    def kernel(ids, out_rows, grad_rows, core, w_in, w_out, *outs):
+        more_out, more_grad = half_rows(1 - ids[1], core, w_in, w_out)
+        pack(capacity, out_rows[...] + more_out, grad_rows[...] + more_grad, outs)
+
+    shape = jax.ShapeDtypeStruct((2 * capacity, weights[1].shape[1]), BF)
+    return call(kernel, "down", [shape] * count, [ids], out_rows, grad_rows, core, *weights)
 
 
 def grads_kernel(count, ids, *refs):
@@ -402,52 +498,68 @@
         shapes = jax.eval_shape(body, *args)
         return lax.cond(inside, body, lambda *_: jax.tree.map(lambda x: jnp.zeros(x.shape, x.dtype), shapes), *args)
 
-    def up_part(blocks, *earlier):
+    def up_part(blocks, weights, *earlier):
         first, *others = blocks
-        rows, grads, send, keep = up_step(ids, [after(first, *earlier), *others], weights, capacity, True)
-        return rows, grads, keep, beside(send, 1)
-
-    def x_part(state, *earlier):
+        return up_step(ids, [after(first, *earlier), *others], weights, capacity)
+
+    def core_part(state, *earlier):
+        rows, grads, send, keep = state
+        return rows, grads, keep, beside(after(send, *earlier) if earlier else send, 1)
+
+    def up_in_halves(blocks):
+        rows, grads, send, *weights = other_half(ids, blocks, w_in, w_out, capacity)
+        core = beside(send, 1)
+        return (rows, grads, own_half(ids, after(rows, send), grads, weights), core), weights
+
+    def sum_part(state, *earlier, cuts=1):
         rows, grads, keep, core = state
-        total = sum_step(after(keep, *earlier), core)
-        return (rows, grads, keep, core, beside(total, 2)), total
+        return rows, grads, keep, core, sum_step(after(keep, *earlier), core, cuts)
+
+    def x_part(state):
+        rows, grads, keep, core, totals = state
+        return rows, grads, keep, core, [beside(total, 2) for total in totals]
 
     def act_part(state, *earlier):
-        rows, grads, keep, core, other = state
-        own = act_step(after(keep, *earlier), core, other)
+        rows, grads, keep, core, others = state
+        own = act_step(after(keep, *earlier), core, others)
         return rows, grads, own, beside(own, 1)
 
-    def down_part(group, count):
-        return down_step(ids, *group[2:], weights, count, capacity, 1)
-
-    def with_next(state, count, next_blocks):
-        state, total = x_part(state)
-        next_state = up_part(next_blocks, total)
-        group = act_part(state)
-        next_state, _ = x_part(next_state, group[2])
-        return group, down_part(group, count), next_state
-
-    def own_stage(begun, next_blocks):
-        rows, grads, send, keep = begun
-        return with_next((rows, grads, keep, beside(send, 1)), size, next_blocks)
-
-    def far_stage(blocks, before):
-        state, total = x_part(up_part(blocks))
-        before = act_part(before, total)
-        back = down_part(before, size)
-        group = act_part(state, *[x for parts in back for x in parts])
-        return group, down_part(group, len(blocks)), before, back
-
-    def last_stage(blocks, next_blocks):
-        return with_next(up_part(blocks), len(blocks), next_blocks)
+    def down_part(group, weights, count, cuts=1):
+        return down_step(ids, *group[2:], weights, count, capacity, cuts)
+
+    def down_in_halves(group, weights, count):
+        _, _, own, core = group
+        sums = down_own(ids, own, weights)
+        return [[x] for x in down_other(ids, *sums, after(core, *sums), weights, count, capacity)]
+
+    def act_both(state, next_state, *earlier):
+        rows, grads, keep, core, (other,) = state
+        own, next_total = act_and_sum(after(keep, *earlier), core, other, *next_state[2:])
+        return (rows, grads, own, beside(own, 1)), (*next_state, [next_total])
+
+    def first_stage(blocks):
+        state, _ = up_in_halves(blocks)
+        return sum_part(state, cuts=2)
+
+    def far_stage(blocks, before, before_count, next_blocks):
+        state, held = up_in_halves(blocks)
+        state = sum_part(state)
+        before = act_part(before, *state[4])
+        next_state = up_part(next_blocks, held, before[2])
+        back = down_part((*before[:2], after(before[2], next_state[2]), before[3]), held, before_count)
+        ends = [x for parts in back for x in parts]
+        group, next_state = act_both(x_part(state), core_part(next_state, *ends), *ends)
+        return group, down_in_halves(group, held, len(blocks)), next_state, before, back
 
     def rest_stage(state):
-        group = act_part(state)
-        return group, down_part(group, half - 2 * size)
+        rows, grads, keep, core, (other,) = state
+        own, *weights = act_and_load(ids, keep, core, other, w_in, w_out)
+        group = rows, grads, own, beside(own, 1)
+        return group, down_part(group, weights, size, 2)
 
     half, quarter = n_expert // 2, n_expert // 4
-    size = half // 4
-    near, rest = [list(range(size)), list(range(size, 2 * size))], list(range(2 * size, half))
+    size = quarter // 2
+    near = [list(range(quarter)), list(range(quarter, quarter + size)), list(range(quarter + size, half))]
     far, last = list(range(half, half + quarter)), list(range(half + quarter, n_expert))
     sent = prep(ids, tokens, routes, route_weight, cotangent, n_expert, capacity)
     came, home = {0: sent[0]}, {}
@@ -466,28 +578,31 @@
     def arrived(sources):
         return [x for s in sources for x in home[s]]
 
-    rest_first, rest_second = rest[:size], rest[size:]
-    start(far + near[0] + near[1] + rest_first)
-    begun = up_step(ids, blocks(near[0]), [w_in, w_out], capacity, False)
-    begun, weights = begun[:4], begun[4:]
-    group_0, back_0, state_1 = stage(own_stage, begun, blocks(near[1]))
-    start_back(near[0], back_0)
-    start(last + rest_second, *blocks(far + rest_first), group_0[3])
-    group_far, back_far, group_1, back_1 = stage(far_stage, blocks(far, group_0[3]), state_1)
-    start_back(far + near[1], back_far + back_1, *blocks(last))
-    group_last, back_last, state_rest = stage(last_stage, blocks(last, group_far[3]), blocks(rest))
-    start_back(last, back_last, *arrived(far + near[1]))
-    group_rest, back_rest = stage(rest_stage, state_rest)
-    start_back(rest, back_rest)
+    start(far + near[0] + near[1])
+    state_0 = stage(first_stage, blocks(near[0]))
+    start(last, *blocks(far + near[1]), *state_0[4])
+    state_0 = x_part(state_0)
+    start(near[2], *blocks(far), *state_0[4])
+    group_far, back_far, state_1, group_0, back_0 = stage(
+        lambda a, b, c: far_stage(a, b, quarter, c), blocks(far), state_0, blocks(near[1])
+    )
+    start_back(far + near[0], back_far + back_0, *blocks(last))
+    group_last, back_last, state_2, group_1, back_1 = stage(
+        lambda a, b, c: far_stage(a, b, size, c), blocks(last, group_far[3]), x_part(state_1), blocks(near[2])
+    )
+    start_back(last, back_last, *arrived(far + near[0]))
+    start_back(near[1], back_1)
+    group_2, back_2 = stage(rest_stage, x_part(state_2))
+    start_back(near[2], back_2)
 
     def add(sources, partial, dtype):
         return final(ids, routes, route_weight, [home[s] for s in sources], sources, capacity, partial, dtype)
 
-    groups = [group_0, group_far, group_1, group_last, group_rest]
+    groups = [group_0, group_far, group_1, group_last, group_2]
     grad_in, grad_out = grads_step(ids, groups, units)
     partial = add(near[0] + near[1] + far, [], F32)
-    partial = add(last, partial, F32)
-    mixed, grad_tokens = add(rest, partial, BF)
+    partial = add(near[2], partial, F32)
+    mixed, grad_tokens = add(last, partial, BF)
     return mixed, grad_tokens, grad_in[None], grad_out[None]
 
 

time: 134 us -> 127 us (0.948)
  waiting for transfers between devices: 30.9 us -> 19.7 us
  starting transfers between devices: 31.5 us -> 36.8 us
    ppermute x15 -> x16, waiting for transfers between devices: 30.2 us -> 10.5 us  [beside(): return lax.ppermute(x, 'dp', [(i, i ^ s) for i in range(n_dp)])]
    ppermute x14 -> x15, waiting for transfers between devices: 0.69 us -> 9.22 us  [across(): lax.ppermute(x, 'expert', [(i, i ^ s) for i in range(n_expert)])]
    pallas_call x5 -> x4, Pallas kernels: 24.1 us -> 15.9 us  [the longest x3 11.7 us: other_half(): pl.pallas_call(kernel, out_shape=[shape((rows, features), BF), shape((row...]
    pallas_call x18 -> x22, Pallas kernels: 34.4 us -> 42.1 us  [call(): pl.pallas_call(kernel, out_shape=out_shapes, in_specs=[pl.BlockSpec(memor...]
    ppermute x14 -> x15, starting transfers between devices: 23.7 us -> 27.6 us  [across(): lax.ppermute(x, 'expert', [(i, i ^ s) for i in range(n_expert)])]
    ppermute x15 -> x16, starting transfers between devices: 7.81 us -> 9.24 us  [beside(): return lax.ppermute(x, 'dp', [(i, i ^ s) for i in range(n_dp)])]
  transfers between devices with their start and end apart: 29 -> 31, of which waited for: 13 -> 9; matrix products, arithmetic and copies ran while one was open for 0% -> 0% of each run, Pallas kernels for 47% -> 49%
where the time goes in v3:
time: 127 us; the launch traced here: 126 us
  Pallas kernels  68.4 us (54%)
  starting transfers between devices  36.8 us (29%)
  waiting for transfers between devices  19.7 us (16%)
    pallas_call x22, Pallas kernels, call(): pl.pallas_call(kernel, out_shape=out_shapes, in_specs=[pl.BlockSpec(memor...  42.1 us
    ppermute x15, starting transfers between devices, across(): lax.ppermute(x, 'expert', [(i, i ^ s) for i in range(n_expert)])  27.6 us
    pallas_call x3, Pallas kernels, other_half(): pl.pallas_call(kernel, out_shape=[shape((rows, features), BF), shape((row...  11.7 us
    ppermute x16, waiting for transfers between devices, beside(): return lax.ppermute(x, 'dp', [(i, i ^ s) for i in range(n_dp)])  10.5 us
    ppermute x16, starting transfers between devices, beside(): return lax.ppermute(x, 'dp', [(i, i ^ s) for i in range(n_dp)])  9.24 us
    ppermute x15, waiting for transfers between devices, across(): lax.ppermute(x, 'expert', [(i, i ^ s) for i in range(n_expert)])  9.22 us
    pallas_call x1, Pallas kernels, grads_step(): pl.pallas_call(lambda *refs: grads_kernel(len(groups), *refs), out_shape=...  6.61 us
    pallas_call x1, Pallas kernels, act_and_load(): pl.pallas_call(kernel, out_shape=[shape(keep.shape, BF), shape(w_in.shape...  4.22 us
  transfers between devices with their start and end apart: 31, of which 9 were waited for; matrix products, arithmetic and copies ran while one was open for 0% of the time, Pallas kernels for 49%

profile of v3, /device:TPU:0, one launch (start us, length us, event | category | flops | bytes accessed | tf_op | source)
XLA Modules:
  0.0 126.4 jit_solution(1842694920927995527)
XLA Ops:
  0.7 3.8 %prep.1 = (bf16[120,1024]{1,0:T(8,128)(2,1)S(1)}, bf16[120,1024]{1,0:T(8,128)(2,1)}, bf16[120,1024]{1,0:T(8,128)(2,1)}, bf16[120,1024]{1,0:T(8,128)(2,1)}, bf16[...) custom-call(s32[2]{0:T(128)S(1)} %pad_add_fusion.refs_0_, ...), custom_call_target="tpu_custom_call" | custom-call | flops 1 | bytes 1 | tf_op jit(solution)/shard_map/prep/pallas_call | solution.py:76
  4.5 3.0 %collective-permute-start.15 = (bf16[120,1024]{1,0:T(8,128)(2,1)}, bf16[120,1024]{1,0:T(8,128)(2,1)S(1)}, u32[]{:S(2)}, u32[]{:S(2)}) collective-permute-start(bf16[120,1024]{1,0:T(8,128)(2,1)} %get-tuple-element.247), channel_id=1, source_target_pairs={{0,1},{1,0},{2,3},{3,2},{4,5},{5,4},{6,7},{7,6},{8,9},{9,8},{10,11... | collective-permute-start | bytes 737288 | tf_op jit(solution)/shard_map/ppermute | solution.py:484
  7.5 2.6 %collective-permute-start.12 = (bf16[120,1024]{1,0:T(8,128)(2,1)}, bf16[120,1024]{1,0:T(8,128)(2,1)S(1)}, u32[]{:S(2)}, u32[]{:S(2)}) collective-permute-start(bf16[120,1024]{1,0:T(8,128)(2,1)} %get-tuple-element.243), channel_id=1, source_target_pairs={{0,4},{1,5},{2,6},{3,7},{4,0},{5,1},{6,2},{7,3},{8,12},{9,13},{10,... | collective-permute-start | bytes 737288 | tf_op jit(solution)/shard_map/ppermute | solution.py:484
  10.1 1.9 %collective-permute-start.14 = (bf16[120,1024]{1,0:T(8,128)(2,1)}, bf16[120,1024]{1,0:T(8,128)(2,1)S(1)}, u32[]{:S(2)}, u32[]{:S(2)}) collective-permute-start(bf16[120,1024]{1,0:T(8,128)(2,1)} %get-tuple-element.245), channel_id=1, source_target_pairs={{0,2},{1,3},{2,0},{3,1},{4,6},{5,7},{6,4},{7,5},{8,10},{9,11},{10,... | collective-permute-start | bytes 737288 | tf_op jit(solution)/shard_map/ppermute | solution.py:484
  12.0 1.7 %collective-permute-done.15 = bf16[120,1024]{1,0:T(8,128)(2,1)S(1)} collective-permute-done((bf16[120,1024]{1,0:T(8,128)(2,1)}, bf16[120,1024]{1,0:T(8,128)(2,1)S(1)}, u32[]{:S(2)}, u32[]{:S(2)}) %collective-permute-start.15) | collective-permute-done | bytes 245792 | tf_op jit(solution)/shard_map/ppermute | solution.py:484
  13.7 8.5 %conditional.4 = (bf16[128,1024]{1,0:T(8,128)(2,1)}, bf16[128,1024]{1,0:T(8,128)(2,1)}, f32[128,1536]{1,0:T(8,128)}, bf16[128,1536]{1,0:T(8,128)(2,1)}, bf16[128...) conditional(s32[]{:T(128)} %convert_element_type.2, () %tuple.66, (s32[2]{0:T(128)S(1)}, ...), branch_computations={%region_0.1_spmd, %region_1.2_spmd} | conditional | flops 3 | bytes 2097214 | solution.py:499
  13.7 4.4 %up.8 = (bf16[128,1024]{1,0:T(8,128)(2,1)}, bf16[128,1024]{1,0:T(8,128)(2,1)}, bf16[128,1536]{1,0:T(8,128)(2,1)S(1)}, bf16[1024,2048]{1,0:T(8,128)(2,1)S(1)}, bf16[1024,1024]{1,0:T(8,128)(2,1)S(1)}) custom-call(s32[2]{0:T(128)S(1)} %get-tuple-element.72.ids, bf16[120,1024]{1,0:T(8,128)(2,1)S(1)} %get-tuple-element.73.refs_0_, ...), custom_call_target="tpu_custom_call" | custom-call | flops 1 | bytes 1 | tf_op jit(solution)/shard_map/cond/branch_1_fun/up/pallas_call | solution.py:170
  18.2 2.7 %up.9.keep = f32[128,1536]{1,0:T(8,128)} custom-call(s32[2]{0:T(128)S(1)} %get-tuple-element.72.ids, bf16[128,1024]{1,0:T(8,128)(2,1)} %get-tuple-element.80.rows, bf16[128,1024]{1,0:T(8,128)(2,1)} %get-tuple-element.320.grads, bf16[1024,2048]{1,0:T(8,128)(2,1)S(1)} %get-tuple-element.81.w_in, bf16[1024,1024]{1,0:T(8,128)(2,1)S(1)} %get-tuple-element.82.w_out), custom_call_target="tpu_custom_call" | custom-call | flops 1 | bytes 1 | tf_op jit(solution)/shard_map/cond/branch_1_fun/up/pallas_call | solution.py:92
  20.9 1.3 %total.3 = (bf16[128,768]{1,0:T(8,128)(2,1)S(1)}, bf16[128,768]{1,0:T(8,128)(2,1)S(1)}) custom-call(f32[128,1536]{1,0:T(8,128)} %up.9.keep, bf16[128,1536]{1,0:T(8,128)(2,1)} %collective-permute-done.core), custom_call_target="tpu_custom_call" | custom-call | flops 1 | bytes 1 | tf_op jit(solution)/shard_map/cond/branch_1_fun/total/pallas_call | solution.py:92
  22.2 1.8 %collective-permute-start.17 = (bf16[128,768]{1,0:T(8,128)(2,1)S(1)}, bf16[128,768]{1,0:T(8,128)(2,1)S(1)}, u32[]{:S(2)}, u32[]{:S(2)}) collective-permute-start(bf16[128,768]{1,0:T(8,128)(2,1)S(1)} %get-tuple-element.248), channel_id=1, source_target_pairs={{0,16},{8,24},{16,0},{24,8},{1,17},{9,25},{17,1},{25,9},{2,18},{10... | collective-permute-start | bytes 589832 | tf_op jit(solution)/shard_map/ppermute | solution.py:487
  24.3 3.4 %collective-permute-done.12 = bf16[120,1024]{1,0:T(8,128)(2,1)S(1)} collective-permute-done((bf16[120,1024]{1,0:T(8,128)(2,1)}, bf16[120,1024]{1,0:T(8,128)(2,1)S(1)}, u32[]{:S(2)}, u32[]{:S(2)}) %collective-permute-start.12) | collective-permute-done | bytes 245792 | tf_op jit(solution)/shard_map/ppermute | solution.py:484
  27.8 4.0 %collective-permute-done.13 = bf16[120,1024]{1,0:T(8,128)(2,1)S(1)} collective-permute-done((bf16[120,1024]{1,0:T(8,128)(2,1)}, bf16[120,1024]{1,0:T(8,128)(2,1)S(1)}, u32[]{:S(2)}, u32[]{:S(2)}) %collective-permute-start.13) | collective-permute-done | bytes 245792 | tf_op jit(solution)/shard_map/ppermute | solution.py:484
  31.8 3.5 %collective-permute-start.16 = (bf16[120,1024]{1,0:T(8,128)(2,1)}, bf16[120,1024]{1,0:T(8,128)(2,1)S(1)}, u32[]{:S(2)}, u32[]{:S(2)}) collective-permute-start(bf16[120,1024]{1,0:T(8,128)(2,1)} %get-tuple-element.250), channel_id=1, source_target_pairs={{0,6},{1,7},{2,4},{3,5},{4,2},{5,3},{6,0},{7,1},{8,14},{9,15},{10,... | collective-permute-start | bytes 737288 | tf_op jit(solution)/shard_map/ppermute | solution.py:484
  35.3 1.3 %collective-permute-start.19 = (bf16[120,1024]{1,0:T(8,128)(2,1)}, bf16[120,1024]{1,0:T(8,128)(2,1)S(1)}, u32[]{:S(2)}, u32[]{:S(2)}) collective-permute-start(bf16[120,1024]{1,0:T(8,128)(2,1)} %get-tuple-element.258), channel_id=1, source_target_pairs={{0,7},{1,6},{2,5},{3,4},{4,3},{5,2},{6,1},{7,0},{8,15},{9,14},{10,... | collective-permute-start | bytes 737288 | tf_op jit(solution)/shard_map/ppermute | solution.py:484
  36.6 24.9 %conditional.5 = (bf16[128,1024]{1,0:T(8,128)(2,1)S(1)}, bf16[128,1024]{1,0:T(8,128)(2,1)S(1)}, bf16[128,1536]{1,0:T(8,128)(2,1)}, bf16[128,1536]{1,0:T(8,128)(2...) conditional(s32[]{:T(128)} %convert_element_type.2, () %tuple.69, ...), branch_computations={%region_2.3_spmd, %region_3.4_spmd} | conditional | flops 9 | bytes 22282920 | solution.py:499
  36.6 3.6 %up.10 = (bf16[128,1024]{1,0:T(8,128)(2,1)S(1)}, bf16[128,1024]{1,0:T(8,128)(2,1)S(1)}, bf16[128,1536]{1,0:T(8,128)(2,1)S(1)}, bf16[1024,2048]{1,0:T(8,128)(2,1)S(1)}, bf16[1024,1024]{1,0:T(8,128)(2,1)S(1)}) custom-call(s32[2]{0:T(128)S(1)} %get-tuple-element.85.ids, bf16[120,1024]{1,0:T(8,128)(2,1)S(1)} %get-tuple-element.86.refs_0_, ...), custom_call_target="tpu_custom_call" | custom-call | flops 1 | bytes 1 | tf_op jit(solution)/shard_map/cond/branch_1_fun/up/pallas_call | solution.py:170
  40.4 1.3 %up.11.keep = f32[128,1536]{1,0:T(8,128)S(1)} custom-call(s32[2]{0:T(128)S(1)} %get-tuple-element.85.ids, bf16[128,1024]{1,0:T(8,128)(2,1)S(1)} %get-tuple-element.93.rows, bf16[128,1024]{1,0:T(8,128)(2,1)S(1)} %get-tuple-element.343.grads, bf16[1024,2048]{1,0:T(8,128)(2,1)S(1)} %get-tuple-element.94.w_in.refs_1_, ...), custom_call_target="tpu_custom_call" | custom-call | flops 1 | bytes 1 | tf_op jit(solution)/shard_map/cond/branch_1_fun/up/pallas_call | solution.py:92
  42.2 1.5 %act.5.own = bf16[128,1536]{1,0:T(8,128)(2,1)S(1)} custom-call(f32[128,1536]{1,0:T(8,128)} %get-tuple-element.97.keep, bf16[128,1536]{1,0:T(8,128)(2,1)} %get-tuple-element.98.core, bf16[128,768]{1,0:T(8,128)(2,1)S(1)} %get-tuple-element.99.refs_0_, bf16[128,768]{1,0:T(8,128)(2,1)S(1)} %get-tuple-element.100.refs_1_), custom_call_target="tpu_custom_call" | custom-call | flops 1 | bytes 1 | tf_op jit(solution)/shard_map/cond/branch_1_fun/act/pallas_call | solution.py:92
  43.8 1.5 %collective-permute-start.3 = (bf16[128,1536]{1,0:T(8,128)(2,1)S(1)}, bf16[128,1536]{1,0:T(8,128)(2,1)S(1)}, u32[]{:S(2)}, u32[]{:S(2)}) collective-permute-start(bf16[128,1536]{1,0:T(8,128)(2,1)S(1)} %total.4), channel_id=1, source_target_pairs={{0,16},{8,24},{16,0},{24,8},{1,17},{9,25},{17,1},{25,9},{2,18},{10... | collective-permute-start | bytes 1179656 | tf_op jit(solution)/shard_map/cond/branch_1_fun/ppermute | solution.py:487
  45.4 2.1 %up.12 = (bf16[64,1024]{1,0:T(8,128)(2,1)S(1)}, bf16[64,1024]{1,0:T(8,128)(2,1)S(1)}, bf16[64,1536]{1,0:T(8,128)(2,1)S(1)}, f32[64,1536]{1,0:T(8,128)S(1)}) custom-call(s32[2]{0:T(128)S(1)} %get-tuple-element.85.ids, bf16[120,1024]{1,0:T(8,128)(2,1)S(1)} %get-tuple-element.102.refs_0_, bf16[1024,2048]{1,0:T(8,128)(2,1)S(1)} %get-tuple-element.94.w_in.refs_1_, ...), custom_call_target="tpu_custom_call" | custom-call | flops 1 | bytes 1 | tf_op jit(solution)/shard_map/cond/branch_1_fun/up/pallas_call | solution.py:92
  47.5 3.4 %down.7 = (bf16[120,1024]{1,0:T(8,128)(2,1)}, bf16[120,1024]{1,0:T(8,128)(2,1)}) custom-call(s32[2]{0:T(128)S(1)} %get-tuple-element.85.ids, bf16[128,1536]{1,0:T(8,128)(2,1)S(1)} %act.5.own, bf16[128,1536]{1,0:T(8,128)(2,1)S(1)} %collective-permute-done.2.core, bf16[1024,2048]{1,0:T(8,128)(2,1)S(1)} %get-tuple-element.94.w_in.refs_1_, ...), custom_call_target="tpu_custom_call" | custom-call | flops 1 | bytes 1 | tf_op jit(solution)/shard_map/cond/branch_1_fun/down/pallas_call | solution.py:92
  51.0 4.2 %collective-permute-done.3.other = bf16[128,1536]{1,0:T(8,128)(2,1)S(1)} collective-permute-done((bf16[128,1536]{1,0:T(8,128)(2,1)S(1)}, bf16[128,1536]{1,0:T(8,128)(2,1)S(1)}, u32[]{:S(2)}, u32[]{:S(2)}) %collective-permute-start.3) | collective-permute-done | bytes 393248 | tf_op jit(solution)/shard_map/cond/branch_1_fun/ppermute | solution.py:487
  56.2 2.0 %down.8 = (f32[128,1024]{1,0:T(8,128)S(1)}, f32[128,1024]{1,0:T(8,128)S(1)}) custom-call(s32[2]{0:T(128)S(1)} %get-tuple-element.85.ids, bf16[128,1536]{1,0:T(8,128)(2,1)} %get-tuple-element.344.own, bf16[1024,2048]{1,0:T(8,128)(2,1)S(1)} %get-tuple-element.94.w_in.refs_1_, bf16[1024,1024]{1,0:T(8,128)(2,1)S(1)} %get-tuple-element.95.w_out.refs_2_), custom_call_target="tpu_custom_call" | custom-call | flops 1 | bytes 1 | tf_op jit(solution)/shard_map/cond/branch_1_fun/down/pallas_call | solution.py:92
  58.3 3.2 %down.9 = (bf16[120,1024]{1,0:T(8,128)(2,1)}, bf16[120,1024]{1,0:T(8,128)(2,1)}) custom-call(s32[2]{0:T(128)S(1)} %get-tuple-element.85.ids, f32[128,1024]{1,0:T(8,128)S(1)} %get-tuple-element.111.out_rows, f32[128,1024]{1,0:T(8,128)S(1)} %get-tuple-element.112.grad_rows, bf16[128,1536]{1,0:T(8,128)(2,1)} %collective-permute-done.5.core, ...), custom_call_target="tpu_custom_call" | custom-call | flops 1 | bytes 1 | tf_op jit(solution)/shard_map/cond/branch_1_fun/down/pallas_call | solution.py:92
  61.6 1.6 %collective-permute-start.20 = (bf16[64,1536]{1,0:T(8,128)(2,1)S(1)}, bf16[64,1536]{1,0:T(8,128)(2,1)S(1)}, u32[]{:S(2)}, u32[]{:S(2)}) collective-permute-start(bf16[64,1536]{1,0:T(8,128)(2,1)S(1)} %get-tuple-element.261), channel_id=1, source_target_pairs={{0,16},{8,24},{16,0},{24,8},{1,17},{9,25},{17,1},{25,9},{2,18},{10... | collective-permute-start | bytes 589832 | tf_op jit(solution)/shard_map/ppermute | solution.py:487
  63.6 4.9 %collective-permute-start.23 = (bf16[120,1024]{1,0:T(8,128)(2,1)}, bf16[120,1024]{1,0:T(8,128)(2,1)S(1)}, u32[]{:S(2)}, u32[]{:S(2)}) collective-permute-start(bf16[120,1024]{1,0:T(8,128)(2,1)} %get-tuple-element.270), channel_id=1, source_target_pairs={{0,5},{1,4},{2,7},{3,6},{4,1},{5,0},{6,3},{7,2},{8,13},{9,12},{10,... | collective-permute-start | bytes 737288 | tf_op jit(solution)/shard_map/ppermute | solution.py:484
  68.9 23.6 %conditional.6 = (bf16[128,1024]{1,0:T(8,128)(2,1)}, bf16[128,1024]{1,0:T(8,128)(2,1)S(1)}, bf16[128,1536]{1,0:T(8,128)(2,1)}, bf16[128,1536]{1,0:T(8,128)(2,1)}...) conditional(s32[]{:T(128)} %convert_element_type.2, () %tuple.65, ...), branch_computations={%region_4.5_spmd, %region_5.6_spmd} | conditional | flops 9 | bytes 14942769 | solution.py:499
  68.9 3.6 %up.13 = (bf16[128,1024]{1,0:T(8,128)(2,1)S(1)}, bf16[128,1024]{1,0:T(8,128)(2,1)S(1)}, bf16[128,1536]{1,0:T(8,128)(2,1)S(1)}, bf16[1024,2048]{1,0:T(8,128)(2,1)S(1)}, bf16[1024,1024]{1,0:T(8,128)(2,1)S(1)}) custom-call(s32[2]{0:T(128)S(1)} %get-tuple-element.121.ids, bf16[120,1024]{1,0:T(8,128)(2,1)S(1)} %get-tuple-element.122.refs_0_, ...), custom_call_target="tpu_custom_call" | custom-call | flops 1 | bytes 1 | tf_op jit(solution)/shard_map/cond/branch_1_fun/up/pallas_call | solution.py:170
  72.9 1.3 %up.14.keep = f32[128,1536]{1,0:T(8,128)S(1)} custom-call(s32[2]{0:T(128)S(1)} %get-tuple-element.121.ids, bf16[128,1024]{1,0:T(8,128)(2,1)S(1)} %get-tuple-element.129.rows, bf16[128,1024]{1,0:T(8,128)(2,1)S(1)} %get-tuple-element.376.grads, bf16[1024,2048]{1,0:T(8,128)(2,1)S(1)} %get-tuple-element.130.w_in.refs_1_, ...), custom_call_target="tpu_custom_call" | custom-call | flops 1 | bytes 1 | tf_op jit(solution)/shard_map/cond/branch_1_fun/up/pallas_call | solution.py:92
  75.0 1.5 %collective-permute-start.8 = (bf16[128,1536]{1,0:T(8,128)(2,1)S(1)}, bf16[128,1536]{1,0:T(8,128)(2,1)S(1)}, u32[]{:S(2)}, u32[]{:S(2)}) collective-permute-start(bf16[128,1536]{1,0:T(8,128)(2,1)S(1)} %total.5), channel_id=1, source_target_pairs={{0,16},{8,24},{16,0},{24,8},{1,17},{9,25},{17,1},{25,9},{2,18},{10... | collective-permute-start | bytes 1179656 | tf_op jit(solution)/shard_map/cond/branch_1_fun/ppermute | solution.py:487
  76.5 2.5 %up.15 = (bf16[64,1024]{1,0:T(8,128)(2,1)S(1)}, bf16[64,1024]{1,0:T(8,128)(2,1)S(1)}, bf16[64,1536]{1,0:T(8,128)(2,1)S(1)}, f32[64,1536]{1,0:T(8,128)S(1)}) custom-call(s32[2]{0:T(128)S(1)} %get-tuple-element.121.ids, bf16[120,1024]{1,0:T(8,128)(2,1)} %get-tuple-element.137.refs_0_, bf16[1024,2048]{1,0:T(8,128)(2,1)S(1)} %get-tuple-element.130.w_in.refs_1_, ...), custom_call_target="tpu_custom_call" | custom-call | flops 1 | bytes 1 | tf_op jit(solution)/shard_map/cond/branch_1_fun/up/pallas_call | solution.py:92
  79.1 3.8 %down.10 = bf16[120,1024]{1,0:T(8,128)(2,1)} custom-call(s32[2]{0:T(128)S(1)} %get-tuple-element.121.ids, bf16[64,1536]{1,0:T(8,128)(2,1)S(1)} %act.7.own, bf16[64,1536]{1,0:T(8,128)(2,1)} %collective-permute-done.7.core, bf16[1024,2048]{1,0:T(8,128)(2,1)S(1)} %get-tuple-element.130.w_in.refs_1_, bf16[1024,1024]{1,0:T(8,128)(2,1)S(1)} %get-tuple-element.131.w_out.refs_2_), custom_call_target="tpu_custom_call" | custom-call | flops 1 | bytes 1 | tf_op jit(solution)/shard_map/cond/branch_1_fun/down/pallas_call | solution.py:92
  82.9 3.5 %collective-permute-done.8.other = bf16[128,1536]{1,0:T(8,128)(2,1)S(1)} collective-permute-done((bf16[128,1536]{1,0:T(8,128)(2,1)S(1)}, bf16[128,1536]{1,0:T(8,128)(2,1)S(1)}, u32[]{:S(2)}, u32[]{:S(2)}) %collective-permute-start.8) | collective-permute-done | bytes 393248 | tf_op jit(solution)/shard_map/cond/branch_1_fun/ppermute | solution.py:487
  87.4 2.0 %down.11 = (f32[128,1024]{1,0:T(8,128)S(1)}, f32[128,1024]{1,0:T(8,128)S(1)}) custom-call(s32[2]{0:T(128)S(1)} %get-tuple-element.121.ids, bf16[128,1536]{1,0:T(8,128)(2,1)} %get-tuple-element.377.own, bf16[1024,2048]{1,0:T(8,128)(2,1)S(1)} %get-tuple-element.130.w_in.refs_1_, bf16[1024,1024]{1,0:T(8,128)(2,1)S(1)} %get-tuple-element.131.w_out.refs_2_), custom_call_target="tpu_custom_call" | custom-call | flops 1 | bytes 1 | tf_op jit(solution)/shard_map/cond/branch_1_fun/down/pallas_call | solution.py:92
  89.4 3.1 %down.12 = (bf16[120,1024]{1,0:T(8,128)(2,1)}, bf16[120,1024]{1,0:T(8,128)(2,1)}) custom-call(s32[2]{0:T(128)S(1)} %get-tuple-element.121.ids, f32[128,1024]{1,0:T(8,128)S(1)} %get-tuple-element.144.out_rows, f32[128,1024]{1,0:T(8,128)S(1)} %get-tuple-element.145.grad_rows, bf16[128,1536]{1,0:T(8,128)(2,1)} %collective-permute-done.10.core, ...), custom_call_target="tpu_custom_call" | custom-call | flops 1 | bytes 1 | tf_op jit(solution)/shard_map/cond/branch_1_fun/down/pallas_call | solution.py:92
  92.6 1.6 %collective-permute-start.27 = (bf16[64,1536]{1,0:T(8,128)(2,1)S(1)}, bf16[64,1536]{1,0:T(8,128)(2,1)S(1)}, u32[]{:S(2)}, u32[]{:S(2)}) collective-permute-start(bf16[64,1536]{1,0:T(8,128)(2,1)S(1)} %get-tuple-element.280), channel_id=1, source_target_pairs={{0,16},{8,24},{16,0},{24,8},{1,17},{9,25},{17,1},{25,9},{2,18},{10... | collective-permute-start | bytes 589832 | tf_op jit(solution)/shard_map/ppermute | solution.py:487
  94.1 1.9 %collective-permute-start.30 = (bf16[120,1024]{1,0:T(8,128)(2,1)}, bf16[120,1024]{1,0:T(8,128)(2,1)S(1)}, u32[]{:S(2)}, u32[]{:S(2)}) collective-permute-start(bf16[120,1024]{1,0:T(8,128)(2,1)} %get-tuple-element.285), channel_id=1, source_target_pairs={{0,2},{1,3},{2,0},{3,1},{4,6},{5,7},{6,4},{7,5},{8,10},{9,11},{10,... | collective-permute-start | bytes 737288 | tf_op jit(solution)/shard_map/ppermute | solution.py:484
  96.1 4.5 %collective-permute-start.26 = (bf16[120,1024]{1,0:T(8,128)(2,1)}, bf16[120,1024]{1,0:T(8,128)(2,1)S(1)}, u32[]{:S(2)}, u32[]{:S(2)}) collective-permute-start(bf16[120,1024]{1,0:T(8,128)(2,1)} %get-tuple-element.277), channel_id=1, source_target_pairs={{0,7},{1,6},{2,5},{3,4},{4,3},{5,2},{6,1},{7,0},{8,15},{9,14},{10,... | collective-permute-start | bytes 737288 | tf_op jit(solution)/shard_map/ppermute | solution.py:484
  101.0 9.8 %conditional.7 = (bf16[64,1024]{1,0:T(8,128)(2,1)S(1)}, bf16[64,1024]{1,0:T(8,128)(2,1)S(1)}, bf16[64,1536]{1,0:T(8,128)(2,1)}, bf16[64,1536]{1,0:T(8,128)(2,1)}...) conditional(s32[]{:T(128)} %convert_element_type.2, () %tuple.81, (s32[2]{0:T(128)S(1)}, ...), branch_computations={%region_6.7_spmd, %region_7.8_spmd} | conditional | flops 2 | bytes 901180 | solution.py:499
  101.0 4.2 %act.9 = (bf16[64,1536]{1,0:T(8,128)(2,1)}, bf16[1024,2048]{1,0:T(8,128)(2,1)S(1)}, bf16[1024,1024]{1,0:T(8,128)(2,1)S(1)}) custom-call(s32[2]{0:T(128)S(1)} %get-tuple-element.156.ids, f32[64,1536]{1,0:T(8,128)S(1)} %get-tuple-element.157.keep, bf16[64,1536]{1,0:T(8,128)(2,1)S(1)} %get-tuple-element.158.core, ...), custom_call_target="tpu_custom_call" | custom-call | flops 1 | bytes 1 | tf_op jit(solution)/shard_map/cond/branch_1_fun/act/pallas_call | solution.py:281
  105.3 1.8 %collective-permute-done.11.core = bf16[64,1536]{1,0:T(8,128)(2,1)} collective-permute-done((bf16[64,1536]{1,0:T(8,128)(2,1)}, bf16[64,1536]{1,0:T(8,128)(2,1)}, u32[]{:S(2)}, u32[]{:S(2)}) %collective-permute-start.11) | collective-permute-done | bytes 196640 | tf_op jit(solution)/shard_map/cond/branch_1_fun/ppermute | solution.py:487
  107.0 3.7 %down.13 = (bf16[120,512]{1,0:T(8,128)(2,1)}, bf16[120,512]{1,0:T(8,128)(2,1)}) custom-call(s32[2]{0:T(128)S(1)} %get-tuple-element.156.ids, bf16[64,1536]{1,0:T(8,128)(2,1)} %get-tuple-element.399.own, bf16[64,1536]{1,0:T(8,128)(2,1)} %collective-permute-done.11.core, bf16[1024,2048]{1,0:T(8,128)(2,1)S(1)} %get-tuple-element.163.w_in, ...), custom_call_target="tpu_custom_call" | custom-call | flops 1 | bytes 1 | tf_op jit(solution)/shard_map/cond/branch_1_fun/down/pallas_call | solution.py:92
  110.8 2.0 %collective-permute-start.28 = (bf16[120,512]{1,0:T(8,128)(2,1)}, bf16[120,512]{1,0:T(8,128)(2,1)S(1)}, u32[]{:S(2)}, u32[]{:S(2)}) collective-permute-start(bf16[120,512]{1,0:T(8,128)(2,1)} %get-tuple-element.283), channel_id=1, source_target_pairs={{0,3},{1,2},{2,1},{3,0},{4,7},{5,6},{6,5},{7,4},{8,11},{9,10},{10,... | collective-permute-start | bytes 368648 | tf_op jit(solution)/shard_map/ppermute | solution.py:484
  112.8 1.0 collective-permute-start.29
  113.8 6.6 %grads.1 = (bf16[1024,2048]{1,0:T(8,128)(2,1)}, bf16[1024,1024]{1,0:T(8,128)(2,1)}) custom-call(s32[2]{0:T(128)S(1)} %pad_add_fusion.refs_0_, bf16[128,1024]{1,0:T(8,128)(2,1)} %get-tuple-element.292.refs_1_, bf16[128,1024]{1,0:T(8,128)(2,1)} %get-tuple-element.293.refs_2_, bf16[128,1536]{1,0:T(8,128)(2,1)S(1)} %get-tuple-element.294.refs_3_, ...), custom_call_target="tpu_custom_call" | custom-call | flops 1 | bytes 1 | tf_op jit(solution)/shard_map/grads/pallas_call | solution.py:392
  120.4 2.2 %final.3 = (f32[192,1024]{1,0:T(8,128)S(1)}, f32[192,1024]{1,0:T(8,128)S(1)}) custom-call(s32[2]{0:T(128)S(1)} %pad_add_fusion.refs_0_, s32[2,192]{1,0:T(2,128)S(1)} %bitcast.9, f32[2,192]{1,0:T(2,128)S(1)} %bitcast.13, bf16[120,1024]{1,0:T(8,128)(2,1)S(1)} %copy-done.22, bf16[120,1024]{1,0:T(8,128)(2,1)S(1)} %collective-permute-done.24.refs_4_, ...), custom_call_target="tpu_custom_call" | custom-call | flops 1 | bytes 1 | tf_op jit(solution)/shard_map/final/pallas_call | solution.py:92
  122.7 1.3 %final.4 = (f32[192,1024]{1,0:T(8,128)S(1)}, f32[192,1024]{1,0:T(8,128)S(1)}) custom-call(s32[2]{0:T(128)S(1)} %pad_add_fusion.refs_0_, s32[2,192]{1,0:T(2,128)S(1)} %bitcast.10, f32[2,192]{1,0:T(2,128)S(1)} %bitcast.14, bf16[120,512]{1,0:T(8,128)(2,1)S(1)} %collective-permute-done.28.refs_3_, bf16[120,512]{1,0:T(8,128)(2,1)S(1)} %collective-permute-done.29.refs_4_, ...), custom_call_target="tpu_custom_call" | custom-call | flops 1 | bytes 1 | tf_op jit(solution)/shard_map/final/pallas_call | solution.py:92
  124.1 2.3 %final.5 = (bf16[192,1024]{1,0:T(8,128)(2,1)}, bf16[192,1024]{1,0:T(8,128)(2,1)}) custom-call(s32[2]{0:T(128)S(1)} %pad_add_fusion.refs_0_, s32[2,192]{1,0:T(2,128)S(1)} %bitcast.11, f32[2,192]{1,0:T(2,128)S(1)} %bitcast.15, bf16[120,1024]{1,0:T(8,128)(2,1)S(1)} %collective-permute-done.25.refs_3_, bf16[120,1024]{1,0:T(8,128)(2,1)S(1)} %collective-permute-done.26.refs_4_, ...), custom_call_target="tpu_custom_call" | custom-call | flops 1 | bytes 1 | tf_op jit(solution)/shard_map/final/pallas_call | solution.py:92
  (101 shorter events, 5.8 us)
Async XLA Ops:
  4.5 9.2 %collective-permute-start.15 = (bf16[120,1024]{1,0:T(8,128)(2,1)}, bf16[120,1024]{1,0:T(8,128)(2,1)S(1)}, u32[]{:S(2)}, u32[]{:S(2)}) collective-permute-start(bf16[120,1024]{1,0:T(8,128)(2,1)} %get-tuple-element.247), channel_id=1, source_target_pairs={{0,1},{1,0},{2,3},{3,2},{4,5},{5,4},{6,7},{7,6},{8,9},{9,8},{10,11... | collective-permute-start | bytes 737288 | tf_op jit(solution)/shard_map/ppermute | solution.py:484
  7.5 20.2 %collective-permute-start.12 = (bf16[120,1024]{1,0:T(8,128)(2,1)}, bf16[120,1024]{1,0:T(8,128)(2,1)S(1)}, u32[]{:S(2)}, u32[]{:S(2)}) collective-permute-start(bf16[120,1024]{1,0:T(8,128)(2,1)} %get-tuple-element.243), channel_id=1, source_target_pairs={{0,4},{1,5},{2,6},{3,7},{4,0},{5,1},{6,2},{7,3},{8,12},{9,13},{10,... | collective-permute-start | bytes 737288 | tf_op jit(solution)/shard_map/ppermute | solution.py:484
  10.1 21.6 %collective-permute-start.13 = (bf16[120,1024]{1,0:T(8,128)(2,1)}, bf16[120,1024]{1,0:T(8,128)(2,1)S(1)}, u32[]{:S(2)}, u32[]{:S(2)}) collective-permute-start(bf16[120,1024]{1,0:T(8,128)(2,1)} %get-tuple-element.244), channel_id=1, source_target_pairs={{0,5},{1,4},{2,7},{3,6},{4,1},{5,0},{6,3},{7,2},{8,13},{9,12},{10,... | collective-permute-start | bytes 737288 | tf_op jit(solution)/shard_map/ppermute | solution.py:484
  10.1 21.6 %collective-permute-start.14 = (bf16[120,1024]{1,0:T(8,128)(2,1)}, bf16[120,1024]{1,0:T(8,128)(2,1)S(1)}, u32[]{:S(2)}, u32[]{:S(2)}) collective-permute-start(bf16[120,1024]{1,0:T(8,128)(2,1)} %get-tuple-element.245), channel_id=1, source_target_pairs={{0,2},{1,3},{2,0},{3,1},{4,6},{5,7},{6,4},{7,5},{8,10},{9,11},{10,... | collective-permute-start | bytes 737288 | tf_op jit(solution)/shard_map/ppermute | solution.py:484
  18.1 2.8 %collective-permute-start = (bf16[128,1536]{1,0:T(8,128)(2,1)S(1)}, bf16[128,1536]{1,0:T(8,128)(2,1)}, u32[]{:S(2)}, u32[]{:S(2)}) collective-permute-start(bf16[128,1536]{1,0:T(8,128)(2,1)S(1)} %get-tuple-element.79), channel_id=1, source_target_pairs={{0,8},{8,0},{16,24},{24,16},{1,9},{9,1},{17,25},{25,17},{2,10},{10... | collective-permute-start | bytes 1179656 | tf_op jit(solution)/shard_map/cond/branch_1_fun/ppermute | solution.py:487
  22.2 14.4 %collective-permute-start.17 = (bf16[128,768]{1,0:T(8,128)(2,1)S(1)}, bf16[128,768]{1,0:T(8,128)(2,1)S(1)}, u32[]{:S(2)}, u32[]{:S(2)}) collective-permute-start(bf16[128,768]{1,0:T(8,128)(2,1)S(1)} %get-tuple-element.248), channel_id=1, source_target_pairs={{0,16},{8,24},{16,0},{24,8},{1,17},{9,25},{17,1},{25,9},{2,18},{10... | collective-permute-start | bytes 589832 | tf_op jit(solution)/shard_map/ppermute | solution.py:487
  24.0 12.6 %collective-permute-start.18 = (bf16[128,768]{1,0:T(8,128)(2,1)S(1)}, bf16[128,768]{1,0:T(8,128)(2,1)S(1)}, u32[]{:S(2)}, u32[]{:S(2)}) collective-permute-start(bf16[128,768]{1,0:T(8,128)(2,1)S(1)} %get-tuple-element.249), channel_id=1, source_target_pairs={{0,16},{8,24},{16,0},{24,8},{1,17},{9,25},{17,1},{25,9},{2,18},{10... | collective-permute-start | bytes 589832 | tf_op jit(solution)/shard_map/ppermute | solution.py:487
  31.8 31.4 %collective-permute-start.16 = (bf16[120,1024]{1,0:T(8,128)(2,1)}, bf16[120,1024]{1,0:T(8,128)(2,1)S(1)}, u32[]{:S(2)}, u32[]{:S(2)}) collective-permute-start(bf16[120,1024]{1,0:T(8,128)(2,1)} %get-tuple-element.250), channel_id=1, source_target_pairs={{0,6},{1,7},{2,4},{3,5},{4,2},{5,3},{6,0},{7,1},{8,14},{9,15},{10,... | collective-permute-start | bytes 737288 | tf_op jit(solution)/shard_map/ppermute | solution.py:484
  35.3 27.8 %collective-permute-start.19 = (bf16[120,1024]{1,0:T(8,128)(2,1)}, bf16[120,1024]{1,0:T(8,128)(2,1)S(1)}, u32[]{:S(2)}, u32[]{:S(2)}) collective-permute-start(bf16[120,1024]{1,0:T(8,128)(2,1)} %get-tuple-element.258), channel_id=1, source_target_pairs={{0,7},{1,6},{2,5},{3,4},{4,3},{5,2},{6,1},{7,0},{8,15},{9,14},{10,... | collective-permute-start | bytes 737288 | tf_op jit(solution)/shard_map/ppermute | solution.py:484
  36.6 32.0 %collective-permute-start.21 = (bf16[120,1024]{1,0:T(8,128)(2,1)}, bf16[120,1024]{1,0:T(8,128)(2,1)}, u32[]{:S(2)}, u32[]{:S(2)}) collective-permute-start(bf16[120,1024]{1,0:T(8,128)(2,1)} %get-tuple-element.263), channel_id=1, source_target_pairs={{0,3},{1,2},{2,1},{3,0},{4,7},{5,6},{6,5},{7,4},{8,11},{9,10},{10,... | collective-permute-start | bytes 737288 | tf_op jit(solution)/shard_map/ppermute | solution.py:484
  40.3 1.8 %collective-permute-start.1 = (bf16[128,1536]{1,0:T(8,128)(2,1)S(1)}, bf16[128,1536]{1,0:T(8,128)(2,1)S(1)}, u32[]{:S(2)}, u32[]{:S(2)}) collective-permute-start(bf16[128,1536]{1,0:T(8,128)(2,1)S(1)} %get-tuple-element.92), channel_id=1, source_target_pairs={{0,8},{8,0},{16,24},{24,16},{1,9},{9,1},{17,25},{25,17},{2,10},{10... | collective-permute-start | bytes 1179656 | tf_op jit(solution)/shard_map/cond/branch_1_fun/ppermute | solution.py:487
  43.6 7.3 %copy-start.6 = (bf16[128,1536]{1,0:T(8,128)(2,1)}, bf16[128,1536]{1,0:T(8,128)(2,1)S(1)}, u32[]{:S(2)}) copy-start(bf16[128,1536]{1,0:T(8,128)(2,1)S(1)} %act.5.own) | copy-start | bytes 1179652 | tf_op jit(solution)/shard_map/cond
  43.6 3.9 %collective-permute-start.2 = (bf16[128,1536]{1,0:T(8,128)(2,1)S(1)}, bf16[128,1536]{1,0:T(8,128)(2,1)S(1)}, u32[]{:S(2)}, u32[]{:S(2)}) collective-permute-start(bf16[128,1536]{1,0:T(8,128)(2,1)S(1)} %act.5.own), channel_id=1, source_target_pairs={{0,8},{8,0},{16,24},{24,16},{1,9},{9,1},{17,25},{25,17},{2,10},{10... | collective-permute-start | bytes 1179656 | tf_op jit(solution)/shard_map/cond/branch_1_fun/ppermute | solution.py:487
  43.8 11.4 %collective-permute-start.3 = (bf16[128,1536]{1,0:T(8,128)(2,1)S(1)}, bf16[128,1536]{1,0:T(8,128)(2,1)S(1)}, u32[]{:S(2)}, u32[]{:S(2)}) collective-permute-start(bf16[128,1536]{1,0:T(8,128)(2,1)S(1)} %total.4), channel_id=1, source_target_pairs={{0,16},{8,24},{16,0},{24,8},{1,17},{9,25},{17,1},{25,9},{2,18},{10... | collective-permute-start | bytes 1179656 | tf_op jit(solution)/shard_map/cond/branch_1_fun/ppermute | solution.py:487
  47.5 8.7 %copy-start.8 = (f32[64,1536]{1,0:T(8,128)}, f32[64,1536]{1,0:T(8,128)S(1)}, u32[]{:S(2)}) copy-start(f32[64,1536]{1,0:T(8,128)S(1)} %get-tuple-element.350.next_keep) | copy-start | bytes 1179652 | tf_op jit(solution)/shard_map/cond
  47.5 8.7 %copy-start.4 = (bf16[128,1536]{1,0:T(8,128)(2,1)}, bf16[128,1536]{1,0:T(8,128)(2,1)S(1)}, u32[]{:S(2)}) copy-start(bf16[128,1536]{1,0:T(8,128)(2,1)S(1)} %collective-permute-done.2.core) | copy-start | bytes 1179652 | tf_op jit(solution)/shard_map/cond
  50.9 4.3 %collective-permute-start.4 = (bf16[64,1536]{1,0:T(8,128)(2,1)S(1)}, bf16[64,1536]{1,0:T(8,128)(2,1)S(1)}, u32[]{:S(2)}, u32[]{:S(2)}) collective-permute-start(bf16[64,1536]{1,0:T(8,128)(2,1)S(1)} %get-tuple-element.109), channel_id=1, source_target_pairs={{0,8},{8,0},{16,24},{24,16},{1,9},{9,1},{17,25},{25,17},{2,10},{10... | collective-permute-start | bytes 589832 | tf_op jit(solution)/shard_map/cond/branch_1_fun/ppermute | solution.py:487
  56.2 2.1 %collective-permute-start.5 = (bf16[128,1536]{1,0:T(8,128)(2,1)}, bf16[128,1536]{1,0:T(8,128)(2,1)}, u32[]{:S(2)}, u32[]{:S(2)}) collective-permute-start(bf16[128,1536]{1,0:T(8,128)(2,1)} %get-tuple-element.344.own), channel_id=1, source_target_pairs={{0,8},{8,0},{16,24},{24,16},{1,9},{9,1},{17,25},{25,17},{2,10},{10... | collective-permute-start | bytes 1179656 | tf_op jit(solution)/shard_map/cond/branch_1_fun/ppermute | solution.py:487
  58.2 3.3 %copy-start.5 = (bf16[128,1536]{1,0:T(8,128)(2,1)S(1)}, bf16[128,1536]{1,0:T(8,128)(2,1)}, u32[]{:S(2)}) copy-start(bf16[128,1536]{1,0:T(8,128)(2,1)} %copy-done.4) | copy-start | bytes 1179652 | tf_op jit(solution)/shard_map/cond
  58.2 3.3 %copy-start.7 = (bf16[128,1536]{1,0:T(8,128)(2,1)S(1)}, bf16[128,1536]{1,0:T(8,128)(2,1)}, u32[]{:S(2)}) copy-start(bf16[128,1536]{1,0:T(8,128)(2,1)} %copy-done.6) | copy-start | bytes 1179652 | tf_op jit(solution)/shard_map/cond
  58.3 3.3 %copy-start.9 = (f32[64,1536]{1,0:T(8,128)S(1)}, f32[64,1536]{1,0:T(8,128)}, u32[]{:S(2)}) copy-start(f32[64,1536]{1,0:T(8,128)} %copy-done.8) | copy-start | bytes 1179652 | tf_op jit(solution)/shard_map/cond
  58.3 3.3 %copy-start.11 = (bf16[128,1024]{1,0:T(8,128)(2,1)S(1)}, bf16[128,1024]{1,0:T(8,128)(2,1)}, u32[]{:S(2)}) copy-start(bf16[128,1024]{1,0:T(8,128)(2,1)} %copy-done.10) | copy-start | bytes 786436 | tf_op jit(solution)/shard_map/cond
  58.3 3.3 %copy-start.13 = (bf16[128,1024]{1,0:T(8,128)(2,1)S(1)}, bf16[128,1024]{1,0:T(8,128)(2,1)}, u32[]{:S(2)}) copy-start(bf16[128,1024]{1,0:T(8,128)(2,1)} %copy-done.12) | copy-start | bytes 786436 | tf_op jit(solution)/shard_map/cond
  58.3 3.2 %copy-start.21 = (bf16[64,1536]{1,0:T(8,128)(2,1)S(1)}, bf16[64,1536]{1,0:T(8,128)(2,1)}, u32[]{:S(2)}) copy-start(bf16[64,1536]{1,0:T(8,128)(2,1)} %copy-done.20) | copy-start | bytes 589828 | tf_op jit(solution)/shard_map/cond
  61.6 7.4 %collective-permute-start.20 = (bf16[64,1536]{1,0:T(8,128)(2,1)S(1)}, bf16[64,1536]{1,0:T(8,128)(2,1)S(1)}, u32[]{:S(2)}, u32[]{:S(2)}) collective-permute-start(bf16[64,1536]{1,0:T(8,128)(2,1)S(1)} %get-tuple-element.261), channel_id=1, source_target_pairs={{0,16},{8,24},{16,0},{24,8},{1,17},{9,25},{17,1},{25,9},{2,18},{10... | collective-permute-start | bytes 589832 | tf_op jit(solution)/shard_map/ppermute | solution.py:487
  63.1 33.0 %collective-permute-start.24 = (bf16[120,1024]{1,0:T(8,128)(2,1)}, bf16[120,1024]{1,0:T(8,128)(2,1)S(1)}, u32[]{:S(2)}, u32[]{:S(2)}) collective-permute-start(bf16[120,1024]{1,0:T(8,128)(2,1)} %get-tuple-element.274), channel_id=1, source_target_pairs={{0,1},{1,0},{2,3},{3,2},{4,5},{5,4},{6,7},{7,6},{8,9},{9,8},{10,11... | collective-permute-start | bytes 737288 | tf_op jit(solution)/shard_map/ppermute | solution.py:484
  63.6 32.5 %collective-permute-start.23 = (bf16[120,1024]{1,0:T(8,128)(2,1)}, bf16[120,1024]{1,0:T(8,128)(2,1)S(1)}, u32[]{:S(2)}, u32[]{:S(2)}) collective-permute-start(bf16[120,1024]{1,0:T(8,128)(2,1)} %get-tuple-element.270), channel_id=1, source_target_pairs={{0,5},{1,4},{2,7},{3,6},{4,1},{5,0},{6,3},{7,2},{8,13},{9,12},{10,... | collective-permute-start | bytes 737288 | tf_op jit(solution)/shard_map/ppermute | solution.py:484
  68.6 27.5 %collective-permute-start.22 = (bf16[120,1024]{1,0:T(8,128)(2,1)}, bf16[120,1024]{1,0:T(8,128)(2,1)S(1)}, u32[]{:S(2)}, u32[]{:S(2)}) collective-permute-start(bf16[120,1024]{1,0:T(8,128)(2,1)} %get-tuple-element.268), channel_id=1, source_target_pairs={{0,4},{1,5},{2,6},{3,7},{4,0},{5,1},{6,2},{7,3},{8,12},{9,13},{10,... | collective-permute-start | bytes 737288 | tf_op jit(solution)/shard_map/ppermute | solution.py:484
  72.6 14.8 %copy-start.16 = (bf16[128,1024]{1,0:T(8,128)(2,1)}, bf16[128,1024]{1,0:T(8,128)(2,1)S(1)}, u32[]{:S(2)}) copy-start(bf16[128,1024]{1,0:T(8,128)(2,1)S(1)} %get-tuple-element.129.rows) | copy-start | bytes 786436 | tf_op jit(solution)/shard_map/cond
  72.6 2.0 %collective-permute-start.6 = (bf16[128,1536]{1,0:T(8,128)(2,1)S(1)}, bf16[128,1536]{1,0:T(8,128)(2,1)S(1)}, u32[]{:S(2)}, u32[]{:S(2)}) collective-permute-start(bf16[128,1536]{1,0:T(8,128)(2,1)S(1)} %get-tuple-element.128), channel_id=1, source_target_pairs={{0,8},{8,0},{16,24},{24,16},{1,9},{9,1},{17,25},{25,17},{2,10},{10... | collective-permute-start | bytes 1179656 | tf_op jit(solution)/shard_map/cond/branch_1_fun/ppermute | solution.py:487
  74.8 8.1 %copy-start.19 = (bf16[64,1536]{1,0:T(8,128)(2,1)}, bf16[64,1536]{1,0:T(8,128)(2,1)S(1)}, u32[]{:S(2)}) copy-start(bf16[64,1536]{1,0:T(8,128)(2,1)S(1)} %act.7.own) | copy-start | bytes 589828 | tf_op jit(solution)/shard_map/cond
  74.8 4.3 %collective-permute-start.7 = (bf16[64,1536]{1,0:T(8,128)(2,1)S(1)}, bf16[64,1536]{1,0:T(8,128)(2,1)}, u32[]{:S(2)}, u32[]{:S(2)}) collective-permute-start(bf16[64,1536]{1,0:T(8,128)(2,1)S(1)} %act.7.own), channel_id=1, source_target_pairs={{0,8},{8,0},{16,24},{24,16},{1,9},{9,1},{17,25},{25,17},{2,10},{10... | collective-permute-start | bytes 589832 | tf_op jit(solution)/shard_map/cond/branch_1_fun/ppermute | solution.py:487
  75.0 11.4 %collective-permute-start.8 = (bf16[128,1536]{1,0:T(8,128)(2,1)S(1)}, bf16[128,1536]{1,0:T(8,128)(2,1)S(1)}, u32[]{:S(2)}, u32[]{:S(2)}) collective-permute-start(bf16[128,1536]{1,0:T(8,128)(2,1)S(1)} %total.5), channel_id=1, source_target_pairs={{0,16},{8,24},{16,0},{24,8},{1,17},{9,25},{17,1},{25,9},{2,18},{10... | collective-permute-start | bytes 1179656 | tf_op jit(solution)/shard_map/cond/branch_1_fun/ppermute | solution.py:487
  79.0 8.3 %copy-start.2 = (f32[64,1536]{1,0:T(8,128)}, f32[64,1536]{1,0:T(8,128)S(1)}, u32[]{:S(2)}) copy-start(f32[64,1536]{1,0:T(8,128)S(1)} %get-tuple-element.383.next_keep) | copy-start | bytes 1179652 | tf_op jit(solution)/shard_map/cond
  82.9 3.5 %collective-permute-start.9 = (bf16[64,1536]{1,0:T(8,128)(2,1)S(1)}, bf16[64,1536]{1,0:T(8,128)(2,1)S(1)}, u32[]{:S(2)}, u32[]{:S(2)}) collective-permute-start(bf16[64,1536]{1,0:T(8,128)(2,1)S(1)} %get-tuple-element.142), channel_id=1, source_target_pairs={{0,8},{8,0},{16,24},{24,16},{1,9},{9,1},{17,25},{25,17},{2,10},{10... | collective-permute-start | bytes 589832 | tf_op jit(solution)/shard_map/cond/branch_1_fun/ppermute | solution.py:487
  87.4 2.1 %collective-permute-start.10 = (bf16[128,1536]{1,0:T(8,128)(2,1)}, bf16[128,1536]{1,0:T(8,128)(2,1)}, u32[]{:S(2)}, u32[]{:S(2)}) collective-permute-start(bf16[128,1536]{1,0:T(8,128)(2,1)} %get-tuple-element.377.own), channel_id=1, source_target_pairs={{0,8},{8,0},{16,24},{24,16},{1,9},{9,1},{17,25},{25,17},{2,10},{10... | collective-permute-start | bytes 1179656 | tf_op jit(solution)/shard_map/cond/branch_1_fun/ppermute | solution.py:487
  92.6 3.5 %copy-start.23 = (bf16[64,1024]{1,0:T(8,128)(2,1)}, bf16[64,1024]{1,0:T(8,128)(2,1)S(1)}, u32[]{:S(2)}) copy-start(bf16[64,1024]{1,0:T(8,128)(2,1)S(1)} %get-tuple-element.300.refs_10_) | copy-start | bytes 393220
  92.6 3.5 %copy-start.24 = (bf16[64,1024]{1,0:T(8,128)(2,1)}, bf16[64,1024]{1,0:T(8,128)(2,1)S(1)}, u32[]{:S(2)}) copy-start(bf16[64,1024]{1,0:T(8,128)(2,1)S(1)} %get-tuple-element.299.refs_9_) | copy-start | bytes 393220
  92.6 8.4 %collective-permute-start.27 = (bf16[64,1536]{1,0:T(8,128)(2,1)S(1)}, bf16[64,1536]{1,0:T(8,128)(2,1)S(1)}, u32[]{:S(2)}, u32[]{:S(2)}) collective-permute-start(bf16[64,1536]{1,0:T(8,128)(2,1)S(1)} %get-tuple-element.280), channel_id=1, source_target_pairs={{0,16},{8,24},{16,0},{24,8},{1,17},{9,25},{17,1},{25,9},{2,18},{10... | collective-permute-start | bytes 589832 | tf_op jit(solution)/shard_map/ppermute | solution.py:487
  94.1 26.3 %collective-permute-start.30 = (bf16[120,1024]{1,0:T(8,128)(2,1)}, bf16[120,1024]{1,0:T(8,128)(2,1)S(1)}, u32[]{:S(2)}, u32[]{:S(2)}) collective-permute-start(bf16[120,1024]{1,0:T(8,128)(2,1)} %get-tuple-element.285), channel_id=1, source_target_pairs={{0,2},{1,3},{2,0},{3,1},{4,6},{5,7},{6,4},{7,5},{8,10},{9,11},{10,... | collective-permute-start | bytes 737288 | tf_op jit(solution)/shard_map/ppermute | solution.py:484
  96.1 27.9 %collective-permute-start.26 = (bf16[120,1024]{1,0:T(8,128)(2,1)}, bf16[120,1024]{1,0:T(8,128)(2,1)S(1)}, u32[]{:S(2)}, u32[]{:S(2)}) collective-permute-start(bf16[120,1024]{1,0:T(8,128)(2,1)} %get-tuple-element.277), channel_id=1, source_target_pairs={{0,7},{1,6},{2,5},{3,4},{4,3},{5,2},{6,1},{7,0},{8,15},{9,14},{10,... | collective-permute-start | bytes 737288 | tf_op jit(solution)/shard_map/ppermute | solution.py:484
  100.6 23.4 %collective-permute-start.25 = (bf16[120,1024]{1,0:T(8,128)(2,1)}, bf16[120,1024]{1,0:T(8,128)(2,1)S(1)}, u32[]{:S(2)}, u32[]{:S(2)}) collective-permute-start(bf16[120,1024]{1,0:T(8,128)(2,1)} %get-tuple-element.275), channel_id=1, source_target_pairs={{0,6},{1,7},{2,4},{3,5},{4,2},{5,3},{6,0},{7,1},{8,14},{9,15},{10,... | collective-permute-start | bytes 737288 | tf_op jit(solution)/shard_map/ppermute | solution.py:484
  105.2 1.8 %collective-permute-start.11 = (bf16[64,1536]{1,0:T(8,128)(2,1)}, bf16[64,1536]{1,0:T(8,128)(2,1)}, u32[]{:S(2)}, u32[]{:S(2)}) collective-permute-start(bf16[64,1536]{1,0:T(8,128)(2,1)} %get-tuple-element.399.own), channel_id=1, source_target_pairs={{0,8},{8,0},{16,24},{24,16},{1,9},{9,1},{17,25},{25,17},{2,10},{10... | collective-permute-start | bytes 589832 | tf_op jit(solution)/shard_map/cond/branch_1_fun/ppermute | solution.py:487
  110.8 9.7 %copy-start = (s32[192,2]{0,1:T(2,128)S(1)}, s32[192,2]{0,1:T(2,128)}, u32[]{:S(2)}) copy-start(s32[192,2]{0,1:T(2,128)} %param.15) | copy-start | bytes 4612
  110.8 9.7 %copy-start.1 = (f32[192,2]{0,1:T(2,128)S(1)}, f32[192,2]{0,1:T(2,128)}, u32[]{:S(2)}) copy-start(f32[192,2]{0,1:T(2,128)} %param.16) | copy-start | bytes 4612
  110.8 9.7 %copy-start.22 = (bf16[120,1024]{1,0:T(8,128)(2,1)S(1)}, bf16[120,1024]{1,0:T(8,128)(2,1)}, u32[]{:S(2)}) copy-start(bf16[120,1024]{1,0:T(8,128)(2,1)} %get-tuple-element.272.refs_3_) | copy-start | bytes 737284
  110.8 11.8 %collective-permute-start.28 = (bf16[120,512]{1,0:T(8,128)(2,1)}, bf16[120,512]{1,0:T(8,128)(2,1)S(1)}, u32[]{:S(2)}, u32[]{:S(2)}) collective-permute-start(bf16[120,512]{1,0:T(8,128)(2,1)} %get-tuple-element.283), channel_id=1, source_target_pairs={{0,3},{1,2},{2,1},{3,0},{4,7},{5,6},{6,5},{7,4},{8,11},{9,10},{10,... | collective-permute-start | bytes 368648 | tf_op jit(solution)/shard_map/ppermute | solution.py:484
  112.8 9.9 %collective-permute-start.29 = (bf16[120,512]{1,0:T(8,128)(2,1)}, bf16[120,512]{1,0:T(8,128)(2,1)S(1)}, u32[]{:S(2)}, u32[]{:S(2)}) collective-permute-start(bf16[120,512]{1,0:T(8,128)(2,1)} %get-tuple-element.284), channel_id=1, source_target_pairs={{0,3},{1,2},{2,1},{3,0},{4,7},{5,6},{6,5},{7,4},{8,11},{9,10},{10,... | collective-permute-start | bytes 368648 | tf_op jit(solution)/shard_map/ppermute | solution.py:484
  (10 other events, 25.3 us)

commit v4 on v3

--- a/solution.py
+++ b/solution.py
@@ -128,11 +128,11 @@
 PIECES = 4
 
 
-def weight_copies(ids, far_in, far_out, w_in, w_out, sems):
+def weight_copies(halves, far_in, far_out, w_in, w_out, sems):
     units = far_out.shape[0]
     span, depth = units // 2, far_in.shape[0] // PIECES
     copies = []
-    for half in (1 - ids[1], ids[1]):
+    for half in halves:
         at = pl.ds(pl.multiple_of(half * span, span), span)
         at_up = pl.ds(pl.multiple_of(units + half * span, span), span)
         for k in range(PIECES):
@@ -159,7 +159,7 @@
 
     def kernel(ids, *refs):
         held, (far_in, far_out, row_out, grad_out, send, near_in, near_out, sems) = refs[:-8], refs[-8:]
-        copies = weight_copies(ids, far_in, far_out, near_in, near_out, sems)
+        copies = weight_copies((1 - ids[1], ids[1]), far_in, far_out, near_in, near_out, sems)
         lay_out(capacity, held, row_out, grad_out)
         for copy in copies[: 3 * PIECES]:
             copy.wait()
@@ -267,29 +267,6 @@
     return call(kernel, "act", shapes, [], keep, core, other, next_keep, next_core)
 
 
-def act_and_load(ids, keep, core, other, w_in, w_out):
-    shape = jax.ShapeDtypeStruct
-    whole = pl.BlockSpec(memory_space=pltpu.VMEM)
-    away = pl.BlockSpec(memory_space=pl.ANY)
-
-    def kernel(ids, keep, core, other, far_in, far_out, out, near_in, near_out, sems):
-        copies = weight_copies(ids, far_in, far_out, near_in, near_out, sems)
-        activated(keep, core, [other], out)
-        for copy in copies:
-            copy.wait()
-
-    return pl.pallas_call(
-        kernel,
-        out_shape=[shape(keep.shape, BF), shape(w_in.shape, BF), shape(w_out.shape, BF)],
-        in_specs=[pl.BlockSpec(memory_space=pltpu.SMEM)] + [whole] * 3 + [away] * 2,
-        out_specs=[whole] * 3,
-        scratch_shapes=[pltpu.SemaphoreType.DMA((6 * PIECES,))],
-        compiler_params=pltpu.CompilerParams(vmem_limit_bytes=VMEM_LIMIT),
-        cost_estimate=COST,
-        name="act",
-    )(ids, keep, core, other, w_in, w_out)
-
-
 def half_rows(half, held, w_in, w_out):
     units = w_out.shape[0]
     width = units // 4
@@ -323,15 +300,14 @@
             outs[i * cuts + j][...] = packed[:, j * cut : (j + 1) * cut]
 
 
-def down_step(ids, own, core, weights, count, capacity, cuts):
+def down_step(ids, own, core, weights, count, capacity):
     def kernel(ids, own, core, w_in, w_out, *outs):
         out_rows, grad_rows = half_rows(ids[1], own, w_in, w_out)
         more_out, more_grad = half_rows(1 - ids[1], core, w_in, w_out)
         pack(capacity, out_rows + more_out, grad_rows + more_grad, outs)
 
-    shape = jax.ShapeDtypeStruct((2 * capacity, weights[1].shape[1] // cuts), BF)
-    outs = call(kernel, "down", [shape] * (count * cuts), [ids], own, core, *weights)
-    return [outs[i * cuts : (i + 1) * cuts] for i in range(count)]
+    shape = jax.ShapeDtypeStruct((2 * capacity, weights[1].shape[1]), BF)
+    return [[x] for x in call(kernel, "down", [shape] * count, [ids], own, core, *weights)]
 
 
 def down_own(ids, own, weights):
@@ -342,13 +318,40 @@
     return call(kernel, "down", [shape] * 2, [ids], own, *weights)
 
 
-def down_other(ids, out_rows, grad_rows, core, weights, count, capacity):
+def down_own_alone(ids, own, w_in, w_out):
+    shape = jax.ShapeDtypeStruct
+    whole = pl.BlockSpec(memory_space=pltpu.VMEM)
+    away = pl.BlockSpec(memory_space=pl.ANY)
+
+    def kernel(ids, own, far_in, far_out, out_rows, grad_rows, near_in, near_out, sems):
+        copies = weight_copies((ids[1], 1 - ids[1]), far_in, far_out, near_in, near_out, sems)
+        for copy in copies[: 3 * PIECES]:
+            copy.wait()
+        out_rows[...], grad_rows[...] = half_rows(ids[1], own, near_in, near_out)
+        for copy in copies[3 * PIECES :]:
+            copy.wait()
+
+    sums = shape((own.shape[0], w_out.shape[1]), F32)
+    return pl.pallas_call(
+        kernel,
+        out_shape=[sums, sums, shape(w_in.shape, BF), shape(w_out.shape, BF)],
+        in_specs=[pl.BlockSpec(memory_space=pltpu.SMEM), whole] + [away] * 2,
+        out_specs=[whole] * 4,
+        scratch_shapes=[pltpu.SemaphoreType.DMA((6 * PIECES,))],
+        compiler_params=pltpu.CompilerParams(vmem_limit_bytes=VMEM_LIMIT),
+        cost_estimate=COST,
+        name="down",
+    )(ids, own, w_in, w_out)
+
+
+def down_other(ids, out_rows, grad_rows, core, weights, count, capacity, cuts=1):
     def kernel(ids, out_rows, grad_rows, core, w_in, w_out, *outs):
         more_out, more_grad = half_rows(1 - ids[1], core, w_in, w_out)
         pack(capacity, out_rows[...] + more_out, grad_rows[...] + more_grad, outs)
 
-    shape = jax.ShapeDtypeStruct((2 * capacity, weights[1].shape[1]), BF)
-    return call(kernel, "down", [shape] * count, [ids], out_rows, grad_rows, core, *weights)
+    shape = jax.ShapeDtypeStruct((2 * capacity, weights[1].shape[1] // cuts), BF)
+    outs = call(kernel, "down", [shape] * (count * cuts), [ids], out_rows, grad_rows, core, *weights)
+    return [outs[i * cuts : (i + 1) * cuts] for i in range(count)]
 
 
 def grads_kernel(count, ids, *refs):
@@ -412,9 +415,10 @@
     )(ids, *arrays)
 
 
-def final_kernel(capacity, sources, cuts, ids, routes, weight, *refs):
-    taken = cuts * len(sources)
-    homes, partial, (mixed, grad_tokens) = refs[:taken], refs[taken:-2], refs[-2:]
+def final_kernel(capacity, sources, parts, ids, routes, weight, *refs):
+    taken, cuts = sum(parts), max(parts)
+    partial, (mixed, grad_tokens) = refs[taken:-2], refs[-2:]
+    homes = [refs[sum(parts[:i]) : sum(parts[: i + 1])] for i in range(len(parts))]
     rows = routes.shape[1]
     me = ids[0]
     count = len(sources)
@@ -443,12 +447,12 @@
         at = slice(j * width, (j + 1) * width)
         total_out, total_grad = (p[:, at] for p in partial) if partial else (None, None)
         for i in range(count):
-            home = homes[i * cuts + j]
+            home = homes[i][j][...] if len(homes[i]) == cuts else homes[i][0][:, at]
             row_key = key[:, i : i + 1]
             pick_out = (row_key == slot).astype(F32).astype(BF)
             pick_grad = (row_key + capacity == slot).astype(F32).astype(BF)
-            out = w_named[:, i : i + 1] * dot(pick_out, home[...])
-            grad = dot(pick_grad, home[...])
+            out = w_named[:, i : i + 1] * dot(pick_out, home)
+            grad = dot(pick_grad, home)
             total_out = out if total_out is None else total_out + out
             total_grad = grad if total_grad is None else total_grad + grad
         mixed[:, at] = total_out.astype(mixed.dtype)
@@ -456,10 +460,10 @@
 
 
 def final(ids, routes, weight, homes, sources, capacity, partial, dtype):
-    cuts = len(homes[0])
-    shape = (routes.shape[0], homes[0][0].shape[1] * cuts)
+    parts = [len(home) for home in homes]
+    shape = (routes.shape[0], homes[0][0].shape[1] * parts[0])
     return call(
-        lambda *refs: final_kernel(capacity, sources, cuts, *refs),
+        lambda *refs: final_kernel(capacity, sources, parts, *refs),
         "final",
         [jax.ShapeDtypeStruct(shape, dtype)] * 2,
         [ids],
@@ -524,13 +528,13 @@
         own = act_step(after(keep, *earlier), core, others)
         return rows, grads, own, beside(own, 1)
 
-    def down_part(group, weights, count, cuts=1):
-        return down_step(ids, *group[2:], weights, count, capacity, cuts)
+    def down_part(group, weights, count):
+        return down_step(ids, *group[2:], weights, count, capacity)
 
     def down_in_halves(group, weights, count):
         _, _, own, core = group
         sums = down_own(ids, own, weights)
-        return [[x] for x in down_other(ids, *sums, after(core, *sums), weights, count, capacity)]
+        return down_other(ids, *sums, after(core, *sums), weights, count, capacity)
 
     def act_both(state, next_state, *earlier):
         rows, grads, keep, core, (other,) = state
@@ -552,10 +556,10 @@
         return group, down_in_halves(group, held, len(blocks)), next_state, before, back
 
     def rest_stage(state):
-        rows, grads, keep, core, (other,) = state
-        own, *weights = act_and_load(ids, keep, core, other, w_in, w_out)
-        group = rows, grads, own, beside(own, 1)
-        return group, down_part(group, weights, size, 2)
+        group = act_part(state)
+        _, _, own, core = group
+        *sums, held_in, held_out = down_own_alone(ids, own, w_in, w_out)
+        return group, down_other(ids, *sums, after(core, *sums), (held_in, held_out), size, capacity, 2)
 
     half, quarter = n_expert // 2, n_expert // 4
     size = quarter // 2
@@ -600,9 +604,9 @@
 
     groups = [group_0, group_far, group_1, group_last, group_2]
     grad_in, grad_out = grads_step(ids, groups, units)
-    partial = add(near[0] + near[1] + far, [], F32)
-    partial = add(near[2], partial, F32)
-    mixed, grad_tokens = add(last, partial, BF)
+    partial = add(near[0] + far, [], F32)
+    partial = add(last, partial, F32)
+    mixed, grad_tokens = add(near[1] + near[2], partial, BF)
     return mixed, grad_tokens, grad_in[None], grad_out[None]
 
 

time: 127 us -> 124 us (0.976)
    pallas_call x22 -> x23, Pallas kernels: 42.1 us -> 41.9 us  [call(): pl.pallas_call(kernel, out_shape=out_shapes, in_specs=[pl.BlockSpec(memor...]
  transfers between devices with their start and end apart: 31 -> 31, of which waited for: 9 -> 10; matrix products, arithmetic and copies ran while one was open for 0% -> 0% of each run, Pallas kernels for 49% -> 50%
where the time goes in v4:
time: 124 us
  Pallas kernels  68 us (55%)
  starting transfers between devices  35.6 us (29%)
  waiting for transfers between devices  18.6 us (15%)
    pallas_call x23, Pallas kernels, call(): pl.pallas_call(kernel, out_shape=out_shapes, in_specs=[pl.BlockSpec(memor...  41.9 us
    ppermute x15, starting transfers between devices, across(): lax.ppermute(x, 'expert', [(i, i ^ s) for i in range(n_expert)])  26.4 us
    pallas_call x3, Pallas kernels, other_half(): pl.pallas_call(kernel, out_shape=[shape((rows, features), BF), shape((row...  11.7 us
    ppermute x16, waiting for transfers between devices, beside(): return lax.ppermute(x, 'dp', [(i, i ^ s) for i in range(n_dp)])  9.46 us
    ppermute x16, starting transfers between devices, beside(): return lax.ppermute(x, 'dp', [(i, i ^ s) for i in range(n_dp)])  9.25 us
    ppermute x15, waiting for transfers between devices, across(): lax.ppermute(x, 'expert', [(i, i ^ s) for i in range(n_expert)])  9.17 us
    pallas_call x1, Pallas kernels, grads_step(): pl.pallas_call(lambda *refs: grads_kernel(len(groups), *refs), out_shape=...  6.7 us
    pallas_call x1, Pallas kernels, down_own_alone(): pl.pallas_call(kernel, out_shape=[sums, sums, shape(w_in.shape, BF), shap...  3.96 us
  transfers between devices with their start and end apart: 31, of which 10 were waited for; matrix products, arithmetic and copies ran while one was open for 0% of the time, Pallas kernels for 50%

profile of v4, /device:TPU:0, one launch (start us, length us, event | category | flops | bytes accessed | tf_op | source)
XLA Modules:
  0.0 123.7 jit_solution(7058065278613223751)
XLA Ops:
  0.7 3.8 %prep.1 = (bf16[120,1024]{1,0:T(8,128)(2,1)S(1)}, bf16[120,1024]{1,0:T(8,128)(2,1)}, bf16[120,1024]{1,0:T(8,128)(2,1)}, bf16[120,1024]{1,0:T(8,128)(2,1)}, bf16[...) custom-call(s32[2]{0:T(128)S(1)} %pad_add_fusion.refs_0_, ...), custom_call_target="tpu_custom_call" | custom-call | flops 1 | bytes 1 | tf_op jit(solution)/shard_map/prep/pallas_call | solution.py:76
  4.5 3.0 %collective-permute-start.15 = (bf16[120,1024]{1,0:T(8,128)(2,1)}, bf16[120,1024]{1,0:T(8,128)(2,1)S(1)}, u32[]{:S(2)}, u32[]{:S(2)}) collective-permute-start(bf16[120,1024]{1,0:T(8,128)(2,1)} %get-tuple-element.249), channel_id=1, source_target_pairs={{0,1},{1,0},{2,3},{3,2},{4,5},{5,4},{6,7},{7,6},{8,9},{9,8},{10,11... | collective-permute-start | bytes 737288 | tf_op jit(solution)/shard_map/ppermute | solution.py:488
  7.5 2.6 %collective-permute-start.12 = (bf16[120,1024]{1,0:T(8,128)(2,1)}, bf16[120,1024]{1,0:T(8,128)(2,1)S(1)}, u32[]{:S(2)}, u32[]{:S(2)}) collective-permute-start(bf16[120,1024]{1,0:T(8,128)(2,1)} %get-tuple-element.245), channel_id=1, source_target_pairs={{0,4},{1,5},{2,6},{3,7},{4,0},{5,1},{6,2},{7,3},{8,12},{9,13},{10,... | collective-permute-start | bytes 737288 | tf_op jit(solution)/shard_map/ppermute | solution.py:488
  10.1 1.9 %collective-permute-start.14 = (bf16[120,1024]{1,0:T(8,128)(2,1)}, bf16[120,1024]{1,0:T(8,128)(2,1)S(1)}, u32[]{:S(2)}, u32[]{:S(2)}) collective-permute-start(bf16[120,1024]{1,0:T(8,128)(2,1)} %get-tuple-element.247), channel_id=1, source_target_pairs={{0,2},{1,3},{2,0},{3,1},{4,6},{5,7},{6,4},{7,5},{8,10},{9,11},{10,... | collective-permute-start | bytes 737288 | tf_op jit(solution)/shard_map/ppermute | solution.py:488
  12.0 1.7 %collective-permute-done.15 = bf16[120,1024]{1,0:T(8,128)(2,1)S(1)} collective-permute-done((bf16[120,1024]{1,0:T(8,128)(2,1)}, bf16[120,1024]{1,0:T(8,128)(2,1)S(1)}, u32[]{:S(2)}, u32[]{:S(2)}) %collective-permute-start.15) | collective-permute-done | bytes 245792 | tf_op jit(solution)/shard_map/ppermute | solution.py:488
  13.7 8.5 %conditional.4 = (bf16[128,1024]{1,0:T(8,128)(2,1)}, bf16[128,1024]{1,0:T(8,128)(2,1)}, f32[128,1536]{1,0:T(8,128)}, bf16[128,1536]{1,0:T(8,128)(2,1)}, bf16[128...) conditional(s32[]{:T(128)} %convert_element_type.2, () %tuple.67, (s32[2]{0:T(128)S(1)}, ...), branch_computations={%region_0.1_spmd, %region_1.2_spmd} | conditional | flops 3 | bytes 2097214 | solution.py:503
  13.7 4.4 %up.8 = (bf16[128,1024]{1,0:T(8,128)(2,1)}, bf16[128,1024]{1,0:T(8,128)(2,1)}, bf16[128,1536]{1,0:T(8,128)(2,1)S(1)}, bf16[1024,2048]{1,0:T(8,128)(2,1)S(1)}, bf16[1024,1024]{1,0:T(8,128)(2,1)S(1)}) custom-call(s32[2]{0:T(128)S(1)} %get-tuple-element.72.ids, bf16[120,1024]{1,0:T(8,128)(2,1)S(1)} %get-tuple-element.73.refs_0_, ...), custom_call_target="tpu_custom_call" | custom-call | flops 1 | bytes 1 | tf_op jit(solution)/shard_map/cond/branch_1_fun/up/pallas_call | solution.py:170
  18.2 2.7 %up.9.keep = f32[128,1536]{1,0:T(8,128)} custom-call(s32[2]{0:T(128)S(1)} %get-tuple-element.72.ids, bf16[128,1024]{1,0:T(8,128)(2,1)} %get-tuple-element.80.rows, bf16[128,1024]{1,0:T(8,128)(2,1)} %get-tuple-element.322.grads, bf16[1024,2048]{1,0:T(8,128)(2,1)S(1)} %get-tuple-element.81.w_in, bf16[1024,1024]{1,0:T(8,128)(2,1)S(1)} %get-tuple-element.82.w_out), custom_call_target="tpu_custom_call" | custom-call | flops 1 | bytes 1 | tf_op jit(solution)/shard_map/cond/branch_1_fun/up/pallas_call | solution.py:92
  20.9 1.3 %total.3 = (bf16[128,768]{1,0:T(8,128)(2,1)S(1)}, bf16[128,768]{1,0:T(8,128)(2,1)S(1)}) custom-call(f32[128,1536]{1,0:T(8,128)} %up.9.keep, bf16[128,1536]{1,0:T(8,128)(2,1)} %collective-permute-done.core), custom_call_target="tpu_custom_call" | custom-call | flops 1 | bytes 1 | tf_op jit(solution)/shard_map/cond/branch_1_fun/total/pallas_call | solution.py:92
  22.2 1.8 %collective-permute-start.17 = (bf16[128,768]{1,0:T(8,128)(2,1)S(1)}, bf16[128,768]{1,0:T(8,128)(2,1)S(1)}, u32[]{:S(2)}, u32[]{:S(2)}) collective-permute-start(bf16[128,768]{1,0:T(8,128)(2,1)S(1)} %get-tuple-element.250), channel_id=1, source_target_pairs={{0,16},{8,24},{16,0},{24,8},{1,17},{9,25},{17,1},{25,9},{2,18},{10... | collective-permute-start | bytes 589832 | tf_op jit(solution)/shard_map/ppermute | solution.py:491
  24.3 3.4 %collective-permute-done.12 = bf16[120,1024]{1,0:T(8,128)(2,1)S(1)} collective-permute-done((bf16[120,1024]{1,0:T(8,128)(2,1)}, bf16[120,1024]{1,0:T(8,128)(2,1)S(1)}, u32[]{:S(2)}, u32[]{:S(2)}) %collective-permute-start.12) | collective-permute-done | bytes 245792 | tf_op jit(solution)/shard_map/ppermute | solution.py:488
  27.8 4.0 %collective-permute-done.13 = bf16[120,1024]{1,0:T(8,128)(2,1)S(1)} collective-permute-done((bf16[120,1024]{1,0:T(8,128)(2,1)}, bf16[120,1024]{1,0:T(8,128)(2,1)S(1)}, u32[]{:S(2)}, u32[]{:S(2)}) %collective-permute-start.13) | collective-permute-done | bytes 245792 | tf_op jit(solution)/shard_map/ppermute | solution.py:488
  31.8 3.5 %collective-permute-start.16 = (bf16[120,1024]{1,0:T(8,128)(2,1)}, bf16[120,1024]{1,0:T(8,128)(2,1)S(1)}, u32[]{:S(2)}, u32[]{:S(2)}) collective-permute-start(bf16[120,1024]{1,0:T(8,128)(2,1)} %get-tuple-element.252), channel_id=1, source_target_pairs={{0,6},{1,7},{2,4},{3,5},{4,2},{5,3},{6,0},{7,1},{8,14},{9,15},{10,... | collective-permute-start | bytes 737288 | tf_op jit(solution)/shard_map/ppermute | solution.py:488
  35.3 1.3 %collective-permute-start.19 = (bf16[120,1024]{1,0:T(8,128)(2,1)}, bf16[120,1024]{1,0:T(8,128)(2,1)S(1)}, u32[]{:S(2)}, u32[]{:S(2)}) collective-permute-start(bf16[120,1024]{1,0:T(8,128)(2,1)} %get-tuple-element.260), channel_id=1, source_target_pairs={{0,7},{1,6},{2,5},{3,4},{4,3},{5,2},{6,1},{7,0},{8,15},{9,14},{10,... | collective-permute-start | bytes 737288 | tf_op jit(solution)/shard_map/ppermute | solution.py:488
  36.6 24.9 %conditional.5 = (bf16[128,1024]{1,0:T(8,128)(2,1)S(1)}, bf16[128,1024]{1,0:T(8,128)(2,1)S(1)}, bf16[128,1536]{1,0:T(8,128)(2,1)}, bf16[128,1536]{1,0:T(8,128)(2...) conditional(s32[]{:T(128)} %convert_element_type.2, () %tuple.70, ...), branch_computations={%region_2.3_spmd, %region_3.4_spmd} | conditional | flops 9 | bytes 22282920 | solution.py:503
  36.6 3.6 %up.10 = (bf16[128,1024]{1,0:T(8,128)(2,1)S(1)}, bf16[128,1024]{1,0:T(8,128)(2,1)S(1)}, bf16[128,1536]{1,0:T(8,128)(2,1)S(1)}, bf16[1024,2048]{1,0:T(8,128)(2,1)S(1)}, bf16[1024,1024]{1,0:T(8,128)(2,1)S(1)}) custom-call(s32[2]{0:T(128)S(1)} %get-tuple-element.85.ids, bf16[120,1024]{1,0:T(8,128)(2,1)S(1)} %get-tuple-element.86.refs_0_, ...), custom_call_target="tpu_custom_call" | custom-call | flops 1 | bytes 1 | tf_op jit(solution)/shard_map/cond/branch_1_fun/up/pallas_call | solution.py:170
  40.4 1.3 %up.11.keep = f32[128,1536]{1,0:T(8,128)S(1)} custom-call(s32[2]{0:T(128)S(1)} %get-tuple-element.85.ids, bf16[128,1024]{1,0:T(8,128)(2,1)S(1)} %get-tuple-element.93.rows, bf16[128,1024]{1,0:T(8,128)(2,1)S(1)} %get-tuple-element.345.grads, bf16[1024,2048]{1,0:T(8,128)(2,1)S(1)} %get-tuple-element.94.w_in.refs_1_, ...), custom_call_target="tpu_custom_call" | custom-call | flops 1 | bytes 1 | tf_op jit(solution)/shard_map/cond/branch_1_fun/up/pallas_call | solution.py:92
  42.2 1.5 %act.5.own = bf16[128,1536]{1,0:T(8,128)(2,1)S(1)} custom-call(f32[128,1536]{1,0:T(8,128)} %get-tuple-element.97.keep, bf16[128,1536]{1,0:T(8,128)(2,1)} %get-tuple-element.98.core, bf16[128,768]{1,0:T(8,128)(2,1)S(1)} %get-tuple-element.99.refs_0_, bf16[128,768]{1,0:T(8,128)(2,1)S(1)} %get-tuple-element.100.refs_1_), custom_call_target="tpu_custom_call" | custom-call | flops 1 | bytes 1 | tf_op jit(solution)/shard_map/cond/branch_1_fun/act/pallas_call | solution.py:92
  43.8 1.5 %collective-permute-start.3 = (bf16[128,1536]{1,0:T(8,128)(2,1)S(1)}, bf16[128,1536]{1,0:T(8,128)(2,1)S(1)}, u32[]{:S(2)}, u32[]{:S(2)}) collective-permute-start(bf16[128,1536]{1,0:T(8,128)(2,1)S(1)} %total.4), channel_id=1, source_target_pairs={{0,16},{8,24},{16,0},{24,8},{1,17},{9,25},{17,1},{25,9},{2,18},{10... | collective-permute-start | bytes 1179656 | tf_op jit(solution)/shard_map/cond/branch_1_fun/ppermute | solution.py:491
  45.4 2.1 %up.12 = (bf16[64,1024]{1,0:T(8,128)(2,1)S(1)}, bf16[64,1024]{1,0:T(8,128)(2,1)S(1)}, bf16[64,1536]{1,0:T(8,128)(2,1)S(1)}, f32[64,1536]{1,0:T(8,128)S(1)}) custom-call(s32[2]{0:T(128)S(1)} %get-tuple-element.85.ids, bf16[120,1024]{1,0:T(8,128)(2,1)S(1)} %get-tuple-element.102.refs_0_, bf16[1024,2048]{1,0:T(8,128)(2,1)S(1)} %get-tuple-element.94.w_in.refs_1_, ...), custom_call_target="tpu_custom_call" | custom-call | flops 1 | bytes 1 | tf_op jit(solution)/shard_map/cond/branch_1_fun/up/pallas_call | solution.py:92
  47.5 3.4 %down.8 = (bf16[120,1024]{1,0:T(8,128)(2,1)}, bf16[120,1024]{1,0:T(8,128)(2,1)}) custom-call(s32[2]{0:T(128)S(1)} %get-tuple-element.85.ids, bf16[128,1536]{1,0:T(8,128)(2,1)S(1)} %act.5.own, bf16[128,1536]{1,0:T(8,128)(2,1)S(1)} %collective-permute-done.2.core, bf16[1024,2048]{1,0:T(8,128)(2,1)S(1)} %get-tuple-element.94.w_in.refs_1_, ...), custom_call_target="tpu_custom_call" | custom-call | flops 1 | bytes 1 | tf_op jit(solution)/shard_map/cond/branch_1_fun/down/pallas_call | solution.py:92
  51.0 4.2 %collective-permute-done.3.other = bf16[128,1536]{1,0:T(8,128)(2,1)S(1)} collective-permute-done((bf16[128,1536]{1,0:T(8,128)(2,1)S(1)}, bf16[128,1536]{1,0:T(8,128)(2,1)S(1)}, u32[]{:S(2)}, u32[]{:S(2)}) %collective-permute-start.3) | collective-permute-done | bytes 393248 | tf_op jit(solution)/shard_map/cond/branch_1_fun/ppermute | solution.py:491
  55.2 1.0 act.6
  56.2 2.0 %down.9 = (f32[128,1024]{1,0:T(8,128)S(1)}, f32[128,1024]{1,0:T(8,128)S(1)}) custom-call(s32[2]{0:T(128)S(1)} %get-tuple-element.85.ids, bf16[128,1536]{1,0:T(8,128)(2,1)} %get-tuple-element.346.own, bf16[1024,2048]{1,0:T(8,128)(2,1)S(1)} %get-tuple-element.94.w_in.refs_1_, bf16[1024,1024]{1,0:T(8,128)(2,1)S(1)} %get-tuple-element.95.w_out.refs_2_), custom_call_target="tpu_custom_call" | custom-call | flops 1 | bytes 1 | tf_op jit(solution)/shard_map/cond/branch_1_fun/down/pallas_call | solution.py:92
  58.3 3.2 %down.10 = (bf16[120,1024]{1,0:T(8,128)(2,1)}, bf16[120,1024]{1,0:T(8,128)(2,1)}) custom-call(s32[2]{0:T(128)S(1)} %get-tuple-element.85.ids, f32[128,1024]{1,0:T(8,128)S(1)} %get-tuple-element.111.out_rows, f32[128,1024]{1,0:T(8,128)S(1)} %get-tuple-element.112.grad_rows, bf16[128,1536]{1,0:T(8,128)(2,1)} %collective-permute-done.5.core, ...), custom_call_target="tpu_custom_call" | custom-call | flops 1 | bytes 1 | tf_op jit(solution)/shard_map/cond/branch_1_fun/down/pallas_call | solution.py:92
  61.6 1.6 %collective-permute-start.20 = (bf16[64,1536]{1,0:T(8,128)(2,1)S(1)}, bf16[64,1536]{1,0:T(8,128)(2,1)S(1)}, u32[]{:S(2)}, u32[]{:S(2)}) collective-permute-start(bf16[64,1536]{1,0:T(8,128)(2,1)S(1)} %get-tuple-element.263), channel_id=1, source_target_pairs={{0,16},{8,24},{16,0},{24,8},{1,17},{9,25},{17,1},{25,9},{2,18},{10... | collective-permute-start | bytes 589832 | tf_op jit(solution)/shard_map/ppermute | solution.py:491
  63.6 4.9 %collective-permute-start.27 = (bf16[120,1024]{1,0:T(8,128)(2,1)}, bf16[120,1024]{1,0:T(8,128)(2,1)S(1)}, u32[]{:S(2)}, u32[]{:S(2)}) collective-permute-start(bf16[120,1024]{1,0:T(8,128)(2,1)} %get-tuple-element.280), channel_id=1, source_target_pairs={{0,5},{1,4},{2,7},{3,6},{4,1},{5,0},{6,3},{7,2},{8,13},{9,12},{10,... | collective-permute-start | bytes 737288 | tf_op jit(solution)/shard_map/ppermute | solution.py:488
  68.9 23.7 %conditional.6 = (bf16[128,1024]{1,0:T(8,128)(2,1)S(1)}, bf16[128,1024]{1,0:T(8,128)(2,1)}, bf16[128,1536]{1,0:T(8,128)(2,1)}, bf16[128,1536]{1,0:T(8,128)(2,1)}...) conditional(s32[]{:T(128)} %convert_element_type.2, () %tuple.66, ...), branch_computations={%region_4.5_spmd, %region_5.6_spmd} | conditional | flops 9 | bytes 15729229 | solution.py:503
  68.9 3.6 %up.13 = (bf16[128,1024]{1,0:T(8,128)(2,1)S(1)}, bf16[128,1024]{1,0:T(8,128)(2,1)S(1)}, bf16[128,1536]{1,0:T(8,128)(2,1)S(1)}, bf16[1024,2048]{1,0:T(8,128)(2,1)S(1)}, bf16[1024,1024]{1,0:T(8,128)(2,1)S(1)}) custom-call(s32[2]{0:T(128)S(1)} %get-tuple-element.121.ids, bf16[120,1024]{1,0:T(8,128)(2,1)S(1)} %get-tuple-element.122.refs_0_, ...), custom_call_target="tpu_custom_call" | custom-call | flops 1 | bytes 1 | tf_op jit(solution)/shard_map/cond/branch_1_fun/up/pallas_call | solution.py:170
  72.8 1.3 %up.14.keep = f32[128,1536]{1,0:T(8,128)S(1)} custom-call(s32[2]{0:T(128)S(1)} %get-tuple-element.121.ids, bf16[128,1024]{1,0:T(8,128)(2,1)S(1)} %get-tuple-element.129.rows, bf16[128,1024]{1,0:T(8,128)(2,1)S(1)} %get-tuple-element.378.grads, bf16[1024,2048]{1,0:T(8,128)(2,1)S(1)} %get-tuple-element.130.w_in.refs_1_, ...), custom_call_target="tpu_custom_call" | custom-call | flops 1 | bytes 1 | tf_op jit(solution)/shard_map/cond/branch_1_fun/up/pallas_call | solution.py:92
  75.0 1.5 %collective-permute-start.8 = (bf16[128,1536]{1,0:T(8,128)(2,1)S(1)}, bf16[128,1536]{1,0:T(8,128)(2,1)S(1)}, u32[]{:S(2)}, u32[]{:S(2)}) collective-permute-start(bf16[128,1536]{1,0:T(8,128)(2,1)S(1)} %total.5), channel_id=1, source_target_pairs={{0,16},{8,24},{16,0},{24,8},{1,17},{9,25},{17,1},{25,9},{2,18},{10... | collective-permute-start | bytes 1179656 | tf_op jit(solution)/shard_map/cond/branch_1_fun/ppermute | solution.py:491
  76.5 2.5 %up.15 = (bf16[64,1024]{1,0:T(8,128)(2,1)S(1)}, bf16[64,1024]{1,0:T(8,128)(2,1)S(1)}, bf16[64,1536]{1,0:T(8,128)(2,1)S(1)}, f32[64,1536]{1,0:T(8,128)S(1)}) custom-call(s32[2]{0:T(128)S(1)} %get-tuple-element.121.ids, bf16[120,1024]{1,0:T(8,128)(2,1)} %get-tuple-element.137.refs_0_, bf16[1024,2048]{1,0:T(8,128)(2,1)S(1)} %get-tuple-element.130.w_in.refs_1_, ...), custom_call_target="tpu_custom_call" | custom-call | flops 1 | bytes 1 | tf_op jit(solution)/shard_map/cond/branch_1_fun/up/pallas_call | solution.py:92
  79.1 3.3 %down.11 = bf16[120,1024]{1,0:T(8,128)(2,1)} custom-call(s32[2]{0:T(128)S(1)} %get-tuple-element.121.ids, bf16[64,1536]{1,0:T(8,128)(2,1)S(1)} %act.7.own, bf16[64,1536]{1,0:T(8,128)(2,1)S(1)} %collective-permute-done.7.core, bf16[1024,2048]{1,0:T(8,128)(2,1)S(1)} %get-tuple-element.130.w_in.refs_1_, bf16[1024,1024]{1,0:T(8,128)(2,1)S(1)} %get-tuple-element.131.w_out.refs_2_), custom_call_target="tpu_custom_call" | custom-call | flops 1 | bytes 1 | tf_op jit(solution)/shard_map/cond/branch_1_fun/down/pallas_call | solution.py:92
  82.4 1.4 %collective-permute-done.9.next_core = bf16[64,1536]{1,0:T(8,128)(2,1)S(1)} collective-permute-done((bf16[64,1536]{1,0:T(8,128)(2,1)S(1)}, bf16[64,1536]{1,0:T(8,128)(2,1)S(1)}, u32[]{:S(2)}, u32[]{:S(2)}) %collective-permute-start.9) | collective-permute-done | bytes 196640 | tf_op jit(solution)/shard_map/cond/branch_1_fun/ppermute | solution.py:491
  83.8 2.6 %collective-permute-done.8.other = bf16[128,1536]{1,0:T(8,128)(2,1)S(1)} collective-permute-done((bf16[128,1536]{1,0:T(8,128)(2,1)S(1)}, bf16[128,1536]{1,0:T(8,128)(2,1)S(1)}, u32[]{:S(2)}, u32[]{:S(2)}) %collective-permute-start.8) | collective-permute-done | bytes 393248 | tf_op jit(solution)/shard_map/cond/branch_1_fun/ppermute | solution.py:491
  87.4 2.0 %down.12 = (f32[128,1024]{1,0:T(8,128)S(1)}, f32[128,1024]{1,0:T(8,128)S(1)}) custom-call(s32[2]{0:T(128)S(1)} %get-tuple-element.121.ids, bf16[128,1536]{1,0:T(8,128)(2,1)} %get-tuple-element.379.own, bf16[1024,2048]{1,0:T(8,128)(2,1)S(1)} %get-tuple-element.130.w_in.refs_1_, bf16[1024,1024]{1,0:T(8,128)(2,1)S(1)} %get-tuple-element.131.w_out.refs_2_), custom_call_target="tpu_custom_call" | custom-call | flops 1 | bytes 1 | tf_op jit(solution)/shard_map/cond/branch_1_fun/down/pallas_call | solution.py:92
  89.5 3.1 %down.13 = (bf16[120,1024]{1,0:T(8,128)(2,1)}, bf16[120,1024]{1,0:T(8,128)(2,1)}) custom-call(s32[2]{0:T(128)S(1)} %get-tuple-element.121.ids, f32[128,1024]{1,0:T(8,128)S(1)} %get-tuple-element.144.out_rows, f32[128,1024]{1,0:T(8,128)S(1)} %get-tuple-element.145.grad_rows, bf16[128,1536]{1,0:T(8,128)(2,1)} %collective-permute-done.10.core, ...), custom_call_target="tpu_custom_call" | custom-call | flops 1 | bytes 1 | tf_op jit(solution)/shard_map/cond/branch_1_fun/down/pallas_call | solution.py:92
  92.6 1.6 %collective-permute-start.23 = (bf16[64,1536]{1,0:T(8,128)(2,1)S(1)}, bf16[64,1536]{1,0:T(8,128)(2,1)S(1)}, u32[]{:S(2)}, u32[]{:S(2)}) collective-permute-start(bf16[64,1536]{1,0:T(8,128)(2,1)S(1)} %get-tuple-element.271), channel_id=1, source_target_pairs={{0,16},{8,24},{16,0},{24,8},{1,17},{9,25},{17,1},{25,9},{2,18},{10... | collective-permute-start | bytes 589832 | tf_op jit(solution)/shard_map/ppermute | solution.py:491
  94.2 3.5 %collective-permute-start.30 = (bf16[120,1024]{1,0:T(8,128)(2,1)}, bf16[120,1024]{1,0:T(8,128)(2,1)S(1)}, u32[]{:S(2)}, u32[]{:S(2)}) collective-permute-start(bf16[120,1024]{1,0:T(8,128)(2,1)} %get-tuple-element.287), channel_id=1, source_target_pairs={{0,7},{1,6},{2,5},{3,4},{4,3},{5,2},{6,1},{7,0},{8,15},{9,14},{10,... | collective-permute-start | bytes 737288 | tf_op jit(solution)/shard_map/ppermute | solution.py:488
  98.1 1.7 %collective-permute-start.22 = (bf16[120,1024]{1,0:T(8,128)(2,1)}, bf16[120,1024]{1,0:T(8,128)(2,1)S(1)}, u32[]{:S(2)}, u32[]{:S(2)}) collective-permute-start(bf16[120,1024]{1,0:T(8,128)(2,1)} %get-tuple-element.268), channel_id=1, source_target_pairs={{0,2},{1,3},{2,0},{3,1},{4,6},{5,7},{6,4},{7,5},{8,10},{9,11},{10,... | collective-permute-start | bytes 737288 | tf_op jit(solution)/shard_map/ppermute | solution.py:488
  100.0 7.6 %conditional.7 = (bf16[64,1024]{1,0:T(8,128)(2,1)S(1)}, bf16[64,1024]{1,0:T(8,128)(2,1)S(1)}, bf16[64,1536]{1,0:T(8,128)(2,1)}, bf16[64,1536]{1,0:T(8,128)(2,1)}...) conditional(s32[]{:T(128)} %convert_element_type.2, () %tuple.76, (f32[64,1536]{1,0:T(8,128)S(1)}, ...), branch_computations={%region_6.7_spmd, %region_7.8_spmd} | conditional | flops 3 | bytes 901180 | solution.py:503
  100.8 4.0 %down.14 = (f32[64,1024]{1,0:T(8,128)S(1)}, f32[64,1024]{1,0:T(8,128)S(1)}, bf16[1024,2048]{1,0:T(8,128)(2,1)S(1)}, bf16[1024,1024]{1,0:T(8,128)(2,1)S(1)}) custom-call(s32[2]{0:T(128)S(1)} %get-tuple-element.159.ids, bf16[64,1536]{1,0:T(8,128)(2,1)} %act.9.own, bf16[1024,2048]{1,0:T(8,128)(2,1)} %get-tuple-element.160.far_in, ...), custom_call_target="tpu_custom_call" | custom-call | flops 1 | bytes 1 | tf_op jit(solution)/shard_map/cond/branch_1_fun/down/pallas_call | solution.py:335
  104.8 2.8 %down.15 = (bf16[120,512]{1,0:T(8,128)(2,1)}, bf16[120,512]{1,0:T(8,128)(2,1)}) custom-call(s32[2]{0:T(128)S(1)} %get-tuple-element.159.ids, f32[64,1024]{1,0:T(8,128)S(1)} %get-tuple-element.162.out_rows, f32[64,1024]{1,0:T(8,128)S(1)} %get-tuple-element.163.grad_rows, bf16[64,1536]{1,0:T(8,128)(2,1)} %collective-permute-done.11.core, ...), custom_call_target="tpu_custom_call" | custom-call | flops 1 | bytes 1 | tf_op jit(solution)/shard_map/cond/branch_1_fun/down/pallas_call | solution.py:92
  107.6 2.9 %collective-permute-start.24 = (bf16[120,512]{1,0:T(8,128)(2,1)}, bf16[120,512]{1,0:T(8,128)(2,1)S(1)}, u32[]{:S(2)}, u32[]{:S(2)}) collective-permute-start(bf16[120,512]{1,0:T(8,128)(2,1)} %get-tuple-element.274), channel_id=1, source_target_pairs={{0,3},{1,2},{2,1},{3,0},{4,7},{5,6},{6,5},{7,4},{8,11},{9,10},{10,... | collective-permute-start | bytes 368648 | tf_op jit(solution)/shard_map/ppermute | solution.py:488
  110.6 2.4 %final.3 = (f32[192,1024]{1,0:T(8,128)S(1)}, f32[192,1024]{1,0:T(8,128)S(1)}) custom-call(s32[2]{0:T(128)S(1)} %pad_add_fusion.refs_0_, s32[2,192]{1,0:T(2,128)S(1)} %bitcast.9, f32[2,192]{1,0:T(2,128)S(1)} %bitcast.13, bf16[120,1024]{1,0:T(8,128)(2,1)} %get-tuple-element.282.refs_3_, bf16[120,1024]{1,0:T(8,128)(2,1)S(1)} %collective-permute-done.28.refs_4_, ...), custom_call_target="tpu_custom_call" | custom-call | flops 1 | bytes 1 | tf_op jit(solution)/shard_map/final/pallas_call | solution.py:92
  113.0 6.7 %grads.1 = (bf16[1024,2048]{1,0:T(8,128)(2,1)}, bf16[1024,1024]{1,0:T(8,128)(2,1)}) custom-call(s32[2]{0:T(128)S(1)} %pad_add_fusion.refs_0_, bf16[128,1024]{1,0:T(8,128)(2,1)} %get-tuple-element.294.refs_1_, bf16[128,1024]{1,0:T(8,128)(2,1)} %get-tuple-element.295.refs_2_, bf16[128,1536]{1,0:T(8,128)(2,1)S(1)} %get-tuple-element.296.refs_3_, ...), custom_call_target="tpu_custom_call" | custom-call | flops 1 | bytes 1 | tf_op jit(solution)/shard_map/grads/pallas_call | solution.py:395
  119.7 1.5 %final.4 = (f32[192,1024]{1,0:T(8,128)S(1)}, f32[192,1024]{1,0:T(8,128)S(1)}) custom-call(s32[2]{0:T(128)S(1)} %pad_add_fusion.refs_0_, s32[2,192]{1,0:T(2,128)S(1)} %bitcast.10, f32[2,192]{1,0:T(2,128)S(1)} %bitcast.14, bf16[120,1024]{1,0:T(8,128)(2,1)S(1)} %collective-permute-done.29.refs_3_, bf16[120,1024]{1,0:T(8,128)(2,1)S(1)} %collective-permute-done.30.refs_4_, ...), custom_call_target="tpu_custom_call" | custom-call | flops 1 | bytes 1 | tf_op jit(solution)/shard_map/final/pallas_call | solution.py:92
  121.3 2.4 %final.5 = (bf16[192,1024]{1,0:T(8,128)(2,1)}, bf16[192,1024]{1,0:T(8,128)(2,1)}) custom-call(s32[2]{0:T(128)S(1)} %pad_add_fusion.refs_0_, s32[2,192]{1,0:T(2,128)S(1)} %bitcast.11, f32[2,192]{1,0:T(2,128)S(1)} %bitcast.15, bf16[120,1024]{1,0:T(8,128)(2,1)S(1)} %collective-permute-done.22.refs_3_, bf16[120,512]{1,0:T(8,128)(2,1)S(1)} %collective-permute-done.24.refs_4_, ...), custom_call_target="tpu_custom_call" | custom-call | flops 1 | bytes 1 | tf_op jit(solution)/shard_map/final/pallas_call | solution.py:92
  (102 shorter events, 5.9 us)
Async XLA Ops:
  4.5 9.2 %collective-permute-start.15 = (bf16[120,1024]{1,0:T(8,128)(2,1)}, bf16[120,1024]{1,0:T(8,128)(2,1)S(1)}, u32[]{:S(2)}, u32[]{:S(2)}) collective-permute-start(bf16[120,1024]{1,0:T(8,128)(2,1)} %get-tuple-element.249), channel_id=1, source_target_pairs={{0,1},{1,0},{2,3},{3,2},{4,5},{5,4},{6,7},{7,6},{8,9},{9,8},{10,11... | collective-permute-start | bytes 737288 | tf_op jit(solution)/shard_map/ppermute | solution.py:488
  7.5 20.2 %collective-permute-start.12 = (bf16[120,1024]{1,0:T(8,128)(2,1)}, bf16[120,1024]{1,0:T(8,128)(2,1)S(1)}, u32[]{:S(2)}, u32[]{:S(2)}) collective-permute-start(bf16[120,1024]{1,0:T(8,128)(2,1)} %get-tuple-element.245), channel_id=1, source_target_pairs={{0,4},{1,5},{2,6},{3,7},{4,0},{5,1},{6,2},{7,3},{8,12},{9,13},{10,... | collective-permute-start | bytes 737288 | tf_op jit(solution)/shard_map/ppermute | solution.py:488
  10.1 21.6 %collective-permute-start.13 = (bf16[120,1024]{1,0:T(8,128)(2,1)}, bf16[120,1024]{1,0:T(8,128)(2,1)S(1)}, u32[]{:S(2)}, u32[]{:S(2)}) collective-permute-start(bf16[120,1024]{1,0:T(8,128)(2,1)} %get-tuple-element.246), channel_id=1, source_target_pairs={{0,5},{1,4},{2,7},{3,6},{4,1},{5,0},{6,3},{7,2},{8,13},{9,12},{10,... | collective-permute-start | bytes 737288 | tf_op jit(solution)/shard_map/ppermute | solution.py:488
  10.1 21.6 %collective-permute-start.14 = (bf16[120,1024]{1,0:T(8,128)(2,1)}, bf16[120,1024]{1,0:T(8,128)(2,1)S(1)}, u32[]{:S(2)}, u32[]{:S(2)}) collective-permute-start(bf16[120,1024]{1,0:T(8,128)(2,1)} %get-tuple-element.247), channel_id=1, source_target_pairs={{0,2},{1,3},{2,0},{3,1},{4,6},{5,7},{6,4},{7,5},{8,10},{9,11},{10,... | collective-permute-start | bytes 737288 | tf_op jit(solution)/shard_map/ppermute | solution.py:488
  18.1 2.8 %collective-permute-start = (bf16[128,1536]{1,0:T(8,128)(2,1)S(1)}, bf16[128,1536]{1,0:T(8,128)(2,1)}, u32[]{:S(2)}, u32[]{:S(2)}) collective-permute-start(bf16[128,1536]{1,0:T(8,128)(2,1)S(1)} %get-tuple-element.79), channel_id=1, source_target_pairs={{0,8},{8,0},{16,24},{24,16},{1,9},{9,1},{17,25},{25,17},{2,10},{10... | collective-permute-start | bytes 1179656 | tf_op jit(solution)/shard_map/cond/branch_1_fun/ppermute | solution.py:491
  22.2 14.4 %collective-permute-start.17 = (bf16[128,768]{1,0:T(8,128)(2,1)S(1)}, bf16[128,768]{1,0:T(8,128)(2,1)S(1)}, u32[]{:S(2)}, u32[]{:S(2)}) collective-permute-start(bf16[128,768]{1,0:T(8,128)(2,1)S(1)} %get-tuple-element.250), channel_id=1, source_target_pairs={{0,16},{8,24},{16,0},{24,8},{1,17},{9,25},{17,1},{25,9},{2,18},{10... | collective-permute-start | bytes 589832 | tf_op jit(solution)/shard_map/ppermute | solution.py:491
  24.0 12.6 %collective-permute-start.18 = (bf16[128,768]{1,0:T(8,128)(2,1)S(1)}, bf16[128,768]{1,0:T(8,128)(2,1)S(1)}, u32[]{:S(2)}, u32[]{:S(2)}) collective-permute-start(bf16[128,768]{1,0:T(8,128)(2,1)S(1)} %get-tuple-element.251), channel_id=1, source_target_pairs={{0,16},{8,24},{16,0},{24,8},{1,17},{9,25},{17,1},{25,9},{2,18},{10... | collective-permute-start | bytes 589832 | tf_op jit(solution)/shard_map/ppermute | solution.py:491
  31.8 31.4 %collective-permute-start.16 = (bf16[120,1024]{1,0:T(8,128)(2,1)}, bf16[120,1024]{1,0:T(8,128)(2,1)S(1)}, u32[]{:S(2)}, u32[]{:S(2)}) collective-permute-start(bf16[120,1024]{1,0:T(8,128)(2,1)} %get-tuple-element.252), channel_id=1, source_target_pairs={{0,6},{1,7},{2,4},{3,5},{4,2},{5,3},{6,0},{7,1},{8,14},{9,15},{10,... | collective-permute-start | bytes 737288 | tf_op jit(solution)/shard_map/ppermute | solution.py:488
  35.3 27.8 %collective-permute-start.19 = (bf16[120,1024]{1,0:T(8,128)(2,1)}, bf16[120,1024]{1,0:T(8,128)(2,1)S(1)}, u32[]{:S(2)}, u32[]{:S(2)}) collective-permute-start(bf16[120,1024]{1,0:T(8,128)(2,1)} %get-tuple-element.260), channel_id=1, source_target_pairs={{0,7},{1,6},{2,5},{3,4},{4,3},{5,2},{6,1},{7,0},{8,15},{9,14},{10,... | collective-permute-start | bytes 737288 | tf_op jit(solution)/shard_map/ppermute | solution.py:488
  36.6 32.0 %collective-permute-start.21 = (bf16[120,1024]{1,0:T(8,128)(2,1)}, bf16[120,1024]{1,0:T(8,128)(2,1)}, u32[]{:S(2)}, u32[]{:S(2)}) collective-permute-start(bf16[120,1024]{1,0:T(8,128)(2,1)} %get-tuple-element.265), channel_id=1, source_target_pairs={{0,3},{1,2},{2,1},{3,0},{4,7},{5,6},{6,5},{7,4},{8,11},{9,10},{10,... | collective-permute-start | bytes 737288 | tf_op jit(solution)/shard_map/ppermute | solution.py:488
  40.3 1.8 %collective-permute-start.1 = (bf16[128,1536]{1,0:T(8,128)(2,1)S(1)}, bf16[128,1536]{1,0:T(8,128)(2,1)S(1)}, u32[]{:S(2)}, u32[]{:S(2)}) collective-permute-start(bf16[128,1536]{1,0:T(8,128)(2,1)S(1)} %get-tuple-element.92), channel_id=1, source_target_pairs={{0,8},{8,0},{16,24},{24,16},{1,9},{9,1},{17,25},{25,17},{2,10},{10... | collective-permute-start | bytes 1179656 | tf_op jit(solution)/shard_map/cond/branch_1_fun/ppermute | solution.py:491
  43.6 7.3 %copy-start.2 = (bf16[128,1536]{1,0:T(8,128)(2,1)}, bf16[128,1536]{1,0:T(8,128)(2,1)S(1)}, u32[]{:S(2)}) copy-start(bf16[128,1536]{1,0:T(8,128)(2,1)S(1)} %act.5.own) | copy-start | bytes 1179652 | tf_op jit(solution)/shard_map/cond
  43.6 3.9 %collective-permute-start.2 = (bf16[128,1536]{1,0:T(8,128)(2,1)S(1)}, bf16[128,1536]{1,0:T(8,128)(2,1)S(1)}, u32[]{:S(2)}, u32[]{:S(2)}) collective-permute-start(bf16[128,1536]{1,0:T(8,128)(2,1)S(1)} %act.5.own), channel_id=1, source_target_pairs={{0,8},{8,0},{16,24},{24,16},{1,9},{9,1},{17,25},{25,17},{2,10},{10... | collective-permute-start | bytes 1179656 | tf_op jit(solution)/shard_map/cond/branch_1_fun/ppermute | solution.py:491
  43.8 11.4 %collective-permute-start.3 = (bf16[128,1536]{1,0:T(8,128)(2,1)S(1)}, bf16[128,1536]{1,0:T(8,128)(2,1)S(1)}, u32[]{:S(2)}, u32[]{:S(2)}) collective-permute-start(bf16[128,1536]{1,0:T(8,128)(2,1)S(1)} %total.4), channel_id=1, source_target_pairs={{0,16},{8,24},{16,0},{24,8},{1,17},{9,25},{17,1},{25,9},{2,18},{10... | collective-permute-start | bytes 1179656 | tf_op jit(solution)/shard_map/cond/branch_1_fun/ppermute | solution.py:491
  47.5 8.7 %copy-start.6 = (f32[64,1536]{1,0:T(8,128)}, f32[64,1536]{1,0:T(8,128)S(1)}, u32[]{:S(2)}) copy-start(f32[64,1536]{1,0:T(8,128)S(1)} %get-tuple-element.352.next_keep) | copy-start | bytes 1179652 | tf_op jit(solution)/shard_map/cond
  47.5 8.7 %copy-start.4 = (bf16[128,1536]{1,0:T(8,128)(2,1)}, bf16[128,1536]{1,0:T(8,128)(2,1)S(1)}, u32[]{:S(2)}) copy-start(bf16[128,1536]{1,0:T(8,128)(2,1)S(1)} %collective-permute-done.2.core) | copy-start | bytes 1179652 | tf_op jit(solution)/shard_map/cond
  50.9 4.3 %collective-permute-start.4 = (bf16[64,1536]{1,0:T(8,128)(2,1)S(1)}, bf16[64,1536]{1,0:T(8,128)(2,1)S(1)}, u32[]{:S(2)}, u32[]{:S(2)}) collective-permute-start(bf16[64,1536]{1,0:T(8,128)(2,1)S(1)} %get-tuple-element.109), channel_id=1, source_target_pairs={{0,8},{8,0},{16,24},{24,16},{1,9},{9,1},{17,25},{25,17},{2,10},{10... | collective-permute-start | bytes 589832 | tf_op jit(solution)/shard_map/cond/branch_1_fun/ppermute | solution.py:491
  56.2 2.1 %collective-permute-start.5 = (bf16[128,1536]{1,0:T(8,128)(2,1)}, bf16[128,1536]{1,0:T(8,128)(2,1)}, u32[]{:S(2)}, u32[]{:S(2)}) collective-permute-start(bf16[128,1536]{1,0:T(8,128)(2,1)} %get-tuple-element.346.own), channel_id=1, source_target_pairs={{0,8},{8,0},{16,24},{24,16},{1,9},{9,1},{17,25},{25,17},{2,10},{10... | collective-permute-start | bytes 1179656 | tf_op jit(solution)/shard_map/cond/branch_1_fun/ppermute | solution.py:491
  58.2 3.3 %copy-start.3 = (bf16[128,1536]{1,0:T(8,128)(2,1)S(1)}, bf16[128,1536]{1,0:T(8,128)(2,1)}, u32[]{:S(2)}) copy-start(bf16[128,1536]{1,0:T(8,128)(2,1)} %copy-done.2) | copy-start | bytes 1179652 | tf_op jit(solution)/shard_map/cond
  58.2 3.3 %copy-start.5 = (bf16[128,1536]{1,0:T(8,128)(2,1)S(1)}, bf16[128,1536]{1,0:T(8,128)(2,1)}, u32[]{:S(2)}) copy-start(bf16[128,1536]{1,0:T(8,128)(2,1)} %copy-done.4) | copy-start | bytes 1179652 | tf_op jit(solution)/shard_map/cond
  58.3 3.3 %copy-start.7 = (f32[64,1536]{1,0:T(8,128)S(1)}, f32[64,1536]{1,0:T(8,128)}, u32[]{:S(2)}) copy-start(f32[64,1536]{1,0:T(8,128)} %copy-done.6) | copy-start | bytes 1179652 | tf_op jit(solution)/shard_map/cond
  58.3 3.3 %copy-start.11 = (bf16[128,1024]{1,0:T(8,128)(2,1)S(1)}, bf16[128,1024]{1,0:T(8,128)(2,1)}, u32[]{:S(2)}) copy-start(bf16[128,1024]{1,0:T(8,128)(2,1)} %copy-done.10) | copy-start | bytes 786436 | tf_op jit(solution)/shard_map/cond
  58.3 3.3 %copy-start.13 = (bf16[128,1024]{1,0:T(8,128)(2,1)S(1)}, bf16[128,1024]{1,0:T(8,128)(2,1)}, u32[]{:S(2)}) copy-start(bf16[128,1024]{1,0:T(8,128)(2,1)} %copy-done.12) | copy-start | bytes 786436 | tf_op jit(solution)/shard_map/cond
  61.6 7.4 %collective-permute-start.20 = (bf16[64,1536]{1,0:T(8,128)(2,1)S(1)}, bf16[64,1536]{1,0:T(8,128)(2,1)S(1)}, u32[]{:S(2)}, u32[]{:S(2)}) collective-permute-start(bf16[64,1536]{1,0:T(8,128)(2,1)S(1)} %get-tuple-element.263), channel_id=1, source_target_pairs={{0,16},{8,24},{16,0},{24,8},{1,17},{9,25},{17,1},{25,9},{2,18},{10... | collective-permute-start | bytes 589832 | tf_op jit(solution)/shard_map/ppermute | solution.py:491
  63.1 31.1 %collective-permute-start.28 = (bf16[120,1024]{1,0:T(8,128)(2,1)}, bf16[120,1024]{1,0:T(8,128)(2,1)S(1)}, u32[]{:S(2)}, u32[]{:S(2)}) collective-permute-start(bf16[120,1024]{1,0:T(8,128)(2,1)} %get-tuple-element.284), channel_id=1, source_target_pairs={{0,1},{1,0},{2,3},{3,2},{4,5},{5,4},{6,7},{7,6},{8,9},{9,8},{10,11... | collective-permute-start | bytes 737288 | tf_op jit(solution)/shard_map/ppermute | solution.py:488
  63.6 30.6 %collective-permute-start.27 = (bf16[120,1024]{1,0:T(8,128)(2,1)}, bf16[120,1024]{1,0:T(8,128)(2,1)S(1)}, u32[]{:S(2)}, u32[]{:S(2)}) collective-permute-start(bf16[120,1024]{1,0:T(8,128)(2,1)} %get-tuple-element.280), channel_id=1, source_target_pairs={{0,5},{1,4},{2,7},{3,6},{4,1},{5,0},{6,3},{7,2},{8,13},{9,12},{10,... | collective-permute-start | bytes 737288 | tf_op jit(solution)/shard_map/ppermute | solution.py:488
  68.6 25.7 %collective-permute-start.26 = (bf16[120,1024]{1,0:T(8,128)(2,1)}, bf16[120,1024]{1,0:T(8,128)(2,1)S(1)}, u32[]{:S(2)}, u32[]{:S(2)}) collective-permute-start(bf16[120,1024]{1,0:T(8,128)(2,1)} %get-tuple-element.278), channel_id=1, source_target_pairs={{0,4},{1,5},{2,6},{3,7},{4,0},{5,1},{6,2},{7,3},{8,12},{9,13},{10,... | collective-permute-start | bytes 737288 | tf_op jit(solution)/shard_map/ppermute | solution.py:488
  72.6 14.8 %copy-start.16 = (bf16[128,1024]{1,0:T(8,128)(2,1)}, bf16[128,1024]{1,0:T(8,128)(2,1)S(1)}, u32[]{:S(2)}) copy-start(bf16[128,1024]{1,0:T(8,128)(2,1)S(1)} %get-tuple-element.378.grads) | copy-start | bytes 786436 | tf_op jit(solution)/shard_map/cond
  72.6 2.0 %collective-permute-start.6 = (bf16[128,1536]{1,0:T(8,128)(2,1)S(1)}, bf16[128,1536]{1,0:T(8,128)(2,1)S(1)}, u32[]{:S(2)}, u32[]{:S(2)}) collective-permute-start(bf16[128,1536]{1,0:T(8,128)(2,1)S(1)} %get-tuple-element.128), channel_id=1, source_target_pairs={{0,8},{8,0},{16,24},{24,16},{1,9},{9,1},{17,25},{25,17},{2,10},{10... | collective-permute-start | bytes 1179656 | tf_op jit(solution)/shard_map/cond/branch_1_fun/ppermute | solution.py:491
  74.8 7.6 %copy-start.17 = (bf16[64,1536]{1,0:T(8,128)(2,1)}, bf16[64,1536]{1,0:T(8,128)(2,1)S(1)}, u32[]{:S(2)}) copy-start(bf16[64,1536]{1,0:T(8,128)(2,1)S(1)} %act.7.own) | copy-start | bytes 589828 | tf_op jit(solution)/shard_map/cond
  74.8 4.3 %collective-permute-start.7 = (bf16[64,1536]{1,0:T(8,128)(2,1)S(1)}, bf16[64,1536]{1,0:T(8,128)(2,1)S(1)}, u32[]{:S(2)}, u32[]{:S(2)}) collective-permute-start(bf16[64,1536]{1,0:T(8,128)(2,1)S(1)} %act.7.own), channel_id=1, source_target_pairs={{0,8},{8,0},{16,24},{24,16},{1,9},{9,1},{17,25},{25,17},{2,10},{10... | collective-permute-start | bytes 589832 | tf_op jit(solution)/shard_map/cond/branch_1_fun/ppermute | solution.py:491
  75.0 11.4 %collective-permute-start.8 = (bf16[128,1536]{1,0:T(8,128)(2,1)S(1)}, bf16[128,1536]{1,0:T(8,128)(2,1)S(1)}, u32[]{:S(2)}, u32[]{:S(2)}) collective-permute-start(bf16[128,1536]{1,0:T(8,128)(2,1)S(1)} %total.5), channel_id=1, source_target_pairs={{0,16},{8,24},{16,0},{24,8},{1,17},{9,25},{17,1},{25,9},{2,18},{10... | collective-permute-start | bytes 1179656 | tf_op jit(solution)/shard_map/cond/branch_1_fun/ppermute | solution.py:491
  79.0 8.3 %copy-start.8 = (f32[64,1536]{1,0:T(8,128)}, f32[64,1536]{1,0:T(8,128)S(1)}, u32[]{:S(2)}) copy-start(f32[64,1536]{1,0:T(8,128)S(1)} %get-tuple-element.385.next_keep) | copy-start | bytes 1179652 | tf_op jit(solution)/shard_map/cond
  79.1 8.3 %copy-start.18 = (bf16[64,1536]{1,0:T(8,128)(2,1)}, bf16[64,1536]{1,0:T(8,128)(2,1)S(1)}, u32[]{:S(2)}) copy-start(bf16[64,1536]{1,0:T(8,128)(2,1)S(1)} %collective-permute-done.7.core) | copy-start | bytes 589828 | tf_op jit(solution)/shard_map/cond
  82.3 1.4 %collective-permute-start.9 = (bf16[64,1536]{1,0:T(8,128)(2,1)S(1)}, bf16[64,1536]{1,0:T(8,128)(2,1)S(1)}, u32[]{:S(2)}, u32[]{:S(2)}) collective-permute-start(bf16[64,1536]{1,0:T(8,128)(2,1)S(1)} %get-tuple-element.142), channel_id=1, source_target_pairs={{0,8},{8,0},{16,24},{24,16},{1,9},{9,1},{17,25},{25,17},{2,10},{10... | collective-permute-start | bytes 589832 | tf_op jit(solution)/shard_map/cond/branch_1_fun/ppermute | solution.py:491
  83.8 5.7 %copy-start.19 = (bf16[64,1536]{1,0:T(8,128)(2,1)}, bf16[64,1536]{1,0:T(8,128)(2,1)S(1)}, u32[]{:S(2)}) copy-start(bf16[64,1536]{1,0:T(8,128)(2,1)S(1)} %collective-permute-done.9.next_core) | copy-start | bytes 589828 | tf_op jit(solution)/shard_map/cond
  87.4 2.1 %collective-permute-start.10 = (bf16[128,1536]{1,0:T(8,128)(2,1)}, bf16[128,1536]{1,0:T(8,128)(2,1)}, u32[]{:S(2)}, u32[]{:S(2)}) collective-permute-start(bf16[128,1536]{1,0:T(8,128)(2,1)} %get-tuple-element.379.own), channel_id=1, source_target_pairs={{0,8},{8,0},{16,24},{24,16},{1,9},{9,1},{17,25},{25,17},{2,10},{10... | collective-permute-start | bytes 1179656 | tf_op jit(solution)/shard_map/cond/branch_1_fun/ppermute | solution.py:491
  92.6 7.4 %collective-permute-start.23 = (bf16[64,1536]{1,0:T(8,128)(2,1)S(1)}, bf16[64,1536]{1,0:T(8,128)(2,1)S(1)}, u32[]{:S(2)}, u32[]{:S(2)}) collective-permute-start(bf16[64,1536]{1,0:T(8,128)(2,1)S(1)} %get-tuple-element.271), channel_id=1, source_target_pairs={{0,16},{8,24},{16,0},{24,8},{1,17},{9,25},{17,1},{25,9},{2,18},{10... | collective-permute-start | bytes 589832 | tf_op jit(solution)/shard_map/ppermute | solution.py:491
  94.2 25.5 %collective-permute-start.30 = (bf16[120,1024]{1,0:T(8,128)(2,1)}, bf16[120,1024]{1,0:T(8,128)(2,1)S(1)}, u32[]{:S(2)}, u32[]{:S(2)}) collective-permute-start(bf16[120,1024]{1,0:T(8,128)(2,1)} %get-tuple-element.287), channel_id=1, source_target_pairs={{0,7},{1,6},{2,5},{3,4},{4,3},{5,2},{6,1},{7,0},{8,15},{9,14},{10,... | collective-permute-start | bytes 737288 | tf_op jit(solution)/shard_map/ppermute | solution.py:488
  97.7 22.0 %collective-permute-start.29 = (bf16[120,1024]{1,0:T(8,128)(2,1)}, bf16[120,1024]{1,0:T(8,128)(2,1)S(1)}, u32[]{:S(2)}, u32[]{:S(2)}) collective-permute-start(bf16[120,1024]{1,0:T(8,128)(2,1)} %get-tuple-element.285), channel_id=1, source_target_pairs={{0,6},{1,7},{2,4},{3,5},{4,2},{5,3},{6,0},{7,1},{8,14},{9,15},{10,... | collective-permute-start | bytes 737288 | tf_op jit(solution)/shard_map/ppermute | solution.py:488
  98.1 23.2 %collective-permute-start.22 = (bf16[120,1024]{1,0:T(8,128)(2,1)}, bf16[120,1024]{1,0:T(8,128)(2,1)S(1)}, u32[]{:S(2)}, u32[]{:S(2)}) collective-permute-start(bf16[120,1024]{1,0:T(8,128)(2,1)} %get-tuple-element.268), channel_id=1, source_target_pairs={{0,2},{1,3},{2,0},{3,1},{4,6},{5,7},{6,4},{7,5},{8,10},{9,11},{10,... | collective-permute-start | bytes 737288 | tf_op jit(solution)/shard_map/ppermute | solution.py:488
  100.0 10.6 %copy-start = (s32[192,2]{0,1:T(2,128)S(1)}, s32[192,2]{0,1:T(2,128)}, u32[]{:S(2)}) copy-start(s32[192,2]{0,1:T(2,128)} %param.15) | copy-start | bytes 4612
  100.0 10.6 %copy-start.1 = (f32[192,2]{0,1:T(2,128)S(1)}, f32[192,2]{0,1:T(2,128)}, u32[]{:S(2)}) copy-start(f32[192,2]{0,1:T(2,128)} %param.16) | copy-start | bytes 4612
  100.8 4.0 %collective-permute-start.11 = (bf16[64,1536]{1,0:T(8,128)(2,1)}, bf16[64,1536]{1,0:T(8,128)(2,1)}, u32[]{:S(2)}, u32[]{:S(2)}) collective-permute-start(bf16[64,1536]{1,0:T(8,128)(2,1)} %act.9.own), channel_id=1, source_target_pairs={{0,8},{8,0},{16,24},{24,16},{1,9},{9,1},{17,25},{25,17},{2,10},{10... | collective-permute-start | bytes 589832 | tf_op jit(solution)/shard_map/cond/branch_1_fun/ppermute | solution.py:491
  107.6 5.4 %copy-start.23 = (bf16[64,1024]{1,0:T(8,128)(2,1)}, bf16[64,1024]{1,0:T(8,128)(2,1)S(1)}, u32[]{:S(2)}) copy-start(bf16[64,1024]{1,0:T(8,128)(2,1)S(1)} %get-tuple-element.309.refs_17_) | copy-start | bytes 393220
  107.6 5.4 %copy-start.24 = (bf16[64,1024]{1,0:T(8,128)(2,1)}, bf16[64,1024]{1,0:T(8,128)(2,1)S(1)}, u32[]{:S(2)}) copy-start(bf16[64,1024]{1,0:T(8,128)(2,1)S(1)} %get-tuple-element.310.refs_18_) | copy-start | bytes 393220
  107.6 13.7 %collective-permute-start.24 = (bf16[120,512]{1,0:T(8,128)(2,1)}, bf16[120,512]{1,0:T(8,128)(2,1)S(1)}, u32[]{:S(2)}, u32[]{:S(2)}) collective-permute-start(bf16[120,512]{1,0:T(8,128)(2,1)} %get-tuple-element.274), channel_id=1, source_target_pairs={{0,3},{1,2},{2,1},{3,0},{4,7},{5,6},{6,5},{7,4},{8,11},{9,10},{10,... | collective-permute-start | bytes 368648 | tf_op jit(solution)/shard_map/ppermute | solution.py:488
  110.5 10.8 %collective-permute-start.25 = (bf16[120,512]{1,0:T(8,128)(2,1)}, bf16[120,512]{1,0:T(8,128)(2,1)S(1)}, u32[]{:S(2)}, u32[]{:S(2)}) collective-permute-start(bf16[120,512]{1,0:T(8,128)(2,1)} %get-tuple-element.275), channel_id=1, source_target_pairs={{0,3},{1,2},{2,1},{3,0},{4,7},{5,6},{6,5},{7,4},{8,11},{9,10},{10,... | collective-permute-start | bytes 368648 | tf_op jit(solution)/shard_map/ppermute | solution.py:488
  (10 other events, 24.7 us)

commit v5 on v4

--- a/solution.py
+++ b/solution.py
@@ -125,7 +125,7 @@
             out[:, (3 * j + part) * width : (3 * j + part + 1) * width] = term.astype(out.dtype)
 
 
-PIECES = 4
+PIECES = 1
 
 
 def weight_copies(halves, far_in, far_out, w_in, w_out, sems):

time: 124 us -> 123 us (level)
  no operation moved by 1% of the time
where the time goes in v5:
time: 123 us
  Pallas kernels  67.6 us (55%)
  starting transfers between devices  35.5 us (29%)
  waiting for transfers between devices  18.5 us (15%)
    pallas_call x23, Pallas kernels, call(): pl.pallas_call(kernel, out_shape=out_shapes, in_specs=[pl.BlockSpec(memor...  42.1 us
    ppermute x15, starting transfers between devices, across(): lax.ppermute(x, 'expert', [(i, i ^ s) for i in range(n_expert)])  26.4 us
    pallas_call x3, Pallas kernels, other_half(): pl.pallas_call(kernel, out_shape=[shape((rows, features), BF), shape((row...  11.2 us
    ppermute x15, waiting for transfers between devices, across(): lax.ppermute(x, 'expert', [(i, i ^ s) for i in range(n_expert)])  9.28 us
    ppermute x16, waiting for transfers between devices, beside(): return lax.ppermute(x, 'dp', [(i, i ^ s) for i in range(n_dp)])  9.21 us
    ppermute x16, starting transfers between devices, beside(): return lax.ppermute(x, 'dp', [(i, i ^ s) for i in range(n_dp)])  9.15 us
    pallas_call x1, Pallas kernels, grads_step(): pl.pallas_call(lambda *refs: grads_kernel(len(groups), *refs), out_shape=...  6.71 us
    pallas_call x1, Pallas kernels, down_own_alone(): pl.pallas_call(kernel, out_shape=[sums, sums, shape(w_in.shape, BF), shap...  3.83 us
  transfers between devices with their start and end apart: 31, of which 10 were waited for; matrix products, arithmetic and copies ran while one was open for 0% of the time, Pallas kernels for 50%

profile of v5, /device:TPU:0, one launch (start us, length us, event | category | flops | bytes accessed | tf_op | source)
XLA Modules:
  0.0 123.0 jit_solution(10981235759551104837)
XLA Ops:
  0.7 3.8 %prep.1 = (bf16[120,1024]{1,0:T(8,128)(2,1)S(1)}, bf16[120,1024]{1,0:T(8,128)(2,1)}, bf16[120,1024]{1,0:T(8,128)(2,1)}, bf16[120,1024]{1,0:T(8,128)(2,1)}, bf16[...) custom-call(s32[2]{0:T(128)S(1)} %pad_add_fusion.refs_0_, ...), custom_call_target="tpu_custom_call" | custom-call | flops 1 | bytes 1 | tf_op jit(solution)/shard_map/prep/pallas_call | solution.py:76
  4.5 3.0 %collective-permute-start.15 = (bf16[120,1024]{1,0:T(8,128)(2,1)}, bf16[120,1024]{1,0:T(8,128)(2,1)S(1)}, u32[]{:S(2)}, u32[]{:S(2)}) collective-permute-start(bf16[120,1024]{1,0:T(8,128)(2,1)} %get-tuple-element.249), channel_id=1, source_target_pairs={{0,1},{1,0},{2,3},{3,2},{4,5},{5,4},{6,7},{7,6},{8,9},{9,8},{10,11... | collective-permute-start | bytes 737288 | tf_op jit(solution)/shard_map/ppermute | solution.py:488
  7.5 2.6 %collective-permute-start.12 = (bf16[120,1024]{1,0:T(8,128)(2,1)}, bf16[120,1024]{1,0:T(8,128)(2,1)S(1)}, u32[]{:S(2)}, u32[]{:S(2)}) collective-permute-start(bf16[120,1024]{1,0:T(8,128)(2,1)} %get-tuple-element.245), channel_id=1, source_target_pairs={{0,4},{1,5},{2,6},{3,7},{4,0},{5,1},{6,2},{7,3},{8,12},{9,13},{10,... | collective-permute-start | bytes 737288 | tf_op jit(solution)/shard_map/ppermute | solution.py:488
  10.1 1.9 %collective-permute-start.14 = (bf16[120,1024]{1,0:T(8,128)(2,1)}, bf16[120,1024]{1,0:T(8,128)(2,1)S(1)}, u32[]{:S(2)}, u32[]{:S(2)}) collective-permute-start(bf16[120,1024]{1,0:T(8,128)(2,1)} %get-tuple-element.247), channel_id=1, source_target_pairs={{0,2},{1,3},{2,0},{3,1},{4,6},{5,7},{6,4},{7,5},{8,10},{9,11},{10,... | collective-permute-start | bytes 737288 | tf_op jit(solution)/shard_map/ppermute | solution.py:488
  12.0 1.7 %collective-permute-done.15 = bf16[120,1024]{1,0:T(8,128)(2,1)S(1)} collective-permute-done((bf16[120,1024]{1,0:T(8,128)(2,1)}, bf16[120,1024]{1,0:T(8,128)(2,1)S(1)}, u32[]{:S(2)}, u32[]{:S(2)}) %collective-permute-start.15) | collective-permute-done | bytes 245792 | tf_op jit(solution)/shard_map/ppermute | solution.py:488
  13.7 8.4 %conditional.4 = (bf16[128,1024]{1,0:T(8,128)(2,1)}, bf16[128,1024]{1,0:T(8,128)(2,1)}, f32[128,1536]{1,0:T(8,128)}, bf16[128,1536]{1,0:T(8,128)(2,1)}, bf16[128...) conditional(s32[]{:T(128)} %convert_element_type.2, () %tuple.67, (s32[2]{0:T(128)S(1)}, ...), branch_computations={%region_0.1_spmd, %region_1.2_spmd} | conditional | flops 3 | bytes 2097214 | solution.py:503
  13.7 4.3 %up.8 = (bf16[128,1024]{1,0:T(8,128)(2,1)}, bf16[128,1024]{1,0:T(8,128)(2,1)}, bf16[128,1536]{1,0:T(8,128)(2,1)S(1)}, bf16[1024,2048]{1,0:T(8,128)(2,1)S(1)}, bf16[1024,1024]{1,0:T(8,128)(2,1)S(1)}) custom-call(s32[2]{0:T(128)S(1)} %get-tuple-element.72.ids, bf16[120,1024]{1,0:T(8,128)(2,1)S(1)} %get-tuple-element.73.refs_0_, ...), custom_call_target="tpu_custom_call" | custom-call | flops 1 | bytes 1 | tf_op jit(solution)/shard_map/cond/branch_1_fun/up/pallas_call | solution.py:170
  18.1 2.7 %up.9.keep = f32[128,1536]{1,0:T(8,128)} custom-call(s32[2]{0:T(128)S(1)} %get-tuple-element.72.ids, bf16[128,1024]{1,0:T(8,128)(2,1)} %get-tuple-element.80.rows, bf16[128,1024]{1,0:T(8,128)(2,1)} %get-tuple-element.322.grads, bf16[1024,2048]{1,0:T(8,128)(2,1)S(1)} %get-tuple-element.81.w_in, bf16[1024,1024]{1,0:T(8,128)(2,1)S(1)} %get-tuple-element.82.w_out), custom_call_target="tpu_custom_call" | custom-call | flops 1 | bytes 1 | tf_op jit(solution)/shard_map/cond/branch_1_fun/up/pallas_call | solution.py:92
  20.8 1.3 %total.3 = (bf16[128,768]{1,0:T(8,128)(2,1)S(1)}, bf16[128,768]{1,0:T(8,128)(2,1)S(1)}) custom-call(f32[128,1536]{1,0:T(8,128)} %up.9.keep, bf16[128,1536]{1,0:T(8,128)(2,1)} %collective-permute-done.core), custom_call_target="tpu_custom_call" | custom-call | flops 1 | bytes 1 | tf_op jit(solution)/shard_map/cond/branch_1_fun/total/pallas_call | solution.py:92
  22.1 1.8 %collective-permute-start.17 = (bf16[128,768]{1,0:T(8,128)(2,1)S(1)}, bf16[128,768]{1,0:T(8,128)(2,1)S(1)}, u32[]{:S(2)}, u32[]{:S(2)}) collective-permute-start(bf16[128,768]{1,0:T(8,128)(2,1)S(1)} %get-tuple-element.250), channel_id=1, source_target_pairs={{0,16},{8,24},{16,0},{24,8},{1,17},{9,25},{17,1},{25,9},{2,18},{10... | collective-permute-start | bytes 589832 | tf_op jit(solution)/shard_map/ppermute | solution.py:491
  24.2 3.5 %collective-permute-done.12 = bf16[120,1024]{1,0:T(8,128)(2,1)S(1)} collective-permute-done((bf16[120,1024]{1,0:T(8,128)(2,1)}, bf16[120,1024]{1,0:T(8,128)(2,1)S(1)}, u32[]{:S(2)}, u32[]{:S(2)}) %collective-permute-start.12) | collective-permute-done | bytes 245792 | tf_op jit(solution)/shard_map/ppermute | solution.py:488
  27.8 4.0 %collective-permute-done.13 = bf16[120,1024]{1,0:T(8,128)(2,1)S(1)} collective-permute-done((bf16[120,1024]{1,0:T(8,128)(2,1)}, bf16[120,1024]{1,0:T(8,128)(2,1)S(1)}, u32[]{:S(2)}, u32[]{:S(2)}) %collective-permute-start.13) | collective-permute-done | bytes 245792 | tf_op jit(solution)/shard_map/ppermute | solution.py:488
  31.8 3.5 %collective-permute-start.16 = (bf16[120,1024]{1,0:T(8,128)(2,1)}, bf16[120,1024]{1,0:T(8,128)(2,1)S(1)}, u32[]{:S(2)}, u32[]{:S(2)}) collective-permute-start(bf16[120,1024]{1,0:T(8,128)(2,1)} %get-tuple-element.252), channel_id=1, source_target_pairs={{0,6},{1,7},{2,4},{3,5},{4,2},{5,3},{6,0},{7,1},{8,14},{9,15},{10,... | collective-permute-start | bytes 737288 | tf_op jit(solution)/shard_map/ppermute | solution.py:488
  35.3 1.3 %collective-permute-start.19 = (bf16[120,1024]{1,0:T(8,128)(2,1)}, bf16[120,1024]{1,0:T(8,128)(2,1)S(1)}, u32[]{:S(2)}, u32[]{:S(2)}) collective-permute-start(bf16[120,1024]{1,0:T(8,128)(2,1)} %get-tuple-element.260), channel_id=1, source_target_pairs={{0,7},{1,6},{2,5},{3,4},{4,3},{5,2},{6,1},{7,0},{8,15},{9,14},{10,... | collective-permute-start | bytes 737288 | tf_op jit(solution)/shard_map/ppermute | solution.py:488
  36.6 24.8 %conditional.5 = (bf16[128,1024]{1,0:T(8,128)(2,1)S(1)}, bf16[128,1024]{1,0:T(8,128)(2,1)S(1)}, bf16[128,1536]{1,0:T(8,128)(2,1)}, bf16[128,1536]{1,0:T(8,128)(2...) conditional(s32[]{:T(128)} %convert_element_type.2, () %tuple.70, ...), branch_computations={%region_2.3_spmd, %region_3.4_spmd} | conditional | flops 9 | bytes 22282920 | solution.py:503
  36.6 3.5 %up.10 = (bf16[128,1024]{1,0:T(8,128)(2,1)S(1)}, bf16[128,1024]{1,0:T(8,128)(2,1)S(1)}, bf16[128,1536]{1,0:T(8,128)(2,1)S(1)}, bf16[1024,2048]{1,0:T(8,128)(2,1)S(1)}, bf16[1024,1024]{1,0:T(8,128)(2,1)S(1)}) custom-call(s32[2]{0:T(128)S(1)} %get-tuple-element.85.ids, bf16[120,1024]{1,0:T(8,128)(2,1)S(1)} %get-tuple-element.86.refs_0_, ...), custom_call_target="tpu_custom_call" | custom-call | flops 1 | bytes 1 | tf_op jit(solution)/shard_map/cond/branch_1_fun/up/pallas_call | solution.py:170
  40.2 1.3 %up.11.keep = f32[128,1536]{1,0:T(8,128)S(1)} custom-call(s32[2]{0:T(128)S(1)} %get-tuple-element.85.ids, bf16[128,1024]{1,0:T(8,128)(2,1)S(1)} %get-tuple-element.93.rows, bf16[128,1024]{1,0:T(8,128)(2,1)S(1)} %get-tuple-element.345.grads, bf16[1024,2048]{1,0:T(8,128)(2,1)S(1)} %get-tuple-element.94.w_in.refs_1_, ...), custom_call_target="tpu_custom_call" | custom-call | flops 1 | bytes 1 | tf_op jit(solution)/shard_map/cond/branch_1_fun/up/pallas_call | solution.py:92
  42.0 1.5 %act.5.own = bf16[128,1536]{1,0:T(8,128)(2,1)S(1)} custom-call(f32[128,1536]{1,0:T(8,128)} %get-tuple-element.97.keep, bf16[128,1536]{1,0:T(8,128)(2,1)} %get-tuple-element.98.core, bf16[128,768]{1,0:T(8,128)(2,1)S(1)} %get-tuple-element.99.refs_0_, bf16[128,768]{1,0:T(8,128)(2,1)S(1)} %get-tuple-element.100.refs_1_), custom_call_target="tpu_custom_call" | custom-call | flops 1 | bytes 1 | tf_op jit(solution)/shard_map/cond/branch_1_fun/act/pallas_call | solution.py:92
  43.7 1.5 %collective-permute-start.3 = (bf16[128,1536]{1,0:T(8,128)(2,1)S(1)}, bf16[128,1536]{1,0:T(8,128)(2,1)S(1)}, u32[]{:S(2)}, u32[]{:S(2)}) collective-permute-start(bf16[128,1536]{1,0:T(8,128)(2,1)S(1)} %total.4), channel_id=1, source_target_pairs={{0,16},{8,24},{16,0},{24,8},{1,17},{9,25},{17,1},{25,9},{2,18},{10... | collective-permute-start | bytes 1179656 | tf_op jit(solution)/shard_map/cond/branch_1_fun/ppermute | solution.py:491
  45.2 2.1 %up.12 = (bf16[64,1024]{1,0:T(8,128)(2,1)S(1)}, bf16[64,1024]{1,0:T(8,128)(2,1)S(1)}, bf16[64,1536]{1,0:T(8,128)(2,1)S(1)}, f32[64,1536]{1,0:T(8,128)S(1)}) custom-call(s32[2]{0:T(128)S(1)} %get-tuple-element.85.ids, bf16[120,1024]{1,0:T(8,128)(2,1)S(1)} %get-tuple-element.102.refs_0_, bf16[1024,2048]{1,0:T(8,128)(2,1)S(1)} %get-tuple-element.94.w_in.refs_1_, ...), custom_call_target="tpu_custom_call" | custom-call | flops 1 | bytes 1 | tf_op jit(solution)/shard_map/cond/branch_1_fun/up/pallas_call | solution.py:92
  47.3 3.4 %down.8 = (bf16[120,1024]{1,0:T(8,128)(2,1)}, bf16[120,1024]{1,0:T(8,128)(2,1)}) custom-call(s32[2]{0:T(128)S(1)} %get-tuple-element.85.ids, bf16[128,1536]{1,0:T(8,128)(2,1)S(1)} %act.5.own, bf16[128,1536]{1,0:T(8,128)(2,1)S(1)} %collective-permute-done.2.core, bf16[1024,2048]{1,0:T(8,128)(2,1)S(1)} %get-tuple-element.94.w_in.refs_1_, ...), custom_call_target="tpu_custom_call" | custom-call | flops 1 | bytes 1 | tf_op jit(solution)/shard_map/cond/branch_1_fun/down/pallas_call | solution.py:92
  50.8 4.2 %collective-permute-done.3.other = bf16[128,1536]{1,0:T(8,128)(2,1)S(1)} collective-permute-done((bf16[128,1536]{1,0:T(8,128)(2,1)S(1)}, bf16[128,1536]{1,0:T(8,128)(2,1)S(1)}, u32[]{:S(2)}, u32[]{:S(2)}) %collective-permute-start.3) | collective-permute-done | bytes 393248 | tf_op jit(solution)/shard_map/cond/branch_1_fun/ppermute | solution.py:491
  55.1 1.0 act.6
  56.0 2.0 %down.9 = (f32[128,1024]{1,0:T(8,128)S(1)}, f32[128,1024]{1,0:T(8,128)S(1)}) custom-call(s32[2]{0:T(128)S(1)} %get-tuple-element.85.ids, bf16[128,1536]{1,0:T(8,128)(2,1)} %get-tuple-element.346.own, bf16[1024,2048]{1,0:T(8,128)(2,1)S(1)} %get-tuple-element.94.w_in.refs_1_, bf16[1024,1024]{1,0:T(8,128)(2,1)S(1)} %get-tuple-element.95.w_out.refs_2_), custom_call_target="tpu_custom_call" | custom-call | flops 1 | bytes 1 | tf_op jit(solution)/shard_map/cond/branch_1_fun/down/pallas_call | solution.py:92
  58.1 3.2 %down.10 = (bf16[120,1024]{1,0:T(8,128)(2,1)}, bf16[120,1024]{1,0:T(8,128)(2,1)}) custom-call(s32[2]{0:T(128)S(1)} %get-tuple-element.85.ids, f32[128,1024]{1,0:T(8,128)S(1)} %get-tuple-element.111.out_rows, f32[128,1024]{1,0:T(8,128)S(1)} %get-tuple-element.112.grad_rows, bf16[128,1536]{1,0:T(8,128)(2,1)} %collective-permute-done.5.core, ...), custom_call_target="tpu_custom_call" | custom-call | flops 1 | bytes 1 | tf_op jit(solution)/shard_map/cond/branch_1_fun/down/pallas_call | solution.py:92
  61.4 1.6 %collective-permute-start.20 = (bf16[64,1536]{1,0:T(8,128)(2,1)S(1)}, bf16[64,1536]{1,0:T(8,128)(2,1)S(1)}, u32[]{:S(2)}, u32[]{:S(2)}) collective-permute-start(bf16[64,1536]{1,0:T(8,128)(2,1)S(1)} %get-tuple-element.263), channel_id=1, source_target_pairs={{0,16},{8,24},{16,0},{24,8},{1,17},{9,25},{17,1},{25,9},{2,18},{10... | collective-permute-start | bytes 589832 | tf_op jit(solution)/shard_map/ppermute | solution.py:491
  63.4 4.9 %collective-permute-start.27 = (bf16[120,1024]{1,0:T(8,128)(2,1)}, bf16[120,1024]{1,0:T(8,128)(2,1)S(1)}, u32[]{:S(2)}, u32[]{:S(2)}) collective-permute-start(bf16[120,1024]{1,0:T(8,128)(2,1)} %get-tuple-element.280), channel_id=1, source_target_pairs={{0,5},{1,4},{2,7},{3,6},{4,1},{5,0},{6,3},{7,2},{8,13},{9,12},{10,... | collective-permute-start | bytes 737288 | tf_op jit(solution)/shard_map/ppermute | solution.py:488
  68.8 23.3 %conditional.6 = (bf16[128,1024]{1,0:T(8,128)(2,1)S(1)}, bf16[128,1024]{1,0:T(8,128)(2,1)}, bf16[128,1536]{1,0:T(8,128)(2,1)}, bf16[128,1536]{1,0:T(8,128)(2,1)}...) conditional(s32[]{:T(128)} %convert_element_type.2, () %tuple.66, ...), branch_computations={%region_4.5_spmd, %region_5.6_spmd} | conditional | flops 9 | bytes 15729229 | solution.py:503
  68.8 3.5 %up.13 = (bf16[128,1024]{1,0:T(8,128)(2,1)S(1)}, bf16[128,1024]{1,0:T(8,128)(2,1)S(1)}, bf16[128,1536]{1,0:T(8,128)(2,1)S(1)}, bf16[1024,2048]{1,0:T(8,128)(2,1)S(1)}, bf16[1024,1024]{1,0:T(8,128)(2,1)S(1)}) custom-call(s32[2]{0:T(128)S(1)} %get-tuple-element.121.ids, bf16[120,1024]{1,0:T(8,128)(2,1)S(1)} %get-tuple-element.122.refs_0_, ...), custom_call_target="tpu_custom_call" | custom-call | flops 1 | bytes 1 | tf_op jit(solution)/shard_map/cond/branch_1_fun/up/pallas_call | solution.py:170
  72.3 1.5 %up.14.keep = f32[128,1536]{1,0:T(8,128)S(1)} custom-call(s32[2]{0:T(128)S(1)} %get-tuple-element.121.ids, bf16[128,1024]{1,0:T(8,128)(2,1)S(1)} %get-tuple-element.129.rows, bf16[128,1024]{1,0:T(8,128)(2,1)S(1)} %get-tuple-element.378.grads, bf16[1024,2048]{1,0:T(8,128)(2,1)S(1)} %get-tuple-element.130.w_in.refs_1_, ...), custom_call_target="tpu_custom_call" | custom-call | flops 1 | bytes 1 | tf_op jit(solution)/shard_map/cond/branch_1_fun/up/pallas_call | solution.py:92
  74.7 1.5 %collective-permute-start.8 = (bf16[128,1536]{1,0:T(8,128)(2,1)S(1)}, bf16[128,1536]{1,0:T(8,128)(2,1)S(1)}, u32[]{:S(2)}, u32[]{:S(2)}) collective-permute-start(bf16[128,1536]{1,0:T(8,128)(2,1)S(1)} %total.5), channel_id=1, source_target_pairs={{0,16},{8,24},{16,0},{24,8},{1,17},{9,25},{17,1},{25,9},{2,18},{10... | collective-permute-start | bytes 1179656 | tf_op jit(solution)/shard_map/cond/branch_1_fun/ppermute | solution.py:491
  76.1 2.5 %up.15 = (bf16[64,1024]{1,0:T(8,128)(2,1)S(1)}, bf16[64,1024]{1,0:T(8,128)(2,1)S(1)}, bf16[64,1536]{1,0:T(8,128)(2,1)S(1)}, f32[64,1536]{1,0:T(8,128)S(1)}) custom-call(s32[2]{0:T(128)S(1)} %get-tuple-element.121.ids, bf16[120,1024]{1,0:T(8,128)(2,1)} %get-tuple-element.137.refs_0_, bf16[1024,2048]{1,0:T(8,128)(2,1)S(1)} %get-tuple-element.130.w_in.refs_1_, ...), custom_call_target="tpu_custom_call" | custom-call | flops 1 | bytes 1 | tf_op jit(solution)/shard_map/cond/branch_1_fun/up/pallas_call | solution.py:92
  78.7 3.3 %down.11 = bf16[120,1024]{1,0:T(8,128)(2,1)} custom-call(s32[2]{0:T(128)S(1)} %get-tuple-element.121.ids, bf16[64,1536]{1,0:T(8,128)(2,1)S(1)} %act.7.own, bf16[64,1536]{1,0:T(8,128)(2,1)S(1)} %collective-permute-done.7.core, bf16[1024,2048]{1,0:T(8,128)(2,1)S(1)} %get-tuple-element.130.w_in.refs_1_, bf16[1024,1024]{1,0:T(8,128)(2,1)S(1)} %get-tuple-element.131.w_out.refs_2_), custom_call_target="tpu_custom_call" | custom-call | flops 1 | bytes 1 | tf_op jit(solution)/shard_map/cond/branch_1_fun/down/pallas_call | solution.py:92
  82.0 1.4 %collective-permute-done.9.next_core = bf16[64,1536]{1,0:T(8,128)(2,1)S(1)} collective-permute-done((bf16[64,1536]{1,0:T(8,128)(2,1)S(1)}, bf16[64,1536]{1,0:T(8,128)(2,1)S(1)}, u32[]{:S(2)}, u32[]{:S(2)}) %collective-permute-start.9) | collective-permute-done | bytes 196640 | tf_op jit(solution)/shard_map/cond/branch_1_fun/ppermute | solution.py:491
  83.4 2.4 %collective-permute-done.8.other = bf16[128,1536]{1,0:T(8,128)(2,1)S(1)} collective-permute-done((bf16[128,1536]{1,0:T(8,128)(2,1)S(1)}, bf16[128,1536]{1,0:T(8,128)(2,1)S(1)}, u32[]{:S(2)}, u32[]{:S(2)}) %collective-permute-start.8) | collective-permute-done | bytes 393248 | tf_op jit(solution)/shard_map/cond/branch_1_fun/ppermute | solution.py:491
  86.9 2.0 %down.12 = (f32[128,1024]{1,0:T(8,128)S(1)}, f32[128,1024]{1,0:T(8,128)S(1)}) custom-call(s32[2]{0:T(128)S(1)} %get-tuple-element.121.ids, bf16[128,1536]{1,0:T(8,128)(2,1)} %get-tuple-element.379.own, bf16[1024,2048]{1,0:T(8,128)(2,1)S(1)} %get-tuple-element.130.w_in.refs_1_, bf16[1024,1024]{1,0:T(8,128)(2,1)S(1)} %get-tuple-element.131.w_out.refs_2_), custom_call_target="tpu_custom_call" | custom-call | flops 1 | bytes 1 | tf_op jit(solution)/shard_map/cond/branch_1_fun/down/pallas_call | solution.py:92
  89.0 3.1 %down.13 = (bf16[120,1024]{1,0:T(8,128)(2,1)}, bf16[120,1024]{1,0:T(8,128)(2,1)}) custom-call(s32[2]{0:T(128)S(1)} %get-tuple-element.121.ids, f32[128,1024]{1,0:T(8,128)S(1)} %get-tuple-element.144.out_rows, f32[128,1024]{1,0:T(8,128)S(1)} %get-tuple-element.145.grad_rows, bf16[128,1536]{1,0:T(8,128)(2,1)} %collective-permute-done.10.core, ...), custom_call_target="tpu_custom_call" | custom-call | flops 1 | bytes 1 | tf_op jit(solution)/shard_map/cond/branch_1_fun/down/pallas_call | solution.py:92
  92.1 1.6 %collective-permute-start.23 = (bf16[64,1536]{1,0:T(8,128)(2,1)S(1)}, bf16[64,1536]{1,0:T(8,128)(2,1)S(1)}, u32[]{:S(2)}, u32[]{:S(2)}) collective-permute-start(bf16[64,1536]{1,0:T(8,128)(2,1)S(1)} %get-tuple-element.271), channel_id=1, source_target_pairs={{0,16},{8,24},{16,0},{24,8},{1,17},{9,25},{17,1},{25,9},{2,18},{10... | collective-permute-start | bytes 589832 | tf_op jit(solution)/shard_map/ppermute | solution.py:491
  93.7 3.5 %collective-permute-start.30 = (bf16[120,1024]{1,0:T(8,128)(2,1)}, bf16[120,1024]{1,0:T(8,128)(2,1)S(1)}, u32[]{:S(2)}, u32[]{:S(2)}) collective-permute-start(bf16[120,1024]{1,0:T(8,128)(2,1)} %get-tuple-element.287), channel_id=1, source_target_pairs={{0,7},{1,6},{2,5},{3,4},{4,3},{5,2},{6,1},{7,0},{8,15},{9,14},{10,... | collective-permute-start | bytes 737288 | tf_op jit(solution)/shard_map/ppermute | solution.py:488
  97.5 1.7 %collective-permute-start.22 = (bf16[120,1024]{1,0:T(8,128)(2,1)}, bf16[120,1024]{1,0:T(8,128)(2,1)S(1)}, u32[]{:S(2)}, u32[]{:S(2)}) collective-permute-start(bf16[120,1024]{1,0:T(8,128)(2,1)} %get-tuple-element.268), channel_id=1, source_target_pairs={{0,2},{1,3},{2,0},{3,1},{4,6},{5,7},{6,4},{7,5},{8,10},{9,11},{10,... | collective-permute-start | bytes 737288 | tf_op jit(solution)/shard_map/ppermute | solution.py:488
  99.5 7.5 %conditional.7 = (bf16[64,1024]{1,0:T(8,128)(2,1)S(1)}, bf16[64,1024]{1,0:T(8,128)(2,1)S(1)}, bf16[64,1536]{1,0:T(8,128)(2,1)}, bf16[64,1536]{1,0:T(8,128)(2,1)}...) conditional(s32[]{:T(128)} %convert_element_type.2, () %tuple.76, (f32[64,1536]{1,0:T(8,128)S(1)}, ...), branch_computations={%region_6.7_spmd, %region_7.8_spmd} | conditional | flops 3 | bytes 901180 | solution.py:503
  100.3 3.8 %down.14 = (f32[64,1024]{1,0:T(8,128)S(1)}, f32[64,1024]{1,0:T(8,128)S(1)}, bf16[1024,2048]{1,0:T(8,128)(2,1)S(1)}, bf16[1024,1024]{1,0:T(8,128)(2,1)S(1)}) custom-call(s32[2]{0:T(128)S(1)} %get-tuple-element.159.ids, bf16[64,1536]{1,0:T(8,128)(2,1)} %act.9.own, bf16[1024,2048]{1,0:T(8,128)(2,1)} %get-tuple-element.160.far_in, ...), custom_call_target="tpu_custom_call" | custom-call | flops 1 | bytes 1 | tf_op jit(solution)/shard_map/cond/branch_1_fun/down/pallas_call | solution.py:335
  104.1 2.8 %down.15 = (bf16[120,512]{1,0:T(8,128)(2,1)}, bf16[120,512]{1,0:T(8,128)(2,1)}) custom-call(s32[2]{0:T(128)S(1)} %get-tuple-element.159.ids, f32[64,1024]{1,0:T(8,128)S(1)} %get-tuple-element.162.out_rows, f32[64,1024]{1,0:T(8,128)S(1)} %get-tuple-element.163.grad_rows, bf16[64,1536]{1,0:T(8,128)(2,1)} %collective-permute-done.11.core, ...), custom_call_target="tpu_custom_call" | custom-call | flops 1 | bytes 1 | tf_op jit(solution)/shard_map/cond/branch_1_fun/down/pallas_call | solution.py:92
  106.9 2.9 %collective-permute-start.24 = (bf16[120,512]{1,0:T(8,128)(2,1)}, bf16[120,512]{1,0:T(8,128)(2,1)S(1)}, u32[]{:S(2)}, u32[]{:S(2)}) collective-permute-start(bf16[120,512]{1,0:T(8,128)(2,1)} %get-tuple-element.274), channel_id=1, source_target_pairs={{0,3},{1,2},{2,1},{3,0},{4,7},{5,6},{6,5},{7,4},{8,11},{9,10},{10,... | collective-permute-start | bytes 368648 | tf_op jit(solution)/shard_map/ppermute | solution.py:488
  109.9 2.4 %final.3 = (f32[192,1024]{1,0:T(8,128)S(1)}, f32[192,1024]{1,0:T(8,128)S(1)}) custom-call(s32[2]{0:T(128)S(1)} %pad_add_fusion.refs_0_, s32[2,192]{1,0:T(2,128)S(1)} %bitcast.9, f32[2,192]{1,0:T(2,128)S(1)} %bitcast.13, bf16[120,1024]{1,0:T(8,128)(2,1)} %get-tuple-element.282.refs_3_, bf16[120,1024]{1,0:T(8,128)(2,1)S(1)} %collective-permute-done.28.refs_4_, ...), custom_call_target="tpu_custom_call" | custom-call | flops 1 | bytes 1 | tf_op jit(solution)/shard_map/final/pallas_call | solution.py:92
  112.3 6.7 %grads.1 = (bf16[1024,2048]{1,0:T(8,128)(2,1)}, bf16[1024,1024]{1,0:T(8,128)(2,1)}) custom-call(s32[2]{0:T(128)S(1)} %pad_add_fusion.refs_0_, bf16[128,1024]{1,0:T(8,128)(2,1)} %get-tuple-element.294.refs_1_, bf16[128,1024]{1,0:T(8,128)(2,1)} %get-tuple-element.295.refs_2_, bf16[128,1536]{1,0:T(8,128)(2,1)S(1)} %get-tuple-element.296.refs_3_, ...), custom_call_target="tpu_custom_call" | custom-call | flops 1 | bytes 1 | tf_op jit(solution)/shard_map/grads/pallas_call | solution.py:395
  119.1 1.5 %final.4 = (f32[192,1024]{1,0:T(8,128)S(1)}, f32[192,1024]{1,0:T(8,128)S(1)}) custom-call(s32[2]{0:T(128)S(1)} %pad_add_fusion.refs_0_, s32[2,192]{1,0:T(2,128)S(1)} %bitcast.10, f32[2,192]{1,0:T(2,128)S(1)} %bitcast.14, bf16[120,1024]{1,0:T(8,128)(2,1)S(1)} %collective-permute-done.29.refs_3_, bf16[120,1024]{1,0:T(8,128)(2,1)S(1)} %collective-permute-done.30.refs_4_, ...), custom_call_target="tpu_custom_call" | custom-call | flops 1 | bytes 1 | tf_op jit(solution)/shard_map/final/pallas_call | solution.py:92
  120.7 2.4 %final.5 = (bf16[192,1024]{1,0:T(8,128)(2,1)}, bf16[192,1024]{1,0:T(8,128)(2,1)}) custom-call(s32[2]{0:T(128)S(1)} %pad_add_fusion.refs_0_, s32[2,192]{1,0:T(2,128)S(1)} %bitcast.11, f32[2,192]{1,0:T(2,128)S(1)} %bitcast.15, bf16[120,1024]{1,0:T(8,128)(2,1)S(1)} %collective-permute-done.22.refs_3_, bf16[120,512]{1,0:T(8,128)(2,1)S(1)} %collective-permute-done.24.refs_4_, ...), custom_call_target="tpu_custom_call" | custom-call | flops 1 | bytes 1 | tf_op jit(solution)/shard_map/final/pallas_call | solution.py:92
  (102 shorter events, 5.6 us)
Async XLA Ops:
  4.5 9.2 %collective-permute-start.15 = (bf16[120,1024]{1,0:T(8,128)(2,1)}, bf16[120,1024]{1,0:T(8,128)(2,1)S(1)}, u32[]{:S(2)}, u32[]{:S(2)}) collective-permute-start(bf16[120,1024]{1,0:T(8,128)(2,1)} %get-tuple-element.249), channel_id=1, source_target_pairs={{0,1},{1,0},{2,3},{3,2},{4,5},{5,4},{6,7},{7,6},{8,9},{9,8},{10,11... | collective-permute-start | bytes 737288 | tf_op jit(solution)/shard_map/ppermute | solution.py:488
  7.5 20.2 %collective-permute-start.12 = (bf16[120,1024]{1,0:T(8,128)(2,1)}, bf16[120,1024]{1,0:T(8,128)(2,1)S(1)}, u32[]{:S(2)}, u32[]{:S(2)}) collective-permute-start(bf16[120,1024]{1,0:T(8,128)(2,1)} %get-tuple-element.245), channel_id=1, source_target_pairs={{0,4},{1,5},{2,6},{3,7},{4,0},{5,1},{6,2},{7,3},{8,12},{9,13},{10,... | collective-permute-start | bytes 737288 | tf_op jit(solution)/shard_map/ppermute | solution.py:488
  10.1 21.6 %collective-permute-start.13 = (bf16[120,1024]{1,0:T(8,128)(2,1)}, bf16[120,1024]{1,0:T(8,128)(2,1)S(1)}, u32[]{:S(2)}, u32[]{:S(2)}) collective-permute-start(bf16[120,1024]{1,0:T(8,128)(2,1)} %get-tuple-element.246), channel_id=1, source_target_pairs={{0,5},{1,4},{2,7},{3,6},{4,1},{5,0},{6,3},{7,2},{8,13},{9,12},{10,... | collective-permute-start | bytes 737288 | tf_op jit(solution)/shard_map/ppermute | solution.py:488
  10.1 21.6 %collective-permute-start.14 = (bf16[120,1024]{1,0:T(8,128)(2,1)}, bf16[120,1024]{1,0:T(8,128)(2,1)S(1)}, u32[]{:S(2)}, u32[]{:S(2)}) collective-permute-start(bf16[120,1024]{1,0:T(8,128)(2,1)} %get-tuple-element.247), channel_id=1, source_target_pairs={{0,2},{1,3},{2,0},{3,1},{4,6},{5,7},{6,4},{7,5},{8,10},{9,11},{10,... | collective-permute-start | bytes 737288 | tf_op jit(solution)/shard_map/ppermute | solution.py:488
  18.0 2.8 %collective-permute-start = (bf16[128,1536]{1,0:T(8,128)(2,1)S(1)}, bf16[128,1536]{1,0:T(8,128)(2,1)}, u32[]{:S(2)}, u32[]{:S(2)}) collective-permute-start(bf16[128,1536]{1,0:T(8,128)(2,1)S(1)} %get-tuple-element.79), channel_id=1, source_target_pairs={{0,8},{8,0},{16,24},{24,16},{1,9},{9,1},{17,25},{25,17},{2,10},{10... | collective-permute-start | bytes 1179656 | tf_op jit(solution)/shard_map/cond/branch_1_fun/ppermute | solution.py:491
  22.1 14.5 %collective-permute-start.17 = (bf16[128,768]{1,0:T(8,128)(2,1)S(1)}, bf16[128,768]{1,0:T(8,128)(2,1)S(1)}, u32[]{:S(2)}, u32[]{:S(2)}) collective-permute-start(bf16[128,768]{1,0:T(8,128)(2,1)S(1)} %get-tuple-element.250), channel_id=1, source_target_pairs={{0,16},{8,24},{16,0},{24,8},{1,17},{9,25},{17,1},{25,9},{2,18},{10... | collective-permute-start | bytes 589832 | tf_op jit(solution)/shard_map/ppermute | solution.py:491
  23.9 12.7 %collective-permute-start.18 = (bf16[128,768]{1,0:T(8,128)(2,1)S(1)}, bf16[128,768]{1,0:T(8,128)(2,1)S(1)}, u32[]{:S(2)}, u32[]{:S(2)}) collective-permute-start(bf16[128,768]{1,0:T(8,128)(2,1)S(1)} %get-tuple-element.251), channel_id=1, source_target_pairs={{0,16},{8,24},{16,0},{24,8},{1,17},{9,25},{17,1},{25,9},{2,18},{10... | collective-permute-start | bytes 589832 | tf_op jit(solution)/shard_map/ppermute | solution.py:491
  31.8 31.2 %collective-permute-start.16 = (bf16[120,1024]{1,0:T(8,128)(2,1)}, bf16[120,1024]{1,0:T(8,128)(2,1)S(1)}, u32[]{:S(2)}, u32[]{:S(2)}) collective-permute-start(bf16[120,1024]{1,0:T(8,128)(2,1)} %get-tuple-element.252), channel_id=1, source_target_pairs={{0,6},{1,7},{2,4},{3,5},{4,2},{5,3},{6,0},{7,1},{8,14},{9,15},{10,... | collective-permute-start | bytes 737288 | tf_op jit(solution)/shard_map/ppermute | solution.py:488
  35.3 27.6 %collective-permute-start.19 = (bf16[120,1024]{1,0:T(8,128)(2,1)}, bf16[120,1024]{1,0:T(8,128)(2,1)S(1)}, u32[]{:S(2)}, u32[]{:S(2)}) collective-permute-start(bf16[120,1024]{1,0:T(8,128)(2,1)} %get-tuple-element.260), channel_id=1, source_target_pairs={{0,7},{1,6},{2,5},{3,4},{4,3},{5,2},{6,1},{7,0},{8,15},{9,14},{10,... | collective-permute-start | bytes 737288 | tf_op jit(solution)/shard_map/ppermute | solution.py:488
  36.6 31.8 %collective-permute-start.21 = (bf16[120,1024]{1,0:T(8,128)(2,1)}, bf16[120,1024]{1,0:T(8,128)(2,1)}, u32[]{:S(2)}, u32[]{:S(2)}) collective-permute-start(bf16[120,1024]{1,0:T(8,128)(2,1)} %get-tuple-element.265), channel_id=1, source_target_pairs={{0,3},{1,2},{2,1},{3,0},{4,7},{5,6},{6,5},{7,4},{8,11},{9,10},{10,... | collective-permute-start | bytes 737288 | tf_op jit(solution)/shard_map/ppermute | solution.py:488
  40.1 1.8 %collective-permute-start.1 = (bf16[128,1536]{1,0:T(8,128)(2,1)S(1)}, bf16[128,1536]{1,0:T(8,128)(2,1)S(1)}, u32[]{:S(2)}, u32[]{:S(2)}) collective-permute-start(bf16[128,1536]{1,0:T(8,128)(2,1)S(1)} %get-tuple-element.92), channel_id=1, source_target_pairs={{0,8},{8,0},{16,24},{24,16},{1,9},{9,1},{17,25},{25,17},{2,10},{10... | collective-permute-start | bytes 1179656 | tf_op jit(solution)/shard_map/cond/branch_1_fun/ppermute | solution.py:491
  43.5 7.3 %copy-start.2 = (bf16[128,1536]{1,0:T(8,128)(2,1)}, bf16[128,1536]{1,0:T(8,128)(2,1)S(1)}, u32[]{:S(2)}) copy-start(bf16[128,1536]{1,0:T(8,128)(2,1)S(1)} %act.5.own) | copy-start | bytes 1179652 | tf_op jit(solution)/shard_map/cond
  43.5 3.9 %collective-permute-start.2 = (bf16[128,1536]{1,0:T(8,128)(2,1)S(1)}, bf16[128,1536]{1,0:T(8,128)(2,1)S(1)}, u32[]{:S(2)}, u32[]{:S(2)}) collective-permute-start(bf16[128,1536]{1,0:T(8,128)(2,1)S(1)} %act.5.own), channel_id=1, source_target_pairs={{0,8},{8,0},{16,24},{24,16},{1,9},{9,1},{17,25},{25,17},{2,10},{10... | collective-permute-start | bytes 1179656 | tf_op jit(solution)/shard_map/cond/branch_1_fun/ppermute | solution.py:491
  43.7 11.4 %collective-permute-start.3 = (bf16[128,1536]{1,0:T(8,128)(2,1)S(1)}, bf16[128,1536]{1,0:T(8,128)(2,1)S(1)}, u32[]{:S(2)}, u32[]{:S(2)}) collective-permute-start(bf16[128,1536]{1,0:T(8,128)(2,1)S(1)} %total.4), channel_id=1, source_target_pairs={{0,16},{8,24},{16,0},{24,8},{1,17},{9,25},{17,1},{25,9},{2,18},{10... | collective-permute-start | bytes 1179656 | tf_op jit(solution)/shard_map/cond/branch_1_fun/ppermute | solution.py:491
  47.3 8.7 %copy-start.6 = (f32[64,1536]{1,0:T(8,128)}, f32[64,1536]{1,0:T(8,128)S(1)}, u32[]{:S(2)}) copy-start(f32[64,1536]{1,0:T(8,128)S(1)} %get-tuple-element.352.next_keep) | copy-start | bytes 1179652 | tf_op jit(solution)/shard_map/cond
  47.3 8.7 %copy-start.4 = (bf16[128,1536]{1,0:T(8,128)(2,1)}, bf16[128,1536]{1,0:T(8,128)(2,1)S(1)}, u32[]{:S(2)}) copy-start(bf16[128,1536]{1,0:T(8,128)(2,1)S(1)} %collective-permute-done.2.core) | copy-start | bytes 1179652 | tf_op jit(solution)/shard_map/cond
  50.8 4.3 %collective-permute-start.4 = (bf16[64,1536]{1,0:T(8,128)(2,1)S(1)}, bf16[64,1536]{1,0:T(8,128)(2,1)S(1)}, u32[]{:S(2)}, u32[]{:S(2)}) collective-permute-start(bf16[64,1536]{1,0:T(8,128)(2,1)S(1)} %get-tuple-element.109), channel_id=1, source_target_pairs={{0,8},{8,0},{16,24},{24,16},{1,9},{9,1},{17,25},{25,17},{2,10},{10... | collective-permute-start | bytes 589832 | tf_op jit(solution)/shard_map/cond/branch_1_fun/ppermute | solution.py:491
  56.0 2.1 %collective-permute-start.5 = (bf16[128,1536]{1,0:T(8,128)(2,1)}, bf16[128,1536]{1,0:T(8,128)(2,1)}, u32[]{:S(2)}, u32[]{:S(2)}) collective-permute-start(bf16[128,1536]{1,0:T(8,128)(2,1)} %get-tuple-element.346.own), channel_id=1, source_target_pairs={{0,8},{8,0},{16,24},{24,16},{1,9},{9,1},{17,25},{25,17},{2,10},{10... | collective-permute-start | bytes 1179656 | tf_op jit(solution)/shard_map/cond/branch_1_fun/ppermute | solution.py:491
  58.1 3.3 %copy-start.3 = (bf16[128,1536]{1,0:T(8,128)(2,1)S(1)}, bf16[128,1536]{1,0:T(8,128)(2,1)}, u32[]{:S(2)}) copy-start(bf16[128,1536]{1,0:T(8,128)(2,1)} %copy-done.2) | copy-start | bytes 1179652 | tf_op jit(solution)/shard_map/cond
  58.1 3.3 %copy-start.5 = (bf16[128,1536]{1,0:T(8,128)(2,1)S(1)}, bf16[128,1536]{1,0:T(8,128)(2,1)}, u32[]{:S(2)}) copy-start(bf16[128,1536]{1,0:T(8,128)(2,1)} %copy-done.4) | copy-start | bytes 1179652 | tf_op jit(solution)/shard_map/cond
  58.1 3.3 %copy-start.7 = (f32[64,1536]{1,0:T(8,128)S(1)}, f32[64,1536]{1,0:T(8,128)}, u32[]{:S(2)}) copy-start(f32[64,1536]{1,0:T(8,128)} %copy-done.6) | copy-start | bytes 1179652 | tf_op jit(solution)/shard_map/cond
  58.1 3.3 %copy-start.11 = (bf16[128,1024]{1,0:T(8,128)(2,1)S(1)}, bf16[128,1024]{1,0:T(8,128)(2,1)}, u32[]{:S(2)}) copy-start(bf16[128,1024]{1,0:T(8,128)(2,1)} %copy-done.10) | copy-start | bytes 786436 | tf_op jit(solution)/shard_map/cond
  58.1 3.3 %copy-start.13 = (bf16[128,1024]{1,0:T(8,128)(2,1)S(1)}, bf16[128,1024]{1,0:T(8,128)(2,1)}, u32[]{:S(2)}) copy-start(bf16[128,1024]{1,0:T(8,128)(2,1)} %copy-done.12) | copy-start | bytes 786436 | tf_op jit(solution)/shard_map/cond
  61.4 7.4 %collective-permute-start.20 = (bf16[64,1536]{1,0:T(8,128)(2,1)S(1)}, bf16[64,1536]{1,0:T(8,128)(2,1)S(1)}, u32[]{:S(2)}, u32[]{:S(2)}) collective-permute-start(bf16[64,1536]{1,0:T(8,128)(2,1)S(1)} %get-tuple-element.263), channel_id=1, source_target_pairs={{0,16},{8,24},{16,0},{24,8},{1,17},{9,25},{17,1},{25,9},{2,18},{10... | collective-permute-start | bytes 589832 | tf_op jit(solution)/shard_map/ppermute | solution.py:491
  62.9 30.7 %collective-permute-start.28 = (bf16[120,1024]{1,0:T(8,128)(2,1)}, bf16[120,1024]{1,0:T(8,128)(2,1)S(1)}, u32[]{:S(2)}, u32[]{:S(2)}) collective-permute-start(bf16[120,1024]{1,0:T(8,128)(2,1)} %get-tuple-element.284), channel_id=1, source_target_pairs={{0,1},{1,0},{2,3},{3,2},{4,5},{5,4},{6,7},{7,6},{8,9},{9,8},{10,11... | collective-permute-start | bytes 737288 | tf_op jit(solution)/shard_map/ppermute | solution.py:488
  63.4 30.2 %collective-permute-start.27 = (bf16[120,1024]{1,0:T(8,128)(2,1)}, bf16[120,1024]{1,0:T(8,128)(2,1)S(1)}, u32[]{:S(2)}, u32[]{:S(2)}) collective-permute-start(bf16[120,1024]{1,0:T(8,128)(2,1)} %get-tuple-element.280), channel_id=1, source_target_pairs={{0,5},{1,4},{2,7},{3,6},{4,1},{5,0},{6,3},{7,2},{8,13},{9,12},{10,... | collective-permute-start | bytes 737288 | tf_op jit(solution)/shard_map/ppermute | solution.py:488
  68.4 25.3 %collective-permute-start.26 = (bf16[120,1024]{1,0:T(8,128)(2,1)}, bf16[120,1024]{1,0:T(8,128)(2,1)S(1)}, u32[]{:S(2)}, u32[]{:S(2)}) collective-permute-start(bf16[120,1024]{1,0:T(8,128)(2,1)} %get-tuple-element.278), channel_id=1, source_target_pairs={{0,4},{1,5},{2,6},{3,7},{4,0},{5,1},{6,2},{7,3},{8,12},{9,13},{10,... | collective-permute-start | bytes 737288 | tf_op jit(solution)/shard_map/ppermute | solution.py:488
  72.2 14.6 %copy-start.16 = (bf16[128,1024]{1,0:T(8,128)(2,1)}, bf16[128,1024]{1,0:T(8,128)(2,1)S(1)}, u32[]{:S(2)}) copy-start(bf16[128,1024]{1,0:T(8,128)(2,1)S(1)} %get-tuple-element.378.grads) | copy-start | bytes 786436 | tf_op jit(solution)/shard_map/cond
  72.2 1.8 %collective-permute-start.6 = (bf16[128,1536]{1,0:T(8,128)(2,1)S(1)}, bf16[128,1536]{1,0:T(8,128)(2,1)S(1)}, u32[]{:S(2)}, u32[]{:S(2)}) collective-permute-start(bf16[128,1536]{1,0:T(8,128)(2,1)S(1)} %get-tuple-element.128), channel_id=1, source_target_pairs={{0,8},{8,0},{16,24},{24,16},{1,9},{9,1},{17,25},{25,17},{2,10},{10... | collective-permute-start | bytes 1179656 | tf_op jit(solution)/shard_map/cond/branch_1_fun/ppermute | solution.py:491
  74.2 7.7 %copy-start.17 = (bf16[64,1536]{1,0:T(8,128)(2,1)}, bf16[64,1536]{1,0:T(8,128)(2,1)S(1)}, u32[]{:S(2)}) copy-start(bf16[64,1536]{1,0:T(8,128)(2,1)S(1)} %act.7.own) | copy-start | bytes 589828 | tf_op jit(solution)/shard_map/cond
  74.2 4.5 %collective-permute-start.7 = (bf16[64,1536]{1,0:T(8,128)(2,1)S(1)}, bf16[64,1536]{1,0:T(8,128)(2,1)S(1)}, u32[]{:S(2)}, u32[]{:S(2)}) collective-permute-start(bf16[64,1536]{1,0:T(8,128)(2,1)S(1)} %act.7.own), channel_id=1, source_target_pairs={{0,8},{8,0},{16,24},{24,16},{1,9},{9,1},{17,25},{25,17},{2,10},{10... | collective-permute-start | bytes 589832 | tf_op jit(solution)/shard_map/cond/branch_1_fun/ppermute | solution.py:491
  74.7 11.2 %collective-permute-start.8 = (bf16[128,1536]{1,0:T(8,128)(2,1)S(1)}, bf16[128,1536]{1,0:T(8,128)(2,1)S(1)}, u32[]{:S(2)}, u32[]{:S(2)}) collective-permute-start(bf16[128,1536]{1,0:T(8,128)(2,1)S(1)} %total.5), channel_id=1, source_target_pairs={{0,16},{8,24},{16,0},{24,8},{1,17},{9,25},{17,1},{25,9},{2,18},{10... | collective-permute-start | bytes 1179656 | tf_op jit(solution)/shard_map/cond/branch_1_fun/ppermute | solution.py:491
  78.7 8.1 %copy-start.8 = (f32[64,1536]{1,0:T(8,128)}, f32[64,1536]{1,0:T(8,128)S(1)}, u32[]{:S(2)}) copy-start(f32[64,1536]{1,0:T(8,128)S(1)} %get-tuple-element.385.next_keep) | copy-start | bytes 1179652 | tf_op jit(solution)/shard_map/cond
  78.7 8.1 %copy-start.18 = (bf16[64,1536]{1,0:T(8,128)(2,1)}, bf16[64,1536]{1,0:T(8,128)(2,1)S(1)}, u32[]{:S(2)}) copy-start(bf16[64,1536]{1,0:T(8,128)(2,1)S(1)} %collective-permute-done.7.core) | copy-start | bytes 589828 | tf_op jit(solution)/shard_map/cond
  82.0 1.4 %collective-permute-start.9 = (bf16[64,1536]{1,0:T(8,128)(2,1)S(1)}, bf16[64,1536]{1,0:T(8,128)(2,1)S(1)}, u32[]{:S(2)}, u32[]{:S(2)}) collective-permute-start(bf16[64,1536]{1,0:T(8,128)(2,1)S(1)} %get-tuple-element.142), channel_id=1, source_target_pairs={{0,8},{8,0},{16,24},{24,16},{1,9},{9,1},{17,25},{25,17},{2,10},{10... | collective-permute-start | bytes 589832 | tf_op jit(solution)/shard_map/cond/branch_1_fun/ppermute | solution.py:491
  83.4 5.5 %copy-start.19 = (bf16[64,1536]{1,0:T(8,128)(2,1)}, bf16[64,1536]{1,0:T(8,128)(2,1)S(1)}, u32[]{:S(2)}) copy-start(bf16[64,1536]{1,0:T(8,128)(2,1)S(1)} %collective-permute-done.9.next_core) | copy-start | bytes 589828 | tf_op jit(solution)/shard_map/cond
  86.8 2.1 %collective-permute-start.10 = (bf16[128,1536]{1,0:T(8,128)(2,1)}, bf16[128,1536]{1,0:T(8,128)(2,1)}, u32[]{:S(2)}, u32[]{:S(2)}) collective-permute-start(bf16[128,1536]{1,0:T(8,128)(2,1)} %get-tuple-element.379.own), channel_id=1, source_target_pairs={{0,8},{8,0},{16,24},{24,16},{1,9},{9,1},{17,25},{25,17},{2,10},{10... | collective-permute-start | bytes 1179656 | tf_op jit(solution)/shard_map/cond/branch_1_fun/ppermute | solution.py:491
  92.1 7.4 %collective-permute-start.23 = (bf16[64,1536]{1,0:T(8,128)(2,1)S(1)}, bf16[64,1536]{1,0:T(8,128)(2,1)S(1)}, u32[]{:S(2)}, u32[]{:S(2)}) collective-permute-start(bf16[64,1536]{1,0:T(8,128)(2,1)S(1)} %get-tuple-element.271), channel_id=1, source_target_pairs={{0,16},{8,24},{16,0},{24,8},{1,17},{9,25},{17,1},{25,9},{2,18},{10... | collective-permute-start | bytes 589832 | tf_op jit(solution)/shard_map/ppermute | solution.py:491
  93.7 25.4 %collective-permute-start.30 = (bf16[120,1024]{1,0:T(8,128)(2,1)}, bf16[120,1024]{1,0:T(8,128)(2,1)S(1)}, u32[]{:S(2)}, u32[]{:S(2)}) collective-permute-start(bf16[120,1024]{1,0:T(8,128)(2,1)} %get-tuple-element.287), channel_id=1, source_target_pairs={{0,7},{1,6},{2,5},{3,4},{4,3},{5,2},{6,1},{7,0},{8,15},{9,14},{10,... | collective-permute-start | bytes 737288 | tf_op jit(solution)/shard_map/ppermute | solution.py:488
  97.2 21.9 %collective-permute-start.29 = (bf16[120,1024]{1,0:T(8,128)(2,1)}, bf16[120,1024]{1,0:T(8,128)(2,1)S(1)}, u32[]{:S(2)}, u32[]{:S(2)}) collective-permute-start(bf16[120,1024]{1,0:T(8,128)(2,1)} %get-tuple-element.285), channel_id=1, source_target_pairs={{0,6},{1,7},{2,4},{3,5},{4,2},{5,3},{6,0},{7,1},{8,14},{9,15},{10,... | collective-permute-start | bytes 737288 | tf_op jit(solution)/shard_map/ppermute | solution.py:488
  97.5 23.1 %collective-permute-start.22 = (bf16[120,1024]{1,0:T(8,128)(2,1)}, bf16[120,1024]{1,0:T(8,128)(2,1)S(1)}, u32[]{:S(2)}, u32[]{:S(2)}) collective-permute-start(bf16[120,1024]{1,0:T(8,128)(2,1)} %get-tuple-element.268), channel_id=1, source_target_pairs={{0,2},{1,3},{2,0},{3,1},{4,6},{5,7},{6,4},{7,5},{8,10},{9,11},{10,... | collective-permute-start | bytes 737288 | tf_op jit(solution)/shard_map/ppermute | solution.py:488
  99.5 10.4 %copy-start = (s32[192,2]{0,1:T(2,128)S(1)}, s32[192,2]{0,1:T(2,128)}, u32[]{:S(2)}) copy-start(s32[192,2]{0,1:T(2,128)} %param.15) | copy-start | bytes 4612
  99.5 10.4 %copy-start.1 = (f32[192,2]{0,1:T(2,128)S(1)}, f32[192,2]{0,1:T(2,128)}, u32[]{:S(2)}) copy-start(f32[192,2]{0,1:T(2,128)} %param.16) | copy-start | bytes 4612
  100.3 3.8 %collective-permute-start.11 = (bf16[64,1536]{1,0:T(8,128)(2,1)}, bf16[64,1536]{1,0:T(8,128)(2,1)}, u32[]{:S(2)}, u32[]{:S(2)}) collective-permute-start(bf16[64,1536]{1,0:T(8,128)(2,1)} %act.9.own), channel_id=1, source_target_pairs={{0,8},{8,0},{16,24},{24,16},{1,9},{9,1},{17,25},{25,17},{2,10},{10... | collective-permute-start | bytes 589832 | tf_op jit(solution)/shard_map/cond/branch_1_fun/ppermute | solution.py:491
  106.9 5.4 %copy-start.23 = (bf16[64,1024]{1,0:T(8,128)(2,1)}, bf16[64,1024]{1,0:T(8,128)(2,1)S(1)}, u32[]{:S(2)}) copy-start(bf16[64,1024]{1,0:T(8,128)(2,1)S(1)} %get-tuple-element.309.refs_17_) | copy-start | bytes 393220
  106.9 5.4 %copy-start.24 = (bf16[64,1024]{1,0:T(8,128)(2,1)}, bf16[64,1024]{1,0:T(8,128)(2,1)S(1)}, u32[]{:S(2)}) copy-start(bf16[64,1024]{1,0:T(8,128)(2,1)S(1)} %get-tuple-element.310.refs_18_) | copy-start | bytes 393220
  106.9 13.7 %collective-permute-start.24 = (bf16[120,512]{1,0:T(8,128)(2,1)}, bf16[120,512]{1,0:T(8,128)(2,1)S(1)}, u32[]{:S(2)}, u32[]{:S(2)}) collective-permute-start(bf16[120,512]{1,0:T(8,128)(2,1)} %get-tuple-element.274), channel_id=1, source_target_pairs={{0,3},{1,2},{2,1},{3,0},{4,7},{5,6},{6,5},{7,4},{8,11},{9,10},{10,... | collective-permute-start | bytes 368648 | tf_op jit(solution)/shard_map/ppermute | solution.py:488
  109.9 10.8 %collective-permute-start.25 = (bf16[120,512]{1,0:T(8,128)(2,1)}, bf16[120,512]{1,0:T(8,128)(2,1)S(1)}, u32[]{:S(2)}, u32[]{:S(2)}) collective-permute-start(bf16[120,512]{1,0:T(8,128)(2,1)} %get-tuple-element.275), channel_id=1, source_target_pairs={{0,3},{1,2},{2,1},{3,0},{4,7},{5,6},{6,5},{7,4},{8,11},{9,10},{10,... | collective-permute-start | bytes 368648 | tf_op jit(solution)/shard_map/ppermute | solution.py:488
  (10 other events, 24.5 us)

commit v6 on v5

--- a/solution.py
+++ b/solution.py
@@ -11,6 +11,7 @@
 GRADS_LIMIT = 32 * 1024 * 1024
 PREP_LIMIT = 60 * 1024 * 1024
 COST = pl.CostEstimate(flops=1, bytes_accessed=1, transcendentals=0)
+LONG = pl.CostEstimate(flops=2 * 10**10, bytes_accessed=1, transcendentals=0)
 
 
 def dot(a, b):
@@ -87,7 +88,7 @@
     )(ids, tokens, routes.T, weight.T, cotangent)
 
 
-def call(kernel, name, out_shapes, scalars, *arrays):
+def call(kernel, name, out_shapes, scalars, *arrays, cost=COST):
     whole = pl.BlockSpec(memory_space=pltpu.VMEM)
     return pl.pallas_call(
         kernel,
@@ -95,7 +96,7 @@
         in_specs=[pl.BlockSpec(memory_space=pltpu.SMEM)] * len(scalars) + [whole] * len(arrays),
         out_specs=jax.tree.map(lambda _: whole, out_shapes),
         compiler_params=pltpu.CompilerParams(vmem_limit_bytes=VMEM_LIMIT),
-        cost_estimate=COST,
+        cost_estimate=cost,
         name=name,
     )(*scalars, *arrays)
 
@@ -216,6 +217,7 @@
         [ids],
         *blocks,
         *weights,
+        cost=LONG,
     )
 
 

time: 123 us -> 122 us (level)
  waiting for transfers between devices: 18.5 us -> 16 us
    ppermute x16, waiting for transfers between devices: 9.21 us -> 6.67 us  [beside(): return lax.ppermute(x, 'dp', [(i, i ^ s) for i in range(n_dp)])]
  transfers between devices with their start and end apart: 31 -> 31, of which waited for: 10 -> 10; matrix products, arithmetic and copies ran while one was open for 0% -> 0% of each run, Pallas kernels for 50% -> 51%
where the time goes in v6:
time: 122 us; the launch traced here: 121 us
  Pallas kernels  67.7 us (55%)
  starting transfers between devices  36 us (30%)
  waiting for transfers between devices  16 us (13%)
    pallas_call x23, Pallas kernels, call(): pl.pallas_call(kernel, out_shape=out_shapes, in_specs=[pl.BlockSpec(memor...  42.2 us
    ppermute x15, starting transfers between devices, across(): lax.ppermute(x, 'expert', [(i, i ^ s) for i in range(n_expert)])  26.3 us
    pallas_call x3, Pallas kernels, other_half(): pl.pallas_call(kernel, out_shape=[shape((rows, features), BF), shape((row...  11.2 us
    ppermute x16, starting transfers between devices, beside(): return lax.ppermute(x, 'dp', [(i, i ^ s) for i in range(n_dp)])  9.66 us
    ppermute x15, waiting for transfers between devices, across(): lax.ppermute(x, 'expert', [(i, i ^ s) for i in range(n_expert)])  9.29 us
    pallas_call x1, Pallas kernels, grads_step(): pl.pallas_call(lambda *refs: grads_kernel(len(groups), *refs), out_shape=...  6.71 us
    ppermute x16, waiting for transfers between devices, beside(): return lax.ppermute(x, 'dp', [(i, i ^ s) for i in range(n_dp)])  6.67 us
    pallas_call x1, Pallas kernels, down_own_alone(): pl.pallas_call(kernel, out_shape=[sums, sums, shape(w_in.shape, BF), shap...  3.83 us
  transfers between devices with their start and end apart: 31, of which 10 were waited for; matrix products, arithmetic and copies ran while one was open for 0% of the time, Pallas kernels for 51%

profile of v6, /device:TPU:0, one launch (start us, length us, event | category | flops | bytes accessed | tf_op | source)
XLA Modules:
  0.0 121.1 jit_solution(7792258427508698241)
XLA Ops:
  0.7 3.8 %prep.1 = (bf16[120,1024]{1,0:T(8,128)(2,1)S(1)}, bf16[120,1024]{1,0:T(8,128)(2,1)}, bf16[120,1024]{1,0:T(8,128)(2,1)}, bf16[120,1024]{1,0:T(8,128)(2,1)}, bf16[...) custom-call(s32[2]{0:T(128)S(1)} %pad_add_fusion.refs_0_, ...), custom_call_target="tpu_custom_call" | custom-call | flops 1 | bytes 1 | tf_op jit(solution)/shard_map/prep/pallas_call | solution.py:77
  4.5 3.0 %collective-permute-start.15 = (bf16[120,1024]{1,0:T(8,128)(2,1)}, bf16[120,1024]{1,0:T(8,128)(2,1)S(1)}, u32[]{:S(2)}, u32[]{:S(2)}) collective-permute-start(bf16[120,1024]{1,0:T(8,128)(2,1)} %get-tuple-element.249), channel_id=1, source_target_pairs={{0,1},{1,0},{2,3},{3,2},{4,5},{5,4},{6,7},{7,6},{8,9},{9,8},{10,11... | collective-permute-start | bytes 737288 | tf_op jit(solution)/shard_map/ppermute | solution.py:490
  7.5 2.6 %collective-permute-start.12 = (bf16[120,1024]{1,0:T(8,128)(2,1)}, bf16[120,1024]{1,0:T(8,128)(2,1)S(1)}, u32[]{:S(2)}, u32[]{:S(2)}) collective-permute-start(bf16[120,1024]{1,0:T(8,128)(2,1)} %get-tuple-element.245), channel_id=1, source_target_pairs={{0,4},{1,5},{2,6},{3,7},{4,0},{5,1},{6,2},{7,3},{8,12},{9,13},{10,... | collective-permute-start | bytes 737288 | tf_op jit(solution)/shard_map/ppermute | solution.py:490
  10.1 1.9 %collective-permute-start.14 = (bf16[120,1024]{1,0:T(8,128)(2,1)}, bf16[120,1024]{1,0:T(8,128)(2,1)S(1)}, u32[]{:S(2)}, u32[]{:S(2)}) collective-permute-start(bf16[120,1024]{1,0:T(8,128)(2,1)} %get-tuple-element.247), channel_id=1, source_target_pairs={{0,2},{1,3},{2,0},{3,1},{4,6},{5,7},{6,4},{7,5},{8,10},{9,11},{10,... | collective-permute-start | bytes 737288 | tf_op jit(solution)/shard_map/ppermute | solution.py:490
  12.0 1.7 %collective-permute-done.15 = bf16[120,1024]{1,0:T(8,128)(2,1)S(1)} collective-permute-done((bf16[120,1024]{1,0:T(8,128)(2,1)}, bf16[120,1024]{1,0:T(8,128)(2,1)S(1)}, u32[]{:S(2)}, u32[]{:S(2)}) %collective-permute-start.15) | collective-permute-done | bytes 245792 | tf_op jit(solution)/shard_map/ppermute | solution.py:490
  13.7 8.4 %conditional.4 = (bf16[128,1024]{1,0:T(8,128)(2,1)}, bf16[128,1024]{1,0:T(8,128)(2,1)}, f32[128,1536]{1,0:T(8,128)}, bf16[128,1536]{1,0:T(8,128)(2,1)}, bf16[128...) conditional(s32[]{:T(128)} %convert_element_type.2, () %tuple.67, (s32[2]{0:T(128)S(1)}, ...), branch_computations={%region_0.1_spmd, %region_1.2_spmd} | conditional | flops 3 | bytes 2097214 | solution.py:505
  13.7 4.3 %up.8 = (bf16[128,1024]{1,0:T(8,128)(2,1)}, bf16[128,1024]{1,0:T(8,128)(2,1)}, bf16[128,1536]{1,0:T(8,128)(2,1)S(1)}, bf16[1024,2048]{1,0:T(8,128)(2,1)S(1)}, bf16[1024,1024]{1,0:T(8,128)(2,1)S(1)}) custom-call(s32[2]{0:T(128)S(1)} %get-tuple-element.72.ids, bf16[120,1024]{1,0:T(8,128)(2,1)S(1)} %get-tuple-element.73.refs_0_, ...), custom_call_target="tpu_custom_call" | custom-call | flops 1 | bytes 1 | tf_op jit(solution)/shard_map/cond/branch_1_fun/up/pallas_call | solution.py:171
  18.1 2.7 %up.9.keep = f32[128,1536]{1,0:T(8,128)} custom-call(s32[2]{0:T(128)S(1)} %get-tuple-element.72.ids, bf16[128,1024]{1,0:T(8,128)(2,1)} %get-tuple-element.80.rows, bf16[128,1024]{1,0:T(8,128)(2,1)} %get-tuple-element.322.grads, bf16[1024,2048]{1,0:T(8,128)(2,1)S(1)} %get-tuple-element.81.w_in, bf16[1024,1024]{1,0:T(8,128)(2,1)S(1)} %get-tuple-element.82.w_out), custom_call_target="tpu_custom_call" | custom-call | flops 1 | bytes 1 | tf_op jit(solution)/shard_map/cond/branch_1_fun/up/pallas_call | solution.py:93
  20.8 1.3 %total.3 = (bf16[128,768]{1,0:T(8,128)(2,1)S(1)}, bf16[128,768]{1,0:T(8,128)(2,1)S(1)}) custom-call(f32[128,1536]{1,0:T(8,128)} %up.9.keep, bf16[128,1536]{1,0:T(8,128)(2,1)} %collective-permute-done.core), custom_call_target="tpu_custom_call" | custom-call | flops 1 | bytes 1 | tf_op jit(solution)/shard_map/cond/branch_1_fun/total/pallas_call | solution.py:93
  22.1 1.8 %collective-permute-start.17 = (bf16[128,768]{1,0:T(8,128)(2,1)S(1)}, bf16[128,768]{1,0:T(8,128)(2,1)S(1)}, u32[]{:S(2)}, u32[]{:S(2)}) collective-permute-start(bf16[128,768]{1,0:T(8,128)(2,1)S(1)} %get-tuple-element.250), channel_id=1, source_target_pairs={{0,16},{8,24},{16,0},{24,8},{1,17},{9,25},{17,1},{25,9},{2,18},{10... | collective-permute-start | bytes 589832 | tf_op jit(solution)/shard_map/ppermute | solution.py:493
  24.2 3.5 %collective-permute-done.12 = bf16[120,1024]{1,0:T(8,128)(2,1)S(1)} collective-permute-done((bf16[120,1024]{1,0:T(8,128)(2,1)}, bf16[120,1024]{1,0:T(8,128)(2,1)S(1)}, u32[]{:S(2)}, u32[]{:S(2)}) %collective-permute-start.12) | collective-permute-done | bytes 245792 | tf_op jit(solution)/shard_map/ppermute | solution.py:490
  27.8 4.0 %collective-permute-done.13 = bf16[120,1024]{1,0:T(8,128)(2,1)S(1)} collective-permute-done((bf16[120,1024]{1,0:T(8,128)(2,1)}, bf16[120,1024]{1,0:T(8,128)(2,1)S(1)}, u32[]{:S(2)}, u32[]{:S(2)}) %collective-permute-start.13) | collective-permute-done | bytes 245792 | tf_op jit(solution)/shard_map/ppermute | solution.py:490
  31.8 3.5 %collective-permute-start.16 = (bf16[120,1024]{1,0:T(8,128)(2,1)}, bf16[120,1024]{1,0:T(8,128)(2,1)S(1)}, u32[]{:S(2)}, u32[]{:S(2)}) collective-permute-start(bf16[120,1024]{1,0:T(8,128)(2,1)} %get-tuple-element.252), channel_id=1, source_target_pairs={{0,6},{1,7},{2,4},{3,5},{4,2},{5,3},{6,0},{7,1},{8,14},{9,15},{10,... | collective-permute-start | bytes 737288 | tf_op jit(solution)/shard_map/ppermute | solution.py:490
  35.3 1.3 %collective-permute-start.19 = (bf16[120,1024]{1,0:T(8,128)(2,1)}, bf16[120,1024]{1,0:T(8,128)(2,1)S(1)}, u32[]{:S(2)}, u32[]{:S(2)}) collective-permute-start(bf16[120,1024]{1,0:T(8,128)(2,1)} %get-tuple-element.260), channel_id=1, source_target_pairs={{0,7},{1,6},{2,5},{3,4},{4,3},{5,2},{6,1},{7,0},{8,15},{9,14},{10,... | collective-permute-start | bytes 737288 | tf_op jit(solution)/shard_map/ppermute | solution.py:490
  36.6 23.0 %conditional.5 = (bf16[128,1024]{1,0:T(8,128)(2,1)S(1)}, bf16[128,1024]{1,0:T(8,128)(2,1)S(1)}, bf16[128,1536]{1,0:T(8,128)(2,1)}, bf16[128,1536]{1,0:T(8,128)(2...) conditional(s32[]{:T(128)} %convert_element_type.2, () %tuple.70, ...), branch_computations={%region_2.3_spmd, %region_3.4_spmd} | conditional | flops 20000000000 | bytes 24249056 | solution.py:505
  36.6 3.5 %up.10 = (bf16[128,1024]{1,0:T(8,128)(2,1)S(1)}, bf16[128,1024]{1,0:T(8,128)(2,1)S(1)}, bf16[128,1536]{1,0:T(8,128)(2,1)S(1)}, bf16[1024,2048]{1,0:T(8,128)(2,1)S(1)}, bf16[1024,1024]{1,0:T(8,128)(2,1)S(1)}) custom-call(s32[2]{0:T(128)S(1)} %get-tuple-element.85.ids, bf16[120,1024]{1,0:T(8,128)(2,1)S(1)} %get-tuple-element.86.refs_0_, ...), custom_call_target="tpu_custom_call" | custom-call | flops 1 | bytes 1 | tf_op jit(solution)/shard_map/cond/branch_1_fun/up/pallas_call | solution.py:171
  40.2 1.3 %up.11.keep = f32[128,1536]{1,0:T(8,128)S(1)} custom-call(s32[2]{0:T(128)S(1)} %get-tuple-element.85.ids, bf16[128,1024]{1,0:T(8,128)(2,1)S(1)} %get-tuple-element.93.rows, bf16[128,1024]{1,0:T(8,128)(2,1)S(1)} %get-tuple-element.345.grads, bf16[1024,2048]{1,0:T(8,128)(2,1)S(1)} %get-tuple-element.94.w_in.refs_1_, ...), custom_call_target="tpu_custom_call" | custom-call | flops 1 | bytes 1 | tf_op jit(solution)/shard_map/cond/branch_1_fun/up/pallas_call | solution.py:93
  42.0 1.6 %collective-permute-start.3 = (bf16[128,1536]{1,0:T(8,128)(2,1)S(1)}, bf16[128,1536]{1,0:T(8,128)(2,1)S(1)}, u32[]{:S(2)}, u32[]{:S(2)}) collective-permute-start(bf16[128,1536]{1,0:T(8,128)(2,1)S(1)} %total.4), channel_id=1, source_target_pairs={{0,16},{8,24},{16,0},{24,8},{1,17},{9,25},{17,1},{25,9},{2,18},{10... | collective-permute-start | bytes 1179656 | tf_op jit(solution)/shard_map/cond/branch_1_fun/ppermute | solution.py:493
  43.6 1.5 %act.5.own = bf16[128,1536]{1,0:T(8,128)(2,1)S(1)} custom-call(f32[128,1536]{1,0:T(8,128)} %get-tuple-element.97.keep, bf16[128,1536]{1,0:T(8,128)(2,1)} %get-tuple-element.98.core, bf16[128,768]{1,0:T(8,128)(2,1)S(1)} %get-tuple-element.99.refs_0_, bf16[128,768]{1,0:T(8,128)(2,1)S(1)} %get-tuple-element.100.refs_1_), custom_call_target="tpu_custom_call" | custom-call | flops 1 | bytes 1 | tf_op jit(solution)/shard_map/cond/branch_1_fun/act/pallas_call | solution.py:93
  45.1 2.1 %up.12 = (bf16[64,1024]{1,0:T(8,128)(2,1)S(1)}, bf16[64,1024]{1,0:T(8,128)(2,1)S(1)}, bf16[64,1536]{1,0:T(8,128)(2,1)S(1)}, f32[64,1536]{1,0:T(8,128)S(1)}) custom-call(s32[2]{0:T(128)S(1)} %get-tuple-element.85.ids, bf16[120,1024]{1,0:T(8,128)(2,1)S(1)} %copy-done.28, bf16[1024,2048]{1,0:T(8,128)(2,1)S(1)} %get-tuple-element.94.w_in.refs_1_, ...), custom_call_target="tpu_custom_call" | custom-call | flops 20000000000 | bytes 1 | tf_op jit(solution)/shard_map/cond/branch_1_fun/up/pallas_call | solution.py:93
  47.3 3.4 %down.8 = (bf16[120,1024]{1,0:T(8,128)(2,1)}, bf16[120,1024]{1,0:T(8,128)(2,1)}) custom-call(s32[2]{0:T(128)S(1)} %get-tuple-element.85.ids, bf16[128,1536]{1,0:T(8,128)(2,1)S(1)} %act.5.own, bf16[128,1536]{1,0:T(8,128)(2,1)S(1)} %collective-permute-done.2.core, bf16[1024,2048]{1,0:T(8,128)(2,1)S(1)} %get-tuple-element.94.w_in.refs_1_, ...), custom_call_target="tpu_custom_call" | custom-call | flops 1 | bytes 1 | tf_op jit(solution)/shard_map/cond/branch_1_fun/down/pallas_call | solution.py:93
  51.2 2.0 %collective-permute-done.3.other = bf16[128,1536]{1,0:T(8,128)(2,1)S(1)} collective-permute-done((bf16[128,1536]{1,0:T(8,128)(2,1)S(1)}, bf16[128,1536]{1,0:T(8,128)(2,1)S(1)}, u32[]{:S(2)}, u32[]{:S(2)}) %collective-permute-start.3) | collective-permute-done | bytes 393248 | tf_op jit(solution)/shard_map/cond/branch_1_fun/ppermute | solution.py:493
  53.2 1.1 act.6
  54.3 2.0 %down.9 = (f32[128,1024]{1,0:T(8,128)S(1)}, f32[128,1024]{1,0:T(8,128)S(1)}) custom-call(s32[2]{0:T(128)S(1)} %get-tuple-element.85.ids, bf16[128,1536]{1,0:T(8,128)(2,1)} %get-tuple-element.346.own, bf16[1024,2048]{1,0:T(8,128)(2,1)S(1)} %get-tuple-element.94.w_in.refs_1_, bf16[1024,1024]{1,0:T(8,128)(2,1)S(1)} %get-tuple-element.95.w_out.refs_2_), custom_call_target="tpu_custom_call" | custom-call | flops 1 | bytes 1 | tf_op jit(solution)/shard_map/cond/branch_1_fun/down/pallas_call | solution.py:93
  56.4 3.2 %down.10 = (bf16[120,1024]{1,0:T(8,128)(2,1)}, bf16[120,1024]{1,0:T(8,128)(2,1)}) custom-call(s32[2]{0:T(128)S(1)} %get-tuple-element.85.ids, f32[128,1024]{1,0:T(8,128)S(1)} %get-tuple-element.111.out_rows, f32[128,1024]{1,0:T(8,128)S(1)} %get-tuple-element.112.grad_rows, bf16[128,1536]{1,0:T(8,128)(2,1)} %collective-permute-done.5.core, ...), custom_call_target="tpu_custom_call" | custom-call | flops 1 | bytes 1 | tf_op jit(solution)/shard_map/cond/branch_1_fun/down/pallas_call | solution.py:93
  59.6 1.6 %collective-permute-start.20 = (bf16[64,1536]{1,0:T(8,128)(2,1)}, bf16[64,1536]{1,0:T(8,128)(2,1)S(1)}, u32[]{:S(2)}, u32[]{:S(2)}) collective-permute-start(bf16[64,1536]{1,0:T(8,128)(2,1)} %get-tuple-element.263), channel_id=1, source_target_pairs={{0,16},{8,24},{16,0},{24,8},{1,17},{9,25},{17,1},{25,9},{2,18},{10... | collective-permute-start | bytes 589832 | tf_op jit(solution)/shard_map/ppermute | solution.py:493
  61.7 4.9 %collective-permute-start.27 = (bf16[120,1024]{1,0:T(8,128)(2,1)}, bf16[120,1024]{1,0:T(8,128)(2,1)S(1)}, u32[]{:S(2)}, u32[]{:S(2)}) collective-permute-start(bf16[120,1024]{1,0:T(8,128)(2,1)} %get-tuple-element.280), channel_id=1, source_target_pairs={{0,5},{1,4},{2,7},{3,6},{4,1},{5,0},{6,3},{7,2},{8,13},{9,12},{10,... | collective-permute-start | bytes 737288 | tf_op jit(solution)/shard_map/ppermute | solution.py:490
  67.2 23.0 %conditional.6 = (bf16[128,1024]{1,0:T(8,128)(2,1)S(1)}, bf16[128,1024]{1,0:T(8,128)(2,1)}, bf16[128,1536]{1,0:T(8,128)(2,1)}, bf16[128,1536]{1,0:T(8,128)(2,1)}...) conditional(s32[]{:T(128)} %convert_element_type.2, () %tuple.66, ...), branch_computations={%region_4.5_spmd, %region_5.6_spmd} | conditional | flops 20000000000 | bytes 15729229 | solution.py:505
  67.2 3.5 %up.13 = (bf16[128,1024]{1,0:T(8,128)(2,1)S(1)}, bf16[128,1024]{1,0:T(8,128)(2,1)S(1)}, bf16[128,1536]{1,0:T(8,128)(2,1)S(1)}, bf16[1024,2048]{1,0:T(8,128)(2,1)S(1)}, bf16[1024,1024]{1,0:T(8,128)(2,1)S(1)}) custom-call(s32[2]{0:T(128)S(1)} %get-tuple-element.121.ids, bf16[120,1024]{1,0:T(8,128)(2,1)S(1)} %get-tuple-element.122.refs_0_, ...), custom_call_target="tpu_custom_call" | custom-call | flops 1 | bytes 1 | tf_op jit(solution)/shard_map/cond/branch_1_fun/up/pallas_call | solution.py:171
  70.8 1.5 %up.14.keep = f32[128,1536]{1,0:T(8,128)S(1)} custom-call(s32[2]{0:T(128)S(1)} %get-tuple-element.121.ids, bf16[128,1024]{1,0:T(8,128)(2,1)S(1)} %get-tuple-element.129.rows, bf16[128,1024]{1,0:T(8,128)(2,1)S(1)} %get-tuple-element.378.grads, bf16[1024,2048]{1,0:T(8,128)(2,1)S(1)} %get-tuple-element.130.w_in.refs_1_, ...), custom_call_target="tpu_custom_call" | custom-call | flops 1 | bytes 1 | tf_op jit(solution)/shard_map/cond/branch_1_fun/up/pallas_call | solution.py:93
  72.6 1.6 %collective-permute-start.8 = (bf16[128,1536]{1,0:T(8,128)(2,1)S(1)}, bf16[128,1536]{1,0:T(8,128)(2,1)S(1)}, u32[]{:S(2)}, u32[]{:S(2)}) collective-permute-start(bf16[128,1536]{1,0:T(8,128)(2,1)S(1)} %total.5), channel_id=1, source_target_pairs={{0,16},{8,24},{16,0},{24,8},{1,17},{9,25},{17,1},{25,9},{2,18},{10... | collective-permute-start | bytes 1179656 | tf_op jit(solution)/shard_map/cond/branch_1_fun/ppermute | solution.py:493
  74.4 2.5 %up.15 = (bf16[64,1024]{1,0:T(8,128)(2,1)S(1)}, bf16[64,1024]{1,0:T(8,128)(2,1)S(1)}, bf16[64,1536]{1,0:T(8,128)(2,1)S(1)}, f32[64,1536]{1,0:T(8,128)S(1)}) custom-call(s32[2]{0:T(128)S(1)} %get-tuple-element.121.ids, bf16[120,1024]{1,0:T(8,128)(2,1)} %get-tuple-element.137.refs_0_, bf16[1024,2048]{1,0:T(8,128)(2,1)S(1)} %get-tuple-element.130.w_in.refs_1_, ...), custom_call_target="tpu_custom_call" | custom-call | flops 20000000000 | bytes 1 | tf_op jit(solution)/shard_map/cond/branch_1_fun/up/pallas_call | solution.py:93
  77.0 3.3 %down.11 = bf16[120,1024]{1,0:T(8,128)(2,1)} custom-call(s32[2]{0:T(128)S(1)} %get-tuple-element.121.ids, bf16[64,1536]{1,0:T(8,128)(2,1)S(1)} %act.7.own, bf16[64,1536]{1,0:T(8,128)(2,1)S(1)} %collective-permute-done.7.core, bf16[1024,2048]{1,0:T(8,128)(2,1)S(1)} %get-tuple-element.130.w_in.refs_1_, bf16[1024,1024]{1,0:T(8,128)(2,1)S(1)} %get-tuple-element.131.w_out.refs_2_), custom_call_target="tpu_custom_call" | custom-call | flops 1 | bytes 1 | tf_op jit(solution)/shard_map/cond/branch_1_fun/down/pallas_call | solution.py:93
  80.7 1.1 collective-permute-done.9.next_core
  81.8 2.2 %collective-permute-done.8.other = bf16[128,1536]{1,0:T(8,128)(2,1)S(1)} collective-permute-done((bf16[128,1536]{1,0:T(8,128)(2,1)S(1)}, bf16[128,1536]{1,0:T(8,128)(2,1)S(1)}, u32[]{:S(2)}, u32[]{:S(2)}) %collective-permute-start.8) | collective-permute-done | bytes 393248 | tf_op jit(solution)/shard_map/cond/branch_1_fun/ppermute | solution.py:493
  85.0 2.0 %down.12 = (f32[128,1024]{1,0:T(8,128)S(1)}, f32[128,1024]{1,0:T(8,128)S(1)}) custom-call(s32[2]{0:T(128)S(1)} %get-tuple-element.121.ids, bf16[128,1536]{1,0:T(8,128)(2,1)} %get-tuple-element.379.own, bf16[1024,2048]{1,0:T(8,128)(2,1)S(1)} %get-tuple-element.130.w_in.refs_1_, bf16[1024,1024]{1,0:T(8,128)(2,1)S(1)} %get-tuple-element.131.w_out.refs_2_), custom_call_target="tpu_custom_call" | custom-call | flops 1 | bytes 1 | tf_op jit(solution)/shard_map/cond/branch_1_fun/down/pallas_call | solution.py:93
  87.1 3.1 %down.13 = (bf16[120,1024]{1,0:T(8,128)(2,1)}, bf16[120,1024]{1,0:T(8,128)(2,1)}) custom-call(s32[2]{0:T(128)S(1)} %get-tuple-element.121.ids, f32[128,1024]{1,0:T(8,128)S(1)} %get-tuple-element.144.out_rows, f32[128,1024]{1,0:T(8,128)S(1)} %get-tuple-element.145.grad_rows, bf16[128,1536]{1,0:T(8,128)(2,1)} %collective-permute-done.10.core, ...), custom_call_target="tpu_custom_call" | custom-call | flops 1 | bytes 1 | tf_op jit(solution)/shard_map/cond/branch_1_fun/down/pallas_call | solution.py:93
  90.2 1.6 %collective-permute-start.23 = (bf16[64,1536]{1,0:T(8,128)(2,1)S(1)}, bf16[64,1536]{1,0:T(8,128)(2,1)S(1)}, u32[]{:S(2)}, u32[]{:S(2)}) collective-permute-start(bf16[64,1536]{1,0:T(8,128)(2,1)S(1)} %get-tuple-element.271), channel_id=1, source_target_pairs={{0,16},{8,24},{16,0},{24,8},{1,17},{9,25},{17,1},{25,9},{2,18},{10... | collective-permute-start | bytes 589832 | tf_op jit(solution)/shard_map/ppermute | solution.py:493
  91.8 3.5 %collective-permute-start.30 = (bf16[120,1024]{1,0:T(8,128)(2,1)}, bf16[120,1024]{1,0:T(8,128)(2,1)S(1)}, u32[]{:S(2)}, u32[]{:S(2)}) collective-permute-start(bf16[120,1024]{1,0:T(8,128)(2,1)} %get-tuple-element.287), channel_id=1, source_target_pairs={{0,7},{1,6},{2,5},{3,4},{4,3},{5,2},{6,1},{7,0},{8,15},{9,14},{10,... | collective-permute-start | bytes 737288 | tf_op jit(solution)/shard_map/ppermute | solution.py:490
  95.6 1.7 %collective-permute-start.22 = (bf16[120,1024]{1,0:T(8,128)(2,1)}, bf16[120,1024]{1,0:T(8,128)(2,1)S(1)}, u32[]{:S(2)}, u32[]{:S(2)}) collective-permute-start(bf16[120,1024]{1,0:T(8,128)(2,1)} %get-tuple-element.268), channel_id=1, source_target_pairs={{0,2},{1,3},{2,0},{3,1},{4,6},{5,7},{6,4},{7,5},{8,10},{9,11},{10,... | collective-permute-start | bytes 737288 | tf_op jit(solution)/shard_map/ppermute | solution.py:490
  97.6 7.5 %conditional.7 = (bf16[64,1024]{1,0:T(8,128)(2,1)S(1)}, bf16[64,1024]{1,0:T(8,128)(2,1)S(1)}, bf16[64,1536]{1,0:T(8,128)(2,1)}, bf16[64,1536]{1,0:T(8,128)(2,1)}...) conditional(s32[]{:T(128)} %convert_element_type.2, () %tuple.76, (f32[64,1536]{1,0:T(8,128)S(1)}, ...), branch_computations={%region_6.7_spmd, %region_7.8_spmd} | conditional | flops 3 | bytes 901180 | solution.py:505
  98.4 3.8 %down.14 = (f32[64,1024]{1,0:T(8,128)S(1)}, f32[64,1024]{1,0:T(8,128)S(1)}, bf16[1024,2048]{1,0:T(8,128)(2,1)S(1)}, bf16[1024,1024]{1,0:T(8,128)(2,1)S(1)}) custom-call(s32[2]{0:T(128)S(1)} %get-tuple-element.159.ids, bf16[64,1536]{1,0:T(8,128)(2,1)} %act.9.own, bf16[1024,2048]{1,0:T(8,128)(2,1)} %get-tuple-element.160.far_in, ...), custom_call_target="tpu_custom_call" | custom-call | flops 1 | bytes 1 | tf_op jit(solution)/shard_map/cond/branch_1_fun/down/pallas_call | solution.py:337
  102.2 2.8 %down.15 = (bf16[120,512]{1,0:T(8,128)(2,1)}, bf16[120,512]{1,0:T(8,128)(2,1)}) custom-call(s32[2]{0:T(128)S(1)} %get-tuple-element.159.ids, f32[64,1024]{1,0:T(8,128)S(1)} %get-tuple-element.162.out_rows, f32[64,1024]{1,0:T(8,128)S(1)} %get-tuple-element.163.grad_rows, bf16[64,1536]{1,0:T(8,128)(2,1)} %collective-permute-done.11.core, ...), custom_call_target="tpu_custom_call" | custom-call | flops 1 | bytes 1 | tf_op jit(solution)/shard_map/cond/branch_1_fun/down/pallas_call | solution.py:93
  105.1 2.9 %collective-permute-start.24 = (bf16[120,512]{1,0:T(8,128)(2,1)}, bf16[120,512]{1,0:T(8,128)(2,1)S(1)}, u32[]{:S(2)}, u32[]{:S(2)}) collective-permute-start(bf16[120,512]{1,0:T(8,128)(2,1)} %get-tuple-element.274), channel_id=1, source_target_pairs={{0,3},{1,2},{2,1},{3,0},{4,7},{5,6},{6,5},{7,4},{8,11},{9,10},{10,... | collective-permute-start | bytes 368648 | tf_op jit(solution)/shard_map/ppermute | solution.py:490
  108.0 2.4 %final.3 = (f32[192,1024]{1,0:T(8,128)S(1)}, f32[192,1024]{1,0:T(8,128)S(1)}) custom-call(s32[2]{0:T(128)S(1)} %pad_add_fusion.refs_0_, s32[2,192]{1,0:T(2,128)S(1)} %bitcast.9, f32[2,192]{1,0:T(2,128)S(1)} %bitcast.13, bf16[120,1024]{1,0:T(8,128)(2,1)} %get-tuple-element.282.refs_3_, bf16[120,1024]{1,0:T(8,128)(2,1)S(1)} %collective-permute-done.28.refs_4_, ...), custom_call_target="tpu_custom_call" | custom-call | flops 1 | bytes 1 | tf_op jit(solution)/shard_map/final/pallas_call | solution.py:93
  110.4 6.7 %grads.1 = (bf16[1024,2048]{1,0:T(8,128)(2,1)}, bf16[1024,1024]{1,0:T(8,128)(2,1)}) custom-call(s32[2]{0:T(128)S(1)} %pad_add_fusion.refs_0_, bf16[128,1024]{1,0:T(8,128)(2,1)} %get-tuple-element.294.refs_1_, bf16[128,1024]{1,0:T(8,128)(2,1)} %get-tuple-element.295.refs_2_, bf16[128,1536]{1,0:T(8,128)(2,1)S(1)} %get-tuple-element.296.refs_3_, ...), custom_call_target="tpu_custom_call" | custom-call | flops 1 | bytes 1 | tf_op jit(solution)/shard_map/grads/pallas_call | solution.py:397
  117.2 1.5 %final.4 = (f32[192,1024]{1,0:T(8,128)S(1)}, f32[192,1024]{1,0:T(8,128)S(1)}) custom-call(s32[2]{0:T(128)S(1)} %pad_add_fusion.refs_0_, s32[2,192]{1,0:T(2,128)S(1)} %bitcast.10, f32[2,192]{1,0:T(2,128)S(1)} %bitcast.14, bf16[120,1024]{1,0:T(8,128)(2,1)S(1)} %collective-permute-done.29.refs_3_, bf16[120,1024]{1,0:T(8,128)(2,1)S(1)} %collective-permute-done.30.refs_4_, ...), custom_call_target="tpu_custom_call" | custom-call | flops 1 | bytes 1 | tf_op jit(solution)/shard_map/final/pallas_call | solution.py:93
  118.8 2.4 %final.5 = (bf16[192,1024]{1,0:T(8,128)(2,1)}, bf16[192,1024]{1,0:T(8,128)(2,1)}) custom-call(s32[2]{0:T(128)S(1)} %pad_add_fusion.refs_0_, s32[2,192]{1,0:T(2,128)S(1)} %bitcast.11, f32[2,192]{1,0:T(2,128)S(1)} %bitcast.15, bf16[120,1024]{1,0:T(8,128)(2,1)S(1)} %collective-permute-done.22.refs_3_, bf16[120,512]{1,0:T(8,128)(2,1)S(1)} %collective-permute-done.24.refs_4_, ...), custom_call_target="tpu_custom_call" | custom-call | flops 1 | bytes 1 | tf_op jit(solution)/shard_map/final/pallas_call | solution.py:93
  (106 shorter events, 6.3 us)
Async XLA Ops:
  4.5 9.2 %collective-permute-start.15 = (bf16[120,1024]{1,0:T(8,128)(2,1)}, bf16[120,1024]{1,0:T(8,128)(2,1)S(1)}, u32[]{:S(2)}, u32[]{:S(2)}) collective-permute-start(bf16[120,1024]{1,0:T(8,128)(2,1)} %get-tuple-element.249), channel_id=1, source_target_pairs={{0,1},{1,0},{2,3},{3,2},{4,5},{5,4},{6,7},{7,6},{8,9},{9,8},{10,11... | collective-permute-start | bytes 737288 | tf_op jit(solution)/shard_map/ppermute | solution.py:490
  7.5 20.2 %collective-permute-start.12 = (bf16[120,1024]{1,0:T(8,128)(2,1)}, bf16[120,1024]{1,0:T(8,128)(2,1)S(1)}, u32[]{:S(2)}, u32[]{:S(2)}) collective-permute-start(bf16[120,1024]{1,0:T(8,128)(2,1)} %get-tuple-element.245), channel_id=1, source_target_pairs={{0,4},{1,5},{2,6},{3,7},{4,0},{5,1},{6,2},{7,3},{8,12},{9,13},{10,... | collective-permute-start | bytes 737288 | tf_op jit(solution)/shard_map/ppermute | solution.py:490
  10.1 21.6 %collective-permute-start.13 = (bf16[120,1024]{1,0:T(8,128)(2,1)}, bf16[120,1024]{1,0:T(8,128)(2,1)S(1)}, u32[]{:S(2)}, u32[]{:S(2)}) collective-permute-start(bf16[120,1024]{1,0:T(8,128)(2,1)} %get-tuple-element.246), channel_id=1, source_target_pairs={{0,5},{1,4},{2,7},{3,6},{4,1},{5,0},{6,3},{7,2},{8,13},{9,12},{10,... | collective-permute-start | bytes 737288 | tf_op jit(solution)/shard_map/ppermute | solution.py:490
  10.1 21.6 %collective-permute-start.14 = (bf16[120,1024]{1,0:T(8,128)(2,1)}, bf16[120,1024]{1,0:T(8,128)(2,1)S(1)}, u32[]{:S(2)}, u32[]{:S(2)}) collective-permute-start(bf16[120,1024]{1,0:T(8,128)(2,1)} %get-tuple-element.247), channel_id=1, source_target_pairs={{0,2},{1,3},{2,0},{3,1},{4,6},{5,7},{6,4},{7,5},{8,10},{9,11},{10,... | collective-permute-start | bytes 737288 | tf_op jit(solution)/shard_map/ppermute | solution.py:490
  18.0 2.8 %collective-permute-start = (bf16[128,1536]{1,0:T(8,128)(2,1)S(1)}, bf16[128,1536]{1,0:T(8,128)(2,1)}, u32[]{:S(2)}, u32[]{:S(2)}) collective-permute-start(bf16[128,1536]{1,0:T(8,128)(2,1)S(1)} %get-tuple-element.79), channel_id=1, source_target_pairs={{0,8},{8,0},{16,24},{24,16},{1,9},{9,1},{17,25},{25,17},{2,10},{10... | collective-permute-start | bytes 1179656 | tf_op jit(solution)/shard_map/cond/branch_1_fun/ppermute | solution.py:493
  22.1 14.5 %collective-permute-start.17 = (bf16[128,768]{1,0:T(8,128)(2,1)S(1)}, bf16[128,768]{1,0:T(8,128)(2,1)S(1)}, u32[]{:S(2)}, u32[]{:S(2)}) collective-permute-start(bf16[128,768]{1,0:T(8,128)(2,1)S(1)} %get-tuple-element.250), channel_id=1, source_target_pairs={{0,16},{8,24},{16,0},{24,8},{1,17},{9,25},{17,1},{25,9},{2,18},{10... | collective-permute-start | bytes 589832 | tf_op jit(solution)/shard_map/ppermute | solution.py:493
  23.9 12.7 %collective-permute-start.18 = (bf16[128,768]{1,0:T(8,128)(2,1)S(1)}, bf16[128,768]{1,0:T(8,128)(2,1)S(1)}, u32[]{:S(2)}, u32[]{:S(2)}) collective-permute-start(bf16[128,768]{1,0:T(8,128)(2,1)S(1)} %get-tuple-element.251), channel_id=1, source_target_pairs={{0,16},{8,24},{16,0},{24,8},{1,17},{9,25},{17,1},{25,9},{2,18},{10... | collective-permute-start | bytes 589832 | tf_op jit(solution)/shard_map/ppermute | solution.py:493
  31.8 29.4 %collective-permute-start.16 = (bf16[120,1024]{1,0:T(8,128)(2,1)}, bf16[120,1024]{1,0:T(8,128)(2,1)S(1)}, u32[]{:S(2)}, u32[]{:S(2)}) collective-permute-start(bf16[120,1024]{1,0:T(8,128)(2,1)} %get-tuple-element.252), channel_id=1, source_target_pairs={{0,6},{1,7},{2,4},{3,5},{4,2},{5,3},{6,0},{7,1},{8,14},{9,15},{10,... | collective-permute-start | bytes 737288 | tf_op jit(solution)/shard_map/ppermute | solution.py:490
  35.3 25.9 %collective-permute-start.19 = (bf16[120,1024]{1,0:T(8,128)(2,1)}, bf16[120,1024]{1,0:T(8,128)(2,1)S(1)}, u32[]{:S(2)}, u32[]{:S(2)}) collective-permute-start(bf16[120,1024]{1,0:T(8,128)(2,1)} %get-tuple-element.260), channel_id=1, source_target_pairs={{0,7},{1,6},{2,5},{3,4},{4,3},{5,2},{6,1},{7,0},{8,15},{9,14},{10,... | collective-permute-start | bytes 737288 | tf_op jit(solution)/shard_map/ppermute | solution.py:490
  36.6 30.1 %collective-permute-start.21 = (bf16[120,1024]{1,0:T(8,128)(2,1)}, bf16[120,1024]{1,0:T(8,128)(2,1)}, u32[]{:S(2)}, u32[]{:S(2)}) collective-permute-start(bf16[120,1024]{1,0:T(8,128)(2,1)} %get-tuple-element.265), channel_id=1, source_target_pairs={{0,3},{1,2},{2,1},{3,0},{4,7},{5,6},{6,5},{7,4},{8,11},{9,10},{10,... | collective-permute-start | bytes 737288 | tf_op jit(solution)/shard_map/ppermute | solution.py:490
  36.6 3.6 %copy-start.27 = (bf16[120,1024]{1,0:T(8,128)(2,1)}, bf16[120,1024]{1,0:T(8,128)(2,1)S(1)}, u32[]{:S(2)}) copy-start(bf16[120,1024]{1,0:T(8,128)(2,1)S(1)} %get-tuple-element.102.refs_0_) | copy-start | bytes 737284 | tf_op jit(solution)/shard_map/cond
  40.1 1.8 %collective-permute-start.1 = (bf16[128,1536]{1,0:T(8,128)(2,1)S(1)}, bf16[128,1536]{1,0:T(8,128)(2,1)S(1)}, u32[]{:S(2)}, u32[]{:S(2)}) collective-permute-start(bf16[128,1536]{1,0:T(8,128)(2,1)S(1)} %get-tuple-element.92), channel_id=1, source_target_pairs={{0,8},{8,0},{16,24},{24,16},{1,9},{9,1},{17,25},{25,17},{2,10},{10... | collective-permute-start | bytes 1179656 | tf_op jit(solution)/shard_map/cond/branch_1_fun/ppermute | solution.py:493
  40.2 4.9 %copy-start.28 = (bf16[120,1024]{1,0:T(8,128)(2,1)S(1)}, bf16[120,1024]{1,0:T(8,128)(2,1)}, u32[]{:S(2)}) copy-start(bf16[120,1024]{1,0:T(8,128)(2,1)} %copy-done.27) | copy-start | bytes 737284 | tf_op jit(solution)/shard_map/cond
  42.0 11.2 %collective-permute-start.3 = (bf16[128,1536]{1,0:T(8,128)(2,1)S(1)}, bf16[128,1536]{1,0:T(8,128)(2,1)S(1)}, u32[]{:S(2)}, u32[]{:S(2)}) collective-permute-start(bf16[128,1536]{1,0:T(8,128)(2,1)S(1)} %total.4), channel_id=1, source_target_pairs={{0,16},{8,24},{16,0},{24,8},{1,17},{9,25},{17,1},{25,9},{2,18},{10... | collective-permute-start | bytes 1179656 | tf_op jit(solution)/shard_map/cond/branch_1_fun/ppermute | solution.py:493
  45.0 2.2 %collective-permute-start.2 = (bf16[128,1536]{1,0:T(8,128)(2,1)S(1)}, bf16[128,1536]{1,0:T(8,128)(2,1)S(1)}, u32[]{:S(2)}, u32[]{:S(2)}) collective-permute-start(bf16[128,1536]{1,0:T(8,128)(2,1)S(1)} %act.5.own), channel_id=1, source_target_pairs={{0,8},{8,0},{16,24},{24,16},{1,9},{9,1},{17,25},{25,17},{2,10},{10... | collective-permute-start | bytes 1179656 | tf_op jit(solution)/shard_map/cond/branch_1_fun/ppermute | solution.py:493
  47.2 7.1 %copy-start.6 = (f32[64,1536]{1,0:T(8,128)}, f32[64,1536]{1,0:T(8,128)S(1)}, u32[]{:S(2)}) copy-start(f32[64,1536]{1,0:T(8,128)S(1)} %get-tuple-element.352.next_keep) | copy-start | bytes 1179652 | tf_op jit(solution)/shard_map/cond
  47.3 7.0 %copy-start.4 = (bf16[128,1536]{1,0:T(8,128)(2,1)}, bf16[128,1536]{1,0:T(8,128)(2,1)S(1)}, u32[]{:S(2)}) copy-start(bf16[128,1536]{1,0:T(8,128)(2,1)S(1)} %collective-permute-done.2.core) | copy-start | bytes 1179652 | tf_op jit(solution)/shard_map/cond
  50.7 2.5 %collective-permute-start.4 = (bf16[64,1536]{1,0:T(8,128)(2,1)S(1)}, bf16[64,1536]{1,0:T(8,128)(2,1)S(1)}, u32[]{:S(2)}, u32[]{:S(2)}) collective-permute-start(bf16[64,1536]{1,0:T(8,128)(2,1)S(1)} %get-tuple-element.109), channel_id=1, source_target_pairs={{0,8},{8,0},{16,24},{24,16},{1,9},{9,1},{17,25},{25,17},{2,10},{10... | collective-permute-start | bytes 589832 | tf_op jit(solution)/shard_map/cond/branch_1_fun/ppermute | solution.py:493
  54.3 2.1 %collective-permute-start.5 = (bf16[128,1536]{1,0:T(8,128)(2,1)}, bf16[128,1536]{1,0:T(8,128)(2,1)}, u32[]{:S(2)}, u32[]{:S(2)}) collective-permute-start(bf16[128,1536]{1,0:T(8,128)(2,1)} %get-tuple-element.346.own), channel_id=1, source_target_pairs={{0,8},{8,0},{16,24},{24,16},{1,9},{9,1},{17,25},{25,17},{2,10},{10... | collective-permute-start | bytes 1179656 | tf_op jit(solution)/shard_map/cond/branch_1_fun/ppermute | solution.py:493
  56.3 3.3 %copy-start.3 = (bf16[128,1536]{1,0:T(8,128)(2,1)S(1)}, bf16[128,1536]{1,0:T(8,128)(2,1)}, u32[]{:S(2)}) copy-start(bf16[128,1536]{1,0:T(8,128)(2,1)} %copy-done.2) | copy-start | bytes 1179652 | tf_op jit(solution)/shard_map/cond
  56.4 3.3 %copy-start.5 = (bf16[128,1536]{1,0:T(8,128)(2,1)S(1)}, bf16[128,1536]{1,0:T(8,128)(2,1)}, u32[]{:S(2)}) copy-start(bf16[128,1536]{1,0:T(8,128)(2,1)} %copy-done.4) | copy-start | bytes 1179652 | tf_op jit(solution)/shard_map/cond
  56.4 3.2 %copy-start.7 = (f32[64,1536]{1,0:T(8,128)S(1)}, f32[64,1536]{1,0:T(8,128)}, u32[]{:S(2)}) copy-start(f32[64,1536]{1,0:T(8,128)} %copy-done.6) | copy-start | bytes 1179652 | tf_op jit(solution)/shard_map/cond
  56.4 3.2 %copy-start.11 = (bf16[128,1024]{1,0:T(8,128)(2,1)S(1)}, bf16[128,1024]{1,0:T(8,128)(2,1)}, u32[]{:S(2)}) copy-start(bf16[128,1024]{1,0:T(8,128)(2,1)} %copy-done.10) | copy-start | bytes 786436 | tf_op jit(solution)/shard_map/cond
  56.4 3.2 %copy-start.13 = (bf16[128,1024]{1,0:T(8,128)(2,1)S(1)}, bf16[128,1024]{1,0:T(8,128)(2,1)}, u32[]{:S(2)}) copy-start(bf16[128,1024]{1,0:T(8,128)(2,1)} %copy-done.12) | copy-start | bytes 786436 | tf_op jit(solution)/shard_map/cond
  59.6 7.6 %collective-permute-start.20 = (bf16[64,1536]{1,0:T(8,128)(2,1)}, bf16[64,1536]{1,0:T(8,128)(2,1)S(1)}, u32[]{:S(2)}, u32[]{:S(2)}) collective-permute-start(bf16[64,1536]{1,0:T(8,128)(2,1)} %get-tuple-element.263), channel_id=1, source_target_pairs={{0,16},{8,24},{16,0},{24,8},{1,17},{9,25},{17,1},{25,9},{2,18},{10... | collective-permute-start | bytes 589832 | tf_op jit(solution)/shard_map/ppermute | solution.py:493
  61.2 30.6 %collective-permute-start.28 = (bf16[120,1024]{1,0:T(8,128)(2,1)}, bf16[120,1024]{1,0:T(8,128)(2,1)S(1)}, u32[]{:S(2)}, u32[]{:S(2)}) collective-permute-start(bf16[120,1024]{1,0:T(8,128)(2,1)} %get-tuple-element.284), channel_id=1, source_target_pairs={{0,1},{1,0},{2,3},{3,2},{4,5},{5,4},{6,7},{7,6},{8,9},{9,8},{10,11... | collective-permute-start | bytes 737288 | tf_op jit(solution)/shard_map/ppermute | solution.py:490
  61.7 30.1 %collective-permute-start.27 = (bf16[120,1024]{1,0:T(8,128)(2,1)}, bf16[120,1024]{1,0:T(8,128)(2,1)S(1)}, u32[]{:S(2)}, u32[]{:S(2)}) collective-permute-start(bf16[120,1024]{1,0:T(8,128)(2,1)} %get-tuple-element.280), channel_id=1, source_target_pairs={{0,5},{1,4},{2,7},{3,6},{4,1},{5,0},{6,3},{7,2},{8,13},{9,12},{10,... | collective-permute-start | bytes 737288 | tf_op jit(solution)/shard_map/ppermute | solution.py:490
  66.6 25.1 %collective-permute-start.26 = (bf16[120,1024]{1,0:T(8,128)(2,1)}, bf16[120,1024]{1,0:T(8,128)(2,1)S(1)}, u32[]{:S(2)}, u32[]{:S(2)}) collective-permute-start(bf16[120,1024]{1,0:T(8,128)(2,1)} %get-tuple-element.278), channel_id=1, source_target_pairs={{0,4},{1,5},{2,6},{3,7},{4,0},{5,1},{6,2},{7,3},{8,12},{9,13},{10,... | collective-permute-start | bytes 737288 | tf_op jit(solution)/shard_map/ppermute | solution.py:490
  70.7 6.2 %copy-start.16 = (bf16[128,1024]{1,0:T(8,128)(2,1)}, bf16[128,1024]{1,0:T(8,128)(2,1)S(1)}, u32[]{:S(2)}) copy-start(bf16[128,1024]{1,0:T(8,128)(2,1)S(1)} %get-tuple-element.378.grads) | copy-start | bytes 786436 | tf_op jit(solution)/shard_map/cond
  70.7 1.8 %collective-permute-start.6 = (bf16[128,1536]{1,0:T(8,128)(2,1)S(1)}, bf16[128,1536]{1,0:T(8,128)(2,1)S(1)}, u32[]{:S(2)}, u32[]{:S(2)}) collective-permute-start(bf16[128,1536]{1,0:T(8,128)(2,1)S(1)} %get-tuple-element.128), channel_id=1, source_target_pairs={{0,8},{8,0},{16,24},{24,16},{1,9},{9,1},{17,25},{25,17},{2,10},{10... | collective-permute-start | bytes 1179656 | tf_op jit(solution)/shard_map/cond/branch_1_fun/ppermute | solution.py:493
  72.6 11.4 %collective-permute-start.8 = (bf16[128,1536]{1,0:T(8,128)(2,1)S(1)}, bf16[128,1536]{1,0:T(8,128)(2,1)S(1)}, u32[]{:S(2)}, u32[]{:S(2)}) collective-permute-start(bf16[128,1536]{1,0:T(8,128)(2,1)S(1)} %total.5), channel_id=1, source_target_pairs={{0,16},{8,24},{16,0},{24,8},{1,17},{9,25},{17,1},{25,9},{2,18},{10... | collective-permute-start | bytes 1179656 | tf_op jit(solution)/shard_map/cond/branch_1_fun/ppermute | solution.py:493
  74.3 2.7 %collective-permute-start.7 = (bf16[64,1536]{1,0:T(8,128)(2,1)S(1)}, bf16[64,1536]{1,0:T(8,128)(2,1)S(1)}, u32[]{:S(2)}, u32[]{:S(2)}) collective-permute-start(bf16[64,1536]{1,0:T(8,128)(2,1)S(1)} %act.7.own), channel_id=1, source_target_pairs={{0,8},{8,0},{16,24},{24,16},{1,9},{9,1},{17,25},{25,17},{2,10},{10... | collective-permute-start | bytes 589832 | tf_op jit(solution)/shard_map/cond/branch_1_fun/ppermute | solution.py:493
  76.9 8.0 %copy-start.8 = (f32[64,1536]{1,0:T(8,128)}, f32[64,1536]{1,0:T(8,128)S(1)}, u32[]{:S(2)}) copy-start(f32[64,1536]{1,0:T(8,128)S(1)} %get-tuple-element.385.next_keep) | copy-start | bytes 1179652 | tf_op jit(solution)/shard_map/cond
  77.0 8.0 %copy-start.18 = (bf16[64,1536]{1,0:T(8,128)(2,1)}, bf16[64,1536]{1,0:T(8,128)(2,1)S(1)}, u32[]{:S(2)}) copy-start(bf16[64,1536]{1,0:T(8,128)(2,1)S(1)} %collective-permute-done.7.core) | copy-start | bytes 589828 | tf_op jit(solution)/shard_map/cond
  80.2 1.5 %collective-permute-start.9 = (bf16[64,1536]{1,0:T(8,128)(2,1)S(1)}, bf16[64,1536]{1,0:T(8,128)(2,1)S(1)}, u32[]{:S(2)}, u32[]{:S(2)}) collective-permute-start(bf16[64,1536]{1,0:T(8,128)(2,1)S(1)} %get-tuple-element.142), channel_id=1, source_target_pairs={{0,8},{8,0},{16,24},{24,16},{1,9},{9,1},{17,25},{25,17},{2,10},{10... | collective-permute-start | bytes 589832 | tf_op jit(solution)/shard_map/cond/branch_1_fun/ppermute | solution.py:493
  81.8 5.2 %copy-start.19 = (bf16[64,1536]{1,0:T(8,128)(2,1)}, bf16[64,1536]{1,0:T(8,128)(2,1)S(1)}, u32[]{:S(2)}) copy-start(bf16[64,1536]{1,0:T(8,128)(2,1)S(1)} %collective-permute-done.9.next_core) | copy-start | bytes 589828 | tf_op jit(solution)/shard_map/cond
  85.0 2.1 %collective-permute-start.10 = (bf16[128,1536]{1,0:T(8,128)(2,1)}, bf16[128,1536]{1,0:T(8,128)(2,1)}, u32[]{:S(2)}, u32[]{:S(2)}) collective-permute-start(bf16[128,1536]{1,0:T(8,128)(2,1)} %get-tuple-element.379.own), channel_id=1, source_target_pairs={{0,8},{8,0},{16,24},{24,16},{1,9},{9,1},{17,25},{25,17},{2,10},{10... | collective-permute-start | bytes 1179656 | tf_op jit(solution)/shard_map/cond/branch_1_fun/ppermute | solution.py:493
  90.2 7.4 %collective-permute-start.23 = (bf16[64,1536]{1,0:T(8,128)(2,1)S(1)}, bf16[64,1536]{1,0:T(8,128)(2,1)S(1)}, u32[]{:S(2)}, u32[]{:S(2)}) collective-permute-start(bf16[64,1536]{1,0:T(8,128)(2,1)S(1)} %get-tuple-element.271), channel_id=1, source_target_pairs={{0,16},{8,24},{16,0},{24,8},{1,17},{9,25},{17,1},{25,9},{2,18},{10... | collective-permute-start | bytes 589832 | tf_op jit(solution)/shard_map/ppermute | solution.py:493
  91.8 25.4 %collective-permute-start.30 = (bf16[120,1024]{1,0:T(8,128)(2,1)}, bf16[120,1024]{1,0:T(8,128)(2,1)S(1)}, u32[]{:S(2)}, u32[]{:S(2)}) collective-permute-start(bf16[120,1024]{1,0:T(8,128)(2,1)} %get-tuple-element.287), channel_id=1, source_target_pairs={{0,7},{1,6},{2,5},{3,4},{4,3},{5,2},{6,1},{7,0},{8,15},{9,14},{10,... | collective-permute-start | bytes 737288 | tf_op jit(solution)/shard_map/ppermute | solution.py:490
  95.3 21.9 %collective-permute-start.29 = (bf16[120,1024]{1,0:T(8,128)(2,1)}, bf16[120,1024]{1,0:T(8,128)(2,1)S(1)}, u32[]{:S(2)}, u32[]{:S(2)}) collective-permute-start(bf16[120,1024]{1,0:T(8,128)(2,1)} %get-tuple-element.285), channel_id=1, source_target_pairs={{0,6},{1,7},{2,4},{3,5},{4,2},{5,3},{6,0},{7,1},{8,14},{9,15},{10,... | collective-permute-start | bytes 737288 | tf_op jit(solution)/shard_map/ppermute | solution.py:490
  95.6 23.1 %collective-permute-start.22 = (bf16[120,1024]{1,0:T(8,128)(2,1)}, bf16[120,1024]{1,0:T(8,128)(2,1)S(1)}, u32[]{:S(2)}, u32[]{:S(2)}) collective-permute-start(bf16[120,1024]{1,0:T(8,128)(2,1)} %get-tuple-element.268), channel_id=1, source_target_pairs={{0,2},{1,3},{2,0},{3,1},{4,6},{5,7},{6,4},{7,5},{8,10},{9,11},{10,... | collective-permute-start | bytes 737288 | tf_op jit(solution)/shard_map/ppermute | solution.py:490
  97.6 10.4 %copy-start = (s32[192,2]{0,1:T(2,128)S(1)}, s32[192,2]{0,1:T(2,128)}, u32[]{:S(2)}) copy-start(s32[192,2]{0,1:T(2,128)} %param.15) | copy-start | bytes 4612
  97.6 10.4 %copy-start.1 = (f32[192,2]{0,1:T(2,128)S(1)}, f32[192,2]{0,1:T(2,128)}, u32[]{:S(2)}) copy-start(f32[192,2]{0,1:T(2,128)} %param.16) | copy-start | bytes 4612
  98.4 3.8 %collective-permute-start.11 = (bf16[64,1536]{1,0:T(8,128)(2,1)}, bf16[64,1536]{1,0:T(8,128)(2,1)}, u32[]{:S(2)}, u32[]{:S(2)}) collective-permute-start(bf16[64,1536]{1,0:T(8,128)(2,1)} %act.9.own), channel_id=1, source_target_pairs={{0,8},{8,0},{16,24},{24,16},{1,9},{9,1},{17,25},{25,17},{2,10},{10... | collective-permute-start | bytes 589832 | tf_op jit(solution)/shard_map/cond/branch_1_fun/ppermute | solution.py:493
  105.0 5.4 %copy-start.23 = (bf16[64,1024]{1,0:T(8,128)(2,1)}, bf16[64,1024]{1,0:T(8,128)(2,1)S(1)}, u32[]{:S(2)}) copy-start(bf16[64,1024]{1,0:T(8,128)(2,1)S(1)} %get-tuple-element.309.refs_17_) | copy-start | bytes 393220
  105.1 5.4 %copy-start.24 = (bf16[64,1024]{1,0:T(8,128)(2,1)}, bf16[64,1024]{1,0:T(8,128)(2,1)S(1)}, u32[]{:S(2)}) copy-start(bf16[64,1024]{1,0:T(8,128)(2,1)S(1)} %get-tuple-element.310.refs_18_) | copy-start | bytes 393220
  105.1 13.7 %collective-permute-start.24 = (bf16[120,512]{1,0:T(8,128)(2,1)}, bf16[120,512]{1,0:T(8,128)(2,1)S(1)}, u32[]{:S(2)}, u32[]{:S(2)}) collective-permute-start(bf16[120,512]{1,0:T(8,128)(2,1)} %get-tuple-element.274), channel_id=1, source_target_pairs={{0,3},{1,2},{2,1},{3,0},{4,7},{5,6},{6,5},{7,4},{8,11},{9,10},{10,... | collective-permute-start | bytes 368648 | tf_op jit(solution)/shard_map/ppermute | solution.py:490
  107.9 10.8 %collective-permute-start.25 = (bf16[120,512]{1,0:T(8,128)(2,1)}, bf16[120,512]{1,0:T(8,128)(2,1)S(1)}, u32[]{:S(2)}, u32[]{:S(2)}) collective-permute-start(bf16[120,512]{1,0:T(8,128)(2,1)} %get-tuple-element.275), channel_id=1, source_target_pairs={{0,3},{1,2},{2,1},{3,0},{4,7},{5,6},{6,5},{7,4},{8,11},{9,10},{10,... | collective-permute-start | bytes 368648 | tf_op jit(solution)/shard_map/ppermute | solution.py:490
  (12 other events, 29.6 us)

commit v7 on v6

--- a/solution.py
+++ b/solution.py
@@ -592,11 +592,12 @@
     group_far, back_far, state_1, group_0, back_0 = stage(
         lambda a, b, c: far_stage(a, b, quarter, c), blocks(far), state_0, blocks(near[1])
     )
-    start_back(far + near[0], back_far + back_0, *blocks(last))
+    start_back(far, back_far, *blocks(last))
+    start_back(near[0], back_0, *blocks(last))
     group_last, back_last, state_2, group_1, back_1 = stage(
         lambda a, b, c: far_stage(a, b, size, c), blocks(last, group_far[3]), x_part(state_1), blocks(near[2])
     )
-    start_back(last, back_last, *arrived(far + near[0]))
+    start_back(last, back_last, *arrived(far))
     start_back(near[1], back_1)
     group_2, back_2 = stage(rest_stage, x_part(state_2))
     start_back(near[2], back_2)

time: 122 us -> 122 us (level)
  no operation moved by 1% of the time
where the time goes in v7:
time: 122 us; the launch traced here: 121 us
  Pallas kernels  67.7 us (55%)
  starting transfers between devices  36.1 us (30%)
  waiting for transfers between devices  15.9 us (13%)
    pallas_call x23, Pallas kernels, call(): pl.pallas_call(kernel, out_shape=out_shapes, in_specs=[pl.BlockSpec(memor...  42.1 us
    ppermute x15, starting transfers between devices, across(): lax.ppermute(x, 'expert', [(i, i ^ s) for i in range(n_expert)])  26.4 us
    pallas_call x3, Pallas kernels, other_half(): pl.pallas_call(kernel, out_shape=[shape((rows, features), BF), shape((row...  11.2 us
    ppermute x16, starting transfers between devices, beside(): return lax.ppermute(x, 'dp', [(i, i ^ s) for i in range(n_dp)])  9.66 us
    ppermute x15, waiting for transfers between devices, across(): lax.ppermute(x, 'expert', [(i, i ^ s) for i in range(n_expert)])  9.29 us
    pallas_call x1, Pallas kernels, grads_step(): pl.pallas_call(lambda *refs: grads_kernel(len(groups), *refs), out_shape=...  6.7 us
    ppermute x16, waiting for transfers between devices, beside(): return lax.ppermute(x, 'dp', [(i, i ^ s) for i in range(n_dp)])  6.62 us
    pallas_call x1, Pallas kernels, down_own_alone(): pl.pallas_call(kernel, out_shape=[sums, sums, shape(w_in.shape, BF), shap...  3.83 us
  transfers between devices with their start and end apart: 31, of which 10 were waited for; matrix products, arithmetic and copies ran while one was open for 0% of the time, Pallas kernels for 51%

profile of v7, /device:TPU:0, one launch (start us, length us, event | category | flops | bytes accessed | tf_op | source)
XLA Modules:
  0.0 121.1 jit_solution(17966410760691112408)
XLA Ops:
  0.7 3.8 %prep.1 = (bf16[120,1024]{1,0:T(8,128)(2,1)S(1)}, bf16[120,1024]{1,0:T(8,128)(2,1)}, bf16[120,1024]{1,0:T(8,128)(2,1)}, bf16[120,1024]{1,0:T(8,128)(2,1)}, bf16[...) custom-call(s32[2]{0:T(128)S(1)} %pad_add_fusion.refs_0_, ...), custom_call_target="tpu_custom_call" | custom-call | flops 1 | bytes 1 | tf_op jit(solution)/shard_map/prep/pallas_call | solution.py:77
  4.5 3.0 %collective-permute-start.15 = (bf16[120,1024]{1,0:T(8,128)(2,1)}, bf16[120,1024]{1,0:T(8,128)(2,1)S(1)}, u32[]{:S(2)}, u32[]{:S(2)}) collective-permute-start(bf16[120,1024]{1,0:T(8,128)(2,1)} %get-tuple-element.249), channel_id=1, source_target_pairs={{0,1},{1,0},{2,3},{3,2},{4,5},{5,4},{6,7},{7,6},{8,9},{9,8},{10,11... | collective-permute-start | bytes 737288 | tf_op jit(solution)/shard_map/ppermute | solution.py:490
  7.5 2.6 %collective-permute-start.12 = (bf16[120,1024]{1,0:T(8,128)(2,1)}, bf16[120,1024]{1,0:T(8,128)(2,1)S(1)}, u32[]{:S(2)}, u32[]{:S(2)}) collective-permute-start(bf16[120,1024]{1,0:T(8,128)(2,1)} %get-tuple-element.245), channel_id=1, source_target_pairs={{0,4},{1,5},{2,6},{3,7},{4,0},{5,1},{6,2},{7,3},{8,12},{9,13},{10,... | collective-permute-start | bytes 737288 | tf_op jit(solution)/shard_map/ppermute | solution.py:490
  10.1 1.9 %collective-permute-start.14 = (bf16[120,1024]{1,0:T(8,128)(2,1)}, bf16[120,1024]{1,0:T(8,128)(2,1)S(1)}, u32[]{:S(2)}, u32[]{:S(2)}) collective-permute-start(bf16[120,1024]{1,0:T(8,128)(2,1)} %get-tuple-element.247), channel_id=1, source_target_pairs={{0,2},{1,3},{2,0},{3,1},{4,6},{5,7},{6,4},{7,5},{8,10},{9,11},{10,... | collective-permute-start | bytes 737288 | tf_op jit(solution)/shard_map/ppermute | solution.py:490
  12.0 1.7 %collective-permute-done.15 = bf16[120,1024]{1,0:T(8,128)(2,1)S(1)} collective-permute-done((bf16[120,1024]{1,0:T(8,128)(2,1)}, bf16[120,1024]{1,0:T(8,128)(2,1)S(1)}, u32[]{:S(2)}, u32[]{:S(2)}) %collective-permute-start.15) | collective-permute-done | bytes 245792 | tf_op jit(solution)/shard_map/ppermute | solution.py:490
  13.7 8.4 %conditional.4 = (bf16[128,1024]{1,0:T(8,128)(2,1)}, bf16[128,1024]{1,0:T(8,128)(2,1)}, f32[128,1536]{1,0:T(8,128)}, bf16[128,1536]{1,0:T(8,128)(2,1)}, bf16[128...) conditional(s32[]{:T(128)} %convert_element_type.2, () %tuple.67, (s32[2]{0:T(128)S(1)}, ...), branch_computations={%region_0.1_spmd, %region_1.2_spmd} | conditional | flops 3 | bytes 2097214 | solution.py:505
  13.7 4.3 %up.8 = (bf16[128,1024]{1,0:T(8,128)(2,1)}, bf16[128,1024]{1,0:T(8,128)(2,1)}, bf16[128,1536]{1,0:T(8,128)(2,1)S(1)}, bf16[1024,2048]{1,0:T(8,128)(2,1)S(1)}, bf16[1024,1024]{1,0:T(8,128)(2,1)S(1)}) custom-call(s32[2]{0:T(128)S(1)} %get-tuple-element.72.ids, bf16[120,1024]{1,0:T(8,128)(2,1)S(1)} %get-tuple-element.73.refs_0_, ...), custom_call_target="tpu_custom_call" | custom-call | flops 1 | bytes 1 | tf_op jit(solution)/shard_map/cond/branch_1_fun/up/pallas_call | solution.py:171
  18.1 2.7 %up.9.keep = f32[128,1536]{1,0:T(8,128)} custom-call(s32[2]{0:T(128)S(1)} %get-tuple-element.72.ids, bf16[128,1024]{1,0:T(8,128)(2,1)} %get-tuple-element.80.rows, bf16[128,1024]{1,0:T(8,128)(2,1)} %get-tuple-element.322.grads, bf16[1024,2048]{1,0:T(8,128)(2,1)S(1)} %get-tuple-element.81.w_in, bf16[1024,1024]{1,0:T(8,128)(2,1)S(1)} %get-tuple-element.82.w_out), custom_call_target="tpu_custom_call" | custom-call | flops 1 | bytes 1 | tf_op jit(solution)/shard_map/cond/branch_1_fun/up/pallas_call | solution.py:93
  20.8 1.3 %total.3 = (bf16[128,768]{1,0:T(8,128)(2,1)S(1)}, bf16[128,768]{1,0:T(8,128)(2,1)S(1)}) custom-call(f32[128,1536]{1,0:T(8,128)} %up.9.keep, bf16[128,1536]{1,0:T(8,128)(2,1)} %collective-permute-done.core), custom_call_target="tpu_custom_call" | custom-call | flops 1 | bytes 1 | tf_op jit(solution)/shard_map/cond/branch_1_fun/total/pallas_call | solution.py:93
  22.1 1.8 %collective-permute-start.17 = (bf16[128,768]{1,0:T(8,128)(2,1)S(1)}, bf16[128,768]{1,0:T(8,128)(2,1)S(1)}, u32[]{:S(2)}, u32[]{:S(2)}) collective-permute-start(bf16[128,768]{1,0:T(8,128)(2,1)S(1)} %get-tuple-element.250), channel_id=1, source_target_pairs={{0,16},{8,24},{16,0},{24,8},{1,17},{9,25},{17,1},{25,9},{2,18},{10... | collective-permute-start | bytes 589832 | tf_op jit(solution)/shard_map/ppermute | solution.py:493
  24.2 3.5 %collective-permute-done.12 = bf16[120,1024]{1,0:T(8,128)(2,1)S(1)} collective-permute-done((bf16[120,1024]{1,0:T(8,128)(2,1)}, bf16[120,1024]{1,0:T(8,128)(2,1)S(1)}, u32[]{:S(2)}, u32[]{:S(2)}) %collective-permute-start.12) | collective-permute-done | bytes 245792 | tf_op jit(solution)/shard_map/ppermute | solution.py:490
  27.8 4.0 %collective-permute-done.13 = bf16[120,1024]{1,0:T(8,128)(2,1)S(1)} collective-permute-done((bf16[120,1024]{1,0:T(8,128)(2,1)}, bf16[120,1024]{1,0:T(8,128)(2,1)S(1)}, u32[]{:S(2)}, u32[]{:S(2)}) %collective-permute-start.13) | collective-permute-done | bytes 245792 | tf_op jit(solution)/shard_map/ppermute | solution.py:490
  31.8 3.5 %collective-permute-start.16 = (bf16[120,1024]{1,0:T(8,128)(2,1)}, bf16[120,1024]{1,0:T(8,128)(2,1)S(1)}, u32[]{:S(2)}, u32[]{:S(2)}) collective-permute-start(bf16[120,1024]{1,0:T(8,128)(2,1)} %get-tuple-element.252), channel_id=1, source_target_pairs={{0,6},{1,7},{2,4},{3,5},{4,2},{5,3},{6,0},{7,1},{8,14},{9,15},{10,... | collective-permute-start | bytes 737288 | tf_op jit(solution)/shard_map/ppermute | solution.py:490
  35.3 1.3 %collective-permute-start.19 = (bf16[120,1024]{1,0:T(8,128)(2,1)}, bf16[120,1024]{1,0:T(8,128)(2,1)S(1)}, u32[]{:S(2)}, u32[]{:S(2)}) collective-permute-start(bf16[120,1024]{1,0:T(8,128)(2,1)} %get-tuple-element.260), channel_id=1, source_target_pairs={{0,7},{1,6},{2,5},{3,4},{4,3},{5,2},{6,1},{7,0},{8,15},{9,14},{10,... | collective-permute-start | bytes 737288 | tf_op jit(solution)/shard_map/ppermute | solution.py:490
  36.6 23.0 %conditional.5 = (bf16[128,1024]{1,0:T(8,128)(2,1)S(1)}, bf16[128,1024]{1,0:T(8,128)(2,1)S(1)}, bf16[128,1536]{1,0:T(8,128)(2,1)}, bf16[128,1536]{1,0:T(8,128)(2...) conditional(s32[]{:T(128)} %convert_element_type.2, () %tuple.70, ...), branch_computations={%region_2.3_spmd, %region_3.4_spmd} | conditional | flops 20000000000 | bytes 24249056 | solution.py:505
  36.6 3.5 %up.10 = (bf16[128,1024]{1,0:T(8,128)(2,1)S(1)}, bf16[128,1024]{1,0:T(8,128)(2,1)S(1)}, bf16[128,1536]{1,0:T(8,128)(2,1)S(1)}, bf16[1024,2048]{1,0:T(8,128)(2,1)S(1)}, bf16[1024,1024]{1,0:T(8,128)(2,1)S(1)}) custom-call(s32[2]{0:T(128)S(1)} %get-tuple-element.85.ids, bf16[120,1024]{1,0:T(8,128)(2,1)S(1)} %get-tuple-element.86.refs_0_, ...), custom_call_target="tpu_custom_call" | custom-call | flops 1 | bytes 1 | tf_op jit(solution)/shard_map/cond/branch_1_fun/up/pallas_call | solution.py:171
  40.2 1.3 %up.11.keep = f32[128,1536]{1,0:T(8,128)S(1)} custom-call(s32[2]{0:T(128)S(1)} %get-tuple-element.85.ids, bf16[128,1024]{1,0:T(8,128)(2,1)S(1)} %get-tuple-element.93.rows, bf16[128,1024]{1,0:T(8,128)(2,1)S(1)} %get-tuple-element.345.grads, bf16[1024,2048]{1,0:T(8,128)(2,1)S(1)} %get-tuple-element.94.w_in.refs_1_, ...), custom_call_target="tpu_custom_call" | custom-call | flops 1 | bytes 1 | tf_op jit(solution)/shard_map/cond/branch_1_fun/up/pallas_call | solution.py:93
  42.0 1.6 %collective-permute-start.3 = (bf16[128,1536]{1,0:T(8,128)(2,1)S(1)}, bf16[128,1536]{1,0:T(8,128)(2,1)S(1)}, u32[]{:S(2)}, u32[]{:S(2)}) collective-permute-start(bf16[128,1536]{1,0:T(8,128)(2,1)S(1)} %total.4), channel_id=1, source_target_pairs={{0,16},{8,24},{16,0},{24,8},{1,17},{9,25},{17,1},{25,9},{2,18},{10... | collective-permute-start | bytes 1179656 | tf_op jit(solution)/shard_map/cond/branch_1_fun/ppermute | solution.py:493
  43.6 1.5 %act.5.own = bf16[128,1536]{1,0:T(8,128)(2,1)S(1)} custom-call(f32[128,1536]{1,0:T(8,128)} %get-tuple-element.97.keep, bf16[128,1536]{1,0:T(8,128)(2,1)} %get-tuple-element.98.core, bf16[128,768]{1,0:T(8,128)(2,1)S(1)} %get-tuple-element.99.refs_0_, bf16[128,768]{1,0:T(8,128)(2,1)S(1)} %get-tuple-element.100.refs_1_), custom_call_target="tpu_custom_call" | custom-call | flops 1 | bytes 1 | tf_op jit(solution)/shard_map/cond/branch_1_fun/act/pallas_call | solution.py:93
  45.1 2.1 %up.12 = (bf16[64,1024]{1,0:T(8,128)(2,1)S(1)}, bf16[64,1024]{1,0:T(8,128)(2,1)S(1)}, bf16[64,1536]{1,0:T(8,128)(2,1)S(1)}, f32[64,1536]{1,0:T(8,128)S(1)}) custom-call(s32[2]{0:T(128)S(1)} %get-tuple-element.85.ids, bf16[120,1024]{1,0:T(8,128)(2,1)S(1)} %copy-done.28, bf16[1024,2048]{1,0:T(8,128)(2,1)S(1)} %get-tuple-element.94.w_in.refs_1_, ...), custom_call_target="tpu_custom_call" | custom-call | flops 20000000000 | bytes 1 | tf_op jit(solution)/shard_map/cond/branch_1_fun/up/pallas_call | solution.py:93
  47.3 3.4 %down.8 = (bf16[120,1024]{1,0:T(8,128)(2,1)}, bf16[120,1024]{1,0:T(8,128)(2,1)}) custom-call(s32[2]{0:T(128)S(1)} %get-tuple-element.85.ids, bf16[128,1536]{1,0:T(8,128)(2,1)S(1)} %act.5.own, bf16[128,1536]{1,0:T(8,128)(2,1)S(1)} %collective-permute-done.2.core, bf16[1024,2048]{1,0:T(8,128)(2,1)S(1)} %get-tuple-element.94.w_in.refs_1_, ...), custom_call_target="tpu_custom_call" | custom-call | flops 1 | bytes 1 | tf_op jit(solution)/shard_map/cond/branch_1_fun/down/pallas_call | solution.py:93
  51.2 2.0 %collective-permute-done.3.other = bf16[128,1536]{1,0:T(8,128)(2,1)S(1)} collective-permute-done((bf16[128,1536]{1,0:T(8,128)(2,1)S(1)}, bf16[128,1536]{1,0:T(8,128)(2,1)S(1)}, u32[]{:S(2)}, u32[]{:S(2)}) %collective-permute-start.3) | collective-permute-done | bytes 393248 | tf_op jit(solution)/shard_map/cond/branch_1_fun/ppermute | solution.py:493
  53.2 1.1 act.6
  54.3 2.0 %down.9 = (f32[128,1024]{1,0:T(8,128)S(1)}, f32[128,1024]{1,0:T(8,128)S(1)}) custom-call(s32[2]{0:T(128)S(1)} %get-tuple-element.85.ids, bf16[128,1536]{1,0:T(8,128)(2,1)} %get-tuple-element.346.own, bf16[1024,2048]{1,0:T(8,128)(2,1)S(1)} %get-tuple-element.94.w_in.refs_1_, bf16[1024,1024]{1,0:T(8,128)(2,1)S(1)} %get-tuple-element.95.w_out.refs_2_), custom_call_target="tpu_custom_call" | custom-call | flops 1 | bytes 1 | tf_op jit(solution)/shard_map/cond/branch_1_fun/down/pallas_call | solution.py:93
  56.4 3.2 %down.10 = (bf16[120,1024]{1,0:T(8,128)(2,1)}, bf16[120,1024]{1,0:T(8,128)(2,1)}) custom-call(s32[2]{0:T(128)S(1)} %get-tuple-element.85.ids, f32[128,1024]{1,0:T(8,128)S(1)} %get-tuple-element.111.out_rows, f32[128,1024]{1,0:T(8,128)S(1)} %get-tuple-element.112.grad_rows, bf16[128,1536]{1,0:T(8,128)(2,1)} %collective-permute-done.5.core, ...), custom_call_target="tpu_custom_call" | custom-call | flops 1 | bytes 1 | tf_op jit(solution)/shard_map/cond/branch_1_fun/down/pallas_call | solution.py:93
  59.6 1.6 %collective-permute-start.20 = (bf16[64,1536]{1,0:T(8,128)(2,1)}, bf16[64,1536]{1,0:T(8,128)(2,1)S(1)}, u32[]{:S(2)}, u32[]{:S(2)}) collective-permute-start(bf16[64,1536]{1,0:T(8,128)(2,1)} %get-tuple-element.263), channel_id=1, source_target_pairs={{0,16},{8,24},{16,0},{24,8},{1,17},{9,25},{17,1},{25,9},{2,18},{10... | collective-permute-start | bytes 589832 | tf_op jit(solution)/shard_map/ppermute | solution.py:493
  61.2 4.9 %collective-permute-start.27 = (bf16[120,1024]{1,0:T(8,128)(2,1)}, bf16[120,1024]{1,0:T(8,128)(2,1)S(1)}, u32[]{:S(2)}, u32[]{:S(2)}) collective-permute-start(bf16[120,1024]{1,0:T(8,128)(2,1)} %get-tuple-element.280), channel_id=1, source_target_pairs={{0,5},{1,4},{2,7},{3,6},{4,1},{5,0},{6,3},{7,2},{8,13},{9,12},{10,... | collective-permute-start | bytes 737288 | tf_op jit(solution)/shard_map/ppermute | solution.py:490
  67.2 23.0 %conditional.6 = (bf16[128,1024]{1,0:T(8,128)(2,1)S(1)}, bf16[128,1024]{1,0:T(8,128)(2,1)}, bf16[128,1536]{1,0:T(8,128)(2,1)}, bf16[128,1536]{1,0:T(8,128)(2,1)}...) conditional(s32[]{:T(128)} %convert_element_type.2, () %tuple.66, ...), branch_computations={%region_4.5_spmd, %region_5.6_spmd} | conditional | flops 20000000000 | bytes 15729229 | solution.py:505
  67.2 3.5 %up.13 = (bf16[128,1024]{1,0:T(8,128)(2,1)S(1)}, bf16[128,1024]{1,0:T(8,128)(2,1)S(1)}, bf16[128,1536]{1,0:T(8,128)(2,1)S(1)}, bf16[1024,2048]{1,0:T(8,128)(2,1)S(1)}, bf16[1024,1024]{1,0:T(8,128)(2,1)S(1)}) custom-call(s32[2]{0:T(128)S(1)} %get-tuple-element.121.ids, bf16[120,1024]{1,0:T(8,128)(2,1)S(1)} %get-tuple-element.122.refs_0_, ...), custom_call_target="tpu_custom_call" | custom-call | flops 1 | bytes 1 | tf_op jit(solution)/shard_map/cond/branch_1_fun/up/pallas_call | solution.py:171
  70.8 1.5 %up.14.keep = f32[128,1536]{1,0:T(8,128)S(1)} custom-call(s32[2]{0:T(128)S(1)} %get-tuple-element.121.ids, bf16[128,1024]{1,0:T(8,128)(2,1)S(1)} %get-tuple-element.129.rows, bf16[128,1024]{1,0:T(8,128)(2,1)S(1)} %get-tuple-element.378.grads, bf16[1024,2048]{1,0:T(8,128)(2,1)S(1)} %get-tuple-element.130.w_in.refs_1_, ...), custom_call_target="tpu_custom_call" | custom-call | flops 1 | bytes 1 | tf_op jit(solution)/shard_map/cond/branch_1_fun/up/pallas_call | solution.py:93
  72.6 1.6 %collective-permute-start.8 = (bf16[128,1536]{1,0:T(8,128)(2,1)S(1)}, bf16[128,1536]{1,0:T(8,128)(2,1)S(1)}, u32[]{:S(2)}, u32[]{:S(2)}) collective-permute-start(bf16[128,1536]{1,0:T(8,128)(2,1)S(1)} %total.5), channel_id=1, source_target_pairs={{0,16},{8,24},{16,0},{24,8},{1,17},{9,25},{17,1},{25,9},{2,18},{10... | collective-permute-start | bytes 1179656 | tf_op jit(solution)/shard_map/cond/branch_1_fun/ppermute | solution.py:493
  74.4 2.5 %up.15 = (bf16[64,1024]{1,0:T(8,128)(2,1)S(1)}, bf16[64,1024]{1,0:T(8,128)(2,1)S(1)}, bf16[64,1536]{1,0:T(8,128)(2,1)S(1)}, f32[64,1536]{1,0:T(8,128)S(1)}) custom-call(s32[2]{0:T(128)S(1)} %get-tuple-element.121.ids, bf16[120,1024]{1,0:T(8,128)(2,1)} %get-tuple-element.137.refs_0_, bf16[1024,2048]{1,0:T(8,128)(2,1)S(1)} %get-tuple-element.130.w_in.refs_1_, ...), custom_call_target="tpu_custom_call" | custom-call | flops 20000000000 | bytes 1 | tf_op jit(solution)/shard_map/cond/branch_1_fun/up/pallas_call | solution.py:93
  77.0 3.3 %down.11 = bf16[120,1024]{1,0:T(8,128)(2,1)} custom-call(s32[2]{0:T(128)S(1)} %get-tuple-element.121.ids, bf16[64,1536]{1,0:T(8,128)(2,1)S(1)} %act.7.own, bf16[64,1536]{1,0:T(8,128)(2,1)S(1)} %collective-permute-done.7.core, bf16[1024,2048]{1,0:T(8,128)(2,1)S(1)} %get-tuple-element.130.w_in.refs_1_, bf16[1024,1024]{1,0:T(8,128)(2,1)S(1)} %get-tuple-element.131.w_out.refs_2_), custom_call_target="tpu_custom_call" | custom-call | flops 1 | bytes 1 | tf_op jit(solution)/shard_map/cond/branch_1_fun/down/pallas_call | solution.py:93
  80.7 1.1 collective-permute-done.9.next_core
  81.8 2.2 %collective-permute-done.8.other = bf16[128,1536]{1,0:T(8,128)(2,1)S(1)} collective-permute-done((bf16[128,1536]{1,0:T(8,128)(2,1)S(1)}, bf16[128,1536]{1,0:T(8,128)(2,1)S(1)}, u32[]{:S(2)}, u32[]{:S(2)}) %collective-permute-start.8) | collective-permute-done | bytes 393248 | tf_op jit(solution)/shard_map/cond/branch_1_fun/ppermute | solution.py:493
  85.0 2.0 %down.12 = (f32[128,1024]{1,0:T(8,128)S(1)}, f32[128,1024]{1,0:T(8,128)S(1)}) custom-call(s32[2]{0:T(128)S(1)} %get-tuple-element.121.ids, bf16[128,1536]{1,0:T(8,128)(2,1)} %get-tuple-element.379.own, bf16[1024,2048]{1,0:T(8,128)(2,1)S(1)} %get-tuple-element.130.w_in.refs_1_, bf16[1024,1024]{1,0:T(8,128)(2,1)S(1)} %get-tuple-element.131.w_out.refs_2_), custom_call_target="tpu_custom_call" | custom-call | flops 1 | bytes 1 | tf_op jit(solution)/shard_map/cond/branch_1_fun/down/pallas_call | solution.py:93
  87.1 3.1 %down.13 = (bf16[120,1024]{1,0:T(8,128)(2,1)}, bf16[120,1024]{1,0:T(8,128)(2,1)}) custom-call(s32[2]{0:T(128)S(1)} %get-tuple-element.121.ids, f32[128,1024]{1,0:T(8,128)S(1)} %get-tuple-element.144.out_rows, f32[128,1024]{1,0:T(8,128)S(1)} %get-tuple-element.145.grad_rows, bf16[128,1536]{1,0:T(8,128)(2,1)} %collective-permute-done.10.core, ...), custom_call_target="tpu_custom_call" | custom-call | flops 1 | bytes 1 | tf_op jit(solution)/shard_map/cond/branch_1_fun/down/pallas_call | solution.py:93
  90.2 1.6 %collective-permute-start.23 = (bf16[64,1536]{1,0:T(8,128)(2,1)S(1)}, bf16[64,1536]{1,0:T(8,128)(2,1)S(1)}, u32[]{:S(2)}, u32[]{:S(2)}) collective-permute-start(bf16[64,1536]{1,0:T(8,128)(2,1)S(1)} %get-tuple-element.271), channel_id=1, source_target_pairs={{0,16},{8,24},{16,0},{24,8},{1,17},{9,25},{17,1},{25,9},{2,18},{10... | collective-permute-start | bytes 589832 | tf_op jit(solution)/shard_map/ppermute | solution.py:493
  91.8 3.5 %collective-permute-start.29 = (bf16[120,1024]{1,0:T(8,128)(2,1)}, bf16[120,1024]{1,0:T(8,128)(2,1)S(1)}, u32[]{:S(2)}, u32[]{:S(2)}) collective-permute-start(bf16[120,1024]{1,0:T(8,128)(2,1)} %get-tuple-element.283), channel_id=1, source_target_pairs={{0,7},{1,6},{2,5},{3,4},{4,3},{5,2},{6,1},{7,0},{8,15},{9,14},{10,... | collective-permute-start | bytes 737288 | tf_op jit(solution)/shard_map/ppermute | solution.py:490
  95.6 1.7 %collective-permute-start.22 = (bf16[120,1024]{1,0:T(8,128)(2,1)}, bf16[120,1024]{1,0:T(8,128)(2,1)S(1)}, u32[]{:S(2)}, u32[]{:S(2)}) collective-permute-start(bf16[120,1024]{1,0:T(8,128)(2,1)} %get-tuple-element.268), channel_id=1, source_target_pairs={{0,2},{1,3},{2,0},{3,1},{4,6},{5,7},{6,4},{7,5},{8,10},{9,11},{10,... | collective-permute-start | bytes 737288 | tf_op jit(solution)/shard_map/ppermute | solution.py:490
  97.6 7.4 %conditional.7 = (bf16[64,1024]{1,0:T(8,128)(2,1)S(1)}, bf16[64,1024]{1,0:T(8,128)(2,1)S(1)}, bf16[64,1536]{1,0:T(8,128)(2,1)}, bf16[64,1536]{1,0:T(8,128)(2,1)}...) conditional(s32[]{:T(128)} %convert_element_type.2, () %tuple.76, (f32[64,1536]{1,0:T(8,128)S(1)}, ...), branch_computations={%region_6.7_spmd, %region_7.8_spmd} | conditional | flops 3 | bytes 901180 | solution.py:505
  98.4 3.8 %down.14 = (f32[64,1024]{1,0:T(8,128)S(1)}, f32[64,1024]{1,0:T(8,128)S(1)}, bf16[1024,2048]{1,0:T(8,128)(2,1)S(1)}, bf16[1024,1024]{1,0:T(8,128)(2,1)S(1)}) custom-call(s32[2]{0:T(128)S(1)} %get-tuple-element.159.ids, bf16[64,1536]{1,0:T(8,128)(2,1)} %act.9.own, bf16[1024,2048]{1,0:T(8,128)(2,1)} %get-tuple-element.160.far_in, ...), custom_call_target="tpu_custom_call" | custom-call | flops 1 | bytes 1 | tf_op jit(solution)/shard_map/cond/branch_1_fun/down/pallas_call | solution.py:337
  102.2 2.8 %down.15 = (bf16[120,512]{1,0:T(8,128)(2,1)}, bf16[120,512]{1,0:T(8,128)(2,1)}) custom-call(s32[2]{0:T(128)S(1)} %get-tuple-element.159.ids, f32[64,1024]{1,0:T(8,128)S(1)} %get-tuple-element.162.out_rows, f32[64,1024]{1,0:T(8,128)S(1)} %get-tuple-element.163.grad_rows, bf16[64,1536]{1,0:T(8,128)(2,1)} %collective-permute-done.11.core, ...), custom_call_target="tpu_custom_call" | custom-call | flops 1 | bytes 1 | tf_op jit(solution)/shard_map/cond/branch_1_fun/down/pallas_call | solution.py:93
  105.0 2.9 %collective-permute-start.24 = (bf16[120,512]{1,0:T(8,128)(2,1)}, bf16[120,512]{1,0:T(8,128)(2,1)S(1)}, u32[]{:S(2)}, u32[]{:S(2)}) collective-permute-start(bf16[120,512]{1,0:T(8,128)(2,1)} %get-tuple-element.274), channel_id=1, source_target_pairs={{0,3},{1,2},{2,1},{3,0},{4,7},{5,6},{6,5},{7,4},{8,11},{9,10},{10,... | collective-permute-start | bytes 368648 | tf_op jit(solution)/shard_map/ppermute | solution.py:490
  108.0 2.4 %final.3 = (f32[192,1024]{1,0:T(8,128)S(1)}, f32[192,1024]{1,0:T(8,128)S(1)}) custom-call(s32[2]{0:T(128)S(1)} %pad_add_fusion.refs_0_, s32[2,192]{1,0:T(2,128)S(1)} %bitcast.9, f32[2,192]{1,0:T(2,128)S(1)} %bitcast.13, bf16[120,1024]{1,0:T(8,128)(2,1)} %get-tuple-element.285.refs_3_, bf16[120,1024]{1,0:T(8,128)(2,1)S(1)} %collective-permute-done.30.refs_4_, ...), custom_call_target="tpu_custom_call" | custom-call | flops 1 | bytes 1 | tf_op jit(solution)/shard_map/final/pallas_call | solution.py:93
  110.4 6.7 %grads.1 = (bf16[1024,2048]{1,0:T(8,128)(2,1)}, bf16[1024,1024]{1,0:T(8,128)(2,1)}) custom-call(s32[2]{0:T(128)S(1)} %pad_add_fusion.refs_0_, bf16[128,1024]{1,0:T(8,128)(2,1)} %get-tuple-element.294.refs_1_, bf16[128,1024]{1,0:T(8,128)(2,1)} %get-tuple-element.295.refs_2_, bf16[128,1536]{1,0:T(8,128)(2,1)S(1)} %get-tuple-element.296.refs_3_, ...), custom_call_target="tpu_custom_call" | custom-call | flops 1 | bytes 1 | tf_op jit(solution)/shard_map/grads/pallas_call | solution.py:397
  117.2 1.5 %final.4 = (f32[192,1024]{1,0:T(8,128)S(1)}, f32[192,1024]{1,0:T(8,128)S(1)}) custom-call(s32[2]{0:T(128)S(1)} %pad_add_fusion.refs_0_, s32[2,192]{1,0:T(2,128)S(1)} %bitcast.10, f32[2,192]{1,0:T(2,128)S(1)} %bitcast.14, bf16[120,1024]{1,0:T(8,128)(2,1)S(1)} %collective-permute-done.28.refs_3_, bf16[120,1024]{1,0:T(8,128)(2,1)S(1)} %collective-permute-done.29.refs_4_, ...), custom_call_target="tpu_custom_call" | custom-call | flops 1 | bytes 1 | tf_op jit(solution)/shard_map/final/pallas_call | solution.py:93
  118.7 2.4 %final.5 = (bf16[192,1024]{1,0:T(8,128)(2,1)}, bf16[192,1024]{1,0:T(8,128)(2,1)}) custom-call(s32[2]{0:T(128)S(1)} %pad_add_fusion.refs_0_, s32[2,192]{1,0:T(2,128)S(1)} %bitcast.11, f32[2,192]{1,0:T(2,128)S(1)} %bitcast.15, bf16[120,1024]{1,0:T(8,128)(2,1)S(1)} %collective-permute-done.22.refs_3_, bf16[120,512]{1,0:T(8,128)(2,1)S(1)} %collective-permute-done.24.refs_4_, ...), custom_call_target="tpu_custom_call" | custom-call | flops 1 | bytes 1 | tf_op jit(solution)/shard_map/final/pallas_call | solution.py:93
  (106 shorter events, 6.3 us)
Async XLA Ops:
  4.5 9.2 %collective-permute-start.15 = (bf16[120,1024]{1,0:T(8,128)(2,1)}, bf16[120,1024]{1,0:T(8,128)(2,1)S(1)}, u32[]{:S(2)}, u32[]{:S(2)}) collective-permute-start(bf16[120,1024]{1,0:T(8,128)(2,1)} %get-tuple-element.249), channel_id=1, source_target_pairs={{0,1},{1,0},{2,3},{3,2},{4,5},{5,4},{6,7},{7,6},{8,9},{9,8},{10,11... | collective-permute-start | bytes 737288 | tf_op jit(solution)/shard_map/ppermute | solution.py:490
  7.5 20.2 %collective-permute-start.12 = (bf16[120,1024]{1,0:T(8,128)(2,1)}, bf16[120,1024]{1,0:T(8,128)(2,1)S(1)}, u32[]{:S(2)}, u32[]{:S(2)}) collective-permute-start(bf16[120,1024]{1,0:T(8,128)(2,1)} %get-tuple-element.245), channel_id=1, source_target_pairs={{0,4},{1,5},{2,6},{3,7},{4,0},{5,1},{6,2},{7,3},{8,12},{9,13},{10,... | collective-permute-start | bytes 737288 | tf_op jit(solution)/shard_map/ppermute | solution.py:490
  10.1 21.6 %collective-permute-start.13 = (bf16[120,1024]{1,0:T(8,128)(2,1)}, bf16[120,1024]{1,0:T(8,128)(2,1)S(1)}, u32[]{:S(2)}, u32[]{:S(2)}) collective-permute-start(bf16[120,1024]{1,0:T(8,128)(2,1)} %get-tuple-element.246), channel_id=1, source_target_pairs={{0,5},{1,4},{2,7},{3,6},{4,1},{5,0},{6,3},{7,2},{8,13},{9,12},{10,... | collective-permute-start | bytes 737288 | tf_op jit(solution)/shard_map/ppermute | solution.py:490
  10.1 21.6 %collective-permute-start.14 = (bf16[120,1024]{1,0:T(8,128)(2,1)}, bf16[120,1024]{1,0:T(8,128)(2,1)S(1)}, u32[]{:S(2)}, u32[]{:S(2)}) collective-permute-start(bf16[120,1024]{1,0:T(8,128)(2,1)} %get-tuple-element.247), channel_id=1, source_target_pairs={{0,2},{1,3},{2,0},{3,1},{4,6},{5,7},{6,4},{7,5},{8,10},{9,11},{10,... | collective-permute-start | bytes 737288 | tf_op jit(solution)/shard_map/ppermute | solution.py:490
  18.0 2.8 %collective-permute-start = (bf16[128,1536]{1,0:T(8,128)(2,1)S(1)}, bf16[128,1536]{1,0:T(8,128)(2,1)}, u32[]{:S(2)}, u32[]{:S(2)}) collective-permute-start(bf16[128,1536]{1,0:T(8,128)(2,1)S(1)} %get-tuple-element.79), channel_id=1, source_target_pairs={{0,8},{8,0},{16,24},{24,16},{1,9},{9,1},{17,25},{25,17},{2,10},{10... | collective-permute-start | bytes 1179656 | tf_op jit(solution)/shard_map/cond/branch_1_fun/ppermute | solution.py:493
  22.1 14.5 %collective-permute-start.17 = (bf16[128,768]{1,0:T(8,128)(2,1)S(1)}, bf16[128,768]{1,0:T(8,128)(2,1)S(1)}, u32[]{:S(2)}, u32[]{:S(2)}) collective-permute-start(bf16[128,768]{1,0:T(8,128)(2,1)S(1)} %get-tuple-element.250), channel_id=1, source_target_pairs={{0,16},{8,24},{16,0},{24,8},{1,17},{9,25},{17,1},{25,9},{2,18},{10... | collective-permute-start | bytes 589832 | tf_op jit(solution)/shard_map/ppermute | solution.py:493
  23.9 12.7 %collective-permute-start.18 = (bf16[128,768]{1,0:T(8,128)(2,1)S(1)}, bf16[128,768]{1,0:T(8,128)(2,1)S(1)}, u32[]{:S(2)}, u32[]{:S(2)}) collective-permute-start(bf16[128,768]{1,0:T(8,128)(2,1)S(1)} %get-tuple-element.251), channel_id=1, source_target_pairs={{0,16},{8,24},{16,0},{24,8},{1,17},{9,25},{17,1},{25,9},{2,18},{10... | collective-permute-start | bytes 589832 | tf_op jit(solution)/shard_map/ppermute | solution.py:493
  31.8 29.4 %collective-permute-start.16 = (bf16[120,1024]{1,0:T(8,128)(2,1)}, bf16[120,1024]{1,0:T(8,128)(2,1)S(1)}, u32[]{:S(2)}, u32[]{:S(2)}) collective-permute-start(bf16[120,1024]{1,0:T(8,128)(2,1)} %get-tuple-element.252), channel_id=1, source_target_pairs={{0,6},{1,7},{2,4},{3,5},{4,2},{5,3},{6,0},{7,1},{8,14},{9,15},{10,... | collective-permute-start | bytes 737288 | tf_op jit(solution)/shard_map/ppermute | solution.py:490
  35.3 25.9 %collective-permute-start.19 = (bf16[120,1024]{1,0:T(8,128)(2,1)}, bf16[120,1024]{1,0:T(8,128)(2,1)S(1)}, u32[]{:S(2)}, u32[]{:S(2)}) collective-permute-start(bf16[120,1024]{1,0:T(8,128)(2,1)} %get-tuple-element.260), channel_id=1, source_target_pairs={{0,7},{1,6},{2,5},{3,4},{4,3},{5,2},{6,1},{7,0},{8,15},{9,14},{10,... | collective-permute-start | bytes 737288 | tf_op jit(solution)/shard_map/ppermute | solution.py:490
  36.6 30.2 %collective-permute-start.21 = (bf16[120,1024]{1,0:T(8,128)(2,1)}, bf16[120,1024]{1,0:T(8,128)(2,1)}, u32[]{:S(2)}, u32[]{:S(2)}) collective-permute-start(bf16[120,1024]{1,0:T(8,128)(2,1)} %get-tuple-element.265), channel_id=1, source_target_pairs={{0,3},{1,2},{2,1},{3,0},{4,7},{5,6},{6,5},{7,4},{8,11},{9,10},{10,... | collective-permute-start | bytes 737288 | tf_op jit(solution)/shard_map/ppermute | solution.py:490
  36.6 3.6 %copy-start.27 = (bf16[120,1024]{1,0:T(8,128)(2,1)}, bf16[120,1024]{1,0:T(8,128)(2,1)S(1)}, u32[]{:S(2)}) copy-start(bf16[120,1024]{1,0:T(8,128)(2,1)S(1)} %get-tuple-element.102.refs_0_) | copy-start | bytes 737284 | tf_op jit(solution)/shard_map/cond
  40.1 1.8 %collective-permute-start.1 = (bf16[128,1536]{1,0:T(8,128)(2,1)S(1)}, bf16[128,1536]{1,0:T(8,128)(2,1)S(1)}, u32[]{:S(2)}, u32[]{:S(2)}) collective-permute-start(bf16[128,1536]{1,0:T(8,128)(2,1)S(1)} %get-tuple-element.92), channel_id=1, source_target_pairs={{0,8},{8,0},{16,24},{24,16},{1,9},{9,1},{17,25},{25,17},{2,10},{10... | collective-permute-start | bytes 1179656 | tf_op jit(solution)/shard_map/cond/branch_1_fun/ppermute | solution.py:493
  40.2 4.9 %copy-start.28 = (bf16[120,1024]{1,0:T(8,128)(2,1)S(1)}, bf16[120,1024]{1,0:T(8,128)(2,1)}, u32[]{:S(2)}) copy-start(bf16[120,1024]{1,0:T(8,128)(2,1)} %copy-done.27) | copy-start | bytes 737284 | tf_op jit(solution)/shard_map/cond
  42.0 11.2 %collective-permute-start.3 = (bf16[128,1536]{1,0:T(8,128)(2,1)S(1)}, bf16[128,1536]{1,0:T(8,128)(2,1)S(1)}, u32[]{:S(2)}, u32[]{:S(2)}) collective-permute-start(bf16[128,1536]{1,0:T(8,128)(2,1)S(1)} %total.4), channel_id=1, source_target_pairs={{0,16},{8,24},{16,0},{24,8},{1,17},{9,25},{17,1},{25,9},{2,18},{10... | collective-permute-start | bytes 1179656 | tf_op jit(solution)/shard_map/cond/branch_1_fun/ppermute | solution.py:493
  45.0 2.2 %collective-permute-start.2 = (bf16[128,1536]{1,0:T(8,128)(2,1)S(1)}, bf16[128,1536]{1,0:T(8,128)(2,1)S(1)}, u32[]{:S(2)}, u32[]{:S(2)}) collective-permute-start(bf16[128,1536]{1,0:T(8,128)(2,1)S(1)} %act.5.own), channel_id=1, source_target_pairs={{0,8},{8,0},{16,24},{24,16},{1,9},{9,1},{17,25},{25,17},{2,10},{10... | collective-permute-start | bytes 1179656 | tf_op jit(solution)/shard_map/cond/branch_1_fun/ppermute | solution.py:493
  47.2 7.1 %copy-start.6 = (f32[64,1536]{1,0:T(8,128)}, f32[64,1536]{1,0:T(8,128)S(1)}, u32[]{:S(2)}) copy-start(f32[64,1536]{1,0:T(8,128)S(1)} %get-tuple-element.352.next_keep) | copy-start | bytes 1179652 | tf_op jit(solution)/shard_map/cond
  47.3 7.0 %copy-start.4 = (bf16[128,1536]{1,0:T(8,128)(2,1)}, bf16[128,1536]{1,0:T(8,128)(2,1)S(1)}, u32[]{:S(2)}) copy-start(bf16[128,1536]{1,0:T(8,128)(2,1)S(1)} %collective-permute-done.2.core) | copy-start | bytes 1179652 | tf_op jit(solution)/shard_map/cond
  50.7 2.5 %collective-permute-start.4 = (bf16[64,1536]{1,0:T(8,128)(2,1)S(1)}, bf16[64,1536]{1,0:T(8,128)(2,1)S(1)}, u32[]{:S(2)}, u32[]{:S(2)}) collective-permute-start(bf16[64,1536]{1,0:T(8,128)(2,1)S(1)} %get-tuple-element.109), channel_id=1, source_target_pairs={{0,8},{8,0},{16,24},{24,16},{1,9},{9,1},{17,25},{25,17},{2,10},{10... | collective-permute-start | bytes 589832 | tf_op jit(solution)/shard_map/cond/branch_1_fun/ppermute | solution.py:493
  54.3 2.1 %collective-permute-start.5 = (bf16[128,1536]{1,0:T(8,128)(2,1)}, bf16[128,1536]{1,0:T(8,128)(2,1)}, u32[]{:S(2)}, u32[]{:S(2)}) collective-permute-start(bf16[128,1536]{1,0:T(8,128)(2,1)} %get-tuple-element.346.own), channel_id=1, source_target_pairs={{0,8},{8,0},{16,24},{24,16},{1,9},{9,1},{17,25},{25,17},{2,10},{10... | collective-permute-start | bytes 1179656 | tf_op jit(solution)/shard_map/cond/branch_1_fun/ppermute | solution.py:493
  56.3 3.3 %copy-start.3 = (bf16[128,1536]{1,0:T(8,128)(2,1)S(1)}, bf16[128,1536]{1,0:T(8,128)(2,1)}, u32[]{:S(2)}) copy-start(bf16[128,1536]{1,0:T(8,128)(2,1)} %copy-done.2) | copy-start | bytes 1179652 | tf_op jit(solution)/shard_map/cond
  56.4 3.3 %copy-start.5 = (bf16[128,1536]{1,0:T(8,128)(2,1)S(1)}, bf16[128,1536]{1,0:T(8,128)(2,1)}, u32[]{:S(2)}) copy-start(bf16[128,1536]{1,0:T(8,128)(2,1)} %copy-done.4) | copy-start | bytes 1179652 | tf_op jit(solution)/shard_map/cond
  56.4 3.2 %copy-start.7 = (f32[64,1536]{1,0:T(8,128)S(1)}, f32[64,1536]{1,0:T(8,128)}, u32[]{:S(2)}) copy-start(f32[64,1536]{1,0:T(8,128)} %copy-done.6) | copy-start | bytes 1179652 | tf_op jit(solution)/shard_map/cond
  56.4 3.2 %copy-start.11 = (bf16[128,1024]{1,0:T(8,128)(2,1)S(1)}, bf16[128,1024]{1,0:T(8,128)(2,1)}, u32[]{:S(2)}) copy-start(bf16[128,1024]{1,0:T(8,128)(2,1)} %copy-done.10) | copy-start | bytes 786436 | tf_op jit(solution)/shard_map/cond
  56.4 3.2 %copy-start.13 = (bf16[128,1024]{1,0:T(8,128)(2,1)S(1)}, bf16[128,1024]{1,0:T(8,128)(2,1)}, u32[]{:S(2)}) copy-start(bf16[128,1024]{1,0:T(8,128)(2,1)} %copy-done.12) | copy-start | bytes 786436 | tf_op jit(solution)/shard_map/cond
  59.6 7.6 %collective-permute-start.20 = (bf16[64,1536]{1,0:T(8,128)(2,1)}, bf16[64,1536]{1,0:T(8,128)(2,1)S(1)}, u32[]{:S(2)}, u32[]{:S(2)}) collective-permute-start(bf16[64,1536]{1,0:T(8,128)(2,1)} %get-tuple-element.263), channel_id=1, source_target_pairs={{0,16},{8,24},{16,0},{24,8},{1,17},{9,25},{17,1},{25,9},{2,18},{10... | collective-permute-start | bytes 589832 | tf_op jit(solution)/shard_map/ppermute | solution.py:493
  61.2 30.6 %collective-permute-start.27 = (bf16[120,1024]{1,0:T(8,128)(2,1)}, bf16[120,1024]{1,0:T(8,128)(2,1)S(1)}, u32[]{:S(2)}, u32[]{:S(2)}) collective-permute-start(bf16[120,1024]{1,0:T(8,128)(2,1)} %get-tuple-element.280), channel_id=1, source_target_pairs={{0,5},{1,4},{2,7},{3,6},{4,1},{5,0},{6,3},{7,2},{8,13},{9,12},{10,... | collective-permute-start | bytes 737288 | tf_op jit(solution)/shard_map/ppermute | solution.py:490
  66.1 25.6 %collective-permute-start.26 = (bf16[120,1024]{1,0:T(8,128)(2,1)}, bf16[120,1024]{1,0:T(8,128)(2,1)S(1)}, u32[]{:S(2)}, u32[]{:S(2)}) collective-permute-start(bf16[120,1024]{1,0:T(8,128)(2,1)} %get-tuple-element.278), channel_id=1, source_target_pairs={{0,4},{1,5},{2,6},{3,7},{4,0},{5,1},{6,2},{7,3},{8,12},{9,13},{10,... | collective-permute-start | bytes 737288 | tf_op jit(solution)/shard_map/ppermute | solution.py:490
  66.1 41.8 %collective-permute-start.30 = (bf16[120,1024]{1,0:T(8,128)(2,1)}, bf16[120,1024]{1,0:T(8,128)(2,1)S(1)}, u32[]{:S(2)}, u32[]{:S(2)}) collective-permute-start(bf16[120,1024]{1,0:T(8,128)(2,1)} %get-tuple-element.287), channel_id=1, source_target_pairs={{0,1},{1,0},{2,3},{3,2},{4,5},{5,4},{6,7},{7,6},{8,9},{9,8},{10,11... | collective-permute-start | bytes 737288 | tf_op jit(solution)/shard_map/ppermute | solution.py:490
  70.7 6.2 %copy-start.16 = (bf16[128,1024]{1,0:T(8,128)(2,1)}, bf16[128,1024]{1,0:T(8,128)(2,1)S(1)}, u32[]{:S(2)}) copy-start(bf16[128,1024]{1,0:T(8,128)(2,1)S(1)} %get-tuple-element.378.grads) | copy-start | bytes 786436 | tf_op jit(solution)/shard_map/cond
  70.7 1.8 %collective-permute-start.6 = (bf16[128,1536]{1,0:T(8,128)(2,1)S(1)}, bf16[128,1536]{1,0:T(8,128)(2,1)S(1)}, u32[]{:S(2)}, u32[]{:S(2)}) collective-permute-start(bf16[128,1536]{1,0:T(8,128)(2,1)S(1)} %get-tuple-element.128), channel_id=1, source_target_pairs={{0,8},{8,0},{16,24},{24,16},{1,9},{9,1},{17,25},{25,17},{2,10},{10... | collective-permute-start | bytes 1179656 | tf_op jit(solution)/shard_map/cond/branch_1_fun/ppermute | solution.py:493
  72.6 11.4 %collective-permute-start.8 = (bf16[128,1536]{1,0:T(8,128)(2,1)S(1)}, bf16[128,1536]{1,0:T(8,128)(2,1)S(1)}, u32[]{:S(2)}, u32[]{:S(2)}) collective-permute-start(bf16[128,1536]{1,0:T(8,128)(2,1)S(1)} %total.5), channel_id=1, source_target_pairs={{0,16},{8,24},{16,0},{24,8},{1,17},{9,25},{17,1},{25,9},{2,18},{10... | collective-permute-start | bytes 1179656 | tf_op jit(solution)/shard_map/cond/branch_1_fun/ppermute | solution.py:493
  74.3 2.7 %collective-permute-start.7 = (bf16[64,1536]{1,0:T(8,128)(2,1)S(1)}, bf16[64,1536]{1,0:T(8,128)(2,1)S(1)}, u32[]{:S(2)}, u32[]{:S(2)}) collective-permute-start(bf16[64,1536]{1,0:T(8,128)(2,1)S(1)} %act.7.own), channel_id=1, source_target_pairs={{0,8},{8,0},{16,24},{24,16},{1,9},{9,1},{17,25},{25,17},{2,10},{10... | collective-permute-start | bytes 589832 | tf_op jit(solution)/shard_map/cond/branch_1_fun/ppermute | solution.py:493
  76.9 8.0 %copy-start.8 = (f32[64,1536]{1,0:T(8,128)}, f32[64,1536]{1,0:T(8,128)S(1)}, u32[]{:S(2)}) copy-start(f32[64,1536]{1,0:T(8,128)S(1)} %get-tuple-element.385.next_keep) | copy-start | bytes 1179652 | tf_op jit(solution)/shard_map/cond
  77.0 8.0 %copy-start.18 = (bf16[64,1536]{1,0:T(8,128)(2,1)}, bf16[64,1536]{1,0:T(8,128)(2,1)S(1)}, u32[]{:S(2)}) copy-start(bf16[64,1536]{1,0:T(8,128)(2,1)S(1)} %collective-permute-done.7.core) | copy-start | bytes 589828 | tf_op jit(solution)/shard_map/cond
  80.2 1.5 %collective-permute-start.9 = (bf16[64,1536]{1,0:T(8,128)(2,1)S(1)}, bf16[64,1536]{1,0:T(8,128)(2,1)S(1)}, u32[]{:S(2)}, u32[]{:S(2)}) collective-permute-start(bf16[64,1536]{1,0:T(8,128)(2,1)S(1)} %get-tuple-element.142), channel_id=1, source_target_pairs={{0,8},{8,0},{16,24},{24,16},{1,9},{9,1},{17,25},{25,17},{2,10},{10... | collective-permute-start | bytes 589832 | tf_op jit(solution)/shard_map/cond/branch_1_fun/ppermute | solution.py:493
  81.8 5.2 %copy-start.19 = (bf16[64,1536]{1,0:T(8,128)(2,1)}, bf16[64,1536]{1,0:T(8,128)(2,1)S(1)}, u32[]{:S(2)}) copy-start(bf16[64,1536]{1,0:T(8,128)(2,1)S(1)} %collective-permute-done.9.next_core) | copy-start | bytes 589828 | tf_op jit(solution)/shard_map/cond
  85.0 2.1 %collective-permute-start.10 = (bf16[128,1536]{1,0:T(8,128)(2,1)}, bf16[128,1536]{1,0:T(8,128)(2,1)}, u32[]{:S(2)}, u32[]{:S(2)}) collective-permute-start(bf16[128,1536]{1,0:T(8,128)(2,1)} %get-tuple-element.379.own), channel_id=1, source_target_pairs={{0,8},{8,0},{16,24},{24,16},{1,9},{9,1},{17,25},{25,17},{2,10},{10... | collective-permute-start | bytes 1179656 | tf_op jit(solution)/shard_map/cond/branch_1_fun/ppermute | solution.py:493
  90.2 7.4 %collective-permute-start.23 = (bf16[64,1536]{1,0:T(8,128)(2,1)S(1)}, bf16[64,1536]{1,0:T(8,128)(2,1)S(1)}, u32[]{:S(2)}, u32[]{:S(2)}) collective-permute-start(bf16[64,1536]{1,0:T(8,128)(2,1)S(1)} %get-tuple-element.271), channel_id=1, source_target_pairs={{0,16},{8,24},{16,0},{24,8},{1,17},{9,25},{17,1},{25,9},{2,18},{10... | collective-permute-start | bytes 589832 | tf_op jit(solution)/shard_map/ppermute | solution.py:493
  91.8 25.4 %collective-permute-start.29 = (bf16[120,1024]{1,0:T(8,128)(2,1)}, bf16[120,1024]{1,0:T(8,128)(2,1)S(1)}, u32[]{:S(2)}, u32[]{:S(2)}) collective-permute-start(bf16[120,1024]{1,0:T(8,128)(2,1)} %get-tuple-element.283), channel_id=1, source_target_pairs={{0,7},{1,6},{2,5},{3,4},{4,3},{5,2},{6,1},{7,0},{8,15},{9,14},{10,... | collective-permute-start | bytes 737288 | tf_op jit(solution)/shard_map/ppermute | solution.py:490
  95.3 21.9 %collective-permute-start.28 = (bf16[120,1024]{1,0:T(8,128)(2,1)}, bf16[120,1024]{1,0:T(8,128)(2,1)S(1)}, u32[]{:S(2)}, u32[]{:S(2)}) collective-permute-start(bf16[120,1024]{1,0:T(8,128)(2,1)} %get-tuple-element.281), channel_id=1, source_target_pairs={{0,6},{1,7},{2,4},{3,5},{4,2},{5,3},{6,0},{7,1},{8,14},{9,15},{10,... | collective-permute-start | bytes 737288 | tf_op jit(solution)/shard_map/ppermute | solution.py:490
  95.6 23.1 %collective-permute-start.22 = (bf16[120,1024]{1,0:T(8,128)(2,1)}, bf16[120,1024]{1,0:T(8,128)(2,1)S(1)}, u32[]{:S(2)}, u32[]{:S(2)}) collective-permute-start(bf16[120,1024]{1,0:T(8,128)(2,1)} %get-tuple-element.268), channel_id=1, source_target_pairs={{0,2},{1,3},{2,0},{3,1},{4,6},{5,7},{6,4},{7,5},{8,10},{9,11},{10,... | collective-permute-start | bytes 737288 | tf_op jit(solution)/shard_map/ppermute | solution.py:490
  97.6 10.4 %copy-start = (s32[192,2]{0,1:T(2,128)S(1)}, s32[192,2]{0,1:T(2,128)}, u32[]{:S(2)}) copy-start(s32[192,2]{0,1:T(2,128)} %param.15) | copy-start | bytes 4612
  97.6 10.4 %copy-start.1 = (f32[192,2]{0,1:T(2,128)S(1)}, f32[192,2]{0,1:T(2,128)}, u32[]{:S(2)}) copy-start(f32[192,2]{0,1:T(2,128)} %param.16) | copy-start | bytes 4612
  98.4 3.8 %collective-permute-start.11 = (bf16[64,1536]{1,0:T(8,128)(2,1)}, bf16[64,1536]{1,0:T(8,128)(2,1)}, u32[]{:S(2)}, u32[]{:S(2)}) collective-permute-start(bf16[64,1536]{1,0:T(8,128)(2,1)} %act.9.own), channel_id=1, source_target_pairs={{0,8},{8,0},{16,24},{24,16},{1,9},{9,1},{17,25},{25,17},{2,10},{10... | collective-permute-start | bytes 589832 | tf_op jit(solution)/shard_map/cond/branch_1_fun/ppermute | solution.py:493
  105.0 5.4 %copy-start.23 = (bf16[64,1024]{1,0:T(8,128)(2,1)}, bf16[64,1024]{1,0:T(8,128)(2,1)S(1)}, u32[]{:S(2)}) copy-start(bf16[64,1024]{1,0:T(8,128)(2,1)S(1)} %get-tuple-element.309.refs_17_) | copy-start | bytes 393220
  105.0 5.4 %copy-start.24 = (bf16[64,1024]{1,0:T(8,128)(2,1)}, bf16[64,1024]{1,0:T(8,128)(2,1)S(1)}, u32[]{:S(2)}) copy-start(bf16[64,1024]{1,0:T(8,128)(2,1)S(1)} %get-tuple-element.310.refs_18_) | copy-start | bytes 393220
  105.0 13.7 %collective-permute-start.24 = (bf16[120,512]{1,0:T(8,128)(2,1)}, bf16[120,512]{1,0:T(8,128)(2,1)S(1)}, u32[]{:S(2)}, u32[]{:S(2)}) collective-permute-start(bf16[120,512]{1,0:T(8,128)(2,1)} %get-tuple-element.274), channel_id=1, source_target_pairs={{0,3},{1,2},{2,1},{3,0},{4,7},{5,6},{6,5},{7,4},{8,11},{9,10},{10,... | collective-permute-start | bytes 368648 | tf_op jit(solution)/shard_map/ppermute | solution.py:490
  107.9 10.8 %collective-permute-start.25 = (bf16[120,512]{1,0:T(8,128)(2,1)}, bf16[120,512]{1,0:T(8,128)(2,1)S(1)}, u32[]{:S(2)}, u32[]{:S(2)}) collective-permute-start(bf16[120,512]{1,0:T(8,128)(2,1)} %get-tuple-element.275), channel_id=1, source_target_pairs={{0,3},{1,2},{2,1},{3,0},{4,7},{5,6},{6,5},{7,4},{8,11},{9,10},{10,... | collective-permute-start | bytes 368648 | tf_op jit(solution)/shard_map/ppermute | solution.py:490
  (12 other events, 29.6 us)
